TPU v7x, 32 devices: a whole 2x2x4 slice. The times are simulated.
32 devices in a mesh: dp: 4 (over y, x), seq: 8 (over z, core).
Axes of the slice: x: 2, y: 2, z: 4, core: 2. Of those that a mesh axis runs over, the one named last changes fastest.
Arguments:
- tokens: bfloat16 [16384, 512], P(('dp', 'seq')), may hold values from -6 to 6
- cotangent: bfloat16 [16384, 512], P(('dp', 'seq')), may hold values from -6 to 6
- seq_lengths: int32 [4, 3], P('dp'), may hold values from 0 to 4096, as said below
- norm1_gain: float32 [512], replicated, may hold values from 0.5 to 1.5
- value_weight: bfloat16 [512, 1024], replicated, may hold values from -0.25 to 0.25
- ema_delta: float32 [512, 16], replicated, may hold values from -2 to 2
- ema_alpha: float32 [512, 16], replicated, may hold values from -30 to 0
- ema_beta: float32 [512, 16], replicated, may hold values from -9 to 9
- ema_eta: float32 [512, 16], replicated, may hold values from -5 to 5
- ema_omega: float32 [512], replicated, may hold values from -4 to 4
- mix_weight: bfloat16 [512, 2176], replicated, may hold values from -0.25 to 0.25
- qk_gain: float32 [2, 128], replicated, may hold values from -8 to 8
- qk_bias: float32 [2, 128], replicated, may hold values from -3 to 3
- rel_bias: float32 [128], replicated, may hold values from -4 to 4
- out_weight: bfloat16 [1024, 512], replicated, may hold values from -0.75 to 0.75
- norm2_gain: float32 [512], replicated, may hold values from 0.5 to 1.5
- ffn_in: bfloat16 [512, 1024], replicated, may hold values from -0.25 to 0.25
- ffn_out: bfloat16 [1024, 512], replicated, may hold values from -0.1875 to 0.1875
Outputs:
- block_out: float32 [16384, 512], P(('dp', 'seq'))
- input_grad: float32 [16384, 512], P(('dp', 'seq'))
- norm1_gain_grad: float32 [512], replicated
- value_weight_grad: float32 [512, 1024], replicated
- ema_delta_grad: float32 [512, 16], replicated
- ema_alpha_grad: float32 [512, 16], replicated
- ema_beta_grad: float32 [512, 16], replicated
- ema_eta_grad: float32 [512, 16], replicated
- ema_omega_grad: float32 [512], replicated
- mix_weight_grad: float32 [512, 2176], replicated
- qk_gain_grad: float32 [2, 128], replicated
- qk_bias_grad: float32 [2, 128], replicated
- rel_bias_grad: float32 [128], replicated
- out_weight_grad: float32 [1024, 512], replicated
- norm2_gain_grad: float32 [512], replicated
- ffn_in_grad: float32 [512, 1024], replicated
- ffn_out_grad: float32 [1024, 512], replicated
Inputs may be any that keep to these rules, and one draw needn't show every extreme that they name: `seq_lengths`: row g lists the lengths of group g's sequences in order, each a multiple of 128, summing to 4096, zeros after the last; one sequence of each group begins within the group's first 1024 tokens and ends within its last 1024. Some group holds a single sequence of 4096 tokens.
All inputs are finite; a program needn't handle non-finite values.
Results may differ from a plain program's by a relative error of at most 0.022.
Values sent between devices are 32-bit elements; how exact they have to be, the bound alone decides.
No kernel may reach another device: no remote copies, remote signals or barrier semaphores. Data moves between devices by JAX's collectives and lax.ppermute only.
A program may use at most 256 MiB of HBM per device.

v0:
```python
from functools import partial
import math

import jax
import jax.numpy as jnp
from jax import lax
from jax.sharding import PartitionSpec as P

SPAN = 128
TOK_DEV = 512


def prefix(part, axis, combine, identity, reverse):
    count = lax.axis_size(axis)
    place = lax.axis_index(axis)
    ahead = count - 1 - place if reverse else place
    gathered = jax.tree.map(lambda a: lax.all_gather(a, axis), part)
    state = jax.tree.map(lambda a, e: jnp.zeros_like(a) + jnp.asarray(e, a.dtype), part, identity)

    def one(step, state):
        source = count - 1 - step if reverse else step
        return combine(
            state, jax.tree.map(lambda a: lax.dynamic_index_in_dim(a, source, 0, False), gathered)
        )

    return lax.fori_loop(0, ahead, one, state)


def product_plain(operand, matrix):
    return jnp.dot(
        operand.astype(jnp.bfloat16),
        matrix.astype(jnp.bfloat16),
        preferred_element_type=jnp.float32,
    )


def project_keep(operand, matrix):
    low_operand = operand.astype(jnp.bfloat16)
    low_matrix = matrix.astype(jnp.bfloat16)
    return (
        jnp.dot(low_operand, low_matrix, preferred_element_type=jnp.float32),
        (low_operand, low_matrix),
    )


def project_back(saved, upstream):
    low_operand, low_matrix = saved
    lowrank_gradient = upstream.astype(jnp.bfloat16)
    return (
        jnp.dot(lowrank_gradient, low_matrix.T, preferred_element_type=jnp.float32),
        jnp.dot(low_operand.T, lowrank_gradient, preferred_element_type=jnp.float32),
    )


def rounded_product(operand, matrix):
    wrapped = jax.custom_vjp(product_plain)
    wrapped.defvjp(project_keep, project_back)
    return wrapped(operand, matrix)


def scores_plain(queries, key_rows):
    return jnp.einsum(
        "nqz,nkz->nqk",
        queries.astype(jnp.bfloat16),
        key_rows.astype(jnp.bfloat16),
        preferred_element_type=jnp.float32,
    )


def scores_keep(queries, key_rows):
    low_queries = queries.astype(jnp.bfloat16)
    low_keys = key_rows.astype(jnp.bfloat16)
    return (
        jnp.einsum("nqz,nkz->nqk", low_queries, low_keys, preferred_element_type=jnp.float32),
        (low_queries, low_keys),
    )


def scores_back(saved, upstream):
    low_queries, low_keys = saved
    lowrank_gradient = upstream.astype(jnp.bfloat16)
    return (
        jnp.einsum("nqk,nkz->nqz", lowrank_gradient, low_keys, preferred_element_type=jnp.float32),
        jnp.einsum(
            "nqk,nqz->nkz", lowrank_gradient, low_queries, preferred_element_type=jnp.float32
        ),
    )


def rounded_scores(queries, key_rows):
    wrapped = jax.custom_vjp(scores_plain)
    wrapped.defvjp(scores_keep, scores_back)
    return wrapped(queries, key_rows)


def mixing_plain(attention_weight_matrix, values):
    return jnp.einsum(
        "dlj,djh->dlh",
        attention_weight_matrix.astype(jnp.bfloat16),
        values.astype(jnp.bfloat16),
        preferred_element_type=jnp.float32,
    )


def values_keep(attention_weight_matrix, values):
    lowrank_weight_rows = attention_weight_matrix.astype(jnp.bfloat16)
    lowrank_value_rows = values.astype(jnp.bfloat16)
    return (
        jnp.einsum(
            "dlj,djh->dlh",
            lowrank_weight_rows,
            lowrank_value_rows,
            preferred_element_type=jnp.float32,
        ),
        (lowrank_weight_rows, lowrank_value_rows),
    )


def values_back(saved, upstream):
    lowrank_weight_rows, lowrank_value_rows = saved
    lowrank_gradient = upstream.astype(jnp.bfloat16)
    return (
        jnp.einsum(
            "mzb,mdb->mzd", lowrank_gradient, lowrank_value_rows, preferred_element_type=jnp.float32
        ),
        jnp.einsum(
            "hef,her->hfr",
            lowrank_weight_rows,
            lowrank_gradient,
            preferred_element_type=jnp.float32,
        ),
    )


def rounded_mix(attention_weight_matrix, values):
    wrapped = jax.custom_vjp(mixing_plain)
    wrapped.defvjp(values_keep, values_back)
    return wrapped(attention_weight_matrix, values)


def layer_norm(rows, gain):
    average = jnp.mean(rows, axis=-1, keepdims=True)
    centered = rows - average
    spread = jnp.mean(centered * centered, axis=-1, keepdims=True)
    return centered * lax.rsqrt(spread + 1e-05) * gain


def keep_log(ema_delta, ema_alpha):
    shares = jax.nn.sigmoid(ema_delta)
    return (shares, jnp.log1p(-shares * jax.nn.sigmoid(ema_alpha)))


def chain_step(earlier, later):
    return (earlier[0] * later[0], later[0] * earlier[1] + later[1])


def prepare(
    span_flags, tokens32, norm1_gain, value_weight, ema_delta, ema_alpha, ema_beta, ema_eta
):
    span_count = span_flags.shape[0]
    normed = layer_norm(tokens32, norm1_gain)
    values = jax.nn.silu(rounded_product(normed, value_weight))
    shares, log_keep = keep_log(ema_delta, ema_alpha)
    inflow = shares * ema_beta
    outflow = ema_eta / math.sqrt(ema_eta.shape[1])
    lag_steps = jnp.arange(SPAN).astype(jnp.float32)
    powers = jnp.exp(lag_steps[:, None, None] * log_keep)
    kernel = jnp.sum(powers * (inflow * outflow), axis=2)
    offsets = jnp.arange(SPAN)[:, None] - jnp.arange(SPAN)[None, :]
    toeplitz = jnp.where(
        (offsets >= 0)[:, :, None], jnp.take(kernel, jnp.maximum(offsets, 0), axis=0), 0.0
    )
    blocks = normed.reshape(span_count, SPAN, -1)
    within = jnp.einsum("tjd,njd->ntd", toeplitz, blocks, precision=lax.Precision.HIGHEST)
    tail_powers = powers[::-1] * inflow
    span_ends = jnp.einsum("njd,jdh->ndh", blocks, tail_powers, precision=lax.Precision.HIGHEST)
    span_keep = jnp.exp(SPAN * log_keep)
    running = jnp.zeros_like(log_keep)
    entering = []
    for block_number in range(span_count):
        running = running * (1.0 - span_flags[block_number])
        entering.append(running)
        running = span_keep * running + span_ends[block_number]
    reaching = jnp.prod(1.0 - span_flags)
    passing = jnp.exp(span_count * SPAN * log_keep) * reaching
    return (
        normed,
        values,
        within.reshape(-1, normed.shape[1]),
        jnp.stack(entering),
        running,
        passing,
    )


def finish(
    span_flags,
    tokens32,
    normed,
    values,
    within,
    entering,
    carry_in,
    ema_delta,
    ema_alpha,
    ema_eta,
    ema_omega,
    mix_weight,
    qk_gain,
    qk_bias,
    rel_bias,
    out_weight,
    norm2_gain,
    ffn_in,
    ffn_out,
):
    span_count = span_flags.shape[0]
    model_width = normed.shape[1]
    shared_width = qk_gain.shape[1]
    value_width = out_weight.shape[0]
    shares, log_keep = keep_log(ema_delta, ema_alpha)
    outflow = ema_eta / math.sqrt(ema_eta.shape[1])
    reaching = jnp.cumprod(1.0 - span_flags)
    span_starts = jnp.arange(span_count).astype(jnp.float32) * SPAN
    entry_decay = jnp.exp(span_starts[:, None, None] * log_keep) * reaching[:, None, None]
    states = entering + carry_in * entry_decay
    lag_steps = jnp.arange(SPAN).astype(jnp.float32)
    rise_powers = jnp.exp((lag_steps + 1.0)[:, None, None] * log_keep) * outflow
    carried_part = jnp.einsum("ndh,tdh->ntd", states, rise_powers, precision=lax.Precision.HIGHEST)
    smooth = within + carried_part.reshape(-1, model_width)
    smoothed = jax.nn.silu(smooth + ema_omega * normed)
    mixed_rows = rounded_product(smoothed, mix_weight)
    update = jax.nn.sigmoid(mixed_rows[:, :model_width])
    shared = jax.nn.silu(mixed_rows[:, model_width : model_width + shared_width])
    reset_gate = jax.nn.silu(
        mixed_rows[:, model_width + shared_width : model_width + shared_width + value_width]
    )
    candidate = mixed_rows[:, model_width + shared_width + value_width :]
    queries = (shared * qk_gain[0] + qk_bias[0]).reshape(span_count, SPAN, shared_width)
    key_rows = (shared * qk_gain[1] + qk_bias[1]).reshape(span_count, SPAN, shared_width)
    offsets = jnp.arange(SPAN)[:, None] - jnp.arange(SPAN)[None, :]
    causal = offsets >= 0
    bias_table = jnp.sum(
        jnp.where(offsets[:, :, None] == jnp.arange(SPAN)[None, None, :], rel_bias, 0.0), axis=2
    )
    scores = rounded_scores(queries, key_rows) * (1.0 / math.sqrt(shared_width)) + bias_table
    scores = jnp.where(causal, scores, -1e30)
    highest = jnp.max(scores, axis=-1, keepdims=True)
    powers = jnp.exp(scores - highest)
    attention_weight_matrix = powers / jnp.sum(powers, axis=-1, keepdims=True)
    attended = rounded_mix(
        attention_weight_matrix, values.reshape(span_count, SPAN, value_width)
    ).reshape(-1, value_width)
    hidden = jax.nn.silu(candidate + rounded_product(reset_gate * attended, out_weight))
    residual = tokens32 + update * (hidden - tokens32)
    expanded = jax.nn.silu(rounded_product(layer_norm(residual, norm2_gain), ffn_in))
    return residual + rounded_product(expanded, ffn_out)


def shards(
    tokens,
    cotangent,
    seq_lengths,
    norm1_gain,
    value_weight,
    ema_delta,
    ema_alpha,
    ema_beta,
    ema_eta,
    ema_omega,
    mix_weight,
    qk_gain,
    qk_bias,
    rel_bias,
    out_weight,
    norm2_gain,
    ffn_in,
    ffn_out,
):
    span_count = TOK_DEV // SPAN
    lengths = seq_lengths[0]
    begins = jnp.cumsum(lengths) - lengths
    positions = (
        lax.axis_index("seq") * span_count + jnp.arange(span_count, dtype=jnp.int32)
    ) * SPAN
    span_flags = jnp.any(
        (positions[:, None] == begins[None, :]) & (lengths > 0)[None, :], axis=1
    ).astype(jnp.float32)
    tokens32 = tokens.astype(jnp.float32)
    front_out, front_back = jax.vjp(
        partial(prepare, span_flags),
        tokens32,
        norm1_gain,
        value_weight.astype(jnp.float32),
        ema_delta,
        ema_alpha,
        ema_beta,
        ema_eta,
    )
    normed, values, within, entering, end_state, passing = front_out
    identity_pair = (jnp.ones_like(passing), jnp.zeros_like(end_state))
    carried = prefix((passing, end_state), "seq", chain_step, identity_pair, False)
    carry_in = carried[1]
    block_out, tail_back = jax.vjp(
        partial(finish, span_flags),
        tokens32,
        normed,
        values,
        within,
        entering,
        carry_in,
        ema_delta,
        ema_alpha,
        ema_eta,
        ema_omega,
        mix_weight.astype(jnp.float32),
        qk_gain,
        qk_bias,
        rel_bias,
        out_weight.astype(jnp.float32),
        norm2_gain,
        ffn_in.astype(jnp.float32),
        ffn_out.astype(jnp.float32),
    )
    tail_grads = tail_back(cotangent.astype(jnp.float32))
    state_later = prefix((passing, tail_grads[5]), "seq", chain_step, identity_pair, True)
    front_grads = front_back(
        (
            tail_grads[1],
            tail_grads[2],
            tail_grads[3],
            tail_grads[4],
            state_later[1],
            state_later[1] * carry_in,
        )
    )
    input_grad = front_grads[0] + tail_grads[0]
    local_grads = (
        front_grads[1],
        front_grads[2],
        front_grads[3] + tail_grads[6],
        front_grads[4] + tail_grads[7],
        front_grads[5],
        front_grads[6] + tail_grads[8],
        tail_grads[9],
        tail_grads[10],
        tail_grads[11],
        tail_grads[12],
        tail_grads[13],
        tail_grads[14],
        tail_grads[15],
        tail_grads[16],
        tail_grads[17],
    )
    summed = lax.psum(
        (
            local_grads[0],
            local_grads[1],
            local_grads[2],
            local_grads[3],
            local_grads[4],
            local_grads[5],
            local_grads[6],
            local_grads[7],
            local_grads[8],
            local_grads[9],
            local_grads[10],
            local_grads[11],
            local_grads[12],
            local_grads[13],
            local_grads[14],
        ),
        ("dp", "seq"),
    )
    return (
        block_out,
        input_grad,
        summed[0],
        summed[1],
        summed[2],
        summed[3],
        summed[4],
        summed[5],
        summed[6],
        summed[7],
        summed[8],
        summed[9],
        summed[10],
        summed[11],
        summed[12],
        summed[13],
        summed[14],
    )


def solution(mesh):
    in_specs = (
        P(("dp", "seq"), None),
        P(("dp", "seq"), None),
        P("dp", None),
        P(),
        P(),
        P(),
        P(),
        P(),
        P(),
        P(),
        P(),
        P(),
        P(),
        P(),
        P(),
        P(),
        P(),
        P(),
    )
    out_specs = (
        P(("dp", "seq"), None),
        P(("dp", "seq"), None),
        P(),
        P(),
        P(),
        P(),
        P(),
        P(),
        P(),
        P(),
        P(),
        P(),
        P(),
        P(),
        P(),
        P(),
        P(),
    )
    return jax.shard_map(shards, mesh=mesh, in_specs=in_specs, out_specs=out_specs, check_vma=False)
```

profile of v0, /device:TPU:0, one launch (start us, length us, event | category | flops | bytes accessed | tf_op | source)
XLA Modules:
  0.0 1082.6 jit_solution(2818659221027913783)
XLA Ops:
  16.9 2.3 fusion.61
  19.2 1.6 copy.281
  23.9 8.7 multiply_exponential_fusion.1
  33.7 69.4 %gather_fusion = f32[16384,512]{1,0:T(8,128)} fusion(f32[128,512]{1,0:T(8,128)S(1)} %copy.279, s32[16384]{0:T(1024)} %broadcast_clamp_fusion), kind=kCustom, calls=%fused_computation | custom fusion | bytes 67174400 | tf_op jit(solution)/shard_map/jvp(jit(_take))/gather | solution.py:171
  103.1 35.5 %copy.280 = f32[128,128,512]{1,0,2:T(8,128)} copy(f32[128,128,512]{2,1,0:T(8,128)} %bitcast.269) | data formatting | bytes 67108864 | tf_op jit(solution)/shard_map/jvp(jit(_take))/gather | solution.py:171
  140.0 7.2 rev.6
  148.1 9.4 fusion.23
  157.5 2.2 copy.285
  162.3 1.5 fusion.108
  165.7 16.1 %all-gather = f32[4096,16]{0,1:T(8,128)S(1)} all-gather(f32[512,16]{0,1:T(8,128)} %get-tuple-element.360), channel_id=2, replica_groups=mesh['dp'=4,'seq'=8] {'seq'}, dimensions={0}, use_global_device_ids=true | all-gather | bytes 294912 | tf_op jit(solution)/shard_map/all_gather | solution.py:17
  182.5 14.2 %all-gather.1 = f32[4096,16]{0,1:T(8,128)S(1)} all-gather(f32[512,16]{0,1:T(8,128)S(1)} %get-tuple-element.337), channel_id=3, replica_groups=mesh['dp'=4,'seq'=8] {'seq'}, dimensions={0}, use_global_device_ids=true | all-gather | bytes 294912 | tf_op jit(solution)/shard_map/all_gather | solution.py:17
  200.8 1.6 copy.282
  202.5 55.9 %fusion.47 = f32[4,128,512]{1,0,2:T(4,128)S(1)} fusion(f32[4,128,512]{1,0,2:T(4,128)S(1)} %copy.281, f32[128,128,512]{1,0,2:T(8,128)} %copy.280, pred[128,128]{1,0:T(8,128)(4,1)S(1)} %copy-done.59, pred[128,128]{1,0:T(8,128)(4,1)S(1)} %copy.275), kind=kOutput, calls=%fused_computation.89 | convolution fusion | flops 419430400 | bytes 35684352 | tf_op jit(solution)/shard_map/jvp(tjd,njd->ntd)/dot_general | solution.py:174
  258.5 6.4 fusion.57
  264.9 2.5 copy.326
  267.5 3.8 multiply_convert_fusion.2
  271.4 5.5 select_reduce_fusion.1
  277.1 1.7 multiply_convert_fusion.4
  285.8 2.5 fusion.27
  288.4 1.5 multiply_reduce_fusion.3
  296.1 3.0 fusion.69
  299.0 2.6 copy.296
  301.6 32.5 %fusion.1 = f32[512,4,128]{2,1,0:T(4,128)} fusion(f32[128,128,512]{1,0,2:T(8,128)} %copy.280, pred[128,128]{1,0:T(8,128)(4,1)} %copy.276, pred[128,128]{1,0:T(8,128)(4,1)S(1)} %copy.275, f32[4,128,512]{1,0,2:T(4,128)} %copy.296), kind=kOutput, calls=%fused_computation.10 | convolution fusion | flops 419430400 | bytes 35684352 | tf_op jit(solution)/shard_map/transpose(jvp(tjd,njd->ntd))/dot_general | solution.py:174
  334.1 9.0 fusion.17
  343.2 3.1 fusion.132
  347.0 56.6 %select_bitcast_fusion = f32[128,128,512]{1,0,2:T(8,128)} fusion(pred[128,128]{1,0:T(8,128)(4,1)S(1)} %copy.275, f32[4,128,512]{1,0,2:T(4,128)S(1)} %copy-done.4, f32[4,128,512]{1,0,2:T(4,128)S(1)} %copy-done.7), kind=kOutput, calls=%fused_computation.8 | convolution fusion | flops 411041792 | bytes 35667968 | tf_op jit(solution)/shard_map/transpose(jvp(tjd,njd->ntd))/dot_general | solution.py:174
  404.3 2.2 copy.297
  406.5 1.7 multiply_reduce_fusion.8
  408.3 1.6 copy.331
  409.9 35.5 %all-gather.2 = f32[4096,16]{1,0:T(8,128)} all-gather(f32[512,16]{1,0:T(8,128)} %copy.331), channel_id=4, replica_groups=mesh['dp'=4,'seq'=8] {'seq'}, dimensions={0}, use_global_device_ids=true | all-gather | bytes 294912 | tf_op jit(solution)/shard_map/all_gather | solution.py:17
  445.4 2.9 copy.301
  448.9 9.9 while.27
  460.4 1.4 add_bitcast_fusion
  461.9 2.2 copy.302
  464.1 13.4 %fusion.15 = (f32[512,16]{1,0:T(8,128)}, f32[128,512,16]{0,2,1:T(8,128)}) fusion(f32[128,512,16]{0,2,1:T(8,128)} %rev.6, f32[512,16]{1,0:T(8,128)S(1)} %copy-done.27, f32[512,16,4]{1,2,0:T(4,128)} %copy.302, f32[4,128,512]{1,0,2:T(4,128)} %copy-done.3), kind=kOutput, calls=%fused_computation.32 | convolution fusion | flops 53469184 | bytes 9633792 | tf_op jit(solution)/shard_map/transpose(jvp(njd,jdh->ndh))/dot_general | solution.py:176
  477.5 5.5 fusion.51
  483.0 2.6 copy.304
  485.6 1.9 bitcast_add_fusion.1
  487.8 2.5 fusion.32
  491.3 1.8 fusion.71
  493.8 7.2 rev.7
  501.0 34.8 %copy.329 = f32[128,128,512]{2,1,0:T(8,128)} copy(f32[128,128,512]{1,0,2:T(8,128)} %select_bitcast_fusion) | data formatting | bytes 67108864 | tf_op jit(solution)/shard_map/transpose(jvp(jit(_where)))/select_n | solution.py:170
  535.8 104.6 %scatter_custom_fusion = f32[128,512]{1,0:T(8,128)S(1)} fusion(s32[16384]{0:T(1024)} %maximum_bitcast_fusion, f32[16384,512]{1,0:T(8,128)} %bitcast.270, f32[]{:T(128)} %constant.128.clone.1), kind=kCustom, calls=%fused_computation.165 | custom fusion | flops 8388608 | bytes 262656 | tf_op jit(solution)/shard_map/transpose(jvp(jit(_take)))/scatter-add | solution.py:171
  641.3 17.5 %fusion.14 = (f32[512,16]{1,0:T(8,128)}, f32[512,16]{1,0:T(8,128)}, f32[512,16]{1,0:T(8,128)}, f32[512,16]{1,0:T(8,128)}) fusion(f32[128]{0:T(128)} %broadcast_add_fusion, f32[512,16]{1,0:T(8,128)} %copy.277, f32[512,16]{1,0:T(8,128)} %copy.282, f32[128,512,16]{0,2,1:T(8,128)} %rev.7, f32[512,16]{1,0:T(8,128)} %copy.278, f32[128,512]{0,1:T(8,128)} %copy.311, ...), kind=kOutput, calls=%fused_computation.29 | convolution fusion | flops 66027520 | bytes 5866496 | tf_op jit(solution)/shard_map/transpose(jvp(ndh,tdh->ntd))/dot_general | solution.py:229
  658.7 1.7 copy.312
  660.4 1.7 copy.316
  662.1 1.7 copy.314
  663.7 1.7 copy.318
  665.4 1.6 copy.319
  667.0 7.0 select_reduce_fusion
  674.0 2.8 fusion.64
  679.2 2.2 fusion.101
  681.4 1.6 fusion.128
  683.3 6.0 fusion.137
  689.4 2.1 fusion.85
  691.5 2.2 fusion.135
  693.7 2.1 fusion.139
  695.8 2.2 fusion.89
  698.7 3.9 add_add_fusion.2
  702.6 1.7 convolution_add_fusion.1
  704.3 103.1 %all-reduce.17.cloned.1.call-done = (f32[512]{0:T(512)}, f32[512,16]{0,1:T(8,128)}, f32[512,16]{0,1:T(8,128)}, f32[512,16]{0,1:T(8,128)}, f32[512,16]{0,1:T(8,12...) async-done(((f32[512]{0:T(512)}, f32[512,16]{0,1:T(8,128)}, f32[512,16]{0,1:T(8,128)}, f32[512,16]{0,1:T(8,128)}, ...) | async-done | bytes 139792 | tf_op jit(solution)/shard_map/psum | solution.py:355
  807.4 249.6 %all-reduce.19.cloned.1.call-done = (f32[512,1024]{1,0:T(8,128)}, f32[512,2176]{1,0:T(8,128)}, f32[1024,512]{1,0:T(8,128)}, f32[512,1024]{1,0:T(8,128)}, f32[1024,512]{1,0:T(8,128)}) async-done(((f32[512,1024]{1,0:T(8,128)}, f32[512,2176]{1,0:T(8,128)}, f32[1024,512]{1,0:T(8,128)}, f32[512,1024]{1,0:T(8,128)}, f32[1024,512]{1,0:T(8,128)}), (f32[512,1024]{1,0:T(8,128)}, f32[512,2176]{1,0:T(8,128)}, ...) | async-done | bytes 12845072 | tf_op jit(solution)/shard_map/psum | solution.py:355
  1058.4 3.2 copy.374
  1066.9 2.2 copy.380
  (329 shorter events, 68.5 us)
Async XLA Ops:
  7.2 271.6 %copy-start = (bf16[512,2176]{1,0:T(8,128)(2,1)S(1)}, bf16[512,2176]{1,0:T(8,128)(2,1)}, u32[]{:S(2)}) copy-start(bf16[512,2176]{1,0:T(8,128)(2,1)} %param.32) | copy-start | bytes 6684676
  7.2 13.6 %copy-start.70 = (f32[512,16]{0,1:T(8,128)S(1)}, f32[512,16]{0,1:T(8,128)}, u32[]{:S(2)}) copy-start(f32[512,16]{0,1:T(8,128)} %param.30) | copy-start | bytes 98308
  7.2 13.6 %copy-start.71 = (f32[512,16]{0,1:T(8,128)S(1)}, f32[512,16]{0,1:T(8,128)}, u32[]{:S(2)}) copy-start(f32[512,16]{0,1:T(8,128)} %param.29) | copy-start | bytes 98308
  7.2 13.6 %copy-start.60 = (f32[512,16]{0,1:T(8,128)S(1)}, f32[512,16]{0,1:T(8,128)}, u32[]{:S(2)}) copy-start(f32[512,16]{0,1:T(8,128)} %param.27) | copy-start | bytes 98308
  7.2 13.6 %copy-start.61 = (f32[512,16]{0,1:T(8,128)S(1)}, f32[512,16]{0,1:T(8,128)}, u32[]{:S(2)}) copy-start(f32[512,16]{0,1:T(8,128)} %param.28) | copy-start | bytes 98308
  7.3 800.2 %all-reduce.17.cloned.1.call-start = ((), (), s32[]{:S(2)}) async-start(), calls=%async_computation | async-start | bytes 279552 | tf_op jit(solution)/shard_map/psum | solution.py:355
  7.3 25.3 %copy-start.107 = (f32[128]{0:T(128)}, f32[128]{0:T(128)S(1)}, u32[]{:S(2)}) copy-start(f32[128]{0:T(128)S(1)} %iota_convert_fusion) | copy-start | bytes 1540
  20.8 181.6 %copy-start.3 = (f32[4,128,512]{1,0,2:T(4,128)}, f32[4,128,512]{1,0,2:T(4,128)S(1)}, u32[]{:S(2)}) copy-start(f32[4,128,512]{1,0,2:T(4,128)S(1)} %copy.281) | copy-start | bytes 3145732
  22.2 10.4 copy-start.28
  103.1 36.2 %copy-start.52 = (pred[128,128]{0,1:T(8,128)(4,1)S(1)}, pred[128,128]{0,1:T(8,128)(4,1)}, u32[]{:S(2)}) copy-start(pred[128,128]{0,1:T(8,128)(4,1)} %fusion.99) | copy-start | bytes 49156
  103.1 36.3 %copy-start.92 = (f32[4]{0:T(128)S(1)}, f32[4]{0:T(128)}, u32[]{:S(2)}) copy-start(f32[4]{0:T(128)} %convert_element_type.118) | copy-start | bytes 52
  148.1 33.7 %copy-start.26 = (f32[512,16]{1,0:T(8,128)}, f32[512,16]{1,0:T(8,128)S(1)}, u32[]{:S(2)}) copy-start(f32[512,16]{1,0:T(8,128)S(1)} %copy.283) | copy-start | bytes 98308
  181.7 20.7 %copy-start.59 = (pred[128,128]{1,0:T(8,128)(4,1)S(1)}, pred[128,128]{1,0:T(8,128)(4,1)}, u32[]{:S(2)}) copy-start(pred[128,128]{1,0:T(8,128)(4,1)} %copy.276) | copy-start | bytes 49156
  197.7 4.7 copy-start.30
  202.4 56.0 %copy-start.43 = (f32[512,16]{1,0:T(8,128)S(1)}, f32[512,16]{1,0:T(8,128)}, u32[]{:S(2)}) copy-start(f32[512,16]{1,0:T(8,128)} %copy.277) | copy-start | bytes 98308
  202.4 56.0 %copy-start.46 = (f32[4,512,16]{2,0,1:T(4,128)S(1)}, f32[4,512,16]{2,0,1:T(4,128)}, u32[]{:S(2)}) copy-start(f32[4,512,16]{2,0,1:T(4,128)} %copy.288) | copy-start | bytes 393220
  202.4 56.0 %copy-start.62 = (f32[512,16]{1,0:T(8,128)S(1)}, f32[512,16]{1,0:T(8,128)}, u32[]{:S(2)}) copy-start(f32[512,16]{1,0:T(8,128)} %copy.282) | copy-start | bytes 98308
  202.5 56.0 %copy-start.111 = (f32[128]{0:T(128)S(1)}, f32[128]{0:T(128)}, u32[]{:S(2)}) copy-start(f32[128]{0:T(128)} %broadcast_add_fusion) | copy-start | bytes 1540
  258.4 9.0 copy-start.2
  258.4 9.0 copy-start.67
  258.4 9.0 copy-start.72
  258.4 9.0 copy-start.76
  267.5 9.6 copy-start.96
  271.4 8.9 copy-start.55
  280.3 15.0 %copy-start.5 = (f32[512,2176]{1,0:T(8,128)}, f32[512,2176]{1,0:T(8,128)S(1)}, u32[]{:S(2)}) copy-start(f32[512,2176]{1,0:T(8,128)S(1)} %fusion.153) | copy-start | bytes 13369348
  280.7 12.9 %copy-start.79 = (f32[4,128]{1,0:T(4,128)}, f32[4,128]{1,0:T(4,128)S(1)}, u32[]{:S(2)}) copy-start(f32[4,128]{1,0:T(4,128)S(1)} %get-tuple-element.374) | copy-start | bytes 6148
  280.8 12.8 %copy-start.80 = (f32[4,128]{1,0:T(4,128)}, f32[4,128]{1,0:T(4,128)S(1)}, u32[]{:S(2)}) copy-start(f32[4,128]{1,0:T(4,128)S(1)} %fusion.95) | copy-start | bytes 6148
  284.1 5.8 copy-start.10
  284.1 5.8 copy-start.84
  284.6 5.3 copy-start.90
  291.4 4.6 copy-start.24
  291.4 4.6 copy-start.47
  292.9 6.1 copy-start.113
  301.6 32.5 %copy-start.6 = (f32[4,128,512]{1,0,2:T(4,128)S(1)}, f32[4,128,512]{1,0,2:T(4,128)}, u32[]{:S(2)}) copy-start(f32[4,128,512]{1,0,2:T(4,128)} %copy.296) | copy-start | bytes 3145732
  301.6 32.5 %copy-start.44 = (f32[512,16]{1,0:T(8,128)S(1)}, f32[512,16]{1,0:T(8,128)}, u32[]{:S(2)}) copy-start(f32[512,16]{1,0:T(8,128)} %copy.277) | copy-start | bytes 98308
  301.6 32.5 %copy-start.63 = (f32[512,16]{1,0:T(8,128)S(1)}, f32[512,16]{1,0:T(8,128)}, u32[]{:S(2)}) copy-start(f32[512,16]{1,0:T(8,128)} %copy.282) | copy-start | bytes 98308
  301.6 32.5 %copy-start.112 = (f32[128]{0:T(128)S(1)}, f32[128]{0:T(128)}, u32[]{:S(2)}) copy-start(f32[128]{0:T(128)} %broadcast_add_fusion) | copy-start | bytes 1540
  347.0 56.7 %copy-start.20 = (f32[4,128,128]{1,2,0:T(8,128)S(1)}, f32[4,128,128]{1,2,0:T(8,128)}, u32[]{:S(2)}) copy-start(f32[4,128,128]{1,2,0:T(8,128)} %copy-done.19) | copy-start | bytes 786436
  347.0 56.7 %copy-start.51 = (pred[4,128,128]{1,2,0:T(32,128)(4,1)S(1)}, pred[4,128,128]{1,2,0:T(32,128)(4,1)}, u32[]{:S(2)}) copy-start(pred[4,128,128]{1,2,0:T(32,128)(4,1)} %copy-done.50) | copy-start | bytes 196612
  347.0 56.7 %copy-start.54 = (pred[128,128]{0,1:T(8,128)(4,1)S(1)}, pred[128,128]{0,1:T(8,128)(4,1)}, u32[]{:S(2)}) copy-start(pred[128,128]{0,1:T(8,128)(4,1)} %fusion.99) | copy-start | bytes 49156
  347.0 56.7 %copy-start.82 = (f32[4,128]{1,0:T(4,128)S(1)}, f32[4,128]{1,0:T(4,128)}, u32[]{:S(2)}) copy-start(f32[4,128]{1,0:T(4,128)} %copy-done.81) | copy-start | bytes 6148
  406.5 57.6 %copy-start.27 = (f32[512,16]{1,0:T(8,128)S(1)}, f32[512,16]{1,0:T(8,128)}, u32[]{:S(2)}) copy-start(f32[512,16]{1,0:T(8,128)} %copy-done.26) | copy-start | bytes 98308
  464.1 13.4 %copy-start.1 = (f32[128,512,16]{0,2,1:T(8,128)S(1)}, f32[128,512,16]{0,2,1:T(8,128)}, u32[]{:S(2)}) copy-start(f32[128,512,16]{0,2,1:T(8,128)} %rev.6) | copy-start | bytes 12582916
  464.1 13.4 %copy-start.14 = (f32[512,16,4]{1,2,0:T(4,128)S(1)}, f32[512,16,4]{1,2,0:T(4,128)}, u32[]{:S(2)}) copy-start(f32[512,16,4]{1,2,0:T(4,128)} %copy.302) | copy-start | bytes 393220
  464.1 13.4 %copy-start.16 = (f32[512,4,128]{2,1,0:T(4,128)S(1)}, f32[512,4,128]{2,1,0:T(4,128)}, u32[]{:S(2)}) copy-start(f32[512,4,128]{2,1,0:T(4,128)} %fusion.1) | copy-start | bytes 3145732
  477.5 8.0 copy-start.98
  485.5 5.7 copy-start.38
  485.5 5.7 copy-start.69
  485.5 5.7 copy-start.74
  487.8 5.3 copy-start.89
  487.8 5.3 copy-start.45
  641.2 32.8 %copy-start.78 = (f32[512]{0:T(512)S(1)}, f32[512]{0:T(512)}, u32[]{:S(2)}) copy-start(f32[512]{0:T(512)} %copy-done.75) | copy-start | bytes 6148
  641.2 37.9 %copy-start.29 = (f32[512,16]{0,1:T(8,128)S(1)}, f32[512,16]{0,1:T(8,128)}, u32[]{:S(2)}) copy-start(f32[512,16]{0,1:T(8,128)} %copy-done.28) | copy-start | bytes 98308
  641.2 37.9 %copy-start.31 = (f32[512,16]{0,1:T(8,128)S(1)}, f32[512,16]{0,1:T(8,128)}, u32[]{:S(2)}) copy-start(f32[512,16]{0,1:T(8,128)} %copy-done.30) | copy-start | bytes 98308
  641.2 37.9 %copy-start.32 = (f32[512,16]{0,1:T(8,128)S(1)}, f32[512,16]{0,1:T(8,128)}, u32[]{:S(2)}) copy-start(f32[512,16]{0,1:T(8,128)} %get-tuple-element.146) | copy-start | bytes 98308
  641.2 37.9 %copy-start.37 = (f32[512,4,16]{0,2,1:T(8,128)S(1)}, f32[512,4,16]{0,2,1:T(8,128)}, u32[]{:S(2)}) copy-start(f32[512,4,16]{0,2,1:T(8,128)} %copy.297) | copy-start | bytes 393220
  641.3 37.9 %copy-start.57 = (f32[512,16]{0,1:T(8,128)S(1)}, f32[512,16]{0,1:T(8,128)}, u32[]{:S(2)}) copy-start(f32[512,16]{0,1:T(8,128)} %copy-done.56) | copy-start | bytes 98308
  683.0 374.0 %all-reduce.19.cloned.1.call-start = ((), (), s32[]{:S(2)}) async-start(), calls=%async_computation.1 | async-start | bytes 25690112 | tf_op jit(solution)/shard_map/psum | solution.py:355
  683.3 6.1 copy-start.22
  683.3 6.1 copy-start.25
  698.1 4.5 copy-start.12
  807.4 258.3 %copy-start.83 = (f32[512,16]{0,1:T(8,128)S(1)}, f32[512,16]{0,1:T(8,128)}, u32[]{:S(2)}) copy-start(f32[512,16]{0,1:T(8,128)} %get-tuple-element.511) | copy-start | bytes 98308
  807.4 258.9 %copy-start.101 = (f32[512]{0:T(512)S(1)}, f32[512]{0:T(512)}, u32[]{:S(2)}) copy-start(f32[512]{0:T(512)} %get-tuple-element.512) | copy-start | bytes 6148
  1057.0 9.9 copy-start.18
  (54 other events, 139.8 us)
Sparse Core Ops, SparseCore 0:
  683.1 124.2 all-reduce.16
  816.7 240.2 all-reduce.18
where the time goes:
time: 1090 us; the launch traced here: 1080 us
  waiting for transfers between devices  353 us (32%)
  matrix products  246 us (23%)
  local copies, waits for them, and re-layouts  217 us (20%)
  other arithmetic  182 us (17%)
  blocking collectives  65.8 us (6%)
  between operations  18.4 us (2%)
    psum x2, waiting for transfers between devices, shards(): lax.psum((local_grads[0], local_grads[1], local_grads[2], local_grads[3],...  353 us
    dot_general x3, matrix products, prepare(): jnp.einsum('tjd,njd->ntd', toeplitz, blocks, precision=lax.Precision.HIGH...  145 us
    gather x2, local copies, waits for them, and re-layouts, prepare(): jnp.take(kernel, jnp.maximum(offsets, 0), axis=0)  105 us
    scatter-add x1, other arithmetic, prepare(): jnp.take(kernel, jnp.maximum(offsets, 0), axis=0)  105 us
    all_gather x3, blocking collectives, prefix(): gathered = jax.tree.map(lambda a: lax.all_gather(a, axis), part)  65.8 us
    select_n x1, local copies, waits for them, and re-layouts, prepare(): jnp.where((offsets >= 0)[:, :, None], jnp.take(kernel, jnp.maximum(offset...  34.8 us
    dot_general x3, matrix products, finish(): jnp.einsum('ndh,tdh->ntd', states, rise_powers, precision=lax.Precision.H...  33 us
    dot_general x3, matrix products, prepare(): jnp.einsum('njd,jdh->ndh', blocks, tail_powers, precision=lax.Precision.H...  28.2 us
  transfers between devices with their start and end apart: 2, of which 2 were waited for; matrix products, arithmetic and copies ran while one was open for 2% of the time, Pallas kernels for 0%

commit v1 on v0

v1 whole, which is shorter than its diff:
```python
import math

import jax
import jax.numpy as jnp
from jax import lax
from jax.experimental import pallas as pl
from jax.experimental.pallas import tpu as pltpu
from jax.sharding import PartitionSpec as P

SPAN = 128
CHUNK = 64
EPS = 1e-05
BF16 = jnp.bfloat16
F32 = jnp.float32
VMEM_LIMIT = 58 * 1024 * 1024


def sigmoid(a):
    return 0.5 * jnp.tanh(0.5 * a) + 0.5


def mm(a, b):
    return lax.dot_general(a, b, (((1,), (0,)), ((), ())), preferred_element_type=F32)


def mm_nt(a, b):
    return lax.dot_general(a, b, (((1,), (1,)), ((), ())), preferred_element_type=F32)


def mm_tn(a, b):
    return lax.dot_general(a, b, (((0,), (0,)), ((), ())), preferred_element_type=F32)


def call(body, ins, outs, scratch=(), flops=0, name=None):
    specs = []
    for a in ins:
        if a.dtype == jnp.int32:
            specs.append(pl.BlockSpec(memory_space=pltpu.SMEM))
        else:
            specs.append(pl.BlockSpec(memory_space=pltpu.VMEM))
    moved = sum(a.size * a.dtype.itemsize for a in ins)
    moved += sum(math.prod(s) * jnp.dtype(d).itemsize for s, d in outs)
    return pl.pallas_call(
        body,
        in_specs=specs,
        out_specs=[pl.BlockSpec(memory_space=pltpu.VMEM)] * len(outs),
        out_shape=[jax.ShapeDtypeStruct(s, d) for s, d in outs],
        scratch_shapes=[pltpu.VMEM(s, d) for s, d in scratch],
        compiler_params=pltpu.CompilerParams(vmem_limit_bytes=VMEM_LIMIT),
        cost_estimate=pl.CostEstimate(flops=int(flops), bytes_accessed=int(moved), transcendentals=0),
        name=name,
    )(*ins)


def clear_range(meta, low, high):
    count = meta.shape[0] - 1
    begin = jnp.int32(0)
    hit = jnp.bool_(False)
    for i in range(count):
        length = meta[1 + i]
        hit = hit | ((length > 0) & (begin >= low) & (begin < high))
        begin = begin + length
    return jnp.where(hit, 0.0, 1.0).astype(F32)


def chunk_masks(meta, first, chunks):
    rows = lax.broadcasted_iota(jnp.int32, (chunks, 128), 0)
    free = jnp.ones((chunks, 128), F32)
    for s in range(0, chunks, SPAN // CHUNK):
        position = first + s * CHUNK
        free = jnp.where(rows == s, clear_range(meta, position, position + 1), free)
    return free


def lanes_of(tile):
    return pl.ds(tile * 128, 128)


def tiled(ref):
    return jnp.concatenate([ref[i] for i in range(ref.shape[0])], axis=1)


def put_tiled(ref, value):
    for i in range(ref.shape[0]):
        ref[i] = value[:, i * 128 : (i + 1) * 128]


def scan_step(masks, values, decay_row, shifts, chunks):
    power = decay_row
    for i, mask in enumerate(masks):
        values = values + power * (mask * pltpu.roll(values, shifts[i], 0))
        power = power * power
    return values


def doubling_masks(mask, chunks, backward):
    masks = []
    distance = 1
    while distance < chunks:
        masks.append(mask)
        shift = chunks - distance if backward else distance
        mask = mask * pltpu.roll(mask, shift, 0)
        distance *= 2
    shifts = []
    distance = 1
    while distance < chunks:
        shifts.append(chunks - distance if backward else distance)
        distance *= 2
    return masks, shifts


def edge_masks(free, chunks, backward):
    rows = lax.broadcasted_iota(jnp.int32, (chunks, 128), 0)
    if backward:
        return jnp.where(rows == chunks - 1, 0.0, pltpu.roll(free, chunks - 1, 0))
    return jnp.where(rows == 0, 0.0, free)


def prefix_mask(free, chunks, backward):
    rows = lax.broadcasted_iota(jnp.int32, (chunks, 128), 0)
    if backward:
        reach = jnp.where(rows == chunks - 1, 1.0, pltpu.roll(free, chunks - 1, 0))
    else:
        reach = free
    distance = 1
    while distance < chunks:
        if backward:
            moved = jnp.where(rows >= chunks - distance, 1.0, pltpu.roll(reach, chunks - distance, 0))
        else:
            moved = jnp.where(rows < distance, 1.0, pltpu.roll(reach, distance, 0))
        reach = reach * moved
        distance *= 2
    return reach


def start_body(meta, tok, gain, delta, alpha, beta, eta, normed, low, enter, end, logk, keep, mix):
    tokens, width = tok.shape
    hidden = delta.shape[1]
    chunks = tokens // CHUNK
    x = tok[...].astype(F32)
    centered = x - jnp.mean(x, axis=1, keepdims=True)
    spread = jnp.mean(centered * centered, axis=1, keepdims=True)
    rows = centered * lax.rsqrt(spread + EPS) * gain[...]
    put_tiled(normed, rows)
    low[...] = rows.astype(BF16)
    share = jax.nn.sigmoid(delta[...].T)
    log_keep = jnp.log1p(-share * jax.nn.sigmoid(alpha[...].T))
    logk[...] = log_keep
    keep[...] = jnp.exp(log_keep)
    mix[...] = share * beta[...].T * (eta[...].T * (1.0 / math.sqrt(hidden)))
    free = chunk_masks(meta, meta[0] * tokens, chunks)
    edge = edge_masks(free, chunks, False)
    masks, shifts = doubling_masks(edge, chunks, False)
    for tile in range(width // 128):
        lanes = lanes_of(tile)
        keeps = [keep[h : h + 1, lanes] for h in range(hidden)]

        def step(t, state):
            value = normed[tile, pl.ds(t, chunks, stride=CHUNK), :]
            return tuple(k * u + value for k, u in zip(keeps, state))

        zero = jnp.zeros((chunks, 128), F32)
        state = lax.fori_loop(0, CHUNK, step, (zero,) * hidden, unroll=8)
        for h in range(hidden):
            decay = jnp.exp(CHUNK * logk[h : h + 1, lanes])
            reached = scan_step(masks, state[h], decay, shifts, chunks)
            enter[h, :, lanes] = edge * pltpu.roll(reached, 1, 0)
            end[h : h + 1, lanes] = reached[chunks - 1 : chunks]


def values_body(low, weight, values, slope):
    blocks = weight.shape[1] // 256
    for b in range(blocks):
        cols = pl.ds(b * 256, 256)
        raw = mm(low[...], weight[:, cols])
        gate = sigmoid(raw)
        out = raw * gate
        values[:, cols] = out.astype(BF16)
        slope[:, cols] = gate + out * (1.0 - gate)


def pair_body(backward, tokens, meta, own, other, logk, out):
    core = meta[0] % 2
    first = (meta[0] - core) * tokens
    middle = first + tokens
    decay = jnp.exp(tokens * logk[...])
    if backward:
        reach = clear_range(meta, first + 1, middle + 1)
        near = jnp.where(core == 0, own[...], other[...])
        far = jnp.where(core == 0, other[...], own[...])
    else:
        reach = clear_range(meta, middle, middle + tokens)
        near = jnp.where(core == 0, other[...], own[...])
        far = jnp.where(core == 0, own[...], other[...])
    out[...] = near + (reach * decay) * far


def carry_of(backward, tokens, meta, other, arrived, logk):
    core = meta[0] % 2
    first = (meta[0] - core) * tokens
    span = 2 * tokens
    chip_decay = jnp.exp(span * logk[...])
    total = None
    power = None
    for k, part in enumerate(arrived):
        if backward:
            reach = clear_range(meta, first + span, first + (k + 1) * span + 1)
        else:
            reach = clear_range(meta, first - k * span, first)
        term = part[...] * reach
        if power is not None:
            term = term * power
        total = term if total is None else total + term
        power = chip_decay if power is None else power * chip_decay
    decay = jnp.exp(tokens * logk[...])
    middle = first + tokens
    if backward:
        crossing = clear_range(meta, middle, middle + 1)
        through = clear_range(meta, middle + 1, middle + tokens)
        passed = crossing * (other[...] + (through * decay) * total)
        return jnp.where(core == 0, passed, total)
    through = clear_range(meta, first, middle)
    return jnp.where(core == 0, total, other[...] + (through * decay) * total)


def layer_grad(weighted, normal, inverse):
    mean_one = jnp.mean(weighted, axis=1, keepdims=True)
    mean_two = jnp.mean(weighted * normal, axis=1, keepdims=True)
    return (weighted - mean_one - normal * mean_two) * inverse


def shift_rows(table, down):
    size = table.shape[0]
    rows = lax.broadcasted_iota(jnp.int32, table.shape, 0)
    bit = 1
    while bit < size:
        moved = pltpu.roll(table, bit if down else size - bit, 1)
        table = jnp.where((rows & bit) != 0, moved, table)
        bit *= 2
    return table


def forward_body(
    chips,
    meta,
    tok,
    cot,
    normed,
    enter,
    other,
    *rest,
):
    arrived = rest[:chips]
    (
        logk,
        keep,
        mix,
        omega,
        mix_weight,
        qk_gain,
        qk_bias,
        rel_rev,
        values,
        out_weight,
        gain2,
        ffn_in,
        ffn_out,
        block_out,
        kept,
        sent,
        states,
        slope_pre,
        low_smoothed,
        update_grad,
        reset_raw,
        attended,
        weights,
        queries,
        keys,
        shared,
        shared_slope,
        out_grad,
        input_part,
        gain2_grad,
        carry,
        smooth,
        update,
        candidate,
        gated,
        expanded,
        slope_exp,
        normal2,
        expand_grad,
    ) = rest[chips:]
    tokens, width = tok.shape
    hidden = mix.shape[0]
    chunks = tokens // CHUNK
    shared_width = qk_gain.shape[1]
    value_width = out_weight.shape[0]
    core = meta[0] % 2
    carry[...] = carry_of(False, tokens, meta, other, arrived, logk)
    free = chunk_masks(meta, meta[0] * tokens, chunks)
    reach = prefix_mask(free, chunks, False)
    offset = (lax.broadcasted_iota(jnp.int32, (chunks, 128), 0) * CHUNK).astype(F32)
    for tile in range(width // 128):
        lanes = lanes_of(tile)
        state = []
        for h in range(hidden):
            entry = jnp.exp(offset * logk[h : h + 1, lanes]) * reach
            first = enter[h, :, lanes] + carry[h : h + 1, lanes] * entry
            states[h, :, lanes] = first
            state.append(first)
        keeps = [keep[h : h + 1, lanes] for h in range(hidden)]
        mixes = [mix[h : h + 1, lanes] for h in range(hidden)]

        def step(t, state):
            place = (tile, pl.ds(t, chunks, stride=CHUNK), slice(None))
            value = normed[place]
            state = tuple(k * u + value for k, u in zip(keeps, state))
            parts = [c * u for c, u in zip(mixes, state)]
            while len(parts) > 1:
                parts = [a + b for a, b in zip(parts[::2], parts[1::2])]
            smooth[place] = parts[0]
            return state

        lax.fori_loop(0, CHUNK, step, tuple(state), unroll=4)
    pre = tiled(smooth) + omega[...] * tiled(normed)
    gate = sigmoid(pre)
    smoothed = pre * gate
    low_smoothed[...] = smoothed.astype(BF16)
    slope_pre[...] = gate + smoothed * (1.0 - gate)
    base = width + shared_width
    for b in range(width // 256):
        cols = pl.ds(b * 256, 256)
        update[:, cols] = sigmoid(mm(low_smoothed[...], mix_weight[:, cols]))
    raw = mm(low_smoothed[...], mix_weight[:, width:base])
    gate = sigmoid(raw)
    silu = raw * gate
    shared[...] = silu
    shared_slope[...] = gate + silu * (1.0 - gate)
    queries[...] = (silu * qk_gain[0:1] + qk_bias[0:1]).astype(BF16)
    keys[...] = (silu * qk_gain[1:2] + qk_bias[1:2]).astype(BF16)
    for b in range(value_width // 256):
        reset_raw[:, b * 256 : (b + 1) * 256] = mm(
            low_smoothed[...], mix_weight[:, base + b * 256 : base + (b + 1) * 256]
        )
    for b in range(width // 256):
        low = base + value_width + b * 256
        candidate[:, b * 256 : (b + 1) * 256] = mm(low_smoothed[...], mix_weight[:, low : low + 256])
    place = lax.broadcasted_iota(jnp.int32, (SPAN, SPAN), 0)
    causal = place >= lax.broadcasted_iota(jnp.int32, (SPAN, SPAN), 1)
    bias = shift_rows(jnp.broadcast_to(rel_rev[...], (SPAN, SPAN)), True)
    scale = 1.0 / math.sqrt(shared_width)
    for s in range(tokens // SPAN):
        rows = pl.ds(s * SPAN, SPAN)
        scores = mm_nt(queries[rows, :], keys[rows, :]) * scale + bias
        scores = jnp.where(causal, scores, -1e30)
        powers = jnp.exp(scores - jnp.max(scores, axis=1, keepdims=True))
        share = powers / jnp.sum(powers, axis=1, keepdims=True)
        weights[rows, :] = share
        attended[rows, :] = mm(share.astype(BF16), values[rows, :])
    for b in range(value_width // 256):
        cols = pl.ds(b * 256, 256)
        raw = reset_raw[:, cols]
        gated[:, cols] = (raw * sigmoid(raw) * attended[:, cols]).astype(BF16)
    total = candidate[...] + mm(gated[...], out_weight[...])
    gate = sigmoid(total)
    hidden_rows = total * gate
    slope_hidden = gate + hidden_rows * (1.0 - gate)
    x = tok[...].astype(F32)
    change = hidden_rows - x
    gates = update[...]
    residual = x + gates * change
    centered = residual - jnp.mean(residual, axis=1, keepdims=True)
    inverse = lax.rsqrt(jnp.mean(centered * centered, axis=1, keepdims=True) + EPS)
    normal = centered * inverse
    normal2[...] = normal
    low2 = (normal * gain2[...]).astype(BF16)
    for b in range(ffn_in.shape[1] // 256):
        cols = pl.ds(b * 256, 256)
        raw = mm(low2, ffn_in[:, cols])
        gate = sigmoid(raw)
        silu = raw * gate
        expanded[:, cols] = silu.astype(BF16)
        slope_exp[:, cols] = gate + silu * (1.0 - gate)
    block_out[...] = residual + mm(expanded[...], ffn_out[...])
    half = width // 2
    low_cot = cot[...]
    mine = core * half
    theirs = (1 - core) * half
    for target, begin in ((sent, theirs), (kept, mine)):
        begin = pl.multiple_of(begin, 128)
        target[:, :width] = mm_tn(expanded[:, pl.ds(begin, half)], low_cot)
        second = pl.multiple_of(begin + width, 128)
        target[:, width : 2 * width] = mm_tn(expanded[:, pl.ds(second, half)], low_cot)
    for b in range(ffn_in.shape[1] // 256):
        cols = pl.ds(b * 256, 256)
        rise = mm_nt(low_cot, ffn_out[cols, :])
        expand_grad[:, cols] = (rise * slope_exp[:, cols]).astype(BF16)
    expanded[:, :width] = low2
    for target, begin in ((sent, theirs), (kept, mine)):
        begin = pl.multiple_of(begin, 128)
        target[:, 2 * width : 4 * width] = mm_tn(expanded[:, pl.ds(begin, half)], expand_grad[...])
    norm_out = mm_nt(expand_grad[...], ffn_in[...])
    normal = normal2[...]
    gain2_grad[...] = jnp.sum(norm_out * normal, axis=0, keepdims=True)
    upstream = low_cot.astype(F32) + layer_grad(norm_out * gain2[...], normal, inverse)
    input_part[...] = upstream * (1.0 - gates)
    update_grad[...] = (upstream * change * gates * (1.0 - gates)).astype(BF16)
    low_out = (upstream * gates * slope_hidden).astype(BF16)
    out_grad[...] = low_out
    for target, begin in ((sent, theirs), (kept, mine)):
        begin = pl.multiple_of(begin, 128)
        target[:, 4 * width : 5 * width] = mm_tn(gated[:, pl.ds(begin, half)], low_out)
        second = pl.multiple_of(begin + width, 128)
        target[:, 5 * width :] = mm_tn(gated[:, pl.ds(second, half)], low_out)


def middle_body(
    meta,
    out_grad,
    out_weight,
    reset_raw,
    attended,
    weights,
    queries,
    keys,
    shared,
    shared_slope,
    values,
    values_slope,
    low_smoothed,
    update_grad,
    normed_low,
    qk_gain,
    kept,
    sent,
    mixed_grad,
    value_grad,
    small,
    attend_grad,
):
    tokens, width = out_grad.shape
    shared_width = qk_gain.shape[1]
    value_width = out_weight.shape[0]
    core = meta[0] % 2
    base = width + shared_width
    mixed_grad[:, :width] = update_grad[...]
    mixed_grad[:, base + value_width :] = out_grad[...]
    for b in range(value_width // 256):
        cols = pl.ds(b * 256, 256)
        rise = mm_nt(out_grad[...], out_weight[cols, :])
        raw = reset_raw[:, cols]
        gate = sigmoid(raw)
        silu = raw * gate
        mixed_grad[:, base + b * 256 : base + (b + 1) * 256] = (
            rise * attended[:, cols] * (gate + silu * (1.0 - gate))
        ).astype(BF16)
        attend_grad[:, cols] = (rise * silu).astype(BF16)
    scale = 1.0 / math.sqrt(shared_width)
    slopes = jnp.zeros((SPAN, SPAN), F32)
    for s in range(tokens // SPAN):
        rows = pl.ds(s * SPAN, SPAN)
        upstream = attend_grad[rows, :]
        share = weights[rows, :]
        rise = mm_nt(upstream, values[rows, :])
        value_rise = mm_tn(share.astype(BF16), upstream)
        value_grad[rows, :] = (value_rise * values_slope[rows, :]).astype(BF16)
        score_grad = share * (rise - jnp.sum(share * rise, axis=1, keepdims=True))
        slopes = slopes + score_grad
        low = (score_grad * scale).astype(BF16)
        query_grad = mm(low, keys[rows, :])
        key_grad = mm_tn(low, queries[rows, :])
        silu = shared[rows, :]
        pieces = (
            jnp.sum(query_grad * silu, axis=0, keepdims=True),
            jnp.sum(key_grad * silu, axis=0, keepdims=True),
            jnp.sum(query_grad, axis=0, keepdims=True),
            jnp.sum(key_grad, axis=0, keepdims=True),
        )
        sums = pieces if s == 0 else tuple(a + b for a, b in zip(sums, pieces))
        shared_grad = query_grad * qk_gain[0:1] + key_grad * qk_gain[1:2]
        mixed_grad[rows, width:base] = (shared_grad * shared_slope[rows, :]).astype(BF16)
    small[...] = jnp.zeros_like(small)
    for i in range(4):
        small[i : i + 1, :] = sums[i]
    small[4:5, :] = jnp.sum(shift_rows(slopes, False), axis=0, keepdims=True)
    half = width // 2
    cut = mixed_grad.shape[1]
    for target, begin in ((sent, (1 - core) * half), (kept, core * half)):
        begin = pl.multiple_of(begin, 128)
        target[:, :cut] = mm_tn(low_smoothed[:, pl.ds(begin, half)], mixed_grad[...])
        target[:, cut:] = mm_tn(normed_low[:, pl.ds(begin, half)], value_grad[...])


def rise_body(
    meta,
    mixed_grad,
    value_grad,
    mix_weight,
    value_weight,
    slope_pre,
    normed,
    omega,
    logk,
    keep,
    smooth_grad,
    norm_grad,
    enter,
    end,
    omega_grad,
):
    width = value_weight.shape[0]
    tokens = value_grad.shape[0]
    hidden = keep.shape[0]
    chunks = tokens // CHUNK
    grad = mm_nt(mixed_grad[...], mix_weight[...]) * slope_pre[...]
    put_tiled(smooth_grad, grad)
    put_tiled(norm_grad, mm_nt(value_grad[...], value_weight[...]) + omega[...] * grad)
    omega_grad[...] = jnp.sum(grad * tiled(normed), axis=0, keepdims=True)
    free = chunk_masks(meta, meta[0] * tokens, chunks)
    edge = edge_masks(free, chunks, True)
    masks, shifts = doubling_masks(edge, chunks, True)
    for tile in range(width // 128):
        lanes = lanes_of(tile)
        keeps = [keep[h : h + 1, lanes] for h in range(hidden)]

        def step(t, state):
            value = smooth_grad[tile, pl.ds(CHUNK - 1 - t, chunks, stride=CHUNK), :]
            return tuple(k * u + value for k, u in zip(keeps, state))

        zero = jnp.zeros((chunks, 128), F32)
        state = lax.fori_loop(0, CHUNK, step, (zero,) * hidden, unroll=8)
        for h in range(hidden):
            decay = jnp.exp(CHUNK * logk[h : h + 1, lanes])
            reached = scan_step(masks, state[h], decay, shifts, chunks)
            enter[h, :, lanes] = edge * pltpu.roll(reached, chunks - 1, 0)
            end[h : h + 1, lanes] = reached[0:1]


def close_body(
    chips,
    meta,
    tok,
    gain,
    normed,
    smooth_grad,
    norm_grad,
    states,
    enter,
    other,
    *rest,
):
    arrived = rest[:chips]
    (
        logk,
        keep,
        mix,
        input_part,
        omega_grad,
        gain2_grad,
        small,
        input_grad,
        packed,
        carry,
        history,
        total,
    ) = rest[chips:]
    tokens, width = tok.shape
    hidden = keep.shape[0]
    chunks = tokens // CHUNK
    carry[...] = carry_of(True, tokens, meta, other, arrived, logk)
    free = chunk_masks(meta, meta[0] * tokens, chunks)
    reach = prefix_mask(free, chunks, True)
    offset = ((chunks - 1 - lax.broadcasted_iota(jnp.int32, (chunks, 128), 0)) * CHUNK).astype(F32)
    group = history.shape[1]
    total[...] = norm_grad[...]
    for tile in range(width // 128):
        lanes = lanes_of(tile)
        for low in range(0, hidden, group):
            heads = range(low, low + group)
            keeps = [keep[h : h + 1, lanes] for h in heads]
            mixes = [mix[h : h + 1, lanes] for h in heads]

            def rise(t, state):
                value = normed[tile, pl.ds(t, chunks, stride=CHUNK), :]
                state = tuple(k * u + value for k, u in zip(keeps, state))
                for i in range(group):
                    history[t, i] = state[i]
                return state

            lax.fori_loop(0, CHUNK, rise, tuple(states[h, :, lanes] for h in heads), unroll=4)
            first = []
            for h in heads:
                entry = jnp.exp(offset * logk[h : h + 1, lanes]) * reach
                first.append(enter[h, :, lanes] + carry[h : h + 1, lanes] * entry)

            def fall(i, held):
                state, reads, marks = held
                t = CHUNK - 1 - i
                place = (tile, pl.ds(t, chunks, stride=CHUNK), slice(None))
                value = smooth_grad[place]
                row = normed[place]
                state = tuple(k * w + value for k, w in zip(keeps, state))
                reads = tuple(r + w * row for r, w in zip(reads, state))
                marks = tuple(m + w * history[t, j] for j, (m, w) in enumerate(zip(marks, state)))
                parts = [c * w for c, w in zip(mixes, state)]
                while len(parts) > 1:
                    parts = [a + b for a, b in zip(parts[::2], parts[1::2])]
                total[place] = total[place] + parts[0]
                return state, reads, marks

            zeros = (jnp.zeros((chunks, 128), F32),) * group
            _, reads, marks = lax.fori_loop(0, CHUNK, fall, (tuple(first), zeros, zeros), unroll=4)
            for j, h in enumerate(heads):
                packed[h : h + 1, lanes] = jnp.sum(reads[j], axis=0, keepdims=True)
                packed[hidden + h : hidden + h + 1, lanes] = jnp.sum(marks[j], axis=0, keepdims=True)
    x = tok[...].astype(F32)
    centered = x - jnp.mean(x, axis=1, keepdims=True)
    inverse = lax.rsqrt(jnp.mean(centered * centered, axis=1, keepdims=True) + EPS)
    normal = centered * inverse
    upstream = tiled(total)
    input_grad[...] = input_part[...] + layer_grad(upstream * gain[...], normal, inverse)
    at = 2 * hidden
    packed[at : at + 8, :] = jnp.zeros((8, width), F32)
    packed[at : at + 1, :] = jnp.sum(upstream * normal, axis=0, keepdims=True)
    packed[at + 1 : at + 2, :] = gain2_grad[...]
    packed[at + 2 : at + 3, :] = omega_grad[...]
    for i in range(5):
        packed[at + 3 + i : at + 4 + i, 0 : small.shape[1]] = small[i : i + 1, :]


def finish_body(packed, delta, alpha, beta, eta, delta_grad, alpha_grad, beta_grad, eta_grad):
    hidden = delta.shape[1]
    scale = 1.0 / math.sqrt(hidden)
    read = packed[0:hidden, :]
    mark = packed[hidden : 2 * hidden, :]
    share = jax.nn.sigmoid(delta[...].T)
    damp = jax.nn.sigmoid(alpha[...].T)
    inflow = share * beta[...].T
    outflow = eta[...].T * scale
    eta_grad[...] = (inflow * read * scale).T
    inflow_grad = outflow * read
    beta_grad[...] = (share * inflow_grad).T
    rate = inflow * outflow * (mark - read) / (share * damp - 1.0)
    share_grad = beta[...].T * inflow_grad + damp * rate
    delta_grad[...] = (share_grad * share * (1.0 - share)).T
    alpha_grad[...] = (share * rate * damp * (1.0 - damp)).T


def swap(a, axis, bit):
    count = lax.axis_size(axis)
    return lax.ppermute(a, axis, [(i, i ^ bit) for i in range(count)])


def bit_of(axis, bit):
    return (lax.axis_index(axis) // bit) % 2


def chip_parts(state, backward):
    count = lax.axis_size("seq")
    parts = []
    for k in range(1, count // 2):
        if backward:
            moves = [(i, i - 2 * k) for i in range(2 * k, count)]
        else:
            moves = [(i, i + 2 * k) for i in range(count - 2 * k)]
        parts.append(lax.ppermute(state, "seq", moves))
    return parts


def axis_bits(axis, least):
    bits = []
    bit = least
    while bit < lax.axis_size(axis):
        bits.append((axis, bit))
        bit *= 2
    return bits


def scatter_sum(kept, arrived, bits):
    for axis, bit in bits:
        total = kept + arrived
        half = total.shape[0] // 2
        place = bit_of(axis, bit)
        arrived = swap(lax.dynamic_slice_in_dim(total, (1 - place) * half, half), axis, bit)
        kept = lax.dynamic_slice_in_dim(total, place * half, half)
    return kept + arrived


def join(own, other, place):
    own_first = jnp.concatenate([own, other], axis=0)
    other_first = jnp.concatenate([other, own], axis=0)
    return jnp.where(place == 0, own_first, other_first)


def gather(part, bits):
    for axis, bit in reversed(bits):
        part = join(part, swap(part, axis, bit), bit_of(axis, bit))
    return part


def sum_stage(kept, sent):
    arrived = swap(sent, "seq", 1)
    flat = axis_bits("dp", 1)
    deep = axis_bits("seq", 2)
    half = kept.shape[0] // 2
    done = []
    for i, order in enumerate((flat + deep, flat[::-1] + deep)):
        part = slice(i * half, (i + 1) * half)
        done.append(gather(scatter_sum(kept[part], arrived[part], order), order))
    own = jnp.concatenate(done, axis=0)
    return join(own, swap(own, "seq", 1), bit_of("seq", 1))


def sum_small(part):
    for axis, bit in axis_bits("seq", 1) + axis_bits("dp", 1):
        part = part + swap(part, axis, bit)
    return part


def shards(
    tokens,
    cotangent,
    seq_lengths,
    norm1_gain,
    value_weight,
    ema_delta,
    ema_alpha,
    ema_beta,
    ema_eta,
    ema_omega,
    mix_weight,
    qk_gain,
    qk_bias,
    rel_bias,
    out_weight,
    norm2_gain,
    ffn_in,
    ffn_out,
):
    rows, width = tokens.shape
    hidden = ema_delta.shape[1]
    chunks = rows // CHUNK
    value_width = value_weight.shape[1]
    inner = ffn_in.shape[1]
    mixed = mix_weight.shape[1]
    shared_width = qk_gain.shape[1]
    meta = jnp.concatenate([lax.axis_index("seq")[None].astype(jnp.int32), seq_lengths[0]])
    gain1 = norm1_gain[None]
    gain2 = norm2_gain[None]
    omega = ema_omega[None]
    rel_rev = jnp.roll(rel_bias[::-1], 1)[None]
    full = (rows, width)
    tiles = (width // 128, rows, 128)
    state = (hidden, width)
    states = (hidden, chunks, width)
    normed, normed_low, enter, end, logk, keep, mix = call(
        start_body,
        (meta, tokens, gain1, ema_delta, ema_alpha, ema_beta, ema_eta),
        [(tiles, F32), (full, BF16), (states, F32), (state, F32), (state, F32), (state, F32), (state, F32)],
        name="norm_and_states",
    )
    other = swap(end, "seq", 1)
    chip_end = call(
        lambda *refs: pair_body(False, rows, *refs),
        (meta, end, other, logk),
        [(state, F32)],
        name="chip_state",
    )[0]
    arrived = chip_parts(chip_end, False)
    values, values_slope = call(
        values_body,
        (normed_low, value_weight),
        [((rows, value_width), BF16), ((rows, value_width), F32)],
        flops=2 * rows * width * value_width,
        name="values",
    )
    half = width // 2
    first_cols = 2 * width + inner + 2 * width
    wide = (rows, value_width)
    thin = (rows, shared_width)
    (
        block_out,
        kept1,
        sent1,
        entering,
        slope_pre,
        low_smoothed,
        update_grad,
        reset_raw,
        attended,
        weights,
        queries,
        keys,
        shared,
        shared_slope,
        out_grad,
        input_part,
        gain2_grad,
    ) = call(
        lambda *refs: forward_body(len(arrived), *refs),
        (meta, tokens, cotangent, normed, enter, other, *arrived, logk, keep, mix, omega, mix_weight)
        + (qk_gain, qk_bias, rel_rev, values, out_weight, gain2, ffn_in, ffn_out),
        [
            (full, F32),
            ((half, first_cols), F32),
            ((half, first_cols), F32),
            (states, F32),
            (full, F32),
            (full, BF16),
            (full, BF16),
            (wide, F32),
            (wide, F32),
            ((rows, SPAN), F32),
            (thin, BF16),
            (thin, BF16),
            (thin, F32),
            (thin, F32),
            (full, BF16),
            (full, F32),
            ((1, width), F32),
        ],
        scratch=[
            (state, F32),
            (tiles, F32),
            (full, F32),
            (full, F32),
            (wide, BF16),
            ((rows, inner), BF16),
            ((rows, inner), F32),
            (full, F32),
            ((rows, inner), BF16),
        ],
        flops=2 * rows * width * (mixed + 4 * value_width + 2 * inner * 3),
        name="forward",
    )
    first = sum_stage(kept1, sent1)
    kept2, sent2, mixed_grad, value_grad, small = call(
        middle_body,
        (meta, out_grad, out_weight, reset_raw, attended, weights, queries, keys, shared, shared_slope)
        + (values, values_slope, low_smoothed, update_grad, normed_low, qk_gain),
        [
            ((half, mixed + value_width), F32),
            ((half, mixed + value_width), F32),
            ((rows, mixed), BF16),
            (wide, BF16),
            ((8, shared_width), F32),
        ],
        scratch=[(wide, BF16)],
        flops=2 * rows * width * (mixed + 2 * value_width),
        name="attention_back",
    )
    second = sum_stage(kept2, sent2)
    smooth_grad, norm_grad, later, begin, omega_grad = call(
        rise_body,
        (meta, mixed_grad, value_grad, mix_weight, value_weight, slope_pre, normed, omega, logk, keep),
        [(tiles, F32), (tiles, F32), (states, F32), (state, F32), ((1, width), F32)],
        flops=2 * rows * width * (mixed + value_width),
        name="smooth_back",
    )
    other_begin = swap(begin, "seq", 1)
    chip_begin = call(
        lambda *refs: pair_body(True, rows, *refs),
        (meta, begin, other_begin, logk),
        [(state, F32)],
        name="chip_grad",
    )[0]
    returned = chip_parts(chip_begin, True)
    input_grad, packed = call(
        lambda *refs: close_body(len(returned), *refs),
        (meta, tokens, gain1, normed, smooth_grad, norm_grad, entering, later, other_begin, *returned)
        + (logk, keep, mix, input_part, omega_grad, gain2_grad, small),
        [(full, F32), ((2 * hidden + 8, width), F32)],
        scratch=[(state, F32), ((CHUNK, hidden // 2, chunks, 128), F32), (tiles, F32)],
        name="state_back",
    )
    packed = sum_small(packed)
    delta_grad, alpha_grad, beta_grad, eta_grad = call(
        finish_body,
        (packed, ema_delta, ema_alpha, ema_beta, ema_eta),
        [((width, hidden), F32)] * 4,
        name="state_parameters",
    )
    at = 2 * hidden
    tail = packed[at + 3 :, :shared_width]
    upper = lambda low: jnp.concatenate([first[:, low : low + width], first[:, low + width : low + 2 * width]], axis=0)
    return (
        block_out,
        input_grad,
        packed[at],
        second[:, mixed:],
        delta_grad,
        alpha_grad,
        beta_grad,
        eta_grad,
        packed[at + 2],
        second[:, :mixed],
        tail[0:2],
        tail[2:4],
        jnp.roll(tail[4][::-1], 1),
        upper(2 * width + inner),
        packed[at + 1],
        first[:, 2 * width : 2 * width + inner],
        upper(0),
    )


def solution(mesh):
    rows = P(("dp", "seq"), None)
    in_specs = (rows, rows, P("dp", None)) + (P(),) * 15
    out_specs = (rows, rows) + (P(),) * 15
    return jax.shard_map(shards, mesh=mesh, in_specs=in_specs, out_specs=out_specs, check_vma=False)
```

time: 1090 us -> 326 us (0.30)
  matrix products: 246 us -> 0 us
  waiting for transfers between devices: 353 us -> 138 us
  local copies, waits for them, and re-layouts: 217 us -> 27.1 us
  other arithmetic: 182 us -> 26 us
  Pallas kernels: 0 us -> 74.1 us
  blocking collectives: 65.8 us -> 0 us
  starting transfers between devices: 0.33 us -> 58.8 us
  between operations: 18.4 us -> 1.21 us
    psum x2 -> x0, waiting for transfers between devices: 353 us -> none  [shards(): lax.psum((local_grads[0], local_grads[1], local_grads[2], local_grads[3],...]
    dot_general x30 -> x0, matrix products: 246 us -> none  [the longest x3 145 us: prepare(): jnp.einsum('tjd,njd->ntd', toeplitz, blocks, precision=lax.Precision.HIGH...]
    ppermute x0 -> x49, waiting for transfers between devices: none -> 138 us  [the longest x43 130 us: swap(): return lax.ppermute(a, axis, [(i, i ^ bit) for i in range(count)])]
    gather x2 -> x0, local copies, waits for them, and re-layouts: 105 us -> none  [prepare(): jnp.take(kernel, jnp.maximum(offsets, 0), axis=0)]
    scatter-add x1 -> x0, other arithmetic: 105 us -> none  [prepare(): jnp.take(kernel, jnp.maximum(offsets, 0), axis=0)]
    pallas_call x0 -> x9, Pallas kernels: none -> 74.1 us  [call(): pl.pallas_call(body, in_specs=specs, out_specs=[pl.BlockSpec(memory_space...]
    all_gather x3 -> x0, blocking collectives: 65.8 us -> none  [prefix(): gathered = jax.tree.map(lambda a: lax.all_gather(a, axis), part)]
    ppermute x0 -> x49, starting transfers between devices: none -> 58.8 us  [the longest x43 44.3 us: swap(): return lax.ppermute(a, axis, [(i, i ^ bit) for i in range(count)])]
  transfers between devices with their start and end apart: 2 -> 49, of which waited for: 2 -> 28; matrix products, arithmetic and copies ran while one was open for 2% -> 11% of each run, Pallas kernels for 0% -> 14%
where the time goes in v1:
time: 326 us; the launch traced here: 325 us
  waiting for transfers between devices  138 us (42%)
  Pallas kernels  74.1 us (23%)
  starting transfers between devices  58.8 us (18%)
  local copies, waits for them, and re-layouts  27.1 us (8%)
  other arithmetic  26 us (8%)
    ppermute x43, waiting for transfers between devices, swap(): return lax.ppermute(a, axis, [(i, i ^ bit) for i in range(count)])  130 us
    pallas_call x9, Pallas kernels, call(): pl.pallas_call(body, in_specs=specs, out_specs=[pl.BlockSpec(memory_space...  74.1 us
    ppermute x43, starting transfers between devices, swap(): return lax.ppermute(a, axis, [(i, i ^ bit) for i in range(count)])  44.3 us
    unnamed x32, local copies, waits for them, and re-layouts  15.7 us
    ppermute x6, starting transfers between devices, chip_parts(): parts.append(lax.ppermute(state, 'seq', moves))  14.5 us
    select_n x18, other arithmetic, join(): return jnp.where(place == 0, own_first, other_first)  10 us
    ppermute x6, waiting for transfers between devices, chip_parts(): parts.append(lax.ppermute(state, 'seq', moves))  7.7 us
  transfers between devices with their start and end apart: 49, of which 28 were waited for; matrix products, arithmetic and copies ran while one was open for 11% of the time, Pallas kernels for 14%

profile of v1, /device:TPU:0, one launch (start us, length us, event | category | flops | bytes accessed | tf_op | source)
XLA Modules:
  0.0 325.2 jit_solution(9068137666851926887)
XLA Ops:
  0.7 1.6 copy.35.delta
  2.3 1.6 copy.36.alpha
  3.9 1.6 copy.37.beta
  5.5 1.6 copy.38.eta
  8.3 4.9 %norm_and_states.1 = (f32[4,512,128]{2,1,0:T(8,128)}, bf16[512,512]{1,0:T(8,128)(2,1)}, f32[16,8,512]{2,1,0:T(8,128)}, f32[16,512]{1,0:T(8,128)}, f32[16,512]{1,...) custom-call(s32[4]{0:T(128)} %pad_add_fusion.meta.refs_0_, bf16[512,512]{1,0:T(8,128)(2,1)} %refs_1_.3, ...), custom_call_target="tpu_custom_call" | custom-call | bytes 2623504 | tf_op jit(solution)/shard_map/norm_and_states/pallas_call | solution.py:43
  16.8 4.8 %collective-permute-start.1 = (f32[16,512]{1,0:T(8,128)}, f32[16,512]{1,0:T(8,128)S(1)}, u32[]{:S(2)}, u32[]{:S(2)}) collective-permute-start(f32[16,512]{1,0:T(8,128)} %chip_state.1), channel_id=1, source_target_pairs={{0,2},{1,3},{2,4},{3,5},{4,6},{5,7},{8,10},{9,11},{10,12},{11,13},... | collective-permute-start | bytes 98312 | tf_op jit(solution)/shard_map/ppermute | solution.py:668
  21.6 4.5 %collective-permute-start.2 = (f32[16,512]{1,0:T(8,128)}, f32[16,512]{1,0:T(8,128)S(1)}, u32[]{:S(2)}, u32[]{:S(2)}) collective-permute-start(f32[16,512]{1,0:T(8,128)} %chip_state.1), channel_id=1, source_target_pairs={{0,4},{1,5},{2,6},{3,7},{8,12},{9,13},{10,14},{11,15},{16,20},{17,... | collective-permute-start | bytes 98312 | tf_op jit(solution)/shard_map/ppermute | solution.py:668
  27.5 4.1 %values.1 = (bf16[512,1024]{1,0:T(8,128)(2,1)}, f32[512,1024]{1,0:T(8,128)}) custom-call(bf16[512,512]{1,0:T(8,128)(2,1)} %get-tuple-element.65.low.normed_low, bf16[512,1024]{1,0:T(8,128)(2,1)} %value_weight.1), custom_call_target="tpu_custom_call" | custom-call | flops 536870912 | bytes 4718592 | tf_op jit(solution)/shard_map/values/pallas_call | solution.py:43
  32.2 21.3 %forward.1 = (f32[512,512]{1,0:T(8,128)}, f32[256,3072]{1,0:T(8,128)}, f32[256,3072]{1,0:T(8,128)}, f32[16,8,512]{2,1,0:T(8,128)}, f32[512,512]{1,0:T(8,128)}, /...) custom-call(s32[4]{0:T(128)} %pad_add_fusion.meta.refs_0_, ...), custom_call_target="tpu_custom_call" | custom-call | flops 6509559808 | bytes 25534992 | tf_op jit(solution)/shard_map/forward/pallas_call | solution.py:43
  53.5 11.3 %attention_back.1 = (f32[256,3200]{1,0:T(8,128)}, f32[256,3200]{1,0:T(8,128)}, bf16[512,2176]{1,0:T(8,128)(2,1)}, bf16[512,1024]{1,0:T(8,128)(2,1)}, f32[8,128]{1,0:T(8,128)}) custom-call(s32[4]{0:T(128)} %pad_add_fusion.meta.refs_0_, bf16[512,512]{1,0:T(8,128)(2,1)} %get-tuple-element.68.out_grad, bf16[1024,512]{1,0:T(8,128)(2,1)} %out_weight.1, ...), custom_call_target="tpu_custom_call" | custom-call | flops 2214592512 | bytes 21369872 | tf_op jit(solution)/shard_map/attention_back/pallas_call | solution.py:43
  65.6 3.3 %slice_add_fusion.3 = (f32[128,3072]{1,0:T(8,128)S(1)}, f32[128,3072]{1,0:T(8,128)S(1)}) fusion(f32[256,3072]{1,0:T(8,128)} %collective-permute-done.31, f32[256,3072]{1,0:T(8,128)} %get-tuple-element.99), kind=kLoop, calls=%fused_computation.11 | loop fusion | flops 786432 | bytes 9437184 | tf_op jit(solution)/shard_map/add | solution.py:683
  69.0 1.6 collective-permute-start.40
  70.6 1.5 collective-permute-start.32
  75.0 14.4 %collective-permute-done.40 = f32[64,3072]{1,0:T(8,128)S(1)} collective-permute-done((f32[64,3072]{1,0:T(8,128)S(1)}, f32[64,3072]{1,0:T(8,128)S(1)}, u32[]{:S(2)}, u32[]{:S(2)}) %collective-permute-start.40) | collective-permute-done | bytes 786464 | tf_op jit(solution)/shard_map/ppermute | solution.py:653
  89.6 1.6 collective-permute-start.41
  91.3 1.6 collective-permute-start.33
  92.8 14.2 %collective-permute-done.22 = f32[64,3200]{1,0:T(8,128)S(1)} collective-permute-done((f32[64,3200]{1,0:T(8,128)S(1)}, f32[64,3200]{1,0:T(8,128)S(1)}, u32[]{:S(2)}, u32[]{:S(2)}) %collective-permute-start.22) | collective-permute-done | bytes 819232 | tf_op jit(solution)/shard_map/ppermute | solution.py:653
  107.2 1.6 collective-permute-start.23
  108.9 1.6 collective-permute-start.15
  110.4 6.7 %collective-permute-done.41 = f32[32,3072]{1,0:T(8,128)S(1)} collective-permute-done((f32[32,3072]{1,0:T(8,128)S(1)}, f32[32,3072]{1,0:T(8,128)S(1)}, u32[]{:S(2)}, u32[]{:S(2)}) %collective-permute-start.41) | collective-permute-done | bytes 393248 | tf_op jit(solution)/shard_map/ppermute | solution.py:653
  117.4 2.1 collective-permute-start.34
  119.4 5.4 %collective-permute-done.23 = f32[32,3200]{1,0:T(8,128)S(1)} collective-permute-done((f32[32,3200]{1,0:T(8,128)S(1)}, f32[32,3200]{1,0:T(8,128)S(1)}, u32[]{:S(2)}, u32[]{:S(2)}) %collective-permute-start.23) | collective-permute-done | bytes 409632 | tf_op jit(solution)/shard_map/ppermute | solution.py:653
  125.1 2.1 collective-permute-start.16
  127.6 2.7 collective-permute-start.35
  130.3 6.0 %collective-permute-done.43 = f32[8,3072]{1,0:T(8,128)S(1)} collective-permute-done((f32[8,3072]{1,0:T(8,128)S(1)}, f32[8,3072]{1,0:T(8,128)S(1)}, u32[]{:S(2)}, u32[]{:S(2)}) %collective-permute-start.43) | collective-permute-done | bytes 98336 | tf_op jit(solution)/shard_map/ppermute | solution.py:653
  136.4 3.5 %collective-permute-start.44 = (f32[8,3072]{1,0:T(8,128)S(1)}, f32[8,3072]{1,0:T(8,128)S(1)}, u32[]{:S(2)}, u32[]{:S(2)}) collective-permute-start(f32[8,3072]{1,0:T(8,128)S(1)} %dynamic-slice_add_fusion.14), channel_id=1, source_target_pairs={{0,4},{1,5},{2,6},{3,7},{4,0},{5,1},{6,2},{7,3},{8,12},{9,13},{10,... | collective-permute-start | bytes 294920 | tf_op jit(solution)/shard_map/ppermute | solution.py:653
  141.4 1.6 collective-permute-start.25
  144.5 6.6 %collective-permute-done.44 = f32[8,3072]{1,0:T(8,128)S(1)} collective-permute-done((f32[8,3072]{1,0:T(8,128)S(1)}, f32[8,3072]{1,0:T(8,128)S(1)}, u32[]{:S(2)}, u32[]{:S(2)}) %collective-permute-start.44) | collective-permute-done | bytes 98336 | tf_op jit(solution)/shard_map/ppermute | solution.py:653
  151.3 2.1 collective-permute-done.36
  153.5 2.1 collective-permute-done.25
  156.9 1.7 collective-permute-start.18
  158.7 6.4 %collective-permute-done.26 = f32[8,3200]{1,0:T(8,128)S(1)} collective-permute-done((f32[8,3200]{1,0:T(8,128)S(1)}, f32[8,3200]{1,0:T(8,128)S(1)}, u32[]{:S(2)}, u32[]{:S(2)}) %collective-permute-start.26) | collective-permute-done | bytes 102432 | tf_op jit(solution)/shard_map/ppermute | solution.py:653
  170.3 3.8 %collective-permute-done.27 = f32[16,3200]{1,0:T(8,128)S(1)} collective-permute-done((f32[16,3200]{1,0:T(8,128)S(1)}, f32[16,3200]{1,0:T(8,128)S(1)}, u32[]{:S(2)}, u32[]{:S(2)}) %collective-permute-start.27) | collective-permute-done | bytes 204832 | tf_op jit(solution)/shard_map/ppermute | solution.py:653
  174.1 1.5 collective-permute-start.28
  175.7 2.7 collective-permute-done.19
  179.1 1.6 collective-permute-start.47
  180.8 1.5 collective-permute-start.39
  182.4 4.2 %collective-permute-done.28 = f32[32,3200]{1,0:T(8,128)S(1)} collective-permute-done((f32[32,3200]{1,0:T(8,128)S(1)}, f32[32,3200]{1,0:T(8,128)S(1)}, u32[]{:S(2)}, u32[]{:S(2)}) %collective-permute-start.28) | collective-permute-done | bytes 409632 | tf_op jit(solution)/shard_map/ppermute | solution.py:653
  187.2 3.7 %collective-permute-done.20 = f32[32,3200]{1,0:T(8,128)S(1)} collective-permute-done((f32[32,3200]{1,0:T(8,128)S(1)}, f32[32,3200]{1,0:T(8,128)S(1)}, u32[]{:S(2)}, u32[]{:S(2)}) %collective-permute-start.20) | collective-permute-done | bytes 409632 | tf_op jit(solution)/shard_map/ppermute | solution.py:653
  190.9 1.6 collective-permute-start.21
  192.5 15.2 %collective-permute-done.47 = f32[64,3072]{1,0:T(8,128)S(1)} collective-permute-done((f32[64,3072]{1,0:T(8,128)S(1)}, f32[64,3072]{1,0:T(8,128)S(1)}, u32[]{:S(2)}, u32[]{:S(2)}) %collective-permute-start.47) | collective-permute-done | bytes 786464 | tf_op jit(solution)/shard_map/ppermute | solution.py:653
  208.0 2.3 pad_maximum_fusion.1
  210.5 13.7 %collective-permute-done.29 = f32[64,3200]{1,0:T(8,128)S(1)} collective-permute-done((f32[64,3200]{1,0:T(8,128)S(1)}, f32[64,3200]{1,0:T(8,128)S(1)}, u32[]{:S(2)}, u32[]{:S(2)}) %collective-permute-start.29) | collective-permute-done | bytes 819232 | tf_op jit(solution)/shard_map/ppermute | solution.py:653
  224.5 1.9 pad_maximum_fusion
  226.5 8.7 %smooth_back.1 = (f32[4,512,128]{2,1,0:T(8,128)}, f32[4,512,128]{2,1,0:T(8,128)}, f32[16,8,512]{2,1,0:T(8,128)}, f32[16,512]{1,0:T(8,128)}, f32[1,512]{1,0:T(1,128)}) custom-call(s32[4]{0:T(128)} %pad_add_fusion.meta.refs_0_, bf16[512,2176]{1,0:T(8,128)(2,1)} %get-tuple-element.79.mixed_grad, bf16[512,1024]{1,0:T(8,128)(2,1)} %get-tuple-element.80.value_grad, ...), custom_call_target="tpu_custom_call" | custom-call | flops 1677721600 | bytes 11112464 | tf_op jit(solution)/shard_map/smooth_back/pallas_call | solution.py:43
  242.6 2.1 collective-permute-done.5.refs_9_
  244.8 2.2 collective-permute-done.6.refs_10_
  247.0 3.4 %collective-permute-done.7.refs_11_ = f32[16,512]{1,0:T(8,128)S(1)} collective-permute-done((f32[16,512]{1,0:T(8,128)}, f32[16,512]{1,0:T(8,128)S(1)}, u32[]{:S(2)}, u32[]{:S(2)}) %collective-permute-start.7) | collective-permute-done | bytes 32800 | tf_op jit(solution)/shard_map/ppermute | solution.py:668
  250.9 18.3 %state_back.1 = (f32[512,512]{1,0:T(8,128)}, f32[40,512]{1,0:T(8,128)}) custom-call(s32[4]{0:T(128)} %pad_add_fusion.meta.refs_0_, bf16[512,512]{1,0:T(8,128)(2,1)} %refs_1_.3, f32[1,512]{1,0:T(1,128)} %bitcast.15, f32[4,512,128]{2,1,0:T(8,128)} %get-tuple-element.59.refs_3_.normed, f32[4,512,128]{2,1,0:T(8,128)} %get-tuple-element.82.refs_4_, ...), custom_call_target="tpu_custom_call" | custom-call | bytes 6613008 | tf_op jit(solution)/shard_map/state_back/pallas_call | solution.py:43
  271.7 4.5 %collective-permute-done.9 = f32[40,512]{1,0:T(8,128)S(1)} collective-permute-done((f32[40,512]{1,0:T(8,128)S(1)}, f32[40,512]{1,0:T(8,128)S(1)}, u32[]{:S(2)}, u32[]{:S(2)}) %collective-permute-start.9) | collective-permute-done | bytes 81952 | tf_op jit(solution)/shard_map/ppermute | solution.py:653
  276.3 6.3 %collective-permute-done.10 = f32[40,512]{1,0:T(8,128)S(1)} collective-permute-done((f32[40,512]{1,0:T(8,128)S(1)}, f32[40,512]{1,0:T(8,128)S(1)}, u32[]{:S(2)}, u32[]{:S(2)}) %collective-permute-start.10) | collective-permute-done | bytes 81952 | tf_op jit(solution)/shard_map/ppermute | solution.py:653
  282.6 1.5 collective-permute-start.11
  284.1 3.0 collective-permute-done.11
  287.7 3.9 %collective-permute-done.12 = f32[40,512]{1,0:T(8,128)S(1)} collective-permute-done((f32[40,512]{1,0:T(8,128)S(1)}, f32[40,512]{1,0:T(8,128)S(1)}, u32[]{:S(2)}, u32[]{:S(2)}) %collective-permute-start.12) | collective-permute-done | bytes 81952 | tf_op jit(solution)/shard_map/ppermute | solution.py:653
  292.3 2.7 state_parameters.1
  296.2 1.7 copy.43
  297.9 1.7 copy.44
  299.5 1.7 copy.45
  301.2 1.7 copy.46
  307.7 5.6 %maximum_select_fusion.1 = f32[512,3072]{1,0:T(8,128)S(1)} fusion(f32[256,3072]{1,0:T(8,128)} %collective-permute-done.48, f32[128,3072]{1,0:T(8,128)} %copy-done, f32[128,3072]{1,0:T(8,128)} %copy-done.1, pred[]{:T(512)S(6)} %eq.63), kind=kLoop, calls=%fused_computation.1 | loop fusion | flops 7864320 | bytes 12582913 | tf_op jit(solution)/shard_map/jit(_where)/select_n | solution.py:694
  315.2 2.5 pad_maximum_fusion.2
  317.7 3.5 %maximum_select_fusion = f32[512,3200]{1,0:T(8,128)S(1)} fusion(f32[256,3200]{1,0:T(8,128)} %collective-permute-done.30, f32[128,3200]{1,0:T(8,128)S(1)} %maximum_select_fusion.3, f32[128,3200]{1,0:T(8,128)S(1)} %maximum_select_fusion.2, pred[]{:T(512)S(6)} %eq.63), kind=kLoop, calls=%fused_computation | loop fusion | flops 8192000 | bytes 13107201 | tf_op jit(solution)/shard_map/jit(_where)/select_n | solution.py:694
  321.2 1.6 slice.126
  322.8 2.4 slice.128
  (149 shorter events, 43.8 us)
Async XLA Ops:
  0.7 13.1 %copy-start.11 = (f32[128]{0:T(128)S(1)}, f32[128]{0:T(128)}, u32[]{:S(2)}) copy-start(f32[128]{0:T(128)} %param.31) | copy-start | bytes 1540
  13.3 1.5 collective-permute-start
  14.8 0.6 copy-start.7
  16.8 14.7 %collective-permute-start.1 = (f32[16,512]{1,0:T(8,128)}, f32[16,512]{1,0:T(8,128)S(1)}, u32[]{:S(2)}, u32[]{:S(2)}) collective-permute-start(f32[16,512]{1,0:T(8,128)} %chip_state.1), channel_id=1, source_target_pairs={{0,2},{1,3},{2,4},{3,5},{4,6},{5,7},{8,10},{9,11},{10,12},{11,13},... | collective-permute-start | bytes 98312 | tf_op jit(solution)/shard_map/ppermute | solution.py:668
  21.6 9.9 %collective-permute-start.2 = (f32[16,512]{1,0:T(8,128)}, f32[16,512]{1,0:T(8,128)S(1)}, u32[]{:S(2)}, u32[]{:S(2)}) collective-permute-start(f32[16,512]{1,0:T(8,128)} %chip_state.1), channel_id=1, source_target_pairs={{0,4},{1,5},{2,6},{3,7},{8,12},{9,13},{10,14},{11,15},{16,20},{17,... | collective-permute-start | bytes 98312 | tf_op jit(solution)/shard_map/ppermute | solution.py:668
  26.2 5.4 %collective-permute-start.3 = (f32[16,512]{1,0:T(8,128)}, f32[16,512]{1,0:T(8,128)S(1)}, u32[]{:S(2)}, u32[]{:S(2)}) collective-permute-start(f32[16,512]{1,0:T(8,128)} %chip_state.1), channel_id=1, source_target_pairs={{0,6},{1,7},{8,14},{9,15},{16,22},{17,23},{24,30},{25,31}} | collective-permute-start | bytes 98312 | tf_op jit(solution)/shard_map/ppermute | solution.py:668
  31.6 0.6 copy-start.8
  31.6 0.6 copy-start.9
  31.6 0.6 copy-start.10
  53.5 12.1 %collective-permute-start.31 = (f32[256,3072]{1,0:T(8,128)}, f32[256,3072]{1,0:T(8,128)}, u32[]{:S(2)}, u32[]{:S(2)}) collective-permute-start(f32[256,3072]{1,0:T(8,128)} %get-tuple-element.100), channel_id=1, source_target_pairs={{0,1},{1,0},{2,3},{3,2},{4,5},{5,4},{6,7},{7,6},{8,9},{9,8},{10,11... | collective-permute-start | bytes 9437192 | tf_op jit(solution)/shard_map/ppermute | solution.py:653
  64.8 7.4 %collective-permute-start.13 = (f32[256,3200]{1,0:T(8,128)}, f32[256,3200]{1,0:T(8,128)S(1)}, u32[]{:S(2)}, u32[]{:S(2)}) collective-permute-start(f32[256,3200]{1,0:T(8,128)} %get-tuple-element.94), channel_id=1, source_target_pairs={{0,1},{1,0},{2,3},{3,2},{4,5},{5,4},{6,7},{7,6},{8,9},{9,8},{10,11... | collective-permute-start | bytes 9830408 | tf_op jit(solution)/shard_map/ppermute | solution.py:653
  65.6 6.6 %copy-start.2 = (f32[256,3200]{1,0:T(8,128)S(1)}, f32[256,3200]{1,0:T(8,128)}, u32[]{:S(2)}) copy-start(f32[256,3200]{1,0:T(8,128)} %get-tuple-element.93) | copy-start | bytes 9830404
  69.0 20.4 %collective-permute-start.40 = (f32[64,3072]{1,0:T(8,128)S(1)}, f32[64,3072]{1,0:T(8,128)S(1)}, u32[]{:S(2)}, u32[]{:S(2)}) collective-permute-start(f32[64,3072]{1,0:T(8,128)S(1)} %constant_dynamic-slice_fusion.3), channel_id=1, source_target_pairs={{0,16},{8,24},{16,0},{24,8},{1,17},{9,25},{17,1},{25,9},{2,18},{10... | collective-permute-start | bytes 2359304 | tf_op jit(solution)/shard_map/ppermute | solution.py:653
  70.6 20.5 %collective-permute-start.32 = (f32[64,3072]{1,0:T(8,128)S(1)}, f32[64,3072]{1,0:T(8,128)S(1)}, u32[]{:S(2)}, u32[]{:S(2)}) collective-permute-start(f32[64,3072]{1,0:T(8,128)S(1)} %constant_dynamic-slice_fusion.7), channel_id=1, source_target_pairs={{0,8},{8,0},{16,24},{24,16},{1,9},{9,1},{17,25},{25,17},{2,10},{10... | collective-permute-start | bytes 2359304 | tf_op jit(solution)/shard_map/ppermute | solution.py:653
  72.8 34.2 %collective-permute-start.22 = (f32[64,3200]{1,0:T(8,128)S(1)}, f32[64,3200]{1,0:T(8,128)S(1)}, u32[]{:S(2)}, u32[]{:S(2)}) collective-permute-start(f32[64,3200]{1,0:T(8,128)S(1)} %constant_dynamic-slice_fusion.11), channel_id=1, source_target_pairs={{0,16},{8,24},{16,0},{24,8},{1,17},{9,25},{17,1},{25,9},{2,18},{10... | collective-permute-start | bytes 2457608 | tf_op jit(solution)/shard_map/ppermute | solution.py:653
  73.5 35.2 %collective-permute-start.14 = (f32[64,3200]{1,0:T(8,128)S(1)}, f32[64,3200]{1,0:T(8,128)S(1)}, u32[]{:S(2)}, u32[]{:S(2)}) collective-permute-start(f32[64,3200]{1,0:T(8,128)S(1)} %constant_dynamic-slice_fusion.15), channel_id=1, source_target_pairs={{0,8},{8,0},{16,24},{24,16},{1,9},{9,1},{17,25},{25,17},{2,10},{10... | collective-permute-start | bytes 2457608 | tf_op jit(solution)/shard_map/ppermute | solution.py:653
  89.6 27.5 %collective-permute-start.41 = (f32[32,3072]{1,0:T(8,128)S(1)}, f32[32,3072]{1,0:T(8,128)S(1)}, u32[]{:S(2)}, u32[]{:S(2)}) collective-permute-start(f32[32,3072]{1,0:T(8,128)S(1)} %constant_dynamic-slice_fusion.2), channel_id=1, source_target_pairs={{0,8},{8,0},{16,24},{24,16},{1,9},{9,1},{17,25},{25,17},{2,10},{10... | collective-permute-start | bytes 1179656 | tf_op jit(solution)/shard_map/ppermute | solution.py:653
  91.3 26.0 %collective-permute-start.33 = (f32[32,3072]{1,0:T(8,128)S(1)}, f32[32,3072]{1,0:T(8,128)S(1)}, u32[]{:S(2)}, u32[]{:S(2)}) collective-permute-start(f32[32,3072]{1,0:T(8,128)S(1)} %constant_dynamic-slice_fusion.6), channel_id=1, source_target_pairs={{0,16},{8,24},{16,0},{24,8},{1,17},{9,25},{17,1},{25,9},{2,18},{10... | collective-permute-start | bytes 1179656 | tf_op jit(solution)/shard_map/ppermute | solution.py:653
  107.2 17.7 %collective-permute-start.23 = (f32[32,3200]{1,0:T(8,128)S(1)}, f32[32,3200]{1,0:T(8,128)S(1)}, u32[]{:S(2)}, u32[]{:S(2)}) collective-permute-start(f32[32,3200]{1,0:T(8,128)S(1)} %constant_dynamic-slice_fusion.10), channel_id=1, source_target_pairs={{0,8},{8,0},{16,24},{24,16},{1,9},{9,1},{17,25},{25,17},{2,10},{10... | collective-permute-start | bytes 1228808 | tf_op jit(solution)/shard_map/ppermute | solution.py:653
  108.9 16.1 %collective-permute-start.15 = (f32[32,3200]{1,0:T(8,128)S(1)}, f32[32,3200]{1,0:T(8,128)S(1)}, u32[]{:S(2)}, u32[]{:S(2)}) collective-permute-start(f32[32,3200]{1,0:T(8,128)S(1)} %constant_dynamic-slice_fusion.14), channel_id=1, source_target_pairs={{0,16},{8,24},{16,0},{24,8},{1,17},{9,25},{17,1},{25,9},{2,18},{10... | collective-permute-start | bytes 1228808 | tf_op jit(solution)/shard_map/ppermute | solution.py:653
  117.2 10.0 %collective-permute-start.42 = (f32[16,3072]{1,0:T(8,128)S(1)}, f32[16,3072]{1,0:T(8,128)S(1)}, u32[]{:S(2)}, u32[]{:S(2)}) collective-permute-start(f32[16,3072]{1,0:T(8,128)S(1)} %constant_dynamic-slice_fusion.1), channel_id=1, source_target_pairs={{0,2},{1,3},{2,0},{3,1},{4,6},{5,7},{6,4},{7,5},{8,10},{9,11},{10,... | collective-permute-start | bytes 589832 | tf_op jit(solution)/shard_map/ppermute | solution.py:653
  117.4 10.2 %collective-permute-start.34 = (f32[16,3072]{1,0:T(8,128)S(1)}, f32[16,3072]{1,0:T(8,128)S(1)}, u32[]{:S(2)}, u32[]{:S(2)}) collective-permute-start(f32[16,3072]{1,0:T(8,128)S(1)} %constant_dynamic-slice_fusion.5), channel_id=1, source_target_pairs={{0,2},{1,3},{2,0},{3,1},{4,6},{5,7},{6,4},{7,5},{8,10},{9,11},{10,... | collective-permute-start | bytes 589832 | tf_op jit(solution)/shard_map/ppermute | solution.py:653
  124.9 16.5 %collective-permute-start.24 = (f32[16,3200]{1,0:T(8,128)S(1)}, f32[16,3200]{1,0:T(8,128)S(1)}, u32[]{:S(2)}, u32[]{:S(2)}) collective-permute-start(f32[16,3200]{1,0:T(8,128)S(1)} %constant_dynamic-slice_fusion.9), channel_id=1, source_target_pairs={{0,2},{1,3},{2,0},{3,1},{4,6},{5,7},{6,4},{7,5},{8,10},{9,11},{10,... | collective-permute-start | bytes 614408 | tf_op jit(solution)/shard_map/ppermute | solution.py:653
  125.1 18.0 %collective-permute-start.16 = (f32[16,3200]{1,0:T(8,128)S(1)}, f32[16,3200]{1,0:T(8,128)S(1)}, u32[]{:S(2)}, u32[]{:S(2)}) collective-permute-start(f32[16,3200]{1,0:T(8,128)S(1)} %constant_dynamic-slice_fusion.13), channel_id=1, source_target_pairs={{0,2},{1,3},{2,0},{3,1},{4,6},{5,7},{6,4},{7,5},{8,10},{9,11},{10,... | collective-permute-start | bytes 614408 | tf_op jit(solution)/shard_map/ppermute | solution.py:653
  127.2 9.1 %collective-permute-start.43 = (f32[8,3072]{1,0:T(8,128)S(1)}, f32[8,3072]{1,0:T(8,128)S(1)}, u32[]{:S(2)}, u32[]{:S(2)}) collective-permute-start(f32[8,3072]{1,0:T(8,128)S(1)} %constant_dynamic-slice_fusion), channel_id=1, source_target_pairs={{0,4},{1,5},{2,6},{3,7},{4,0},{5,1},{6,2},{7,3},{8,12},{9,13},{10,... | collective-permute-start | bytes 294920 | tf_op jit(solution)/shard_map/ppermute | solution.py:653
  127.6 12.3 %collective-permute-start.35 = (f32[8,3072]{1,0:T(8,128)S(1)}, f32[8,3072]{1,0:T(8,128)S(1)}, u32[]{:S(2)}, u32[]{:S(2)}) collective-permute-start(f32[8,3072]{1,0:T(8,128)S(1)} %constant_dynamic-slice_fusion.4), channel_id=1, source_target_pairs={{0,4},{1,5},{2,6},{3,7},{4,0},{5,1},{6,2},{7,3},{8,12},{9,13},{10,... | collective-permute-start | bytes 294920 | tf_op jit(solution)/shard_map/ppermute | solution.py:653
  136.4 14.8 %collective-permute-start.44 = (f32[8,3072]{1,0:T(8,128)S(1)}, f32[8,3072]{1,0:T(8,128)S(1)}, u32[]{:S(2)}, u32[]{:S(2)}) collective-permute-start(f32[8,3072]{1,0:T(8,128)S(1)} %dynamic-slice_add_fusion.14), channel_id=1, source_target_pairs={{0,4},{1,5},{2,6},{3,7},{4,0},{5,1},{6,2},{7,3},{8,12},{9,13},{10,... | collective-permute-start | bytes 294920 | tf_op jit(solution)/shard_map/ppermute | solution.py:653
  139.9 13.4 %collective-permute-start.36 = (f32[8,3072]{1,0:T(8,128)S(1)}, f32[8,3072]{1,0:T(8,128)S(1)}, u32[]{:S(2)}, u32[]{:S(2)}) collective-permute-start(f32[8,3072]{1,0:T(8,128)S(1)} %dynamic-slice_add_fusion.15), channel_id=1, source_target_pairs={{0,4},{1,5},{2,6},{3,7},{4,0},{5,1},{6,2},{7,3},{8,12},{9,13},{10,... | collective-permute-start | bytes 294920 | tf_op jit(solution)/shard_map/ppermute | solution.py:653
  141.4 14.2 %collective-permute-start.25 = (f32[8,3200]{1,0:T(8,128)S(1)}, f32[8,3200]{1,0:T(8,128)S(1)}, u32[]{:S(2)}, u32[]{:S(2)}) collective-permute-start(f32[8,3200]{1,0:T(8,128)S(1)} %constant_dynamic-slice_fusion.8), channel_id=1, source_target_pairs={{0,4},{1,5},{2,6},{3,7},{4,0},{5,1},{6,2},{7,3},{8,12},{9,13},{10,... | collective-permute-start | bytes 307208 | tf_op jit(solution)/shard_map/ppermute | solution.py:653
  143.1 13.8 %collective-permute-start.17 = (f32[8,3200]{1,0:T(8,128)S(1)}, f32[8,3200]{1,0:T(8,128)S(1)}, u32[]{:S(2)}, u32[]{:S(2)}) collective-permute-start(f32[8,3200]{1,0:T(8,128)S(1)} %constant_dynamic-slice_fusion.12), channel_id=1, source_target_pairs={{0,4},{1,5},{2,6},{3,7},{4,0},{5,1},{6,2},{7,3},{8,12},{9,13},{10,... | collective-permute-start | bytes 307208 | tf_op jit(solution)/shard_map/ppermute | solution.py:653
  151.2 16.9 %collective-permute-start.45 = (f32[16,3072]{1,0:T(8,128)S(1)}, f32[16,3072]{1,0:T(8,128)S(1)}, u32[]{:S(2)}, u32[]{:S(2)}) collective-permute-start(f32[16,3072]{1,0:T(8,128)S(1)} %maximum_select_fusion.17), channel_id=1, source_target_pairs={{0,2},{1,3},{2,0},{3,1},{4,6},{5,7},{6,4},{7,5},{8,10},{9,11},{10,... | collective-permute-start | bytes 589832 | tf_op jit(solution)/shard_map/ppermute | solution.py:653
  153.4 16.3 %collective-permute-start.37 = (f32[16,3072]{1,0:T(8,128)S(1)}, f32[16,3072]{1,0:T(8,128)S(1)}, u32[]{:S(2)}, u32[]{:S(2)}) collective-permute-start(f32[16,3072]{1,0:T(8,128)S(1)} %maximum_select_fusion.16), channel_id=1, source_target_pairs={{0,2},{1,3},{2,0},{3,1},{4,6},{5,7},{6,4},{7,5},{8,10},{9,11},{10,... | collective-permute-start | bytes 589832 | tf_op jit(solution)/shard_map/ppermute | solution.py:653
  155.6 9.5 %collective-permute-start.26 = (f32[8,3200]{1,0:T(8,128)S(1)}, f32[8,3200]{1,0:T(8,128)S(1)}, u32[]{:S(2)}, u32[]{:S(2)}) collective-permute-start(f32[8,3200]{1,0:T(8,128)S(1)} %dynamic-slice_add_fusion.12), channel_id=1, source_target_pairs={{0,4},{1,5},{2,6},{3,7},{4,0},{5,1},{6,2},{7,3},{8,12},{9,13},{10,... | collective-permute-start | bytes 307208 | tf_op jit(solution)/shard_map/ppermute | solution.py:653
  156.9 10.3 %collective-permute-start.18 = (f32[8,3200]{1,0:T(8,128)S(1)}, f32[8,3200]{1,0:T(8,128)S(1)}, u32[]{:S(2)}, u32[]{:S(2)}) collective-permute-start(f32[8,3200]{1,0:T(8,128)S(1)} %dynamic-slice_add_fusion.13), channel_id=1, source_target_pairs={{0,4},{1,5},{2,6},{3,7},{4,0},{5,1},{6,2},{7,3},{8,12},{9,13},{10,... | collective-permute-start | bytes 307208 | tf_op jit(solution)/shard_map/ppermute | solution.py:653
  165.1 9.0 %collective-permute-start.27 = (f32[16,3200]{1,0:T(8,128)S(1)}, f32[16,3200]{1,0:T(8,128)S(1)}, u32[]{:S(2)}, u32[]{:S(2)}) collective-permute-start(f32[16,3200]{1,0:T(8,128)S(1)} %maximum_select_fusion.15), channel_id=1, source_target_pairs={{0,2},{1,3},{2,0},{3,1},{4,6},{5,7},{6,4},{7,5},{8,10},{9,11},{10,... | collective-permute-start | bytes 614408 | tf_op jit(solution)/shard_map/ppermute | solution.py:653
  167.3 11.1 %collective-permute-start.19 = (f32[16,3200]{1,0:T(8,128)S(1)}, f32[16,3200]{1,0:T(8,128)S(1)}, u32[]{:S(2)}, u32[]{:S(2)}) collective-permute-start(f32[16,3200]{1,0:T(8,128)S(1)} %maximum_select_fusion.14), channel_id=1, source_target_pairs={{0,2},{1,3},{2,0},{3,1},{4,6},{5,7},{6,4},{7,5},{8,10},{9,11},{10,... | collective-permute-start | bytes 614408 | tf_op jit(solution)/shard_map/ppermute | solution.py:653
  168.1 10.9 %collective-permute-start.46 = (f32[32,3072]{1,0:T(8,128)S(1)}, f32[32,3072]{1,0:T(8,128)S(1)}, u32[]{:S(2)}, u32[]{:S(2)}) collective-permute-start(f32[32,3072]{1,0:T(8,128)S(1)} %maximum_select_fusion.13), channel_id=1, source_target_pairs={{0,8},{8,0},{16,24},{24,16},{1,9},{9,1},{17,25},{25,17},{2,10},{10... | collective-permute-start | bytes 1179656 | tf_op jit(solution)/shard_map/ppermute | solution.py:653
  169.7 11.0 %collective-permute-start.38 = (f32[32,3072]{1,0:T(8,128)S(1)}, f32[32,3072]{1,0:T(8,128)S(1)}, u32[]{:S(2)}, u32[]{:S(2)}) collective-permute-start(f32[32,3072]{1,0:T(8,128)S(1)} %maximum_select_fusion.12), channel_id=1, source_target_pairs={{0,16},{8,24},{16,0},{24,8},{1,17},{9,25},{17,1},{25,9},{2,18},{10... | collective-permute-start | bytes 1179656 | tf_op jit(solution)/shard_map/ppermute | solution.py:653
  174.1 12.4 %collective-permute-start.28 = (f32[32,3200]{1,0:T(8,128)S(1)}, f32[32,3200]{1,0:T(8,128)S(1)}, u32[]{:S(2)}, u32[]{:S(2)}) collective-permute-start(f32[32,3200]{1,0:T(8,128)S(1)} %maximum_select_fusion.11), channel_id=1, source_target_pairs={{0,8},{8,0},{16,24},{24,16},{1,9},{9,1},{17,25},{25,17},{2,10},{10... | collective-permute-start | bytes 1228808 | tf_op jit(solution)/shard_map/ppermute | solution.py:653
  178.4 12.4 %collective-permute-start.20 = (f32[32,3200]{1,0:T(8,128)S(1)}, f32[32,3200]{1,0:T(8,128)S(1)}, u32[]{:S(2)}, u32[]{:S(2)}) collective-permute-start(f32[32,3200]{1,0:T(8,128)S(1)} %maximum_select_fusion.10), channel_id=1, source_target_pairs={{0,16},{8,24},{16,0},{24,8},{1,17},{9,25},{17,1},{25,9},{2,18},{10... | collective-permute-start | bytes 1228808 | tf_op jit(solution)/shard_map/ppermute | solution.py:653
  179.1 28.6 %collective-permute-start.47 = (f32[64,3072]{1,0:T(8,128)S(1)}, f32[64,3072]{1,0:T(8,128)S(1)}, u32[]{:S(2)}, u32[]{:S(2)}) collective-permute-start(f32[64,3072]{1,0:T(8,128)S(1)} %maximum_select_fusion.9), channel_id=1, source_target_pairs={{0,16},{8,24},{16,0},{24,8},{1,17},{9,25},{17,1},{25,9},{2,18},{10... | collective-permute-start | bytes 2359304 | tf_op jit(solution)/shard_map/ppermute | solution.py:653
  180.8 27.0 %collective-permute-start.39 = (f32[64,3072]{1,0:T(8,128)S(1)}, f32[64,3072]{1,0:T(8,128)S(1)}, u32[]{:S(2)}, u32[]{:S(2)}) collective-permute-start(f32[64,3072]{1,0:T(8,128)S(1)} %maximum_select_fusion.8), channel_id=1, source_target_pairs={{0,8},{8,0},{16,24},{24,16},{1,9},{9,1},{17,25},{25,17},{2,10},{10... | collective-permute-start | bytes 2359304 | tf_op jit(solution)/shard_map/ppermute | solution.py:653
  186.6 37.7 %collective-permute-start.29 = (f32[64,3200]{1,0:T(8,128)S(1)}, f32[64,3200]{1,0:T(8,128)S(1)}, u32[]{:S(2)}, u32[]{:S(2)}) collective-permute-start(f32[64,3200]{1,0:T(8,128)S(1)} %maximum_select_fusion.7), channel_id=1, source_target_pairs={{0,16},{8,24},{16,0},{24,8},{1,17},{9,25},{17,1},{25,9},{2,18},{10... | collective-permute-start | bytes 2457608 | tf_op jit(solution)/shard_map/ppermute | solution.py:653
  190.9 33.5 %collective-permute-start.21 = (f32[64,3200]{1,0:T(8,128)S(1)}, f32[64,3200]{1,0:T(8,128)S(1)}, u32[]{:S(2)}, u32[]{:S(2)}) collective-permute-start(f32[64,3200]{1,0:T(8,128)S(1)} %maximum_select_fusion.6), channel_id=1, source_target_pairs={{0,8},{8,0},{16,24},{24,16},{1,9},{9,1},{17,25},{25,17},{2,10},{10... | collective-permute-start | bytes 2457608 | tf_op jit(solution)/shard_map/ppermute | solution.py:653
  207.8 2.5 copy-start
  208.0 2.5 copy-start.1
  210.5 97.1 %collective-permute-start.48 = (f32[256,3072]{1,0:T(8,128)}, f32[256,3072]{1,0:T(8,128)}, u32[]{:S(2)}, u32[]{:S(2)}) collective-permute-start(f32[256,3072]{1,0:T(8,128)} %pad_maximum_fusion.1), channel_id=1, source_target_pairs={{0,1},{1,0},{2,3},{3,2},{4,5},{5,4},{6,7},{7,6},{8,9},{9,8},{10,11... | collective-permute-start | bytes 9437192 | tf_op jit(solution)/shard_map/ppermute | solution.py:653
  226.5 91.2 %collective-permute-start.30 = (f32[256,3200]{1,0:T(8,128)}, f32[256,3200]{1,0:T(8,128)}, u32[]{:S(2)}, u32[]{:S(2)}) collective-permute-start(f32[256,3200]{1,0:T(8,128)} %pad_maximum_fusion), channel_id=1, source_target_pairs={{0,1},{1,0},{2,3},{3,2},{4,5},{5,4},{6,7},{7,6},{8,9},{9,8},{10,11... | collective-permute-start | bytes 9830408 | tf_op jit(solution)/shard_map/ppermute | solution.py:653
  235.1 1.6 collective-permute-start.4
  236.7 0.6 copy-start.3
  238.7 6.0 %collective-permute-start.5 = (f32[16,512]{1,0:T(8,128)}, f32[16,512]{1,0:T(8,128)S(1)}, u32[]{:S(2)}, u32[]{:S(2)}) collective-permute-start(f32[16,512]{1,0:T(8,128)} %chip_grad.1), channel_id=1, source_target_pairs={{2,0},{3,1},{4,2},{5,3},{6,4},{7,5},{10,8},{11,9},{12,10},{13,11},... | collective-permute-start | bytes 98312 | tf_op jit(solution)/shard_map/ppermute | solution.py:668
  240.0 6.9 %collective-permute-start.6 = (f32[16,512]{1,0:T(8,128)}, f32[16,512]{1,0:T(8,128)S(1)}, u32[]{:S(2)}, u32[]{:S(2)}) collective-permute-start(f32[16,512]{1,0:T(8,128)} %chip_grad.1), channel_id=1, source_target_pairs={{4,0},{5,1},{6,2},{7,3},{12,8},{13,9},{14,10},{15,11},{20,16},{21,... | collective-permute-start | bytes 98312 | tf_op jit(solution)/shard_map/ppermute | solution.py:668
  241.3 9.0 %collective-permute-start.7 = (f32[16,512]{1,0:T(8,128)}, f32[16,512]{1,0:T(8,128)S(1)}, u32[]{:S(2)}, u32[]{:S(2)}) collective-permute-start(f32[16,512]{1,0:T(8,128)} %chip_grad.1), channel_id=1, source_target_pairs={{6,0},{7,1},{14,8},{15,9},{22,16},{23,17},{30,24},{31,25}} | collective-permute-start | bytes 98312 | tf_op jit(solution)/shard_map/ppermute | solution.py:668
  244.8 5.6 %copy-start.4 = (f32[16,512]{1,0:T(8,128)}, f32[16,512]{1,0:T(8,128)S(1)}, u32[]{:S(2)}) copy-start(f32[16,512]{1,0:T(8,128)S(1)} %collective-permute-done.5.refs_9_) | copy-start | bytes 98308
  247.0 3.4 %copy-start.5 = (f32[16,512]{1,0:T(8,128)}, f32[16,512]{1,0:T(8,128)S(1)}, u32[]{:S(2)}) copy-start(f32[16,512]{1,0:T(8,128)S(1)} %collective-permute-done.6.refs_10_) | copy-start | bytes 98308
  250.3 0.6 copy-start.6
  269.2 1.5 collective-permute-start.8
  271.6 4.6 %collective-permute-start.9 = (f32[40,512]{1,0:T(8,128)S(1)}, f32[40,512]{1,0:T(8,128)S(1)}, u32[]{:S(2)}, u32[]{:S(2)}) collective-permute-start(f32[40,512]{1,0:T(8,128)S(1)} %add.181), channel_id=1, source_target_pairs={{0,2},{1,3},{2,0},{3,1},{4,6},{5,7},{6,4},{7,5},{8,10},{9,11},{10,... | collective-permute-start | bytes 245768 | tf_op jit(solution)/shard_map/ppermute | solution.py:653
  276.2 6.4 %collective-permute-start.10 = (f32[40,512]{1,0:T(8,128)S(1)}, f32[40,512]{1,0:T(8,128)S(1)}, u32[]{:S(2)}, u32[]{:S(2)}) collective-permute-start(f32[40,512]{1,0:T(8,128)S(1)} %add.182), channel_id=1, source_target_pairs={{0,4},{1,5},{2,6},{3,7},{4,0},{5,1},{6,2},{7,3},{8,12},{9,13},{10,... | collective-permute-start | bytes 245768 | tf_op jit(solution)/shard_map/ppermute | solution.py:653
  282.6 4.5 %collective-permute-start.11 = (f32[40,512]{1,0:T(8,128)S(1)}, f32[40,512]{1,0:T(8,128)S(1)}, u32[]{:S(2)}, u32[]{:S(2)}) collective-permute-start(f32[40,512]{1,0:T(8,128)S(1)} %add.183), channel_id=1, source_target_pairs={{0,8},{8,0},{16,24},{24,16},{1,9},{9,1},{17,25},{25,17},{2,10},{10... | collective-permute-start | bytes 245768 | tf_op jit(solution)/shard_map/ppermute | solution.py:653
  287.1 4.5 %collective-permute-start.12 = (f32[40,512]{1,0:T(8,128)S(1)}, f32[40,512]{1,0:T(8,128)S(1)}, u32[]{:S(2)}, u32[]{:S(2)}) collective-permute-start(f32[40,512]{1,0:T(8,128)S(1)} %add.184), channel_id=1, source_target_pairs={{0,16},{8,24},{16,0},{24,8},{1,17},{9,25},{17,1},{25,9},{2,18},{10... | collective-permute-start | bytes 245768 | tf_op jit(solution)/shard_map/ppermute | solution.py:653

commit v2 on v1

v2 whole, which is shorter than its diff:
```python
import math

import jax
import jax.numpy as jnp
from jax import lax
from jax.experimental import pallas as pl
from jax.experimental.pallas import tpu as pltpu
from jax.sharding import PartitionSpec as P

SPAN = 128
CHUNK = 64
EPS = 1e-05
BF16 = jnp.bfloat16
F32 = jnp.float32
ROOM = 2 * 1024 * 1024


def sigmoid(a):
    return 0.5 * jnp.tanh(0.5 * a) + 0.5


def mm(a, b):
    return lax.dot_general(a, b, (((1,), (0,)), ((), ())), preferred_element_type=F32)


def mm_nt(a, b):
    return lax.dot_general(a, b, (((1,), (1,)), ((), ())), preferred_element_type=F32)


def mm_tn(a, b):
    return lax.dot_general(a, b, (((0,), (0,)), ((), ())), preferred_element_type=F32)


COSTS = {
    "norm_and_states": 2.7,
    "values": 1.0,
    "local_average": 3.1,
    "carried_average": 2.7,
    "mix": 1.4,
    "attention": 1.9,
    "hidden": 1.4,
    "expand": 1.1,
    "expand_back": 0.8,
    "hidden_back": 1.4,
    "reset_back": 1.2,
    "attention_back": 1.9,
    "smooth_back": 2.0,
    "states_back": 2.5,
    "state_back": 2.7,
    "norm_back": 1.8,
    "block_out": 1.7,
    "grad": 1.4,
    "split": 0.35,
    "join": 0.35,
    "sum": 0.25,
    "out": 1.6,
}
PACE = 1e10


def cost_of(name):
    return COSTS.get(name, COSTS.get(name.split("_")[-1], 0.6))


class Line:
    def __init__(self):
        self.token = None

    def __call__(self, body, ins, outs, scratch=(), name=None, held=None, alias=None, dma=0):
        count = len(ins)
        before = () if self.token is None else (self.token,)
        alias = alias or {}
        specs = []
        for i, a in enumerate(ins):
            if i in alias:
                specs.append(pl.BlockSpec(memory_space=pl.ANY))
            else:
                specs.append(pl.BlockSpec(memory_space=pltpu.SMEM if a.dtype == jnp.int32 else pltpu.VMEM))
        specs += [pl.BlockSpec(memory_space=pl.ANY)] * len(before)
        if held is None:
            held = sum(a.size * a.dtype.itemsize for a in ins if a.dtype != jnp.int32)
            held += sum(math.prod(s) * jnp.dtype(d).itemsize for s, d in tuple(outs) + tuple(scratch))

        def run(*refs):
            body(*refs[:count], *refs[count + len(before) : count + len(before) + len(outs)], *refs[count + len(before) + len(outs) + 1 :])
            refs[count + len(before) + len(outs)][...] = jnp.zeros((8, 128), F32)

        place = pl.ANY if dma else pltpu.VMEM
        scratches = [pltpu.VMEM(s, d) for s, d in scratch]
        if dma:
            scratches.append(pltpu.SemaphoreType.DMA((dma,)))
        result = pl.pallas_call(
            run,
            in_specs=specs,
            out_specs=[pl.BlockSpec(memory_space=place)] * len(outs) + [pl.BlockSpec(memory_space=pltpu.VMEM)],
            out_shape=[jax.ShapeDtypeStruct(s, d) for s, d in outs] + [jax.ShapeDtypeStruct((8, 128), F32)],
            scratch_shapes=scratches,
            input_output_aliases=alias,
            compiler_params=pltpu.CompilerParams(vmem_limit_bytes=int(held * 1.05) + ROOM),
            cost_estimate=pl.CostEstimate(flops=int(cost_of(name) * PACE), bytes_accessed=0, transcendentals=0),
            name=name,
        )(*ins, *before)
        self.token = result[-1]
        return result[:-1]


def clear_range(meta, low, high):
    count = meta.shape[0] - 2
    begin = jnp.int32(0)
    hit = jnp.bool_(False)
    for i in range(count):
        length = meta[1 + i]
        hit = hit | ((length > 0) & (begin >= low) & (begin < high))
        begin = begin + length
    return jnp.where(hit, 0.0, 1.0).astype(F32)


def chunk_masks(meta, first, chunks):
    rows = lax.broadcasted_iota(jnp.int32, (chunks, 128), 0)
    free = jnp.ones((chunks, 128), F32)
    for s in range(0, chunks, SPAN // CHUNK):
        position = first + s * CHUNK
        free = jnp.where(rows == s, clear_range(meta, position, position + 1), free)
    return free


def lanes_of(tile):
    return pl.ds(tile * 128, 128)


def tiled(ref):
    return jnp.concatenate([ref[i] for i in range(ref.shape[0])], axis=1)


def put_tiled(ref, value):
    for i in range(ref.shape[0]):
        ref[i] = value[:, i * 128 : (i + 1) * 128]


def scan_step(masks, values, decay_row, shifts, chunks):
    power = decay_row
    for i, mask in enumerate(masks):
        values = values + power * (mask * pltpu.roll(values, shifts[i], 0))
        power = power * power
    return values


def doubling_masks(mask, chunks, backward):
    masks = []
    distance = 1
    while distance < chunks:
        masks.append(mask)
        shift = chunks - distance if backward else distance
        mask = mask * pltpu.roll(mask, shift, 0)
        distance *= 2
    shifts = []
    distance = 1
    while distance < chunks:
        shifts.append(chunks - distance if backward else distance)
        distance *= 2
    return masks, shifts


def edge_masks(free, chunks, backward):
    rows = lax.broadcasted_iota(jnp.int32, (chunks, 128), 0)
    if backward:
        return jnp.where(rows == chunks - 1, 0.0, pltpu.roll(free, chunks - 1, 0))
    return jnp.where(rows == 0, 0.0, free)


def prefix_mask(free, chunks, backward):
    rows = lax.broadcasted_iota(jnp.int32, (chunks, 128), 0)
    if backward:
        reach = jnp.where(rows == chunks - 1, 1.0, pltpu.roll(free, chunks - 1, 0))
    else:
        reach = free
    distance = 1
    while distance < chunks:
        if backward:
            moved = jnp.where(rows >= chunks - distance, 1.0, pltpu.roll(reach, chunks - distance, 0))
        else:
            moved = jnp.where(rows < distance, 1.0, pltpu.roll(reach, distance, 0))
        reach = reach * moved
        distance *= 2
    return reach


def start_body(meta, tok, gain, delta, alpha, beta, eta, normed, low, enter, end, logk, keep, mix):
    tokens, width = tok.shape
    hidden = delta.shape[0]
    chunks = tokens // CHUNK
    x = tok[...].astype(F32)
    centered = x - jnp.mean(x, axis=1, keepdims=True)
    spread = jnp.mean(centered * centered, axis=1, keepdims=True)
    rows = centered * lax.rsqrt(spread + EPS) * gain[...]
    put_tiled(normed, rows)
    low[...] = rows.astype(BF16)
    share = jax.nn.sigmoid(delta[...])
    log_keep = jnp.log1p(-share * jax.nn.sigmoid(alpha[...]))
    logk[...] = log_keep
    keep[...] = jnp.exp(log_keep)
    mix[...] = share * beta[...] * (eta[...] * (1.0 / math.sqrt(hidden)))
    free = chunk_masks(meta, meta[0] * tokens, chunks)
    edge = edge_masks(free, chunks, False)
    masks, shifts = doubling_masks(edge, chunks, False)
    for tile in range(width // 128):
        lanes = lanes_of(tile)
        keeps = [keep[h : h + 1, lanes] for h in range(hidden)]

        def step(t, state):
            value = normed[tile, pl.ds(t, chunks, stride=CHUNK), :]
            return tuple(k * u + value for k, u in zip(keeps, state))

        zero = jnp.zeros((chunks, 128), F32)
        state = lax.fori_loop(0, CHUNK, step, (zero,) * hidden, unroll=8)
        for h in range(hidden):
            decay = jnp.exp(CHUNK * logk[h : h + 1, lanes])
            reached = scan_step(masks, state[h], decay, shifts, chunks)
            enter[h, :, lanes] = edge * pltpu.roll(reached, 1, 0)
            end[h : h + 1, lanes] = reached[chunks - 1 : chunks]


def values_body(low, weight, values, slope):
    for b in range(weight.shape[1] // 256):
        cols = pl.ds(b * 256, 256)
        raw = mm(low[...], weight[:, cols])
        gate = sigmoid(raw)
        out = raw * gate
        values[:, cols] = out.astype(BF16)
        slope[:, cols] = gate + out * (1.0 - gate)


def add_up(parts):
    while len(parts) > 1:
        parts = [a + b for a, b in zip(parts[::2], parts[1::2])]
    return parts[0]


def local_body(normed, enter, keep, mix, smooth):
    chunks = enter.shape[1]
    hidden = keep.shape[0]
    for tile in range(normed.shape[0]):
        lanes = lanes_of(tile)
        keeps = [keep[h : h + 1, lanes] for h in range(hidden)]
        mixes = [mix[h : h + 1, lanes] for h in range(hidden)]

        def step(t, state):
            place = (tile, pl.ds(t, chunks, stride=CHUNK), slice(None))
            value = normed[place]
            state = tuple(k * u + value for k, u in zip(keeps, state))
            smooth[place] = add_up([c * u for c, u in zip(mixes, state)])
            return state

        lax.fori_loop(0, CHUNK, step, tuple(enter[h, :, lanes] for h in range(hidden)), unroll=8)


def pair_body(backward, tokens, meta, own, other, logk, out):
    core = meta[0] % 2
    first = (meta[0] - core) * tokens
    middle = first + tokens
    decay = jnp.exp(tokens * logk[...])
    if backward:
        reach = clear_range(meta, first + 1, middle + 1)
        near = jnp.where(core == 0, own[...], other[...])
        far = jnp.where(core == 0, other[...], own[...])
    else:
        reach = clear_range(meta, middle, middle + tokens)
        near = jnp.where(core == 0, other[...], own[...])
        far = jnp.where(core == 0, own[...], other[...])
    out[...] = near + (reach * decay) * far


def carry_of(backward, tokens, meta, other, arrived, logk):
    core = meta[0] % 2
    first = (meta[0] - core) * tokens
    span = 2 * tokens
    chip_decay = jnp.exp(span * logk[...])
    total = None
    power = None
    for k, part in enumerate(arrived):
        if backward:
            reach = clear_range(meta, first + span, first + (k + 1) * span + 1)
        else:
            reach = clear_range(meta, first - k * span, first)
        term = part[...] * reach
        if power is not None:
            term = term * power
        total = term if total is None else total + term
        power = chip_decay if power is None else power * chip_decay
    decay = jnp.exp(tokens * logk[...])
    middle = first + tokens
    if backward:
        crossing = clear_range(meta, middle, middle + 1)
        through = clear_range(meta, middle + 1, middle + tokens)
        passed = crossing * (other[...] + (through * decay) * total)
        return jnp.where(core == 0, passed, total)
    through = clear_range(meta, first, middle)
    return jnp.where(core == 0, total, other[...] + (through * decay) * total)


def carried_body(chips, meta, other, *rest):
    arrived = rest[:chips]
    logk, keep, mix, omega, normed, smooth, enter, low, slope, states, carry, extra = rest[chips:]
    tiles, tokens, _ = normed.shape
    hidden = keep.shape[0]
    chunks = tokens // CHUNK
    carry[...] = carry_of(False, tokens, meta, other, arrived, logk)
    free = chunk_masks(meta, meta[0] * tokens, chunks)
    reach = prefix_mask(free, chunks, False)
    offset = (lax.broadcasted_iota(jnp.int32, (chunks, 128), 0) * CHUNK).astype(F32)
    for tile in range(tiles):
        lanes = lanes_of(tile)
        state = []
        for h in range(hidden):
            entry = jnp.exp(offset * logk[h : h + 1, lanes]) * reach
            first = carry[h : h + 1, lanes] * entry
            states[h, :, lanes] = enter[h, :, lanes] + first
            state.append(mix[h : h + 1, lanes] * first)
        keeps = [keep[h : h + 1, lanes] for h in range(hidden)]

        def step(t, state):
            place = pl.ds(t, chunks, stride=CHUNK)
            state = tuple(k * u for k, u in zip(keeps, state))
            extra[place, :] = add_up(list(state))
            return state

        lax.fori_loop(0, CHUNK, step, tuple(state), unroll=8)
        pre = smooth[tile] + extra[...] + omega[:, lanes] * normed[tile]
        gate = sigmoid(pre)
        smoothed = pre * gate
        low[:, lanes] = smoothed.astype(BF16)
        slope[:, lanes] = gate + smoothed * (1.0 - gate)


def layer_grad(weighted, normal, inverse):
    mean_one = jnp.mean(weighted, axis=1, keepdims=True)
    mean_two = jnp.mean(weighted * normal, axis=1, keepdims=True)
    return (weighted - mean_one - normal * mean_two) * inverse


def shift_rows(table, down):
    size = table.shape[0]
    rows = lax.broadcasted_iota(jnp.int32, table.shape, 0)
    bit = 1
    while bit < size:
        moved = pltpu.roll(table, bit if down else size - bit, 1)
        table = jnp.where((rows & bit) != 0, moved, table)
        bit *= 2
    return table


def mix_body(low, mix_weight, qk_gain, qk_bias, update, candidate, reset, queries, keys, shared, shared_slope):
    width = update.shape[1]
    base = width + shared.shape[1]
    top = base + reset.shape[1]
    raw = mm(low[...], mix_weight[:, width:base])
    gate = sigmoid(raw)
    silu = raw * gate
    shared[...] = silu
    shared_slope[...] = gate + silu * (1.0 - gate)
    queries[...] = (silu * qk_gain[0:1] + qk_bias[0:1]).astype(BF16)
    keys[...] = (silu * qk_gain[1:2] + qk_bias[1:2]).astype(BF16)
    for b in range(width // 256):
        update[:, b * 256 : (b + 1) * 256] = sigmoid(mm(low[...], mix_weight[:, b * 256 : (b + 1) * 256]))
    for b in range(reset.shape[1] // 256):
        reset[:, b * 256 : (b + 1) * 256] = mm(low[...], mix_weight[:, base + b * 256 : base + (b + 1) * 256])
    for b in range(width // 256):
        candidate[:, b * 256 : (b + 1) * 256] = mm(low[...], mix_weight[:, top + b * 256 : top + (b + 1) * 256])


def attend_body(queries, keys, values, rel_rev, reset, weights, attended, gated):
    tokens, shared_width = queries.shape
    place = lax.broadcasted_iota(jnp.int32, (SPAN, SPAN), 0)
    causal = place >= lax.broadcasted_iota(jnp.int32, (SPAN, SPAN), 1)
    bias = shift_rows(jnp.broadcast_to(rel_rev[...], (SPAN, SPAN)), True)
    scale = 1.0 / math.sqrt(shared_width)
    for s in range(tokens // SPAN):
        rows = pl.ds(s * SPAN, SPAN)
        scores = mm_nt(queries[rows, :], keys[rows, :]) * scale + bias
        scores = jnp.where(causal, scores, -1e30)
        powers = jnp.exp(scores - jnp.max(scores, axis=1, keepdims=True))
        share = powers / jnp.sum(powers, axis=1, keepdims=True)
        weights[rows, :] = share
        rise = mm(share.astype(BF16), values[rows, :])
        attended[rows, :] = rise
        raw = reset[rows, :]
        gated[rows, :] = (raw * sigmoid(raw) * rise).astype(BF16)


def hidden_body(
    gated, out_weight, candidate, update, tok, gain2, residual, change, slope_hidden, normal2, inverse2, low2
):
    total = candidate[...] + mm(gated[...], out_weight[...])
    gate = sigmoid(total)
    hidden_rows = total * gate
    slope_hidden[...] = gate + hidden_rows * (1.0 - gate)
    x = tok[...].astype(F32)
    moved = hidden_rows - x
    change[...] = moved
    rows = x + update[...] * moved
    residual[...] = rows
    centered = rows - jnp.mean(rows, axis=1, keepdims=True)
    inverse = lax.rsqrt(jnp.mean(centered * centered, axis=1, keepdims=True) + EPS)
    normal = centered * inverse
    normal2[...] = normal
    inverse2[...] = jnp.broadcast_to(inverse, inverse2.shape)
    low2[...] = (normal * gain2[...]).astype(BF16)


def expand_body(low2, ffn_in, expanded, slope_exp):
    for b in range(ffn_in.shape[1] // 256):
        cols = pl.ds(b * 256, 256)
        raw = mm(low2[...], ffn_in[:, cols])
        gate = sigmoid(raw)
        silu = raw * gate
        expanded[:, cols] = silu.astype(BF16)
        slope_exp[:, cols] = gate + silu * (1.0 - gate)


def weights_body(parts, meta, *refs):
    kept, sent = refs[-2:]
    pairs = refs[:-2]
    half = kept.shape[0]
    core = meta[0] % 2
    for target, side in ((sent, 1 - core), (kept, core)):
        for i, (column, block) in enumerate(parts):
            left, right = pairs[2 * i], pairs[2 * i + 1]
            begin = pl.multiple_of(side * half + block, 128)
            target[:, column : column + right.shape[1]] = mm_tn(left[:, pl.ds(begin, half)], right[...])


def block_body(residual, expanded, ffn_out, out):
    out[...] = residual[...] + mm(expanded[...], ffn_out[...])


def expand_back_body(cot, ffn_out, slope_exp, expand_grad):
    for b in range(ffn_out.shape[0] // 256):
        cols = pl.ds(b * 256, 256)
        expand_grad[:, cols] = (mm_nt(cot[...], ffn_out[cols, :]) * slope_exp[:, cols]).astype(BF16)


def hidden_back_body(
    expand_grad,
    ffn_in,
    normal2,
    inverse2,
    gain2,
    cot,
    update,
    change,
    slope_hidden,
    input_part,
    update_grad,
    out_grad,
    gain2_grad,
):
    norm_out = mm_nt(expand_grad[...], ffn_in[...])
    normal = normal2[...]
    gain2_grad[...] = jnp.sum(norm_out * normal, axis=0, keepdims=True)
    upstream = cot[...].astype(F32) + layer_grad(norm_out * gain2[...], normal, inverse2[:, 0:1])
    gates = update[...]
    input_part[...] = upstream * (1.0 - gates)
    update_grad[...] = (upstream * change[...] * gates * (1.0 - gates)).astype(BF16)
    out_grad[...] = (upstream * gates * slope_hidden[...]).astype(BF16)


def reset_back_body(out_grad, out_weight, reset, attended, reset_grad, attend_grad):
    for b in range(reset.shape[1] // 256):
        cols = pl.ds(b * 256, 256)
        rise = mm_nt(out_grad[...], out_weight[cols, :])
        raw = reset[:, cols]
        gate = sigmoid(raw)
        silu = raw * gate
        reset_grad[:, cols] = (rise * attended[:, cols] * (gate + silu * (1.0 - gate))).astype(BF16)
        attend_grad[:, cols] = (rise * silu).astype(BF16)


def attend_back_body(
    attend_grad,
    weights,
    queries,
    keys,
    shared,
    shared_slope,
    values,
    values_slope,
    qk_gain,
    value_grad,
    shared_grad,
    small,
):
    tokens, shared_width = queries.shape
    scale = 1.0 / math.sqrt(shared_width)
    slopes = jnp.zeros((SPAN, SPAN), F32)
    for s in range(tokens // SPAN):
        rows = pl.ds(s * SPAN, SPAN)
        upstream = attend_grad[rows, :]
        share = weights[rows, :]
        rise = mm_nt(upstream, values[rows, :])
        value_rise = mm_tn(share.astype(BF16), upstream)
        value_grad[rows, :] = (value_rise * values_slope[rows, :]).astype(BF16)
        score_grad = share * (rise - jnp.sum(share * rise, axis=1, keepdims=True))
        slopes = slopes + score_grad
        low = (score_grad * scale).astype(BF16)
        query_grad = mm(low, keys[rows, :])
        key_grad = mm_tn(low, queries[rows, :])
        silu = shared[rows, :]
        pieces = (
            jnp.sum(query_grad * silu, axis=0, keepdims=True),
            jnp.sum(key_grad * silu, axis=0, keepdims=True),
            jnp.sum(query_grad, axis=0, keepdims=True),
            jnp.sum(key_grad, axis=0, keepdims=True),
        )
        sums = pieces if s == 0 else tuple(a + b for a, b in zip(sums, pieces))
        back = query_grad * qk_gain[0:1] + key_grad * qk_gain[1:2]
        shared_grad[rows, :] = (back * shared_slope[rows, :]).astype(BF16)
    small[...] = jnp.zeros_like(small)
    for i in range(4):
        small[i : i + 1, :] = sums[i]
    small[4:5, :] = jnp.sum(shift_rows(slopes, False), axis=0, keepdims=True)


def smooth_back_body(
    update_grad,
    shared_grad,
    reset_grad,
    out_grad,
    value_grad,
    mix_weight,
    value_weight,
    slope_pre,
    normed,
    omega,
    smooth_grad,
    norm_grad,
    omega_grad,
):
    width = update_grad.shape[1]
    base = width + shared_grad.shape[1]
    top = base + reset_grad.shape[1]
    rise = mm_nt(reset_grad[...], mix_weight[:, base:top])
    rise = rise + mm_nt(update_grad[...], mix_weight[:, :width])
    rise = rise + mm_nt(out_grad[...], mix_weight[:, top:])
    rise = rise + mm_nt(shared_grad[...], mix_weight[:, width:base])
    grad = rise * slope_pre[...]
    put_tiled(smooth_grad, grad)
    put_tiled(norm_grad, mm_nt(value_grad[...], value_weight[...]) + omega[...] * grad)
    omega_grad[...] = jnp.sum(grad * tiled(normed), axis=0, keepdims=True)


def rise_body(meta, smooth_grad, logk, keep, enter, end):
    tiles, tokens, _ = smooth_grad.shape
    hidden = keep.shape[0]
    chunks = tokens // CHUNK
    free = chunk_masks(meta, meta[0] * tokens, chunks)
    edge = edge_masks(free, chunks, True)
    masks, shifts = doubling_masks(edge, chunks, True)
    for tile in range(tiles):
        lanes = lanes_of(tile)
        keeps = [keep[h : h + 1, lanes] for h in range(hidden)]

        def step(t, state):
            value = smooth_grad[tile, pl.ds(CHUNK - 1 - t, chunks, stride=CHUNK), :]
            return tuple(k * u + value for k, u in zip(keeps, state))

        zero = jnp.zeros((chunks, 128), F32)
        state = lax.fori_loop(0, CHUNK, step, (zero,) * hidden, unroll=8)
        for h in range(hidden):
            decay = jnp.exp(CHUNK * logk[h : h + 1, lanes])
            reached = scan_step(masks, state[h], decay, shifts, chunks)
            enter[h, :, lanes] = edge * pltpu.roll(reached, chunks - 1, 0)
            end[h : h + 1, lanes] = reached[0:1]


def carry_back_body(chips, meta, other, *rest):
    arrived = rest[:chips]
    logk, enter, later = rest[chips:]
    hidden, chunks, width = enter.shape
    tokens = chunks * CHUNK
    carry = carry_of(True, tokens, meta, other, arrived, logk)
    free = chunk_masks(meta, meta[0] * tokens, chunks)
    reach = prefix_mask(free, chunks, True)
    offset = ((chunks - 1 - lax.broadcasted_iota(jnp.int32, (chunks, 128), 0)) * CHUNK).astype(F32)
    for tile in range(width // 128):
        lanes = lanes_of(tile)
        for h in range(hidden):
            entry = jnp.exp(offset * logk[h : h + 1, lanes]) * reach
            later[h, :, lanes] = enter[h, :, lanes] + carry[h : h + 1, tile * 128 : (tile + 1) * 128] * entry


def state_back_body(tile, normed, smooth_grad, norm_grad, states, later, keep, mix, total, sums, history):
    hidden = keep.shape[0]
    chunks = states.shape[1]
    lanes = lanes_of(tile)
    heads = range(hidden)
    keeps = [keep[h : h + 1, lanes] for h in heads]
    mixes = [mix[h : h + 1, lanes] for h in heads]

    def rise(t, state):
        value = normed[tile, pl.ds(t, chunks, stride=CHUNK), :]
        state = tuple(k * u + value for k, u in zip(keeps, state))
        for i in heads:
            history[t, i] = state[i]
        return state

    lax.fori_loop(0, CHUNK, rise, tuple(states[h, :, lanes] for h in heads), unroll=4)

    def fall(i, held):
        state, reads, marks = held
        t = CHUNK - 1 - i
        place = pl.ds(t, chunks, stride=CHUNK)
        value = smooth_grad[tile, place, :]
        row = normed[tile, place, :]
        state = tuple(k * w + value for k, w in zip(keeps, state))
        reads = tuple(r + w * row for r, w in zip(reads, state))
        marks = tuple(m + w * history[t, j] for j, (m, w) in enumerate(zip(marks, state)))
        total[place, :] = norm_grad[tile, place, :] + add_up([c * w for c, w in zip(mixes, state)])
        return state, reads, marks

    zeros = (jnp.zeros((chunks, 128), F32),) * hidden
    first = tuple(later[h, :, lanes] for h in heads)
    _, reads, marks = lax.fori_loop(0, CHUNK, fall, (first, zeros, zeros), unroll=4)
    for h in heads:
        sums[h : h + 1, :] = jnp.sum(reads[h], axis=0, keepdims=True)
        sums[hidden + h : hidden + h + 1, :] = jnp.sum(marks[h], axis=0, keepdims=True)


def close_body(count, *refs):
    totals = refs[:count]
    sums = refs[count : 2 * count]
    tok, gain, input_part, omega_grad, gain2_grad, small, input_grad, packed = refs[2 * count :]
    x = tok[...].astype(F32)
    centered = x - jnp.mean(x, axis=1, keepdims=True)
    inverse = lax.rsqrt(jnp.mean(centered * centered, axis=1, keepdims=True) + EPS)
    normal = centered * inverse
    upstream = jnp.concatenate([t[...] for t in totals], axis=1)
    input_grad[...] = input_part[...] + layer_grad(upstream * gain[...], normal, inverse)
    at = sums[0].shape[0]
    for i in range(count):
        packed[0:at, i * 128 : (i + 1) * 128] = sums[i][...]
    packed[at : at + 8, :] = jnp.zeros((8, x.shape[1]), F32)
    packed[at : at + 1, :] = jnp.sum(upstream * normal, axis=0, keepdims=True)
    packed[at + 1 : at + 2, :] = gain2_grad[...]
    packed[at + 2 : at + 3, :] = omega_grad[...]
    for i in range(5):
        packed[at + 3 + i : at + 4 + i, 0 : small.shape[1]] = small[i : i + 1, :]


def finish_body(packed, delta, alpha, beta, eta, delta_grad, alpha_grad, beta_grad, eta_grad):
    hidden = delta.shape[0]
    scale = 1.0 / math.sqrt(hidden)
    read = packed[0:hidden, :]
    mark = packed[hidden : 2 * hidden, :]
    share = jax.nn.sigmoid(delta[...])
    damp = jax.nn.sigmoid(alpha[...])
    inflow = share * beta[...]
    outflow = eta[...] * scale
    eta_grad[...] = inflow * read * scale
    inflow_grad = outflow * read
    beta_grad[...] = share * inflow_grad
    rate = inflow * outflow * (mark - read) / (share * damp - 1.0)
    share_grad = beta[...] * inflow_grad + damp * rate
    delta_grad[...] = share_grad * share * (1.0 - share)
    alpha_grad[...] = share * rate * damp * (1.0 - damp)


def swap(a, axis, bit):
    count = lax.axis_size(axis)
    return lax.ppermute(a, axis, [(i, i ^ bit) for i in range(count)])


def chip_parts(state, backward):
    count = lax.axis_size("seq")
    parts = []
    for k in range(1, count // 2):
        if backward:
            moves = [(i, i - 2 * k) for i in range(2 * k, count)]
        else:
            moves = [(i, i + 2 * k) for i in range(count - 2 * k)]
        parts.append(lax.ppermute(state, "seq", moves))
    return parts


def axis_bits(axis, least):
    bits = []
    bit = least
    while bit < lax.axis_size(axis):
        bits.append((axis, bit))
        bit *= 2
    return bits


def cross(a, step):
    seq = lax.axis_size("seq")
    moves = []
    for i in range(lax.axis_size("dp") * seq):
        axis, bit = step[i % 2]
        moves.append((i, i ^ (bit * seq if axis == "dp" else bit)))
    return lax.ppermute(a, ("dp", "seq"), moves)


ROUTES = (
    (("xy1", "yx1"), "2"),
    (("xy1", "yx1"), "2"),
    (("1xy", "1yx"), "2"),
    (("xy1", "yx1"), "2"),
    (("xy1", "yx1"), "2"),
)
ORDER = "0KK3014K0231KK0412034201K3K04K21032413K24K3KK41K312K34K24"
BITS = {"x": ("dp", 1), "y": ("dp", 2), "1": ("seq", 2), "2": ("seq", 4)}


def route(halving, doubling):
    named = lambda pair: all(BITS[c][1] < lax.axis_size(BITS[c][0]) for c in pair)
    halves = [tuple(BITS[c] for c in pair) for pair in zip(*halving) if named(pair)]
    wholes = [(BITS[c], BITS[c]) for c in doubling if named(c)]
    for bit in axis_bits("dp", 1) + axis_bits("seq", 2):
        if bit not in BITS.values():
            halves.append((bit, bit))
    return halves, wholes


def masks_body(steps, meta, out):
    for i, step in enumerate(steps):
        place = [(meta[0] if axis == "seq" else meta[meta.shape[0] - 1]) // bit % 2 for axis, bit in step]
        side = jnp.where(meta[0] % 2 == 0, place[0], place[1])
        out[i] = jnp.full((8, 128), side.astype(F32))


def split_body(index, masks, kept, arrived, keep, send):
    half = keep.shape[0]
    upper = masks[index, 0:1, 0:1] > 0.5
    low = kept[:half, :] + arrived[:half, :]
    high = kept[half:, :] + arrived[half:, :]
    keep[...] = jnp.where(upper, high, low)
    send[...] = jnp.where(upper, low, high)


def sum_body(kept, arrived, out):
    out[...] = kept[...] + arrived[...]


def join_body(index, masks, own, other, out):
    half = own.shape[0]
    upper = masks[index, 0:1, 0:1] > 0.5
    out[:half, :] = jnp.where(upper, other[...], own[...])
    out[half:, :] = jnp.where(upper, own[...], other[...])


class Piece:
    def __init__(self, line, masks, steps, kept, sent, routes, outputs, name):
        self.line, self.masks, self.steps, self.name = line, masks, steps, name
        self.outputs = outputs
        self.work = self.run(kept, sent, *routes)
        self.done = False
        self.advance()

    def advance(self):
        if not self.done:
            self.done = next(self.work, "end") == "end"

    def run(self, kept, sent, halves, wholes):
        line, masks = self.line, self.masks
        arrived = swap(sent, "seq", 1)
        yield
        for step in halves:
            rows, cols = kept.shape
            kept, send = line(
                lambda *refs, index=self.steps.index(step): split_body(index, *refs),
                (masks, kept, arrived),
                [((rows // 2, cols), F32)] * 2,
                name=self.name + "_split",
            )
            arrived = cross(send, step)
            yield
        for step in wholes:
            kept = line(sum_body, (kept, arrived), [(kept.shape, F32)], name=self.name + "_sum")[0]
            arrived = cross(kept, step)
            yield
        part = line(sum_body, (kept, arrived), [(kept.shape, F32)], name=self.name + "_sum")[0]
        for i, step in enumerate(reversed(halves)):
            other = cross(part, step)
            yield
            rows, cols = part.shape
            part = line(
                lambda *refs, index=self.steps.index(step): join_body(index, *refs),
                (masks, part, other),
                [((2 * rows, cols), F32)],
                name=self.name + "_join",
            )[0]
        other = swap(part, "seq", 1)
        self.outputs(part, False)
        yield
        self.outputs(other, True)


def place_body(plans, far, count, meta, part, *refs):
    outs = refs[count : count + len(plans)]
    sems = refs[-1]
    side = meta[0] % 2
    side = 1 - side if far else side
    rows = part.shape[0]
    copies = []
    for out, plan in zip(outs, plans):
        for column, width, row, place in plan:
            begin = pl.multiple_of(side * rows + row, 8)
            copies.append(
                pltpu.make_async_copy(
                    part.at[:, pl.ds(column, width)],
                    out.at[pl.ds(begin, rows), pl.ds(place, width)],
                    sems.at[len(copies)],
                )
            )
            copies[-1].start()
    for copy in copies:
        copy.wait()


class Outputs:
    def __init__(self, line, meta, shapes):
        self.line, self.meta, self.shapes, self.arrays = line, meta, shapes, {}

    def placer(self, plans, name):
        def place(part, far):
            names = list(plans)
            held = [n for n in names if n in self.arrays]
            alias = {2 + i: names.index(n) for i, n in enumerate(held)}
            results = self.line(
                lambda *refs: place_body(list(plans.values()), far, len(held), *refs),
                (self.meta, part, *[self.arrays[n] for n in held]),
                [(self.shapes[n], F32) for n in names],
                name=name + "_out",
                held=part.size * 4,
                alias=alias,
                dma=sum(len(p) for p in plans.values()),
            )
            self.arrays.update(zip(names, results))

        return place


def shards(
    tokens,
    cotangent,
    seq_lengths,
    norm1_gain,
    value_weight,
    ema_delta,
    ema_alpha,
    ema_beta,
    ema_eta,
    ema_omega,
    mix_weight,
    qk_gain,
    qk_bias,
    rel_bias,
    out_weight,
    norm2_gain,
    ffn_in,
    ffn_out,
):
    rows, width = tokens.shape
    hidden = ema_delta.shape[1]
    chunks = rows // CHUNK
    value_width = value_weight.shape[1]
    inner = ffn_in.shape[1]
    mixed = mix_weight.shape[1]
    shared_width = qk_gain.shape[1]
    places = jnp.stack([lax.axis_index("seq"), lax.axis_index("dp")]).astype(jnp.int32)
    meta = jnp.concatenate([places[:1], seq_lengths[0], places[1:]])
    gain1 = norm1_gain[None]
    gain2 = norm2_gain[None]
    omega = ema_omega[None]
    rel_rev = jnp.roll(rel_bias[::-1], 1)[None]
    ema = (ema_delta.T, ema_alpha.T, ema_beta.T, ema_eta.T)
    full = (rows, width)
    wide = (rows, value_width)
    thin = (rows, shared_width)
    tiles = (width // 128, rows, 128)
    state = (hidden, width)
    states = (hidden, chunks, width)
    line = Line()

    normed, low_normed, enter, end, logk, keep, mix = line(
        start_body,
        (meta, tokens, gain1, *ema),
        [(tiles, F32), (full, BF16), (states, F32), (state, F32), (state, F32), (state, F32), (state, F32)],
        name="norm_and_states",
    )
    other = swap(end, "seq", 1)
    chip_end = line(
        lambda *refs: pair_body(False, rows, *refs), (meta, end, other, logk), [(state, F32)], name="chip_state"
    )[0]
    arrived = chip_parts(chip_end, False)
    routes = [route(halving, doubling) for halving, doubling in ROUTES]
    steps = sorted({step for halves, wholes in routes for step in halves})
    masks = line(lambda *refs: masks_body(steps, *refs), (meta,), [((len(steps), 8, 128), F32)], name="masks")[0]
    values, values_slope = line(values_body, (low_normed, value_weight), [(wide, BF16), (wide, F32)], name="values")
    smooth = line(local_body, (normed, enter, keep, mix), [(tiles, F32)], name="local_average")[0]
    low_smoothed, slope_pre, entering = line(
        lambda *refs: carried_body(len(arrived), *refs),
        (meta, other, *arrived, logk, keep, mix, omega, normed, smooth, enter),
        [(full, BF16), (full, F32), (states, F32)],
        scratch=[(state, F32), ((rows, 128), F32)],
        name="carried_average",
    )
    update, candidate, reset, queries, keys, shared, shared_slope = line(
        mix_body,
        (low_smoothed, mix_weight, qk_gain, qk_bias),
        [(full, F32), (full, F32), (wide, F32), (thin, BF16), (thin, BF16), (thin, F32), (thin, F32)],
        name="mix",
    )
    weights, attended, gated = line(
        attend_body,
        (queries, keys, values, rel_rev, reset),
        [((rows, SPAN), F32), (wide, F32), (wide, BF16)],
        name="attention",
    )
    residual, change, slope_hidden, normal2, inverse2, low2 = line(
        hidden_body,
        (gated, out_weight, candidate, update, tokens, gain2),
        [(full, F32), (full, F32), (full, F32), (full, F32), ((rows, 128), F32), (full, BF16)],
        name="hidden",
    )
    expanded, slope_exp = line(
        expand_body, (low2, ffn_in), [((rows, inner), BF16), ((rows, inner), F32)], name="expand"
    )
    half = width // 2
    outputs = Outputs(
        line,
        meta,
        {
            "ffn_out": (inner, width),
            "ffn_in": (width, inner),
            "out": (value_width, width),
            "mix": (width, mixed),
            "value": (width, value_width),
        },
    )
    pieces = []

    def start_piece(parts, pairs, height, cols, plans, name):
        kept, sent = line(
            lambda *refs: weights_body(parts, *refs),
            (meta, *[a for pair in pairs for a in pair]),
            [((height, cols), F32)] * 2,
            name=name + "_grad",
        )
        pieces.append(
            Piece(line, masks, steps, kept, sent, routes[len(pieces)], outputs.placer(plans, name), name)
        )

    def step(*which):
        for i in which:
            pieces[i].advance()

    start_piece(
        [(0, 0)], [(expanded, cotangent)], inner // 2, width, {"ffn_out": [(0, width, 0, 0)]}, "ffn_out"
    )
    expand_grad = line(
        expand_back_body, (cotangent, ffn_out, slope_exp), [((rows, inner), BF16)], name="expand_back"
    )[0]
    step(0)
    input_part, update_grad, out_grad, gain2_grad = line(
        hidden_back_body,
        (expand_grad, ffn_in, normal2, inverse2, gain2, cotangent, update, change, slope_hidden),
        [(full, F32), (full, BF16), (full, BF16), ((1, width), F32)],
        name="hidden_back",
    )
    start_piece(
        [(0, 0), (inner, 0)],
        [(low2, expand_grad), (low_smoothed, update_grad)],
        half,
        inner + width,
        {"ffn_in": [(0, inner, 0, 0)], "mix": [(inner, width, 0, 0)]},
        "ffn_in",
    )
    start_piece(
        [(0, 0), (width, width), (2 * width, 0)],
        [(gated, out_grad), (gated, out_grad), (low_smoothed, out_grad)],
        half,
        3 * width,
        {
            "out": [(0, width, 0, 0), (width, width, width, 0)],
            "mix": [(2 * width, width, 0, width + shared_width + value_width)],
        },
        "out",
    )
    step(1)
    reset_grad, attend_grad = line(
        reset_back_body, (out_grad, out_weight, reset, attended), [(wide, BF16)] * 2, name="reset_back"
    )
    step(2)
    value_grad, shared_grad, small = line(
        attend_back_body,
        (attend_grad, weights, queries, keys, shared, shared_slope, values, values_slope, qk_gain),
        [(wide, BF16), (thin, BF16), ((8, shared_width), F32)],
        name="attention_back",
    )
    start_piece(
        [(0, 0)],
        [(low_smoothed, reset_grad)],
        half,
        value_width,
        {"mix": [(0, value_width, 0, width + shared_width)]},
        "reset",
    )
    start_piece(
        [(0, 0), (value_width, 0)],
        [(low_normed, value_grad), (low_smoothed, shared_grad)],
        half,
        value_width + shared_width,
        {"value": [(0, value_width, 0, 0)], "mix": [(value_width, shared_width, 0, width)]},
        "value",
    )

    def rest():
        smooth_grad, norm_grad, omega_grad = line(
            smooth_back_body,
            (update_grad, shared_grad, reset_grad, out_grad, value_grad, mix_weight, value_weight, slope_pre)
            + (normed, omega),
            [(tiles, F32), (tiles, F32), ((1, width), F32)],
            name="smooth_back",
        )
        yield
        later, begin = line(
            rise_body, (meta, smooth_grad, logk, keep), [(states, F32), (state, F32)], name="states_back"
        )
        other_begin = swap(begin, "seq", 1)
        yield
        chip_begin = line(
            lambda *refs: pair_body(True, rows, *refs),
            (meta, begin, other_begin, logk),
            [(state, F32)],
            name="chip_grad",
        )[0]
        returned = chip_parts(chip_begin, True)
        yield
        later = line(
            lambda *refs: carry_back_body(len(returned), *refs),
            (meta, other_begin, *returned, logk, later),
            [(states, F32)],
            name="carry_back",
        )[0]
        yield
        backs = []
        for tile in range(width // 128):
            backs.append(
                line(
                    lambda *refs, tile=tile: state_back_body(tile, *refs),
                    (normed, smooth_grad, norm_grad, entering, later, keep, mix),
                    [((rows, 128), F32), ((2 * hidden, 128), F32)],
                    scratch=[((CHUNK, hidden, chunks, 128), F32)],
                    name="state_back",
                )
            )
            yield
        input_grad, packed = line(
            lambda *refs: close_body(len(backs), *refs),
            (*[b[0] for b in backs], *[b[1] for b in backs], tokens, gain1, input_part, omega_grad, gain2_grad, small),
            [(full, F32), ((2 * hidden + 8, width), F32)],
            name="norm_back",
        )
        results["input_grad"] = input_grad
        for axis, bit in axis_bits("seq", 1) + axis_bits("dp", 1):
            moved = swap(packed, axis, bit)
            yield
            packed = line(sum_body, (packed, moved), [(packed.shape, F32)], name="small_sum")[0]
        results["packed"] = packed
        results["ema"] = line(finish_body, (packed, *ema), [(state, F32)] * 4, name="state_parameters")
        yield
        results["block_out"] = line(block_body, (residual, expanded, ffn_out), [(full, F32)], name="block_out")[0]

    results = {}
    work = rest()
    for item in ORDER:
        if item == "K":
            next(work, None)
        else:
            step(int(item))
    for _ in work:
        pass
    while not all(p.done for p in pieces):
        step(*range(len(pieces)))
    packed = results["packed"]
    at = 2 * hidden
    tail = packed[at + 3 :, :shared_width]
    sums = outputs.arrays
    return (
        results["block_out"],
        results["input_grad"],
        packed[at],
        sums["value"],
        *[g.T for g in results["ema"]],
        packed[at + 2],
        sums["mix"],
        tail[0:2],
        tail[2:4],
        jnp.roll(tail[4][::-1], 1),
        sums["out"],
        packed[at + 1],
        sums["ffn_in"],
        sums["ffn_out"],
    )


def solution(mesh):
    rows = P(("dp", "seq"), None)
    in_specs = (rows, rows, P("dp", None)) + (P(),) * 15
    out_specs = (rows, rows) + (P(),) * 15
    return jax.shard_map(shards, mesh=mesh, in_specs=in_specs, out_specs=out_specs, check_vma=False)
```

time: 326 us -> 198 us (0.61)
  waiting for transfers between devices: 138 us -> 48.5 us
  other arithmetic: 26 us -> 2.05 us
  local copies, waits for them, and re-layouts: 27.1 us -> 10 us
  starting transfers between devices: 58.8 us -> 62.4 us
    ppermute x43 -> x17, waiting for transfers between devices: 130 us -> 4.15 us  [swap(): return lax.ppermute(a, axis, [(i, i ^ bit) for i in range(count)])]
    ppermute x0 -> x35, waiting for transfers between devices: none -> 44.4 us  [cross(): return lax.ppermute(a, ('dp', 'seq'), moves)]
    ppermute x0 -> x35, starting transfers between devices: none -> 38.6 us  [cross(): return lax.ppermute(a, ('dp', 'seq'), moves)]
    ppermute x43 -> x17, starting transfers between devices: 44.3 us -> 9.41 us  [swap(): return lax.ppermute(a, axis, [(i, i ^ bit) for i in range(count)])]
    select_n x18 -> x0, other arithmetic: 10 us -> none  [join(): return jnp.where(place == 0, own_first, other_first)]
    ppermute x6, waiting for transfers between devices: 7.7 us -> 0.02 us  [chip_parts(): parts.append(lax.ppermute(state, 'seq', moves))]
    unnamed x32 -> x74, local copies, waits for them, and re-layouts: 15.7 us -> 8.02 us
    concatenate x4 -> x1, other arithmetic: 7.93 us -> 0.73 us  [shards(): meta = jnp.concatenate([places[:1], seq_lengths[0], places[1:]])]
  transfers between devices with their start and end apart: 49 -> 58, of which waited for: 28 -> 16; matrix products, arithmetic and copies ran while one was open for 11% -> 2% of each run, Pallas kernels for 14% -> 27%
where the time goes in v2:
time: 198 us
  Pallas kernels  72.5 us (37%)
  starting transfers between devices  62.4 us (32%)
  waiting for transfers between devices  48.5 us (24%)
  local copies, waits for them, and re-layouts  10 us (5%)
  other arithmetic  2.05 us (1%)
  between operations  2.01 us (1%)
    pallas_call x85, Pallas kernels, __call__(): pl.pallas_call(run, in_specs=specs, out_specs=[pl.BlockSpec(memory_space=...  72.5 us
    ppermute x35, waiting for transfers between devices, cross(): return lax.ppermute(a, ('dp', 'seq'), moves)  44.4 us
    ppermute x35, starting transfers between devices, cross(): return lax.ppermute(a, ('dp', 'seq'), moves)  38.6 us
    ppermute x6, starting transfers between devices, chip_parts(): parts.append(lax.ppermute(state, 'seq', moves))  14.5 us
    ppermute x17, starting transfers between devices, swap(): return lax.ppermute(a, axis, [(i, i ^ bit) for i in range(count)])  9.41 us
    unnamed x74, local copies, waits for them, and re-layouts  8.02 us
    ppermute x17, waiting for transfers between devices, swap(): return lax.ppermute(a, axis, [(i, i ^ bit) for i in range(count)])  4.15 us
  transfers between devices with their start and end apart: 58, of which 16 were waited for; matrix products, arithmetic and copies ran while one was open for 2% of the time, Pallas kernels for 27%

profile of v2, /device:TPU:0, one launch (start us, length us, event | category | flops | bytes accessed | tf_op | source)
XLA Modules:
  0.0 197.6 jit_solution(2809734102790382153)
XLA Ops:
  6.2 2.8 %norm_and_states.1 = (f32[4,512,128]{2,1,0:T(8,128)S(1)}, bf16[512,512]{1,0:T(8,128)(2,1)S(1)}, f32[16,8,512]{2,1,0:T(8,128)S(1)}, f32[16,512]{1,0:T(8,128)S(1)}...) custom-call(s32[5]{0:T(128)S(1)} %pad_add_fusion.refs_0_, ...), custom_call_target="tpu_custom_call" | custom-call | flops 27000000512 | tf_op jit(solution)/shard_map/norm_and_states/pallas_call | solution.py:92
  10.9 6.8 %collective-permute-start.3 = (f32[16,512]{1,0:T(8,128)S(1)}, f32[16,512]{1,0:T(8,128)S(1)}, u32[]{:S(2)}, u32[]{:S(2)}) collective-permute-start(f32[16,512]{1,0:T(8,128)S(1)} %get-tuple-element.255), channel_id=1, source_target_pairs={{0,6},{1,7},{8,14},{9,15},{16,22},{17,23},{24,30},{25,31}} | collective-permute-start | bytes 98312 | tf_op jit(solution)/shard_map/ppermute | solution.py:680
  19.1 2.5 %collective-permute-start.1 = (f32[16,512]{1,0:T(8,128)S(1)}, f32[16,512]{1,0:T(8,128)S(1)}, u32[]{:S(2)}, u32[]{:S(2)}) collective-permute-start(f32[16,512]{1,0:T(8,128)S(1)} %get-tuple-element.255), channel_id=1, source_target_pairs={{0,2},{1,3},{2,4},{3,5},{4,6},{5,7},{8,10},{9,11},{10,12},{11,13},... | collective-permute-start | bytes 98312 | tf_op jit(solution)/shard_map/ppermute | solution.py:680
  23.8 3.1 %local_average.1 = (f32[4,512,128]{2,1,0:T(8,128)S(1)}, f32[8,128]{1,0:T(8,128)S(1)}) custom-call(f32[4,512,128]{2,1,0:T(8,128)S(1)} %get-tuple-element.258.refs_0_.refs_9_.refs_8_, f32[16,8,512]{2,1,0:T(8,128)S(1)} %get-tuple-element.259.refs_1_.refs_11_, f32[16,512]{1,0:T(8,128)S(1)} %get-tuple-element.256.refs_2_.refs_6_.refs_3_.refs_5_, ...), custom_call_target="tpu_custom_call" | custom-call | flops 31000000512 | tf_op jit(solution)/shard_map/local_average/pallas_call | solution.py:92
  27.1 2.8 %carried_average.1 = (bf16[512,512]{1,0:T(8,128)(2,1)S(1)}, f32[512,512]{1,0:T(8,128)S(1)}, f32[16,8,512]{2,1,0:T(8,128)S(1)}, f32[8,128]{1,0:T(8,128)S(1)}) custom-call(s32[5]{0:T(128)S(1)} %pad_add_fusion.refs_0_, f32[16,512]{1,0:T(8,128)S(1)} %collective-permute-done.refs_2_.refs_1_, f32[16,512]{1,0:T(8,128)S(1)} %collective-permute-done.1.refs_2_, ...), custom_call_target="tpu_custom_call" | custom-call | flops 27000000512 | tf_op jit(solution)/shard_map/carried_average/pallas_call | solution.py:92
  29.9 1.4 mix.1
  31.3 1.9 attention.1
  33.3 1.4 hidden.1
  38.3 1.9 collective-permute-done.4.refs_2_
  40.4 1.4 hidden_back.1
  41.8 1.6 ffn_in_grad.1
  43.6 1.6 out_grad.1
  45.6 1.5 collective-permute-start.9
  47.4 1.3 collective-permute-start.8
  50.4 1.9 attention_back.1
  52.2 1.5 reset_grad.1
  53.8 1.4 value_grad.1
  55.4 1.6 collective-permute-start.10
  57.2 2.0 %smooth_back.1 = (f32[4,512,128]{2,1,0:T(8,128)S(1)}, f32[4,512,128]{2,1,0:T(8,128)S(1)}, f32[1,512]{1,0:T(1,128)S(1)}, f32[8,128]{1,0:T(8,128)S(1)}) custom-call(bf16[512,512]{1,0:T(8,128)(2,1)S(1)} %get-tuple-element.296.refs_4_.refs_0_, bf16[512,128]{1,0:T(8,128)(2,1)S(1)} %get-tuple-element.313.refs_4_.refs_1_, ...), custom_call_target="tpu_custom_call" | custom-call | flops 20000000000 | tf_op jit(solution)/shard_map/smooth_back/pallas_call | solution.py:92
  59.2 2.5 %states_back.1 = (f32[16,8,512]{2,1,0:T(8,128)S(1)}, f32[16,512]{1,0:T(8,128)S(1)}, f32[8,128]{1,0:T(8,128)S(1)}) custom-call(s32[5]{0:T(128)S(1)} %pad_add_fusion.refs_0_, f32[4,512,128]{2,1,0:T(8,128)S(1)} %get-tuple-element.330.refs_1_, f32[16,512]{1,0:T(8,128)S(1)} %copy-done.31, f32[16,512]{1,0:T(8,128)S(1)} %copy-done.33, ...), custom_call_target="tpu_custom_call" | custom-call | flops 24999999488 | tf_op jit(solution)/shard_map/states_back/pallas_call | solution.py:92
  62.5 2.2 %collective-permute-done.10.refs_2_ = f32[128,512]{1,0:T(8,128)S(1)} collective-permute-done((f32[128,512]{1,0:T(8,128)S(1)}, f32[128,512]{1,0:T(8,128)S(1)}, u32[]{:S(2)}, u32[]{:S(2)}) %collective-permute-start.10) | collective-permute-done | bytes 262176 | tf_op jit(solution)/shard_map/ppermute | solution.py:699
  66.2 1.6 collective-permute-start.19
  67.7 1.5 collective-permute-start.20
  70.0 1.3 collective-permute-start.18
  73.8 1.3 collective-permute-start.16
  75.3 3.3 %collective-permute-done.20.refs_2_ = f32[128,1024]{1,0:T(8,128)S(1)} collective-permute-done((f32[128,1024]{1,0:T(8,128)S(1)}, f32[128,1024]{1,0:T(8,128)S(1)}, u32[]{:S(2)}, u32[]{:S(2)}) %collective-permute-start.20) | collective-permute-done | bytes 524320 | tf_op jit(solution)/shard_map/ppermute | solution.py:699
  79.6 1.6 collective-permute-start.25
  81.9 2.0 %collective-permute-start.26 = (f32[32,1536]{1,0:T(8,128)S(1)}, f32[32,1536]{1,0:T(8,128)S(1)}, u32[]{:S(2)}, u32[]{:S(2)}) collective-permute-start(f32[32,1536]{1,0:T(8,128)S(1)} %get-tuple-element.370), channel_id=1, source_target_pairs={{0,2},{1,3},{2,0},{3,1},{4,6},{5,7},{6,4},{7,5},{8,10},{9,11},{10,... | collective-permute-start | bytes 589832 | tf_op jit(solution)/shard_map/ppermute | solution.py:699
  85.5 2.6 %state_back.4 = (f32[512,128]{1,0:T(8,128)S(1)}, f32[32,128]{1,0:T(8,128)S(1)}, f32[8,128]{1,0:T(8,128)S(1)}) custom-call(f32[4,512,128]{2,1,0:T(8,128)S(1)} %get-tuple-element.258.refs_0_.refs_9_.refs_8_, f32[4,512,128]{2,1,0:T(8,128)S(1)} %get-tuple-element.330.refs_1_, f32[4,512,128]{2,1,0:T(8,128)S(1)} %get-tuple-element.344.refs_2_, ...), custom_call_target="tpu_custom_call" | custom-call | flops 27000000512 | tf_op jit(solution)/shard_map/state_back/pallas_call | solution.py:92
  88.4 8.2 %collective-permute-done.12.refs_2_ = f32[128,1152]{1,0:T(8,128)S(1)} collective-permute-done((f32[128,1152]{1,0:T(8,128)S(1)}, f32[128,1152]{1,0:T(8,128)S(1)}, u32[]{:S(2)}, u32[]{:S(2)}) %collective-permute-start.12) | collective-permute-done | bytes 589856 | tf_op jit(solution)/shard_map/ppermute | solution.py:699
  97.8 2.7 %collective-permute-start.32 = (f32[32,1536]{1,0:T(8,128)S(1)}, f32[32,1536]{1,0:T(8,128)S(1)}, u32[]{:S(2)}, u32[]{:S(2)}) collective-permute-start(f32[32,1536]{1,0:T(8,128)S(1)} %get-tuple-element.386.refs_0_), channel_id=1, source_target_pairs={{0,4},{1,5},{2,6},{3,7},{4,0},{5,1},{6,2},{7,3},{8,12},{9,13},{10,... | collective-permute-start | bytes 589832 | tf_op jit(solution)/shard_map/ppermute | solution.py:699
  101.1 1.5 collective-permute-start.22
  103.1 7.1 %collective-permute-done.22.refs_2_ = f32[64,1152]{1,0:T(8,128)S(1)} collective-permute-done((f32[64,1152]{1,0:T(8,128)S(1)}, f32[64,1152]{1,0:T(8,128)S(1)}, u32[]{:S(2)}, u32[]{:S(2)}) %collective-permute-start.22) | collective-permute-done | bytes 294944 | tf_op jit(solution)/shard_map/ppermute | solution.py:699
  110.9 1.6 collective-permute-start.38
  113.0 2.6 %state_back.5 = (f32[512,128]{1,0:T(8,128)S(1)}, f32[32,128]{1,0:T(8,128)S(1)}, f32[8,128]{1,0:T(8,128)S(1)}) custom-call(f32[4,512,128]{2,1,0:T(8,128)S(1)} %get-tuple-element.258.refs_0_.refs_9_.refs_8_, f32[4,512,128]{2,1,0:T(8,128)S(1)} %get-tuple-element.330.refs_1_, f32[4,512,128]{2,1,0:T(8,128)S(1)} %get-tuple-element.344.refs_2_, ...), custom_call_target="tpu_custom_call" | custom-call | flops 27000000512 | tf_op jit(solution)/shard_map/state_back/pallas_call | solution.py:92
  115.7 2.5 %collective-permute-start.36 = (f32[32,1024]{1,0:T(8,128)S(1)}, f32[32,1024]{1,0:T(8,128)S(1)}, u32[]{:S(2)}, u32[]{:S(2)}) collective-permute-start(f32[32,1024]{1,0:T(8,128)S(1)} %get-tuple-element.400.refs_0_), channel_id=1, source_target_pairs={{0,4},{1,5},{2,6},{3,7},{4,0},{5,1},{6,2},{7,3},{8,12},{9,13},{10,... | collective-permute-start | bytes 393224 | tf_op jit(solution)/shard_map/ppermute | solution.py:699
  119.2 2.6 %state_back.6 = (f32[512,128]{1,0:T(8,128)S(1)}, f32[32,128]{1,0:T(8,128)S(1)}, f32[8,128]{1,0:T(8,128)S(1)}) custom-call(f32[4,512,128]{2,1,0:T(8,128)S(1)} %get-tuple-element.258.refs_0_.refs_9_.refs_8_, f32[4,512,128]{2,1,0:T(8,128)S(1)} %get-tuple-element.330.refs_1_, f32[4,512,128]{2,1,0:T(8,128)S(1)} %get-tuple-element.344.refs_2_, ...), custom_call_target="tpu_custom_call" | custom-call | flops 27000000512 | tf_op jit(solution)/shard_map/state_back/pallas_call | solution.py:92
  121.9 5.5 %collective-permute-done.30.refs_2_ = f32[256,512]{1,0:T(8,128)S(1)} collective-permute-done((f32[256,512]{1,0:T(8,128)S(1)}, f32[256,512]{1,0:T(8,128)S(1)}, u32[]{:S(2)}, u32[]{:S(2)}) %collective-permute-start.30) | collective-permute-done | bytes 524320 | tf_op jit(solution)/shard_map/ppermute | solution.py:699
  127.6 1.5 ffn_out_out.2
  129.2 2.6 %state_back.7 = (f32[512,128]{1,0:T(8,128)S(1)}, f32[32,128]{1,0:T(8,128)S(1)}, f32[8,128]{1,0:T(8,128)S(1)}) custom-call(f32[4,512,128]{2,1,0:T(8,128)S(1)} %get-tuple-element.258.refs_0_.refs_9_.refs_8_, f32[4,512,128]{2,1,0:T(8,128)S(1)} %get-tuple-element.330.refs_1_, f32[4,512,128]{2,1,0:T(8,128)S(1)} %get-tuple-element.344.refs_2_, ...), custom_call_target="tpu_custom_call" | custom-call | flops 27000000512 | tf_op jit(solution)/shard_map/state_back/pallas_call | solution.py:92
  132.4 1.6 collective-permute-start.35
  134.6 1.5 ffn_out_out.3
  136.2 1.9 collective-permute-start.41
  138.2 4.0 %collective-permute-done.33.refs_1_ = f32[32,1152]{1,0:T(8,128)S(1)} collective-permute-done((f32[32,1152]{1,0:T(8,128)S(1)}, f32[32,1152]{1,0:T(8,128)S(1)}, u32[]{:S(2)}, u32[]{:S(2)}) %collective-permute-start.33) | collective-permute-done | bytes 147488 | tf_op jit(solution)/shard_map/ppermute | solution.py:699
  145.6 1.8 norm_back.1
  148.5 1.7 collective-permute-done.40.refs_2_
  150.4 2.0 %collective-permute-start.45 = (f32[40,512]{1,0:T(8,128)S(1)}, f32[40,512]{1,0:T(8,128)S(1)}, u32[]{:S(2)}, u32[]{:S(2)}) collective-permute-start(f32[40,512]{1,0:T(8,128)S(1)} %get-tuple-element.432.refs_0_), channel_id=1, source_target_pairs={{0,2},{1,3},{2,0},{3,1},{4,6},{5,7},{6,4},{7,5},{8,10},{9,11},{10,... | collective-permute-start | bytes 245768 | tf_op jit(solution)/shard_map/ppermute | solution.py:669
  152.4 4.3 %collective-permute-done.46.refs_2_ = f32[64,1024]{1,0:T(8,128)S(1)} collective-permute-done((f32[64,1024]{1,0:T(8,128)S(1)}, f32[64,1024]{1,0:T(8,128)S(1)}, u32[]{:S(2)}, u32[]{:S(2)}) %collective-permute-start.46) | collective-permute-done | bytes 262176 | tf_op jit(solution)/shard_map/ppermute | solution.py:699
  156.8 2.0 %collective-permute-start.47 = (f32[40,512]{1,0:T(8,128)S(1)}, f32[40,512]{1,0:T(8,128)S(1)}, u32[]{:S(2)}, u32[]{:S(2)}) collective-permute-start(f32[40,512]{1,0:T(8,128)S(1)} %get-tuple-element.436.refs_0_), channel_id=1, source_target_pairs={{0,4},{1,5},{2,6},{3,7},{4,0},{5,1},{6,2},{7,3},{8,12},{9,13},{10,... | collective-permute-start | bytes 245768 | tf_op jit(solution)/shard_map/ppermute | solution.py:669
  158.8 1.5 collective-permute-start.43
  161.8 1.7 collective-permute-done.47.refs_1_
  164.7 3.9 %collective-permute-done.43.refs_2_ = f32[64,1152]{1,0:T(8,128)S(1)} collective-permute-done((f32[64,1152]{1,0:T(8,128)S(1)}, f32[64,1152]{1,0:T(8,128)S(1)}, u32[]{:S(2)}, u32[]{:S(2)}) %collective-permute-start.43) | collective-permute-done | bytes 294944 | tf_op jit(solution)/shard_map/ppermute | solution.py:699
  169.5 1.5 collective-permute-start.48
  171.3 1.7 ffn_in_out.2
  174.7 1.5 reset_out.2
  176.2 1.7 ffn_in_out.3
  177.9 2.0 %collective-permute-done.53.refs_2_ = f32[128,1536]{1,0:T(8,128)S(1)} collective-permute-done((f32[128,1536]{1,0:T(8,128)S(1)}, f32[128,1536]{1,0:T(8,128)S(1)}, u32[]{:S(2)}, u32[]{:S(2)}) %collective-permute-start.53) | collective-permute-done | bytes 786464 | tf_op jit(solution)/shard_map/ppermute | solution.py:699
  180.3 1.7 out_out.2
  183.5 1.5 reset_out.3
  186.4 1.4 value_join.5
  189.5 1.6 value_out.2
  191.8 1.7 block_out.1
  193.5 1.7 out_out.3
  195.2 2.2 %value_out.3 = (f32[512,1024]{1,0:T(8,128)}, f32[512,2176]{1,0:T(8,128)}, f32[8,128]{1,0:T(8,128)}) custom-call(s32[5]{0:T(128)S(1)} %pad_add_fusion.refs_0_, f32[256,1152]{1,0:T(8,128)S(1)} %collective-permute-done.56.refs_1_, f32[512,1024]{1,0:T(8,128)} %get-tuple-element.472.refs_2_, ...), custom_call_target="tpu_custom_call", output_to_operand_aliasing={{0}: (2, {}), {1}: (3, {})} | custom-call | flops 16000000000 | tf_op jit(solution)/shard_map/value_out/pallas_call | solution.py:92
  (221 shorter events, 48.7 us)
Async XLA Ops:
  6.2 3.3 %copy-start.36 = (f32[128]{0:T(128)S(1)}, f32[128]{0:T(128)}, u32[]{:S(2)}) copy-start(f32[128]{0:T(128)} %param.31) | copy-start | bytes 1540
  8.9 18.1 %copy-start.30 = (f32[16,512]{1,0:T(8,128)}, f32[16,512]{1,0:T(8,128)S(1)}, u32[]{:S(2)}) copy-start(f32[16,512]{1,0:T(8,128)S(1)} %get-tuple-element.253.refs_3_.refs_5_.refs_2_) | copy-start | bytes 98308
  8.9 18.1 %copy-start.32 = (f32[16,512]{1,0:T(8,128)}, f32[16,512]{1,0:T(8,128)S(1)}, u32[]{:S(2)}) copy-start(f32[16,512]{1,0:T(8,128)S(1)} %get-tuple-element.256.refs_2_.refs_6_.refs_3_.refs_5_) | copy-start | bytes 98308
  8.9 18.1 %copy-start.34 = (f32[16,512]{1,0:T(8,128)}, f32[16,512]{1,0:T(8,128)S(1)}, u32[]{:S(2)}) copy-start(f32[16,512]{1,0:T(8,128)S(1)} %get-tuple-element.257.refs_3_.refs_7_.refs_6_) | copy-start | bytes 98308
  8.9 1.4 collective-permute-start
  10.9 16.1 %collective-permute-start.3 = (f32[16,512]{1,0:T(8,128)S(1)}, f32[16,512]{1,0:T(8,128)S(1)}, u32[]{:S(2)}, u32[]{:S(2)}) collective-permute-start(f32[16,512]{1,0:T(8,128)S(1)} %get-tuple-element.255), channel_id=1, source_target_pairs={{0,6},{1,7},{8,14},{9,15},{16,22},{17,23},{24,30},{25,31}} | collective-permute-start | bytes 98312 | tf_op jit(solution)/shard_map/ppermute | solution.py:680
  17.8 9.2 %collective-permute-start.2 = (f32[16,512]{1,0:T(8,128)S(1)}, f32[16,512]{1,0:T(8,128)S(1)}, u32[]{:S(2)}, u32[]{:S(2)}) collective-permute-start(f32[16,512]{1,0:T(8,128)S(1)} %get-tuple-element.255), channel_id=1, source_target_pairs={{0,4},{1,5},{2,6},{3,7},{8,12},{9,13},{10,14},{11,15},{16,20},{17,... | collective-permute-start | bytes 98312 | tf_op jit(solution)/shard_map/ppermute | solution.py:680
  19.1 7.9 %collective-permute-start.1 = (f32[16,512]{1,0:T(8,128)S(1)}, f32[16,512]{1,0:T(8,128)S(1)}, u32[]{:S(2)}, u32[]{:S(2)}) collective-permute-start(f32[16,512]{1,0:T(8,128)S(1)} %get-tuple-element.255), channel_id=1, source_target_pairs={{0,2},{1,3},{2,4},{3,5},{4,6},{5,7},{8,10},{9,11},{10,12},{11,13},... | collective-permute-start | bytes 98312 | tf_op jit(solution)/shard_map/ppermute | solution.py:680
  23.8 3.2 %copy-start.21 = (f32[512]{0:T(512)S(1)}, f32[512]{0:T(512)}, u32[]{:S(2)}) copy-start(f32[512]{0:T(512)} %param.27) | copy-start | bytes 6148
  27.0 2.8 %copy-start = (bf16[512,2176]{1,0:T(8,128)(2,1)S(1)}, bf16[512,2176]{1,0:T(8,128)(2,1)}, u32[]{:S(2)}) copy-start(bf16[512,2176]{1,0:T(8,128)(2,1)} %refs_5_.3) | copy-start | bytes 6684676
  37.4 2.7 %collective-permute-start.4 = (f32[512,512]{1,0:T(8,128)S(1)}, f32[512,512]{1,0:T(8,128)S(1)}, u32[]{:S(2)}, u32[]{:S(2)}) collective-permute-start(f32[512,512]{1,0:T(8,128)S(1)} %get-tuple-element.291), channel_id=1, source_target_pairs={{0,1},{1,0},{2,3},{3,2},{4,5},{5,4},{6,7},{7,6},{8,9},{9,8},{10,11... | collective-permute-start | bytes 3145736 | tf_op jit(solution)/shard_map/ppermute | solution.py:669
  43.4 3.7 %collective-permute-start.5 = (f32[256,1536]{1,0:T(8,128)S(1)}, f32[256,1536]{1,0:T(8,128)S(1)}, u32[]{:S(2)}, u32[]{:S(2)}) collective-permute-start(f32[256,1536]{1,0:T(8,128)S(1)} %get-tuple-element.299), channel_id=1, source_target_pairs={{0,1},{1,0},{2,3},{3,2},{4,5},{5,4},{6,7},{7,6},{8,9},{9,8},{10,11... | collective-permute-start | bytes 4718600 | tf_op jit(solution)/shard_map/ppermute | solution.py:669
  45.1 4.8 %collective-permute-start.6 = (f32[256,1536]{1,0:T(8,128)S(1)}, f32[256,1536]{1,0:T(8,128)S(1)}, u32[]{:S(2)}, u32[]{:S(2)}) collective-permute-start(f32[256,1536]{1,0:T(8,128)S(1)} %get-tuple-element.309), channel_id=1, source_target_pairs={{0,1},{1,0},{2,3},{3,2},{4,5},{5,4},{6,7},{7,6},{8,9},{9,8},{10,11... | collective-permute-start | bytes 4718600 | tf_op jit(solution)/shard_map/ppermute | solution.py:669
  45.6 9.7 %collective-permute-start.9 = (f32[256,512]{1,0:T(8,128)S(1)}, f32[256,512]{1,0:T(8,128)S(1)}, u32[]{:S(2)}, u32[]{:S(2)}) collective-permute-start(f32[256,512]{1,0:T(8,128)S(1)} %get-tuple-element.322), channel_id=1, source_target_pairs={{0,8},{1,17},{2,10},{3,19},{4,12},{5,21},{6,14},{7,23},{8,0},{9,25... | collective-permute-start | bytes 1572872 | tf_op jit(solution)/shard_map/ppermute | solution.py:699
  47.4 18.6 %collective-permute-start.8 = (f32[128,1536]{1,0:T(8,128)S(1)}, f32[128,1536]{1,0:T(8,128)S(1)}, u32[]{:S(2)}, u32[]{:S(2)}) collective-permute-start(f32[128,1536]{1,0:T(8,128)S(1)} %get-tuple-element.320), channel_id=1, source_target_pairs={{0,8},{1,17},{2,10},{3,19},{4,12},{5,21},{6,14},{7,23},{8,0},{9,25... | collective-permute-start | bytes 2359304 | tf_op jit(solution)/shard_map/ppermute | solution.py:699
  50.3 23.5 %collective-permute-start.21 = (f32[128,1536]{1,0:T(8,128)S(1)}, f32[128,1536]{1,0:T(8,128)S(1)}, u32[]{:S(2)}, u32[]{:S(2)}) collective-permute-start(f32[128,1536]{1,0:T(8,128)S(1)} %get-tuple-element.353), channel_id=1, source_target_pairs={{0,2},{1,3},{2,0},{3,1},{4,6},{5,7},{6,4},{7,5},{8,10},{9,11},{10,... | collective-permute-start | bytes 2359304 | tf_op jit(solution)/shard_map/ppermute | solution.py:699
  53.8 7.9 %collective-permute-start.11 = (f32[256,1024]{1,0:T(8,128)S(1)}, f32[256,1024]{1,0:T(8,128)S(1)}, u32[]{:S(2)}, u32[]{:S(2)}) collective-permute-start(f32[256,1024]{1,0:T(8,128)S(1)} %get-tuple-element.327), channel_id=1, source_target_pairs={{0,1},{1,0},{2,3},{3,2},{4,5},{5,4},{6,7},{7,6},{8,9},{9,8},{10,11... | collective-permute-start | bytes 3145736 | tf_op jit(solution)/shard_map/ppermute | solution.py:669
  55.4 9.3 %collective-permute-start.10 = (f32[128,512]{1,0:T(8,128)S(1)}, f32[128,512]{1,0:T(8,128)S(1)}, u32[]{:S(2)}, u32[]{:S(2)}) collective-permute-start(f32[128,512]{1,0:T(8,128)S(1)} %get-tuple-element.325), channel_id=1, source_target_pairs={{0,16},{1,9},{2,18},{3,11},{4,20},{5,13},{6,22},{7,15},{8,24},{9,1... | collective-permute-start | bytes 786440 | tf_op jit(solution)/shard_map/ppermute | solution.py:699
  57.0 10.7 %collective-permute-start.7 = (f32[256,1152]{1,0:T(8,128)S(1)}, f32[256,1152]{1,0:T(8,128)S(1)}, u32[]{:S(2)}, u32[]{:S(2)}) collective-permute-start(f32[256,1152]{1,0:T(8,128)S(1)} %get-tuple-element.318), channel_id=1, source_target_pairs={{0,1},{1,0},{2,3},{3,2},{4,5},{5,4},{6,7},{7,6},{8,9},{9,8},{10,11... | collective-permute-start | bytes 3538952 | tf_op jit(solution)/shard_map/ppermute | solution.py:669
  61.7 7.8 %collective-permute-start.14 = (f32[16,512]{1,0:T(8,128)S(1)}, f32[16,512]{1,0:T(8,128)S(1)}, u32[]{:S(2)}, u32[]{:S(2)}) collective-permute-start(f32[16,512]{1,0:T(8,128)S(1)} %get-tuple-element.340.refs_1_), channel_id=1, source_target_pairs={{0,1},{1,0},{2,3},{3,2},{4,5},{5,4},{6,7},{7,6},{8,9},{9,8},{10,11... | collective-permute-start | bytes 98312 | tf_op jit(solution)/shard_map/ppermute | solution.py:669
  64.8 7.7 %collective-permute-start.13 = (f32[64,512]{1,0:T(8,128)S(1)}, f32[64,512]{1,0:T(8,128)S(1)}, u32[]{:S(2)}, u32[]{:S(2)}) collective-permute-start(f32[64,512]{1,0:T(8,128)S(1)} %get-tuple-element.339), channel_id=1, source_target_pairs={{0,2},{1,3},{2,0},{3,1},{4,6},{5,7},{6,4},{7,5},{8,10},{9,11},{10,... | collective-permute-start | bytes 393224 | tf_op jit(solution)/shard_map/ppermute | solution.py:699
  66.2 13.5 %collective-permute-start.19 = (f32[64,1536]{1,0:T(8,128)S(1)}, f32[64,1536]{1,0:T(8,128)S(1)}, u32[]{:S(2)}, u32[]{:S(2)}) collective-permute-start(f32[64,1536]{1,0:T(8,128)S(1)} %get-tuple-element.349), channel_id=1, source_target_pairs={{0,16},{1,9},{2,18},{3,11},{4,20},{5,13},{6,22},{7,15},{8,24},{9,1... | collective-permute-start | bytes 1179656 | tf_op jit(solution)/shard_map/ppermute | solution.py:699
  67.7 10.9 %collective-permute-start.20 = (f32[128,1024]{1,0:T(8,128)S(1)}, f32[128,1024]{1,0:T(8,128)S(1)}, u32[]{:S(2)}, u32[]{:S(2)}) collective-permute-start(f32[128,1024]{1,0:T(8,128)S(1)} %get-tuple-element.351), channel_id=1, source_target_pairs={{0,8},{1,17},{2,10},{3,19},{4,12},{5,21},{6,14},{7,23},{8,0},{9,25... | collective-permute-start | bytes 1572872 | tf_op jit(solution)/shard_map/ppermute | solution.py:699
  70.0 11.2 %collective-permute-start.18 = (f32[16,512]{1,0:T(8,128)S(1)}, f32[16,512]{1,0:T(8,128)S(1)}, u32[]{:S(2)}, u32[]{:S(2)}) collective-permute-start(f32[16,512]{1,0:T(8,128)S(1)} %get-tuple-element.346), channel_id=1, source_target_pairs={{6,0},{7,1},{14,8},{15,9},{22,16},{23,17},{30,24},{31,25}} | collective-permute-start | bytes 98312 | tf_op jit(solution)/shard_map/ppermute | solution.py:680
  72.5 9.4 %collective-permute-start.17 = (f32[16,512]{1,0:T(8,128)S(1)}, f32[16,512]{1,0:T(8,128)S(1)}, u32[]{:S(2)}, u32[]{:S(2)}) collective-permute-start(f32[16,512]{1,0:T(8,128)S(1)} %get-tuple-element.346), channel_id=1, source_target_pairs={{4,0},{5,1},{6,2},{7,3},{12,8},{13,9},{14,10},{15,11},{20,16},{21,... | collective-permute-start | bytes 98312 | tf_op jit(solution)/shard_map/ppermute | solution.py:680
  73.8 10.1 %collective-permute-start.16 = (f32[16,512]{1,0:T(8,128)S(1)}, f32[16,512]{1,0:T(8,128)S(1)}, u32[]{:S(2)}, u32[]{:S(2)}) collective-permute-start(f32[16,512]{1,0:T(8,128)S(1)} %get-tuple-element.346), channel_id=1, source_target_pairs={{2,0},{3,1},{4,2},{5,3},{6,4},{7,5},{10,8},{11,9},{12,10},{13,11},... | collective-permute-start | bytes 98312 | tf_op jit(solution)/shard_map/ppermute | solution.py:680
  78.6 9.7 %collective-permute-start.15 = (f32[64,512]{1,0:T(8,128)S(1)}, f32[64,512]{1,0:T(8,128)S(1)}, u32[]{:S(2)}, u32[]{:S(2)}) collective-permute-start(f32[64,512]{1,0:T(8,128)S(1)} %get-tuple-element.343.refs_0_), channel_id=1, source_target_pairs={{0,4},{1,5},{2,6},{3,7},{4,0},{5,1},{6,2},{7,3},{8,12},{9,13},{10,... | collective-permute-start | bytes 393224 | tf_op jit(solution)/shard_map/ppermute | solution.py:699
  79.6 17.1 %collective-permute-start.25 = (f32[64,1536]{1,0:T(8,128)S(1)}, f32[64,1536]{1,0:T(8,128)S(1)}, u32[]{:S(2)}, u32[]{:S(2)}) collective-permute-start(f32[64,1536]{1,0:T(8,128)S(1)} %get-tuple-element.368), channel_id=1, source_target_pairs={{0,8},{1,17},{2,10},{3,19},{4,12},{5,21},{6,14},{7,23},{8,0},{9,25... | collective-permute-start | bytes 1179656 | tf_op jit(solution)/shard_map/ppermute | solution.py:699
  81.3 15.3 %collective-permute-start.12 = (f32[128,1152]{1,0:T(8,128)S(1)}, f32[128,1152]{1,0:T(8,128)S(1)}, u32[]{:S(2)}, u32[]{:S(2)}) collective-permute-start(f32[128,1152]{1,0:T(8,128)S(1)} %get-tuple-element.337), channel_id=1, source_target_pairs={{0,8},{1,17},{2,10},{3,19},{4,12},{5,21},{6,14},{7,23},{8,0},{9,25... | collective-permute-start | bytes 1769480 | tf_op jit(solution)/shard_map/ppermute | solution.py:699
  81.9 14.9 %collective-permute-start.26 = (f32[32,1536]{1,0:T(8,128)S(1)}, f32[32,1536]{1,0:T(8,128)S(1)}, u32[]{:S(2)}, u32[]{:S(2)}) collective-permute-start(f32[32,1536]{1,0:T(8,128)S(1)} %get-tuple-element.370), channel_id=1, source_target_pairs={{0,2},{1,3},{2,0},{3,1},{4,6},{5,7},{6,4},{7,5},{8,10},{9,11},{10,... | collective-permute-start | bytes 589832 | tf_op jit(solution)/shard_map/ppermute | solution.py:699
  83.9 18.7 %collective-permute-start.23 = (f32[64,1024]{1,0:T(8,128)S(1)}, f32[64,1024]{1,0:T(8,128)S(1)}, u32[]{:S(2)}, u32[]{:S(2)}) collective-permute-start(f32[64,1024]{1,0:T(8,128)S(1)} %get-tuple-element.365), channel_id=1, source_target_pairs={{0,16},{1,9},{2,18},{3,11},{4,20},{5,13},{6,22},{7,15},{8,24},{9,1... | collective-permute-start | bytes 786440 | tf_op jit(solution)/shard_map/ppermute | solution.py:699
  88.3 12.1 %collective-permute-start.24 = (f32[64,512]{1,0:T(8,128)S(1)}, f32[64,512]{1,0:T(8,128)S(1)}, u32[]{:S(2)}, u32[]{:S(2)}) collective-permute-start(f32[64,512]{1,0:T(8,128)S(1)} %get-tuple-element.366.refs_1_), channel_id=1, source_target_pairs={{0,2},{1,3},{2,0},{3,1},{4,6},{5,7},{6,4},{7,5},{8,10},{9,11},{10,... | collective-permute-start | bytes 393224 | tf_op jit(solution)/shard_map/ppermute | solution.py:699
  96.9 13.8 %collective-permute-start.29 = (f32[32,1536]{1,0:T(8,128)S(1)}, f32[32,1536]{1,0:T(8,128)S(1)}, u32[]{:S(2)}, u32[]{:S(2)}) collective-permute-start(f32[32,1536]{1,0:T(8,128)S(1)} %get-tuple-element.380), channel_id=1, source_target_pairs={{0,16},{1,9},{2,18},{3,11},{4,20},{5,13},{6,22},{7,15},{8,24},{9,1... | collective-permute-start | bytes 589832 | tf_op jit(solution)/shard_map/ppermute | solution.py:699
  97.8 13.0 %collective-permute-start.32 = (f32[32,1536]{1,0:T(8,128)S(1)}, f32[32,1536]{1,0:T(8,128)S(1)}, u32[]{:S(2)}, u32[]{:S(2)}) collective-permute-start(f32[32,1536]{1,0:T(8,128)S(1)} %get-tuple-element.386.refs_0_), channel_id=1, source_target_pairs={{0,4},{1,5},{2,6},{3,7},{4,0},{5,1},{6,2},{7,3},{8,12},{9,13},{10,... | collective-permute-start | bytes 589832 | tf_op jit(solution)/shard_map/ppermute | solution.py:699
  100.5 10.2 %collective-permute-start.28 = (f32[128,512]{1,0:T(8,128)S(1)}, f32[128,512]{1,0:T(8,128)S(1)}, u32[]{:S(2)}, u32[]{:S(2)}) collective-permute-start(f32[128,512]{1,0:T(8,128)S(1)} %get-tuple-element.378.refs_1_), channel_id=1, source_target_pairs={{0,16},{1,9},{2,18},{3,11},{4,20},{5,13},{6,22},{7,15},{8,24},{9,1... | collective-permute-start | bytes 786440 | tf_op jit(solution)/shard_map/ppermute | solution.py:699
  101.1 9.0 %collective-permute-start.22 = (f32[64,1152]{1,0:T(8,128)S(1)}, f32[64,1152]{1,0:T(8,128)S(1)}, u32[]{:S(2)}, u32[]{:S(2)}) collective-permute-start(f32[64,1152]{1,0:T(8,128)S(1)} %get-tuple-element.363), channel_id=1, source_target_pairs={{0,16},{1,9},{2,18},{3,11},{4,20},{5,13},{6,22},{7,15},{8,24},{9,1... | collective-permute-start | bytes 884744 | tf_op jit(solution)/shard_map/ppermute | solution.py:699
  102.7 12.9 %collective-permute-start.31 = (f32[32,1024]{1,0:T(8,128)S(1)}, f32[32,1024]{1,0:T(8,128)S(1)}, u32[]{:S(2)}, u32[]{:S(2)}) collective-permute-start(f32[32,1024]{1,0:T(8,128)S(1)} %get-tuple-element.385), channel_id=1, source_target_pairs={{0,2},{1,3},{2,0},{3,1},{4,6},{5,7},{6,4},{7,5},{8,10},{9,11},{10,... | collective-permute-start | bytes 393224 | tf_op jit(solution)/shard_map/ppermute | solution.py:699
  110.2 18.9 %collective-permute-start.27 = (f32[32,1152]{1,0:T(8,128)S(1)}, f32[32,1152]{1,0:T(8,128)S(1)}, u32[]{:S(2)}, u32[]{:S(2)}) collective-permute-start(f32[32,1152]{1,0:T(8,128)S(1)} %get-tuple-element.377), channel_id=1, source_target_pairs={{0,2},{1,3},{2,0},{3,1},{4,6},{5,7},{6,4},{7,5},{8,10},{9,11},{10,... | collective-permute-start | bytes 442376 | tf_op jit(solution)/shard_map/ppermute | solution.py:699
  110.9 23.1 %collective-permute-start.38 = (f32[32,1536]{1,0:T(8,128)S(1)}, f32[32,1536]{1,0:T(8,128)S(1)}, u32[]{:S(2)}, u32[]{:S(2)}) collective-permute-start(f32[32,1536]{1,0:T(8,128)S(1)} %get-tuple-element.402.refs_1_), channel_id=1, source_target_pairs={{0,2},{1,3},{2,0},{3,1},{4,6},{5,7},{6,4},{7,5},{8,10},{9,11},{10,... | collective-permute-start | bytes 589832 | tf_op jit(solution)/shard_map/ppermute | solution.py:699
  112.5 19.8 %collective-permute-start.34 = (f32[32,1536]{1,0:T(8,128)S(1)}, f32[32,1536]{1,0:T(8,128)S(1)}, u32[]{:S(2)}, u32[]{:S(2)}) collective-permute-start(f32[32,1536]{1,0:T(8,128)S(1)} %get-tuple-element.396.refs_0_), channel_id=1, source_target_pairs={{0,4},{1,5},{2,6},{3,7},{4,0},{5,1},{6,2},{7,3},{8,12},{9,13},{10,... | collective-permute-start | bytes 589832 | tf_op jit(solution)/shard_map/ppermute | solution.py:699
  115.7 20.5 %collective-permute-start.36 = (f32[32,1024]{1,0:T(8,128)S(1)}, f32[32,1024]{1,0:T(8,128)S(1)}, u32[]{:S(2)}, u32[]{:S(2)}) collective-permute-start(f32[32,1024]{1,0:T(8,128)S(1)} %get-tuple-element.400.refs_0_), channel_id=1, source_target_pairs={{0,4},{1,5},{2,6},{3,7},{4,0},{5,1},{6,2},{7,3},{8,12},{9,13},{10,... | collective-permute-start | bytes 393224 | tf_op jit(solution)/shard_map/ppermute | solution.py:699
  118.2 9.2 %collective-permute-start.30 = (f32[256,512]{1,0:T(8,128)S(1)}, f32[256,512]{1,0:T(8,128)S(1)}, u32[]{:S(2)}, u32[]{:S(2)}) collective-permute-start(f32[256,512]{1,0:T(8,128)S(1)} %get-tuple-element.383.refs_1_), channel_id=1, source_target_pairs={{0,8},{1,17},{2,10},{3,19},{4,12},{5,21},{6,14},{7,23},{8,0},{9,25... | collective-permute-start | bytes 1572872 | tf_op jit(solution)/shard_map/ppermute | solution.py:699
  127.5 7.1 %collective-permute-start.37 = (f32[512,512]{1,0:T(8,128)S(1)}, f32[512,512]{1,0:T(8,128)S(1)}, u32[]{:S(2)}, u32[]{:S(2)}) collective-permute-start(f32[512,512]{1,0:T(8,128)S(1)} %get-tuple-element.392.refs_1_), channel_id=1, source_target_pairs={{0,1},{1,0},{2,3},{3,2},{4,5},{5,4},{6,7},{7,6},{8,9},{9,8},{10,11... | collective-permute-start | bytes 3145736 | tf_op jit(solution)/shard_map/ppermute | solution.py:669
  131.8 10.4 %collective-permute-start.33 = (f32[32,1152]{1,0:T(8,128)S(1)}, f32[32,1152]{1,0:T(8,128)S(1)}, u32[]{:S(2)}, u32[]{:S(2)}) collective-permute-start(f32[32,1152]{1,0:T(8,128)S(1)} %get-tuple-element.395.refs_0_), channel_id=1, source_target_pairs={{0,4},{1,5},{2,6},{3,7},{4,0},{5,1},{6,2},{7,3},{8,12},{9,13},{10,... | collective-permute-start | bytes 442376 | tf_op jit(solution)/shard_map/ppermute | solution.py:699
  132.4 5.7 %collective-permute-start.35 = (f32[32,1536]{1,0:T(8,128)S(1)}, f32[32,1536]{1,0:T(8,128)S(1)}, u32[]{:S(2)}, u32[]{:S(2)}) collective-permute-start(f32[32,1536]{1,0:T(8,128)S(1)} %get-tuple-element.399.refs_1_), channel_id=1, source_target_pairs={{0,16},{1,9},{2,18},{3,11},{4,20},{5,13},{6,22},{7,15},{8,24},{9,1... | collective-permute-start | bytes 589832 | tf_op jit(solution)/shard_map/ppermute | solution.py:699
  134.0 9.5 %collective-permute-start.42 = (f32[64,1536]{1,0:T(8,128)S(1)}, f32[64,1536]{1,0:T(8,128)S(1)}, u32[]{:S(2)}, u32[]{:S(2)}) collective-permute-start(f32[64,1536]{1,0:T(8,128)S(1)} %get-tuple-element.423.refs_1_), channel_id=1, source_target_pairs={{0,16},{1,9},{2,18},{3,11},{4,20},{5,13},{6,22},{7,15},{8,24},{9,1... | collective-permute-start | bytes 1179656 | tf_op jit(solution)/shard_map/ppermute | solution.py:699
  136.2 8.4 %collective-permute-start.41 = (f32[32,1024]{1,0:T(8,128)S(1)}, f32[32,1024]{1,0:T(8,128)S(1)}, u32[]{:S(2)}, u32[]{:S(2)}) collective-permute-start(f32[32,1024]{1,0:T(8,128)S(1)} %get-tuple-element.422.refs_1_), channel_id=1, source_target_pairs={{0,2},{1,3},{2,0},{3,1},{4,6},{5,7},{6,4},{7,5},{8,10},{9,11},{10,... | collective-permute-start | bytes 393224 | tf_op jit(solution)/shard_map/ppermute | solution.py:699
  142.2 8.1 %collective-permute-start.39 = (f32[32,1152]{1,0:T(8,128)S(1)}, f32[32,1152]{1,0:T(8,128)S(1)}, u32[]{:S(2)}, u32[]{:S(2)}) collective-permute-start(f32[32,1152]{1,0:T(8,128)S(1)} %get-tuple-element.408.refs_1_), channel_id=1, source_target_pairs={{0,2},{1,3},{2,0},{3,1},{4,6},{5,7},{6,4},{7,5},{8,10},{9,11},{10,... | collective-permute-start | bytes 442376 | tf_op jit(solution)/shard_map/ppermute | solution.py:699
  142.3 7.8 %collective-permute-start.40 = (f32[64,1536]{1,0:T(8,128)S(1)}, f32[64,1536]{1,0:T(8,128)S(1)}, u32[]{:S(2)}, u32[]{:S(2)}) collective-permute-start(f32[64,1536]{1,0:T(8,128)S(1)} %get-tuple-element.409.refs_1_), channel_id=1, source_target_pairs={{0,8},{1,17},{2,10},{3,19},{4,12},{5,21},{6,14},{7,23},{8,0},{9,25... | collective-permute-start | bytes 1179656 | tf_op jit(solution)/shard_map/ppermute | solution.py:699
  143.6 27.4 %collective-permute-start.51 = (f32[128,1536]{1,0:T(8,128)S(1)}, f32[128,1536]{1,0:T(8,128)S(1)}, u32[]{:S(2)}, u32[]{:S(2)}) collective-permute-start(f32[128,1536]{1,0:T(8,128)S(1)} %get-tuple-element.442.refs_1_), channel_id=1, source_target_pairs={{0,8},{1,17},{2,10},{3,19},{4,12},{5,21},{6,14},{7,23},{8,0},{9,25... | collective-permute-start | bytes 2359304 | tf_op jit(solution)/shard_map/ppermute | solution.py:699
  147.4 2.9 %collective-permute-start.44 = (f32[40,512]{1,0:T(8,128)S(1)}, f32[40,512]{1,0:T(8,128)S(1)}, u32[]{:S(2)}, u32[]{:S(2)}) collective-permute-start(f32[40,512]{1,0:T(8,128)S(1)} %get-tuple-element.430.refs_0_), channel_id=1, source_target_pairs={{0,1},{1,0},{2,3},{3,2},{4,5},{5,4},{6,7},{7,6},{8,9},{9,8},{10,11... | collective-permute-start | bytes 245768 | tf_op jit(solution)/shard_map/ppermute | solution.py:669
  147.4 9.2 %collective-permute-start.46 = (f32[64,1024]{1,0:T(8,128)S(1)}, f32[64,1024]{1,0:T(8,128)S(1)}, u32[]{:S(2)}, u32[]{:S(2)}) collective-permute-start(f32[64,1024]{1,0:T(8,128)S(1)} %get-tuple-element.433.refs_1_), channel_id=1, source_target_pairs={{0,16},{1,9},{2,18},{3,11},{4,20},{5,13},{6,22},{7,15},{8,24},{9,1... | collective-permute-start | bytes 786440 | tf_op jit(solution)/shard_map/ppermute | solution.py:699
  150.4 6.4 %collective-permute-start.45 = (f32[40,512]{1,0:T(8,128)S(1)}, f32[40,512]{1,0:T(8,128)S(1)}, u32[]{:S(2)}, u32[]{:S(2)}) collective-permute-start(f32[40,512]{1,0:T(8,128)S(1)} %get-tuple-element.432.refs_0_), channel_id=1, source_target_pairs={{0,2},{1,3},{2,0},{3,1},{4,6},{5,7},{6,4},{7,5},{8,10},{9,11},{10,... | collective-permute-start | bytes 245768 | tf_op jit(solution)/shard_map/ppermute | solution.py:669
  156.8 6.7 %collective-permute-start.47 = (f32[40,512]{1,0:T(8,128)S(1)}, f32[40,512]{1,0:T(8,128)S(1)}, u32[]{:S(2)}, u32[]{:S(2)}) collective-permute-start(f32[40,512]{1,0:T(8,128)S(1)} %get-tuple-element.436.refs_0_), channel_id=1, source_target_pairs={{0,4},{1,5},{2,6},{3,7},{4,0},{5,1},{6,2},{7,3},{8,12},{9,13},{10,... | collective-permute-start | bytes 245768 | tf_op jit(solution)/shard_map/ppermute | solution.py:669
  158.8 9.8 %collective-permute-start.43 = (f32[64,1152]{1,0:T(8,128)S(1)}, f32[64,1152]{1,0:T(8,128)S(1)}, u32[]{:S(2)}, u32[]{:S(2)}) collective-permute-start(f32[64,1152]{1,0:T(8,128)S(1)} %get-tuple-element.429.refs_1_), channel_id=1, source_target_pairs={{0,16},{1,9},{2,18},{3,11},{4,20},{5,13},{6,22},{7,15},{8,24},{9,1... | collective-permute-start | bytes 884744 | tf_op jit(solution)/shard_map/ppermute | solution.py:699
  160.3 13.9 %collective-permute-start.49 = (f32[128,1024]{1,0:T(8,128)S(1)}, f32[128,1024]{1,0:T(8,128)S(1)}, u32[]{:S(2)}, u32[]{:S(2)}) collective-permute-start(f32[128,1024]{1,0:T(8,128)S(1)} %get-tuple-element.440.refs_1_), channel_id=1, source_target_pairs={{0,8},{1,17},{2,10},{3,19},{4,12},{5,21},{6,14},{7,23},{8,0},{9,25... | collective-permute-start | bytes 1572872 | tf_op jit(solution)/shard_map/ppermute | solution.py:699
  161.4 18.6 %collective-permute-start.53 = (f32[128,1536]{1,0:T(8,128)S(1)}, f32[128,1536]{1,0:T(8,128)S(1)}, u32[]{:S(2)}, u32[]{:S(2)}) collective-permute-start(f32[128,1536]{1,0:T(8,128)S(1)} %get-tuple-element.449.refs_1_), channel_id=1, source_target_pairs={{0,2},{1,3},{2,0},{3,1},{4,6},{5,7},{6,4},{7,5},{8,10},{9,11},{10,... | collective-permute-start | bytes 2359304 | tf_op jit(solution)/shard_map/ppermute | solution.py:699
  163.5 9.5 %collective-permute-start.50 = (f32[40,512]{1,0:T(8,128)S(1)}, f32[40,512]{1,0:T(8,128)S(1)}, u32[]{:S(2)}, u32[]{:S(2)}) collective-permute-start(f32[40,512]{1,0:T(8,128)S(1)} %get-tuple-element.441.refs_0_), channel_id=1, source_target_pairs={{0,8},{8,0},{16,24},{24,16},{1,9},{9,1},{17,25},{25,17},{2,10},{10... | collective-permute-start | bytes 245768 | tf_op jit(solution)/shard_map/ppermute | solution.py:669
  169.5 16.8 %collective-permute-start.48 = (f32[128,1152]{1,0:T(8,128)}, f32[128,1152]{1,0:T(8,128)}, u32[]{:S(2)}, u32[]{:S(2)}) collective-permute-start(f32[128,1152]{1,0:T(8,128)} %get-tuple-element.439.refs_1_), channel_id=1, source_target_pairs={{0,8},{1,17},{2,10},{3,19},{4,12},{5,21},{6,14},{7,23},{8,0},{9,25... | collective-permute-start | bytes 1769480 | tf_op jit(solution)/shard_map/ppermute | solution.py:699
  171.2 5.0 %collective-permute-start.54 = (f32[256,1536]{1,0:T(8,128)S(1)}, f32[256,1536]{1,0:T(8,128)S(1)}, u32[]{:S(2)}, u32[]{:S(2)}) collective-permute-start(f32[256,1536]{1,0:T(8,128)S(1)} %get-tuple-element.444.refs_1_), channel_id=1, source_target_pairs={{0,1},{1,0},{2,3},{3,2},{4,5},{5,4},{6,7},{7,6},{8,9},{9,8},{10,11... | collective-permute-start | bytes 4718600 | tf_op jit(solution)/shard_map/ppermute | solution.py:669
  173.0 9.0 %collective-permute-start.55 = (f32[40,512]{1,0:T(8,128)S(1)}, f32[40,512]{1,0:T(8,128)S(1)}, u32[]{:S(2)}, u32[]{:S(2)}) collective-permute-start(f32[40,512]{1,0:T(8,128)S(1)} %get-tuple-element.460.refs_0_), channel_id=1, source_target_pairs={{0,16},{8,24},{16,0},{24,8},{1,17},{9,25},{17,1},{25,9},{2,18},{10... | collective-permute-start | bytes 245768 | tf_op jit(solution)/shard_map/ppermute | solution.py:669
  174.4 9.1 %collective-permute-start.52 = (f32[256,1024]{1,0:T(8,128)S(1)}, f32[256,1024]{1,0:T(8,128)S(1)}, u32[]{:S(2)}, u32[]{:S(2)}) collective-permute-start(f32[256,1024]{1,0:T(8,128)S(1)} %get-tuple-element.448.refs_1_), channel_id=1, source_target_pairs={{0,1},{1,0},{2,3},{3,2},{4,5},{5,4},{6,7},{7,6},{8,9},{9,8},{10,11... | collective-permute-start | bytes 3145736 | tf_op jit(solution)/shard_map/ppermute | solution.py:669
  180.2 13.3 %collective-permute-start.57 = (f32[256,1536]{1,0:T(8,128)S(1)}, f32[256,1536]{1,0:T(8,128)S(1)}, u32[]{:S(2)}, u32[]{:S(2)}) collective-permute-start(f32[256,1536]{1,0:T(8,128)S(1)} %get-tuple-element.456.refs_1_), channel_id=1, source_target_pairs={{0,1},{1,0},{2,3},{3,2},{4,5},{5,4},{6,7},{7,6},{8,9},{9,8},{10,11... | collective-permute-start | bytes 4718600 | tf_op jit(solution)/shard_map/ppermute | solution.py:669
  187.8 7.4 %collective-permute-start.56 = (f32[256,1152]{1,0:T(8,128)S(1)}, f32[256,1152]{1,0:T(8,128)S(1)}, u32[]{:S(2)}, u32[]{:S(2)}) collective-permute-start(f32[256,1152]{1,0:T(8,128)S(1)} %get-tuple-element.466.refs_1_), channel_id=1, source_target_pairs={{0,1},{1,0},{2,3},{3,2},{4,5},{5,4},{6,7},{7,6},{8,9},{9,8},{10,11... | collective-permute-start | bytes 3538952 | tf_op jit(solution)/shard_map/ppermute | solution.py:669
  (31 other events, 43.6 us)

commit v3 on v2

--- a/solution.py
+++ b/solution.py
@@ -13,6 +13,8 @@
 BF16 = jnp.bfloat16
 F32 = jnp.float32
 ROOM = 2 * 1024 * 1024
+SWAPS = 1
+SMALL_ROWS = 24
 
 
 def sigmoid(a):
@@ -31,48 +33,32 @@
     return lax.dot_general(a, b, (((0,), (0,)), ((), ())), preferred_element_type=F32)
 
 
-COSTS = {
-    "norm_and_states": 2.7,
-    "values": 1.0,
-    "local_average": 3.1,
-    "carried_average": 2.7,
-    "mix": 1.4,
-    "attention": 1.9,
-    "hidden": 1.4,
-    "expand": 1.1,
-    "expand_back": 0.8,
-    "hidden_back": 1.4,
-    "reset_back": 1.2,
-    "attention_back": 1.9,
-    "smooth_back": 2.0,
-    "states_back": 2.5,
-    "state_back": 2.7,
-    "norm_back": 1.8,
-    "block_out": 1.7,
-    "grad": 1.4,
-    "split": 0.35,
-    "join": 0.35,
-    "sum": 0.25,
-    "out": 1.6,
-}
-PACE = 1e10
-
-
-def cost_of(name):
-    return COSTS.get(name, COSTS.get(name.split("_")[-1], 0.6))
+class Place:
+    def __init__(self, lengths):
+        self.lengths = lengths
+        self.shape = (lengths.shape[1] + 2,)
+
+    def __getitem__(self, i):
+        if i == 0:
+            return lax.axis_index("seq")
+        return self.lengths[0, i - 1]
 
 
 class Line:
-    def __init__(self):
+    def __init__(self, paces):
         self.token = None
-
-    def __call__(self, body, ins, outs, scratch=(), name=None, held=None, alias=None, dma=0):
+        self.paces = paces
+        self.count = 0
+
+    def __call__(self, body, ins, outs, scratch=(), name=None, held=None, left=(), alias=None, out_left=0, dma=0):
         count = len(ins)
         before = () if self.token is None else (self.token,)
         alias = alias or {}
         specs = []
         for i, a in enumerate(ins):
-            if i in alias:
+            if i in left:
+                specs.append(pl.BlockSpec(memory_space=pltpu.HBM))
+            elif i in alias:
                 specs.append(pl.BlockSpec(memory_space=pl.ANY))
             else:
                 specs.append(pl.BlockSpec(memory_space=pltpu.SMEM if a.dtype == jnp.int32 else pltpu.VMEM))
@@ -80,24 +66,27 @@
         if held is None:
             held = sum(a.size * a.dtype.itemsize for a in ins if a.dtype != jnp.int32)
             held += sum(math.prod(s) * jnp.dtype(d).itemsize for s, d in tuple(outs) + tuple(scratch))
+        first = count + len(before)
 
         def run(*refs):
-            body(*refs[:count], *refs[count + len(before) : count + len(before) + len(outs)], *refs[count + len(before) + len(outs) + 1 :])
-            refs[count + len(before) + len(outs)][...] = jnp.zeros((8, 128), F32)
-
-        place = pl.ANY if dma else pltpu.VMEM
+            body(*refs[:count], *refs[first : first + len(outs)], *refs[first + len(outs) + 1 :])
+            refs[first + len(outs)][...] = jnp.zeros((8, 128), F32)
+
+        places = [pl.ANY if i < out_left else pltpu.VMEM for i in range(len(outs))]
         scratches = [pltpu.VMEM(s, d) for s, d in scratch]
         if dma:
             scratches.append(pltpu.SemaphoreType.DMA((dma,)))
+        pace = self.paces[self.count] if self.count < len(self.paces) else 0
+        self.count += 1
         result = pl.pallas_call(
             run,
             in_specs=specs,
-            out_specs=[pl.BlockSpec(memory_space=place)] * len(outs) + [pl.BlockSpec(memory_space=pltpu.VMEM)],
+            out_specs=[pl.BlockSpec(memory_space=m) for m in places + [pltpu.VMEM]],
             out_shape=[jax.ShapeDtypeStruct(s, d) for s, d in outs] + [jax.ShapeDtypeStruct((8, 128), F32)],
             scratch_shapes=scratches,
             input_output_aliases=alias,
             compiler_params=pltpu.CompilerParams(vmem_limit_bytes=int(held * 1.05) + ROOM),
-            cost_estimate=pl.CostEstimate(flops=int(cost_of(name) * PACE), bytes_accessed=0, transcendentals=0),
+            cost_estimate=pl.CostEstimate(flops=int(pace * 1e9), bytes_accessed=0, transcendentals=0),
             name=name,
         )(*ins, *before)
         self.token = result[-1]
@@ -185,21 +174,17 @@
     return reach
 
 
-def start_body(meta, tok, gain, delta, alpha, beta, eta, normed, low, enter, end, logk, keep, mix):
+def start_body(lengths, tok, gain, logk, keep, normed, low, enter, end):
+    meta = Place(lengths)
     tokens, width = tok.shape
-    hidden = delta.shape[0]
+    hidden = end.shape[0]
     chunks = tokens // CHUNK
     x = tok[...].astype(F32)
     centered = x - jnp.mean(x, axis=1, keepdims=True)
     spread = jnp.mean(centered * centered, axis=1, keepdims=True)
-    rows = centered * lax.rsqrt(spread + EPS) * gain[...]
+    rows = centered * lax.rsqrt(spread + EPS) * gain[0:1, :]
     put_tiled(normed, rows)
     low[...] = rows.astype(BF16)
-    share = jax.nn.sigmoid(delta[...])
-    log_keep = jnp.log1p(-share * jax.nn.sigmoid(alpha[...]))
-    logk[...] = log_keep
-    keep[...] = jnp.exp(log_keep)
-    mix[...] = share * beta[...] * (eta[...] * (1.0 / math.sqrt(hidden)))
     free = chunk_masks(meta, meta[0] * tokens, chunks)
     edge = edge_masks(free, chunks, False)
     masks, shifts = doubling_masks(edge, chunks, False)
@@ -270,23 +255,27 @@
     out[...] = near + (reach * decay) * far
 
 
+def window_body(count, tokens, meta, near, far, logk, out):
+    span = 2 * tokens
+    first = (meta[0] - meta[0] % 2) * tokens
+    reach = clear_range(meta, first + 1, first + count * span + 1)
+    out[...] = near[...] + (reach * jnp.exp((count * span) * logk[...])) * far[...]
+
+
 def carry_of(backward, tokens, meta, other, arrived, logk):
     core = meta[0] % 2
     first = (meta[0] - core) * tokens
     span = 2 * tokens
-    chip_decay = jnp.exp(span * logk[...])
     total = None
-    power = None
-    for k, part in enumerate(arrived):
+    for k, part in arrived:
         if backward:
             reach = clear_range(meta, first + span, first + (k + 1) * span + 1)
         else:
             reach = clear_range(meta, first - k * span, first)
         term = part[...] * reach
-        if power is not None:
-            term = term * power
+        if k:
+            term = term * jnp.exp((k * span) * logk[...])
         total = term if total is None else total + term
-        power = chip_decay if power is None else power * chip_decay
     decay = jnp.exp(tokens * logk[...])
     middle = first + tokens
     if backward:
@@ -298,13 +287,21 @@
     return jnp.where(core == 0, total, other[...] + (through * decay) * total)
 
 
+def reversed_lanes(row):
+    size = row.shape[1]
+    down = lax.broadcasted_iota(jnp.int32, (size, size), 0)
+    across = lax.broadcasted_iota(jnp.int32, (size, size), 1)
+    turn = jnp.where((down + across) % size == 0, 1.0, 0.0).astype(F32)
+    return jnp.dot(row, turn, precision=lax.Precision.HIGHEST, preferred_element_type=F32)
+
+
 def carried_body(chips, meta, other, *rest):
     arrived = rest[:chips]
     logk, keep, mix, omega, normed, smooth, enter, low, slope, states, carry, extra = rest[chips:]
     tiles, tokens, _ = normed.shape
     hidden = keep.shape[0]
     chunks = tokens // CHUNK
-    carry[...] = carry_of(False, tokens, meta, other, arrived, logk)
+    carry[...] = carry_of(False, tokens, meta, other, list(enumerate(arrived)), logk)
     free = chunk_masks(meta, meta[0] * tokens, chunks)
     reach = prefix_mask(free, chunks, False)
     offset = (lax.broadcasted_iota(jnp.int32, (chunks, 128), 0) * CHUNK).astype(F32)
@@ -368,11 +365,12 @@
         candidate[:, b * 256 : (b + 1) * 256] = mm(low[...], mix_weight[:, top + b * 256 : top + (b + 1) * 256])
 
 
-def attend_body(queries, keys, values, rel_rev, reset, weights, attended, gated):
+def attend_body(queries, keys, values, rel_bias, reset, weights, attended, gated):
     tokens, shared_width = queries.shape
     place = lax.broadcasted_iota(jnp.int32, (SPAN, SPAN), 0)
     causal = place >= lax.broadcasted_iota(jnp.int32, (SPAN, SPAN), 1)
-    bias = shift_rows(jnp.broadcast_to(rel_rev[...], (SPAN, SPAN)), True)
+    turned = jnp.broadcast_to(reversed_lanes(jnp.broadcast_to(rel_bias[...], (8, SPAN)))[0:1], (SPAN, SPAN))
+    bias = shift_rows(turned, True)
     scale = 1.0 / math.sqrt(shared_width)
     for s in range(tokens // SPAN):
         rows = pl.ds(s * SPAN, SPAN)
@@ -418,15 +416,21 @@
 
 
 def weights_body(parts, meta, *refs):
-    kept, sent = refs[-2:]
-    pairs = refs[:-2]
+    kept, sent = refs[-SWAPS - 1], refs[-SWAPS:]
+    pairs = refs[: -SWAPS - 1]
     half = kept.shape[0]
     core = meta[0] % 2
-    for target, side in ((sent, 1 - core), (kept, core)):
+    for mine, side in ((False, 1 - core), (True, core)):
         for i, (column, block) in enumerate(parts):
             left, right = pairs[2 * i], pairs[2 * i + 1]
             begin = pl.multiple_of(side * half + block, 128)
-            target[:, column : column + right.shape[1]] = mm_tn(left[:, pl.ds(begin, half)], right[...])
+            cols = slice(column, column + right.shape[1])
+            value = mm_tn(left[:, pl.ds(begin, half)], right[...])
+            if mine:
+                kept[:, cols] = value
+            else:
+                for j, target in enumerate(sent):
+                    target[:, cols] = value[j * half // SWAPS : (j + 1) * half // SWAPS]
 
 
 def block_body(residual, expanded, ffn_out, out):
@@ -517,7 +521,8 @@
     small[...] = jnp.zeros_like(small)
     for i in range(4):
         small[i : i + 1, :] = sums[i]
-    small[4:5, :] = jnp.sum(shift_rows(slopes, False), axis=0, keepdims=True)
+    turned = jnp.sum(shift_rows(slopes, False), axis=0, keepdims=True)
+    small[4:5, :] = reversed_lanes(jnp.broadcast_to(turned, (8, SPAN)))[0:1]
 
 
 def smooth_back_body(
@@ -577,7 +582,7 @@
     logk, enter, later = rest[chips:]
     hidden, chunks, width = enter.shape
     tokens = chunks * CHUNK
-    carry = carry_of(True, tokens, meta, other, arrived, logk)
+    carry = carry_of(True, tokens, meta, other, [(2**j - 1, part) for j, part in enumerate(arrived)], logk)
     free = chunk_masks(meta, meta[0] * tokens, chunks)
     reach = prefix_mask(free, chunks, True)
     offset = ((chunks - 1 - lax.broadcasted_iota(jnp.int32, (chunks, 128), 0)) * CHUNK).astype(F32)
@@ -630,27 +635,31 @@
     sums = refs[count : 2 * count]
     tok, gain, input_part, omega_grad, gain2_grad, small, input_grad, packed = refs[2 * count :]
     x = tok[...].astype(F32)
+    width = x.shape[1]
     centered = x - jnp.mean(x, axis=1, keepdims=True)
     inverse = lax.rsqrt(jnp.mean(centered * centered, axis=1, keepdims=True) + EPS)
     normal = centered * inverse
     upstream = jnp.concatenate([t[...] for t in totals], axis=1)
     input_grad[...] = input_part[...] + layer_grad(upstream * gain[...], normal, inverse)
-    at = sums[0].shape[0]
+    at = sums[0].shape[0] // 2
+    packed[...] = jnp.zeros_like(packed)
     for i in range(count):
-        packed[0:at, i * 128 : (i + 1) * 128] = sums[i][...]
-    packed[at : at + 8, :] = jnp.zeros((8, x.shape[1]), F32)
-    packed[at : at + 1, :] = jnp.sum(upstream * normal, axis=0, keepdims=True)
-    packed[at + 1 : at + 2, :] = gain2_grad[...]
-    packed[at + 2 : at + 3, :] = omega_grad[...]
-    for i in range(5):
-        packed[at + 3 + i : at + 4 + i, 0 : small.shape[1]] = small[i : i + 1, :]
-
-
-def finish_body(packed, delta, alpha, beta, eta, delta_grad, alpha_grad, beta_grad, eta_grad):
-    hidden = delta.shape[0]
+        packed[0:at, i * 128 : (i + 1) * 128] = sums[i][0:at, :]
+        packed[0:at, width + i * 128 : width + (i + 1) * 128] = sums[i][at : 2 * at, :]
+    packed[at : at + 1, :width] = jnp.sum(upstream * normal, axis=0, keepdims=True)
+    packed[at : at + 1, width : 2 * width] = gain2_grad[...]
+    packed[at + 1 : at + 2, :width] = omega_grad[...]
+    packed[0:8, 2 * width : 2 * width + small.shape[1]] = small[...]
+
+
+def finish_body(own, other, delta, alpha, beta, eta, *outs):
+    delta_grad, alpha_grad, beta_grad, eta_grad, gain1_grad, gain2_grad, omega_grad, qk_gain_grad, qk_bias_grad, rel_grad = outs
+    hidden, width = delta_grad.shape
     scale = 1.0 / math.sqrt(hidden)
-    read = packed[0:hidden, :]
-    mark = packed[hidden : 2 * hidden, :]
+    low = own.shape[0] - SMALL_ROWS
+    packed = own[low:, :] + other[low:, :]
+    read = packed[0:hidden, :width]
+    mark = packed[0:hidden, width : 2 * width]
     share = jax.nn.sigmoid(delta[...])
     damp = jax.nn.sigmoid(alpha[...])
     inflow = share * beta[...]
@@ -662,6 +671,13 @@
     share_grad = beta[...] * inflow_grad + damp * rate
     delta_grad[...] = share_grad * share * (1.0 - share)
     alpha_grad[...] = share * rate * damp * (1.0 - damp)
+    gain1_grad[...] = packed[hidden : hidden + 1, :width]
+    gain2_grad[...] = packed[hidden : hidden + 1, width : 2 * width]
+    omega_grad[...] = packed[hidden + 1 : hidden + 2, :width]
+    tail = slice(2 * width, 2 * width + rel_grad.shape[1])
+    qk_gain_grad[...] = packed[0:2, tail]
+    qk_bias_grad[...] = packed[2:4, tail]
+    rel_grad[...] = packed[4:5, tail]
 
 
 def swap(a, axis, bit):
@@ -669,16 +685,14 @@
     return lax.ppermute(a, axis, [(i, i ^ bit) for i in range(count)])
 
 
-def chip_parts(state, backward):
+def chip_before(state, chips):
     count = lax.axis_size("seq")
-    parts = []
-    for k in range(1, count // 2):
-        if backward:
-            moves = [(i, i - 2 * k) for i in range(2 * k, count)]
-        else:
-            moves = [(i, i + 2 * k) for i in range(count - 2 * k)]
-        parts.append(lax.ppermute(state, "seq", moves))
-    return parts
+    return lax.ppermute(state, "seq", [(i, i + 2 * chips) for i in range(count - 2 * chips)])
+
+
+def chip_after(state, chips):
+    count = lax.axis_size("seq")
+    return lax.ppermute(state, "seq", [(i, i - 2 * chips) for i in range(2 * chips, count)])
 
 
 def axis_bits(axis, least):
@@ -701,12 +715,21 @@
 
 ROUTES = (
     (("xy1", "yx1"), "2"),
-    (("xy1", "yx1"), "2"),
-    (("1xy", "1yx"), "2"),
-    (("xy1", "yx1"), "2"),
+    (("1xy", "yx1"), "2"),
+    (("xy1", "1yx"), "2"),
+    (("xy12", "yx12"), ""),
     (("xy1", "yx1"), "2"),
 )
-ORDER = "0KK3014K0231KK0412034201K3K04K21032413K24K3KK41K312K34K24"
+ORDER = (
+    "C0CC10C231KC02SK01K3042K",
+    "KK0132041K32KK04K1324301",
+    "2340312344313241424",
+)
+PACES = (
+    2, 2, 2, 2, 2, 2, 2, 2, 2, 8, 12, 12, 12, 12, 2, 12, 12, 12, 3, 12, 0, 2, 2, 2, 2, 2, 2, 2, 2,
+    2, 2, 2, 2, 2, 2, 12, 2, 2, 2, 2, 3, 0.5, 0.5, 12, 12, 12, 0, 12, 12, 12, 12, 2, 8, 8, 8, 8, 1,
+    6, 1, 12, 2, 2, 2, 2, 2, 2, 2, 2, 12, 12, 12, 12, 12, 6, 6, 6, 6, 6, 6, 6,
+)
 BITS = {"x": ("dp", 1), "y": ("dp", 2), "1": ("seq", 2), "2": ("seq", 4)}
 
 
@@ -727,11 +750,13 @@
         out[i] = jnp.full((8, 128), side.astype(F32))
 
 
-def split_body(index, masks, kept, arrived, keep, send):
+def split_body(index, masks, kept, *refs):
+    arrived, (keep, send) = refs[:-2], refs[-2:]
     half = keep.shape[0]
     upper = masks[index, 0:1, 0:1] > 0.5
-    low = kept[:half, :] + arrived[:half, :]
-    high = kept[half:, :] + arrived[half:, :]
+    came = jnp.concatenate([a[...] for a in arrived], axis=0) if len(arrived) > 1 else arrived[0][...]
+    total = kept[...] + came
+    low, high = total[:half], total[half:]
     keep[...] = jnp.where(upper, high, low)
     send[...] = jnp.where(upper, low, high)
 
@@ -740,17 +765,25 @@
     out[...] = kept[...] + arrived[...]
 
 
-def join_body(index, masks, own, other, out):
-    half = own.shape[0]
+def sum_more_body(kept, arrived, more, out):
+    rows = kept.shape[0]
+    out[:rows, :] = kept[...] + arrived[...]
+    out[rows:, :] = more[...]
+
+
+def join_body(index, extra, masks, own, other, out):
+    half = own.shape[0] - extra
     upper = masks[index, 0:1, 0:1] > 0.5
-    out[:half, :] = jnp.where(upper, other[...], own[...])
-    out[half:, :] = jnp.where(upper, own[...], other[...])
+    out[:half, :] = jnp.where(upper, other[:half, :], own[:half, :])
+    out[half : 2 * half, :] = jnp.where(upper, own[:half, :], other[:half, :])
+    if extra:
+        out[2 * half :, :] = own[half:, :] + other[half:, :]
 
 
 class Piece:
-    def __init__(self, line, masks, steps, kept, sent, routes, outputs, name):
-        self.line, self.masks, self.steps, self.name = line, masks, steps, name
-        self.outputs = outputs
+    def __init__(self, line, made, steps, kept, sent, routes, outputs, name, more=None):
+        self.line, self.made, self.steps, self.name = line, made, steps, name
+        self.outputs, self.more = outputs, more
         self.work = self.run(kept, sent, *routes)
         self.done = False
         self.advance()
@@ -760,58 +793,71 @@
             self.done = next(self.work, "end") == "end"
 
     def run(self, kept, sent, halves, wholes):
-        line, masks = self.line, self.masks
-        arrived = swap(sent, "seq", 1)
+        line = self.line
+        arrived = [swap(a, "seq", 1) for a in sent]
         yield
+        masks = self.made["masks"]
         for step in halves:
             rows, cols = kept.shape
             kept, send = line(
                 lambda *refs, index=self.steps.index(step): split_body(index, *refs),
-                (masks, kept, arrived),
+                (masks, kept, *arrived),
                 [((rows // 2, cols), F32)] * 2,
                 name=self.name + "_split",
             )
-            arrived = cross(send, step)
+            arrived = [cross(send, step)]
             yield
-        for step in wholes:
-            kept = line(sum_body, (kept, arrived), [(kept.shape, F32)], name=self.name + "_sum")[0]
-            arrived = cross(kept, step)
-            yield
-        part = line(sum_body, (kept, arrived), [(kept.shape, F32)], name=self.name + "_sum")[0]
-        for i, step in enumerate(reversed(halves)):
+        extra = 0
+        for step in list(wholes) + [None]:
+            rows, cols = kept.shape
+            if self.more is not None and not extra:
+                extra = SMALL_ROWS
+                kept = line(
+                    sum_more_body,
+                    (kept, arrived[0], self.more()),
+                    [((rows + extra, cols), F32)],
+                    name=self.name + "_sum",
+                )[0]
+            else:
+                kept = line(sum_body, (kept, arrived[0]), [(kept.shape, F32)], name=self.name + "_sum")[0]
+            if step is not None:
+                arrived = [cross(kept, step)]
+                yield
+        part = kept
+        for step in reversed(halves):
             other = cross(part, step)
             yield
             rows, cols = part.shape
             part = line(
-                lambda *refs, index=self.steps.index(step): join_body(index, *refs),
+                lambda *refs, index=self.steps.index(step): join_body(index, extra, *refs),
                 (masks, part, other),
-                [((2 * rows, cols), F32)],
+                [((2 * rows - extra, cols), F32)],
                 name=self.name + "_join",
             )[0]
         other = swap(part, "seq", 1)
-        self.outputs(part, False)
         yield
-        self.outputs(other, True)
-
-
-def place_body(plans, far, count, meta, part, *refs):
+        self.outputs(part, other, part.shape[0] - extra)
+
+
+def place_body(plans, rows, extra, count, more, meta, own, other, *refs):
     outs = refs[count : count + len(plans)]
     sems = refs[-1]
-    side = meta[0] % 2
-    side = 1 - side if far else side
-    rows = part.shape[0]
+    core = meta[0] % 2
     copies = []
-    for out, plan in zip(outs, plans):
-        for column, width, row, place in plan:
-            begin = pl.multiple_of(side * rows + row, 8)
-            copies.append(
-                pltpu.make_async_copy(
-                    part.at[:, pl.ds(column, width)],
-                    out.at[pl.ds(begin, rows), pl.ds(place, width)],
-                    sems.at[len(copies)],
+    for part, side in ((own, core), (other, 1 - core)):
+        for out, plan in zip(outs, plans):
+            for column, width, row, place in plan:
+                begin = pl.multiple_of(side * rows + row, 8)
+                copies.append(
+                    pltpu.make_async_copy(
+                        part.at[pl.ds(0, rows), pl.ds(column, width)],
+                        out.at[pl.ds(begin, rows), pl.ds(place, width)],
+                        sems.at[len(copies)],
+                    )
                 )
-            )
-            copies[-1].start()
+                copies[-1].start()
+    if more is not None:
+        more(own, other, *refs[:extra], *refs[count + len(plans) : -1])
     for copy in copies:
         copy.wait()
 
@@ -820,21 +866,28 @@
     def __init__(self, line, meta, shapes):
         self.line, self.meta, self.shapes, self.arrays = line, meta, shapes, {}
 
-    def placer(self, plans, name):
-        def place(part, far):
+    def placer(self, plans, name, more=None):
+        def place(own, other, rows):
             names = list(plans)
             held = [n for n in names if n in self.arrays]
-            alias = {2 + i: names.index(n) for i, n in enumerate(held)}
+            body, extra, shapes = (more[0], more[1], more[2]) if more else (None, (), [])
+            at = 3 + len(extra)
+            alias = {at + i: names.index(n) for i, n in enumerate(held)}
             results = self.line(
-                lambda *refs: place_body(list(plans.values()), far, len(held), *refs),
-                (self.meta, part, *[self.arrays[n] for n in held]),
-                [(self.shapes[n], F32) for n in names],
+                lambda *refs: place_body(
+                    list(plans.values()), rows, len(extra), len(extra) + len(held), body, *refs
+                ),
+                (self.meta, own, other, *extra, *[self.arrays[n] for n in held]),
+                [(self.shapes[n], F32) for n in names] + shapes,
                 name=name + "_out",
-                held=part.size * 4,
+                held=own.size * 8 + 2**20 * len(shapes) // 8,
                 alias=alias,
-                dma=sum(len(p) for p in plans.values()),
+                out_left=len(names),
+                dma=2 * sum(len(p) for p in plans.values()),
             )
             self.arrays.update(zip(names, results))
+            if more:
+                more[3](results[len(names) :])
 
         return place
 
@@ -871,7 +924,6 @@
     gain1 = norm1_gain[None]
     gain2 = norm2_gain[None]
     omega = ema_omega[None]
-    rel_rev = jnp.roll(rel_bias[::-1], 1)[None]
     ema = (ema_delta.T, ema_alpha.T, ema_beta.T, ema_eta.T)
     full = (rows, width)
     wide = (rows, value_width)
@@ -879,24 +931,28 @@
     tiles = (width // 128, rows, 128)
     state = (hidden, width)
     states = (hidden, chunks, width)
-    line = Line()
-
-    normed, low_normed, enter, end, logk, keep, mix = line(
+    line = Line(PACES)
+
+    share = jax.nn.sigmoid(ema_delta.T)
+    logk = jnp.log1p(-share * jax.nn.sigmoid(ema_alpha.T))
+    keep = jnp.exp(logk)
+    mix = share * ema_beta.T * (ema_eta.T * (1.0 / math.sqrt(hidden)))
+    gain_rows = jnp.where(share > -1.0, gain1, 0.0)
+    normed, low_normed, enter, end = line(
         start_body,
-        (meta, tokens, gain1, *ema),
-        [(tiles, F32), (full, BF16), (states, F32), (state, F32), (state, F32), (state, F32), (state, F32)],
+        (seq_lengths, tokens, gain_rows, logk, keep),
+        [(tiles, F32), (full, BF16), (states, F32), (state, F32)],
         name="norm_and_states",
     )
     other = swap(end, "seq", 1)
     chip_end = line(
         lambda *refs: pair_body(False, rows, *refs), (meta, end, other, logk), [(state, F32)], name="chip_state"
     )[0]
-    arrived = chip_parts(chip_end, False)
+    arrived = [chip_before(chip_end, k) for k in range(1, lax.axis_size("seq") // 2)]
     routes = [route(halving, doubling) for halving, doubling in ROUTES]
     steps = sorted({step for halves, wholes in routes for step in halves})
-    masks = line(lambda *refs: masks_body(steps, *refs), (meta,), [((len(steps), 8, 128), F32)], name="masks")[0]
+    smooth = line(local_body, (normed, enter, keep, mix), [(tiles, F32)], name="local_average")[0]
     values, values_slope = line(values_body, (low_normed, value_weight), [(wide, BF16), (wide, F32)], name="values")
-    smooth = line(local_body, (normed, enter, keep, mix), [(tiles, F32)], name="local_average")[0]
     low_smoothed, slope_pre, entering = line(
         lambda *refs: carried_body(len(arrived), *refs),
         (meta, other, *arrived, logk, keep, mix, omega, normed, smooth, enter),
@@ -912,7 +968,7 @@
     )
     weights, attended, gated = line(
         attend_body,
-        (queries, keys, values, rel_rev, reset),
+        (queries, keys, values, rel_bias[None], reset),
         [((rows, SPAN), F32), (wide, F32), (wide, BF16)],
         name="attention",
     )
@@ -937,84 +993,128 @@
             "value": (width, value_width),
         },
     )
-    pieces = []
-
-    def start_piece(parts, pairs, height, cols, plans, name):
-        kept, sent = line(
+    made = {}
+    results = {}
+
+    def more():
+        while "packed" not in results:
+            next(work)
+        return results["packed"]
+
+    def take(values):
+        results["small"] = values
+
+    last = (
+        finish_body,
+        ema,
+        [(state, F32)] * 4 + [((1, width), F32)] * 3 + [((2, shared_width), F32)] * 2 + [((1, shared_width), F32)],
+        take,
+    )
+
+    def start_piece(number, parts, pairs, height, cols, plans, name):
+        kept, *sent = line(
             lambda *refs: weights_body(parts, *refs),
             (meta, *[a for pair in pairs for a in pair]),
-            [((height, cols), F32)] * 2,
+            [((height, cols), F32)] + [((height // SWAPS, cols), F32)] * SWAPS,
             name=name + "_grad",
         )
-        pieces.append(
-            Piece(line, masks, steps, kept, sent, routes[len(pieces)], outputs.placer(plans, name), name)
+        end = name == "value"
+        placer = outputs.placer(plans, name, last if end else None)
+        return Piece(line, made, steps, kept, sent, routes[number], placer, name, more if end else None)
+
+    def ffn_out_piece():
+        return start_piece(
+            0,
+            [(0, 0)], [(expanded, cotangent)], inner // 2, width, {"ffn_out": [(0, width, 0, 0)]}, "ffn_out"
         )
 
-    def step(*which):
-        for i in which:
+    def ffn_in_piece():
+        return start_piece(
+            1,
+            [(0, 0), (inner, 0)],
+            [(low2, made["expand_grad"]), (low_smoothed, made["update_grad"])],
+            half,
+            inner + width,
+            {"ffn_in": [(0, inner, 0, 0)], "mix": [(inner, width, 0, 0)]},
+            "ffn_in",
+        )
+
+    def out_piece():
+        return start_piece(
+            2,
+            [(0, 0), (width, width), (2 * width, 0)],
+            [(gated, made["out_grad"]), (gated, made["out_grad"]), (low_smoothed, made["out_grad"])],
+            half,
+            3 * width,
+            {
+                "out": [(0, width, 0, 0), (width, width, width, 0)],
+                "mix": [(2 * width, width, 0, width + shared_width + value_width)],
+            },
+            "out",
+        )
+
+    def reset_piece():
+        return start_piece(
+            3,
+            [(0, 0)],
+            [(low_smoothed, made["reset_grad"])],
+            half,
+            value_width,
+            {"mix": [(0, value_width, 0, width + shared_width)]},
+            "reset",
+        )
+
+    def value_piece():
+        return start_piece(
+            4,
+            [(0, 0), (value_width, 0)],
+            [(low_normed, made["value_grad"]), (low_smoothed, made["shared_grad"])],
+            half,
+            value_width + shared_width,
+            {"value": [(0, value_width, 0, 0)], "mix": [(value_width, shared_width, 0, width)]},
+            "value",
+        )
+
+    makers = (ffn_out_piece, ffn_in_piece, out_piece, reset_piece, value_piece)
+    pieces = []
+
+    def advance(i):
+        if i < len(pieces) and pieces[i] is not None:
             pieces[i].advance()
-
-    start_piece(
-        [(0, 0)], [(expanded, cotangent)], inner // 2, width, {"ffn_out": [(0, width, 0, 0)]}, "ffn_out"
-    )
-    expand_grad = line(
-        expand_back_body, (cotangent, ffn_out, slope_exp), [((rows, inner), BF16)], name="expand_back"
-    )[0]
-    step(0)
-    input_part, update_grad, out_grad, gain2_grad = line(
-        hidden_back_body,
-        (expand_grad, ffn_in, normal2, inverse2, gain2, cotangent, update, change, slope_hidden),
-        [(full, F32), (full, BF16), (full, BF16), ((1, width), F32)],
-        name="hidden_back",
-    )
-    start_piece(
-        [(0, 0), (inner, 0)],
-        [(low2, expand_grad), (low_smoothed, update_grad)],
-        half,
-        inner + width,
-        {"ffn_in": [(0, inner, 0, 0)], "mix": [(inner, width, 0, 0)]},
-        "ffn_in",
-    )
-    start_piece(
-        [(0, 0), (width, width), (2 * width, 0)],
-        [(gated, out_grad), (gated, out_grad), (low_smoothed, out_grad)],
-        half,
-        3 * width,
-        {
-            "out": [(0, width, 0, 0), (width, width, width, 0)],
-            "mix": [(2 * width, width, 0, width + shared_width + value_width)],
-        },
-        "out",
-    )
-    step(1)
-    reset_grad, attend_grad = line(
-        reset_back_body, (out_grad, out_weight, reset, attended), [(wide, BF16)] * 2, name="reset_back"
-    )
-    step(2)
-    value_grad, shared_grad, small = line(
-        attend_back_body,
-        (attend_grad, weights, queries, keys, shared, shared_slope, values, values_slope, qk_gain),
-        [(wide, BF16), (thin, BF16), ((8, shared_width), F32)],
-        name="attention_back",
-    )
-    start_piece(
-        [(0, 0)],
-        [(low_smoothed, reset_grad)],
-        half,
-        value_width,
-        {"mix": [(0, value_width, 0, width + shared_width)]},
-        "reset",
-    )
-    start_piece(
-        [(0, 0), (value_width, 0)],
-        [(low_normed, value_grad), (low_smoothed, shared_grad)],
-        half,
-        value_width + shared_width,
-        {"value": [(0, value_width, 0, 0)], "mix": [(value_width, shared_width, 0, width)]},
-        "value",
-    )
-
-    def rest():
+        else:
+            pieces.extend([None] * (i + 1 - len(pieces)))
+            pieces[i] = makers[i]()
+
+    def compute():
+        yield
+        made["masks"] = line(
+            lambda *refs: masks_body(steps, *refs), (meta,), [((len(steps), 8, 128), F32)], name="masks"
+        )[0]
+        made["expand_grad"] = line(
+            expand_back_body, (cotangent, ffn_out, slope_exp), [((rows, inner), BF16)], name="expand_back"
+        )[0]
+        yield
+        input_part, update_grad, out_grad, gain2_grad = line(
+            hidden_back_body,
+            (made["expand_grad"], ffn_in, normal2, inverse2, gain2, cotangent, update, change, slope_hidden),
+            [(full, F32), (full, BF16), (full, BF16), ((1, width), F32)],
+            name="hidden_back",
+        )
+        made["update_grad"], made["out_grad"] = update_grad, out_grad
+        yield
+        reset_grad, attend_grad = line(
+            reset_back_body, (out_grad, out_weight, reset, attended), [(wide, BF16)] * 2, name="reset_back"
+        )
+        made["reset_grad"] = reset_grad
+        yield
+        value_grad, shared_grad, small = line(
+            attend_back_body,
+            (attend_grad, weights, queries, keys, shared, shared_slope, values, values_slope, qk_gain),
+            [(wide, BF16), (thin, BF16), ((8, shared_width), F32)],
+            name="attention_back",
+        )
+        made["value_grad"], made["shared_grad"] = value_grad, shared_grad
+        yield
         smooth_grad, norm_grad, omega_grad = line(
             smooth_back_body,
             (update_grad, shared_grad, reset_grad, out_grad, value_grad, mix_weight, value_weight, slope_pre)
@@ -1028,14 +1128,25 @@
         )
         other_begin = swap(begin, "seq", 1)
         yield
-        chip_begin = line(
+        window = line(
             lambda *refs: pair_body(True, rows, *refs),
             (meta, begin, other_begin, logk),
             [(state, F32)],
             name="chip_grad",
         )[0]
-        returned = chip_parts(chip_begin, True)
+        returned = [chip_after(window, 1)]
         yield
+        chips = 1
+        while 4 * chips < lax.axis_size("seq"):
+            window = line(
+                lambda *refs, chips=chips: window_body(chips, rows, *refs),
+                (meta, window, returned[-1], logk),
+                [(state, F32)],
+                name="window_grad",
+            )[0]
+            chips *= 2
+            returned.append(chip_after(window, chips))
+            yield
         later = line(
             lambda *refs: carry_back_body(len(returned), *refs),
             (meta, other_begin, *returned, logk, later),
@@ -1055,50 +1166,41 @@
                 )
             )
             yield
-        input_grad, packed = line(
+        results["input_grad"], results["packed"] = line(
             lambda *refs: close_body(len(backs), *refs),
             (*[b[0] for b in backs], *[b[1] for b in backs], tokens, gain1, input_part, omega_grad, gain2_grad, small),
-            [(full, F32), ((2 * hidden + 8, width), F32)],
+            [(full, F32), ((SMALL_ROWS, value_width + shared_width), F32)],
             name="norm_back",
         )
-        results["input_grad"] = input_grad
-        for axis, bit in axis_bits("seq", 1) + axis_bits("dp", 1):
-            moved = swap(packed, axis, bit)
-            yield
-            packed = line(sum_body, (packed, moved), [(packed.shape, F32)], name="small_sum")[0]
-        results["packed"] = packed
-        results["ema"] = line(finish_body, (packed, *ema), [(state, F32)] * 4, name="state_parameters")
         yield
         results["block_out"] = line(block_body, (residual, expanded, ffn_out), [(full, F32)], name="block_out")[0]
 
-    results = {}
-    work = rest()
-    for item in ORDER:
-        if item == "K":
+    work = compute()
+    for item in "".join(ORDER):
+        if item.isdigit():
+            advance(int(item))
+        else:
             next(work, None)
-        else:
-            step(int(item))
     for _ in work:
         pass
     while not all(p.done for p in pieces):
-        step(*range(len(pieces)))
-    packed = results["packed"]
-    at = 2 * hidden
-    tail = packed[at + 3 :, :shared_width]
+        for i in range(len(pieces)):
+            advance(i)
     sums = outputs.arrays
+    small = results["small"]
     return (
         results["block_out"],
         results["input_grad"],
-        packed[at],
+        small[4][0],
         sums["value"],
-        *[g.T for g in results["ema"]],
-        packed[at + 2],
+        *[g.T for g in small[:4]],
+        small[6][0],
         sums["mix"],
-        tail[0:2],
-        tail[2:4],
-        jnp.roll(tail[4][::-1], 1),
+        small[7],
+        small[8],
+        small[9][0],
         sums["out"],
-        packed[at + 1],
+        small[5][0],
         sums["ffn_in"],
         sums["ffn_out"],
     )

time: 198 us -> 184 us (0.929)
  Pallas kernels: 72.5 us -> 65.2 us
  local copies, waits for them, and re-layouts: 10 us -> 3.78 us
    pallas_call x85 -> x76, Pallas kernels: 72.5 us -> 65.2 us  [__call__(): pl.pallas_call(run, in_specs=specs, out_specs=[pl.BlockSpec(memory_space=...]
    unnamed x74 -> x48, local copies, waits for them, and re-layouts: 8.02 us -> 3.78 us
    ppermute x35 -> x36, starting transfers between devices: 38.6 us -> 41.9 us  [cross(): return lax.ppermute(a, ('dp', 'seq'), moves)]
    slice x7 -> x0, local copies, waits for them, and re-layouts: 2.02 us -> none  [the longest x3 0.69 us: shards(): jnp.roll(tail[4][::-1], 1)]
    ppermute x17 -> x12, starting transfers between devices: 9.41 us -> 7.52 us  [swap(): return lax.ppermute(a, axis, [(i, i ^ bit) for i in range(count)])]
    ppermute x6 -> x5, starting transfers between devices: 14.5 us -> 13.2 us  [the longest x3 10.6 us: chip_before(): lax.ppermute(state, 'seq', [(i, i + 2 * chips) for i in range(count - 2 *...]
    ppermute x17 -> x12, waiting for transfers between devices: 4.15 us -> 3.33 us  [swap(): return lax.ppermute(a, axis, [(i, i ^ bit) for i in range(count)])]
    ppermute x35 -> x36, waiting for transfers between devices: 44.4 us -> 45 us  [cross(): return lax.ppermute(a, ('dp', 'seq'), moves)]
  transfers between devices with their start and end apart: 58 -> 53, of which waited for: 16 -> 16; matrix products, arithmetic and copies ran while one was open for 2% -> 0% of each run, Pallas kernels for 27% -> 26%
where the time goes in v3:
time: 184 us
  Pallas kernels  65.2 us (35%)
  starting transfers between devices  62.7 us (34%)
  waiting for transfers between devices  49.4 us (27%)
  local copies, waits for them, and re-layouts  3.78 us (2%)
  between operations  1.84 us (1%)
    pallas_call x76, Pallas kernels, __call__(): pl.pallas_call(run, in_specs=specs, out_specs=[pl.BlockSpec(memory_space=...  65.2 us
    ppermute x36, waiting for transfers between devices, cross(): return lax.ppermute(a, ('dp', 'seq'), moves)  45 us
    ppermute x36, starting transfers between devices, cross(): return lax.ppermute(a, ('dp', 'seq'), moves)  41.9 us
    ppermute x3, starting transfers between devices, chip_before(): lax.ppermute(state, 'seq', [(i, i + 2 * chips) for i in range(count - 2 *...  10.6 us
    ppermute x12, starting transfers between devices, swap(): return lax.ppermute(a, axis, [(i, i ^ bit) for i in range(count)])  7.52 us
    unnamed x48, local copies, waits for them, and re-layouts  3.78 us
  transfers between devices with their start and end apart: 53, of which 16 were waited for; matrix products, arithmetic and copies ran while one was open for 0% of the time, Pallas kernels for 26%

profile of v3, /device:TPU:0, one launch (start us, length us, event | category | flops | bytes accessed | tf_op | source)
XLA Modules:
  0.0 183.8 jit_solution(15773357719463924761)
XLA Ops:
  3.2 2.7 %norm_and_states.1 = (f32[4,512,128]{2,1,0:T(8,128)S(1)}, bf16[512,512]{1,0:T(8,128)(2,1)S(1)}, f32[16,8,512]{2,1,0:T(8,128)S(1)}, f32[16,512]{1,0:T(8,128)S(1)}, f32[8,128]{1,0:T(8,128)S(1)}) custom-call(s32[1,3]{1,0:T(1,128)S(1)} %copy-done.11, bf16[512,512]{1,0:T(8,128)(2,1)S(1)} %copy-done.2, f32[16,512]{1,0:T(8,128)S(1)} %get-tuple-element.458.refs_2_, ...), custom_call_target="tpu_custom_call" | custom-call | flops 2000000000 | tf_op jit(solution)/shard_map/norm_and_states/pallas_call | solution.py:81
  7.9 6.8 %collective-permute-start.3 = (f32[16,512]{1,0:T(8,128)S(1)}, f32[16,512]{1,0:T(8,128)S(1)}, u32[]{:S(2)}, u32[]{:S(2)}) collective-permute-start(f32[16,512]{1,0:T(8,128)S(1)} %get-tuple-element.238), channel_id=1, source_target_pairs={{0,6},{1,7},{8,14},{9,15},{16,22},{17,23},{24,30},{25,31}} | collective-permute-start | bytes 98312 | tf_op jit(solution)/shard_map/ppermute | solution.py:690
  14.8 1.3 collective-permute-start.2
  16.1 2.5 %collective-permute-start.1 = (f32[16,512]{1,0:T(8,128)S(1)}, f32[16,512]{1,0:T(8,128)S(1)}, u32[]{:S(2)}, u32[]{:S(2)}) collective-permute-start(f32[16,512]{1,0:T(8,128)S(1)} %get-tuple-element.238), channel_id=1, source_target_pairs={{0,2},{1,3},{2,4},{3,5},{4,6},{5,7},{8,10},{9,11},{10,12},{11,13},... | collective-permute-start | bytes 98312 | tf_op jit(solution)/shard_map/ppermute | solution.py:690
  18.6 3.1 %local_average.1 = (f32[4,512,128]{2,1,0:T(8,128)S(1)}, f32[8,128]{1,0:T(8,128)S(1)}) custom-call(f32[4,512,128]{2,1,0:T(8,128)S(1)} %get-tuple-element.239.refs_0_.refs_9_.refs_8_, f32[16,8,512]{2,1,0:T(8,128)S(1)} %get-tuple-element.240.refs_1_.refs_11_, f32[16,512]{1,0:T(8,128)S(1)} %get-tuple-element.455.refs_4_.refs_2_.refs_6_.refs_3_.refs_5_, ...), custom_call_target="tpu_custom_call" | custom-call | flops 2000000000 | tf_op jit(solution)/shard_map/local_average/pallas_call | solution.py:81
  22.9 2.7 %carried_average.1 = (bf16[512,512]{1,0:T(8,128)(2,1)S(1)}, f32[512,512]{1,0:T(8,128)S(1)}, f32[16,8,512]{2,1,0:T(8,128)S(1)}, f32[8,128]{1,0:T(8,128)S(1)}) custom-call(s32[5]{0:T(128)S(1)} %pad_add_fusion.refs_0_, f32[16,512]{1,0:T(8,128)S(1)} %collective-permute-done.refs_2_.refs_1_, f32[16,512]{1,0:T(8,128)S(1)} %collective-permute-done.1.refs_2_, ...), custom_call_target="tpu_custom_call" | custom-call | flops 2000000000 | tf_op jit(solution)/shard_map/carried_average/pallas_call | solution.py:81
  25.6 1.4 mix.1
  27.0 2.1 %attention.1 = (f32[512,128]{1,0:T(8,128)S(1)}, f32[512,1024]{1,0:T(8,128)S(1)}, bf16[512,1024]{1,0:T(8,128)(2,1)S(1)}, f32[8,128]{1,0:T(8,128)S(1)}) custom-call(bf16[512,128]{1,0:T(8,128)(2,1)S(1)} %get-tuple-element.248.refs_0_.refs_2_, bf16[512,128]{1,0:T(8,128)(2,1)S(1)} %get-tuple-element.249.refs_1_.refs_3_, ...), custom_call_target="tpu_custom_call" | custom-call | flops 2000000000 | tf_op jit(solution)/shard_map/attention/pallas_call | solution.py:81
  29.2 1.4 hidden.1
  31.7 1.3 ffn_out_grad.1
  35.0 1.4 hidden_back.1
  36.5 1.6 ffn_in_grad.1
  38.3 1.6 collective-permute-start.6
  39.9 1.3 reset_back.1
  41.2 1.6 out_grad.1
  43.1 1.3 reset_grad.1
  45.1 2.3 %attention_back.1 = (bf16[512,1024]{1,0:T(8,128)(2,1)S(1)}, bf16[512,128]{1,0:T(8,128)(2,1)S(1)}, f32[8,128]{1,0:T(8,128)S(1)}, f32[8,128]{1,0:T(8,128)S(1)}) custom-call(bf16[512,1024]{1,0:T(8,128)(2,1)S(1)} %get-tuple-element.280.refs_0_, f32[512,128]{1,0:T(8,128)S(1)} %get-tuple-element.281.refs_1_, ...), custom_call_target="tpu_custom_call" | custom-call | flops 12000000000 | tf_op jit(solution)/shard_map/attention_back/pallas_call | solution.py:81
  47.4 2.0 %smooth_back.1 = (f32[4,512,128]{2,1,0:T(8,128)S(1)}, f32[4,512,128]{2,1,0:T(8,128)S(1)}, f32[1,512]{1,0:T(1,128)S(1)}, f32[8,128]{1,0:T(8,128)S(1)}) custom-call(bf16[512,512]{1,0:T(8,128)(2,1)S(1)} %get-tuple-element.276.refs_4_.refs_0_, bf16[512,128]{1,0:T(8,128)(2,1)S(1)} %get-tuple-element.293.refs_1_.refs_4_, ...), custom_call_target="tpu_custom_call" | custom-call | tf_op jit(solution)/shard_map/smooth_back/pallas_call | solution.py:81
  49.5 1.6 collective-permute-start.7
  51.5 2.5 %states_back.1 = (f32[16,8,512]{2,1,0:T(8,128)S(1)}, f32[16,512]{1,0:T(8,128)S(1)}, f32[8,128]{1,0:T(8,128)S(1)}) custom-call(s32[5]{0:T(128)S(1)} %pad_add_fusion.refs_0_, f32[4,512,128]{2,1,0:T(8,128)S(1)} %get-tuple-element.301.refs_1_, f32[16,512]{1,0:T(8,128)S(1)} %get-tuple-element.456.refs_3_.refs_5_.refs_2_.refs_4_, ...), custom_call_target="tpu_custom_call" | custom-call | flops 2000000000 | tf_op jit(solution)/shard_map/states_back/pallas_call | solution.py:81
  54.2 1.3 collective-permute-start.17
  56.1 1.3 collective-permute-start.12
  57.4 1.5 collective-permute-done.7.refs_2_
  58.9 1.3 collective-permute-start.10
  62.9 1.3 collective-permute-start.16
  65.4 3.5 %collective-permute-start.15 = (f32[64,512]{1,0:T(8,128)S(1)}, f32[64,512]{1,0:T(8,128)S(1)}, u32[]{:S(2)}, u32[]{:S(2)}) collective-permute-start(f32[64,512]{1,0:T(8,128)S(1)} %get-tuple-element.323.refs_0_), channel_id=1, source_target_pairs={{0,4},{1,5},{2,6},{3,7},{4,0},{5,1},{6,2},{7,3},{8,12},{9,13},{10,... | collective-permute-start | bytes 393224 | tf_op jit(solution)/shard_map/ppermute | solution.py:713
  69.0 1.4 value_grad.1
  70.4 5.3 %collective-permute-start.14 = (f32[256,1152]{1,0:T(8,128)S(1)}, f32[256,1152]{1,0:T(8,128)S(1)}, u32[]{:S(2)}, u32[]{:S(2)}) collective-permute-start(f32[256,1152]{1,0:T(8,128)S(1)} %get-tuple-element.322), channel_id=1, source_target_pairs={{0,1},{1,0},{2,3},{3,2},{4,5},{5,4},{6,7},{7,6},{8,9},{9,8},{10,11... | collective-permute-start | bytes 3538952 | tf_op jit(solution)/shard_map/ppermute | solution.py:685
  77.5 2.6 %state_back.4 = (f32[512,128]{1,0:T(8,128)S(1)}, f32[32,128]{1,0:T(8,128)S(1)}, f32[8,128]{1,0:T(8,128)S(1)}) custom-call(f32[4,512,128]{2,1,0:T(8,128)S(1)} %get-tuple-element.239.refs_0_.refs_9_.refs_8_, f32[4,512,128]{2,1,0:T(8,128)S(1)} %get-tuple-element.301.refs_1_, f32[4,512,128]{2,1,0:T(8,128)S(1)} %get-tuple-element.324.refs_2_, ...), custom_call_target="tpu_custom_call" | custom-call | flops 2000000000 | tf_op jit(solution)/shard_map/state_back/pallas_call | solution.py:81
  80.1 2.6 %state_back.5 = (f32[512,128]{1,0:T(8,128)S(1)}, f32[32,128]{1,0:T(8,128)S(1)}, f32[8,128]{1,0:T(8,128)S(1)}) custom-call(f32[4,512,128]{2,1,0:T(8,128)S(1)} %get-tuple-element.239.refs_0_.refs_9_.refs_8_, f32[4,512,128]{2,1,0:T(8,128)S(1)} %get-tuple-element.301.refs_1_, f32[4,512,128]{2,1,0:T(8,128)S(1)} %get-tuple-element.324.refs_2_, ...), custom_call_target="tpu_custom_call" | custom-call | flops 2000000000 | tf_op jit(solution)/shard_map/state_back/pallas_call | solution.py:81
  83.0 1.3 collective-permute-start.24
  85.2 1.8 collective-permute-done.19.refs_2_
  87.4 1.9 %collective-permute-done.18.refs_2_ = f32[64,512]{1,0:T(8,128)S(1)} collective-permute-done((f32[64,512]{1,0:T(8,128)S(1)}, f32[64,512]{1,0:T(8,128)S(1)}, u32[]{:S(2)}, u32[]{:S(2)}) %collective-permute-start.18) | collective-permute-done | bytes 131104 | tf_op jit(solution)/shard_map/ppermute | solution.py:713
  89.3 1.3 collective-permute-start.23
  90.9 1.4 collective-permute-start.30
  92.3 2.6 %state_back.6 = (f32[512,128]{1,0:T(8,128)S(1)}, f32[32,128]{1,0:T(8,128)S(1)}, f32[8,128]{1,0:T(8,128)S(1)}) custom-call(f32[4,512,128]{2,1,0:T(8,128)S(1)} %get-tuple-element.239.refs_0_.refs_9_.refs_8_, f32[4,512,128]{2,1,0:T(8,128)S(1)} %get-tuple-element.301.refs_1_, f32[4,512,128]{2,1,0:T(8,128)S(1)} %get-tuple-element.324.refs_2_, ...), custom_call_target="tpu_custom_call" | custom-call | flops 500000000 | tf_op jit(solution)/shard_map/state_back/pallas_call | solution.py:81
  96.1 2.6 %state_back.7 = (f32[512,128]{1,0:T(8,128)S(1)}, f32[32,128]{1,0:T(8,128)S(1)}, f32[8,128]{1,0:T(8,128)S(1)}) custom-call(f32[4,512,128]{2,1,0:T(8,128)S(1)} %get-tuple-element.239.refs_0_.refs_9_.refs_8_, f32[4,512,128]{2,1,0:T(8,128)S(1)} %get-tuple-element.301.refs_1_, f32[4,512,128]{2,1,0:T(8,128)S(1)} %get-tuple-element.324.refs_2_, ...), custom_call_target="tpu_custom_call" | custom-call | flops 12000000000 | tf_op jit(solution)/shard_map/state_back/pallas_call | solution.py:81
  98.8 1.4 collective-permute-start.28
  100.2 1.8 norm_back.1
  102.1 1.4 collective-permute-start.36
  103.5 1.6 collective-permute-done.22.refs_2_
  106.6 1.7 block_out.1
  108.4 1.6 collective-permute-start.32
  111.0 1.9 %collective-permute-start.34 = (f32[32,1536]{1,0:T(8,128)S(1)}, f32[32,1536]{1,0:T(8,128)S(1)}, u32[]{:S(2)}, u32[]{:S(2)}) collective-permute-start(f32[32,1536]{1,0:T(8,128)S(1)} %get-tuple-element.397.refs_1_), channel_id=1, source_target_pairs={{0,2},{1,9},{2,0},{3,11},{4,6},{5,13},{6,4},{7,15},{8,10},{9,1},{1... | collective-permute-start | bytes 589832 | tf_op jit(solution)/shard_map/ppermute | solution.py:713
  112.9 1.2 collective-permute-start.35
  114.1 2.7 %collective-permute-done.27.refs_2_ = f32[64,1152]{1,0:T(8,128)S(1)} collective-permute-done((f32[64,1152]{1,0:T(8,128)S(1)}, f32[64,1152]{1,0:T(8,128)S(1)}, u32[]{:S(2)}, u32[]{:S(2)}) %collective-permute-start.27) | collective-permute-done | bytes 294944 | tf_op jit(solution)/shard_map/ppermute | solution.py:713
  116.8 1.4 collective-permute-start.33
  118.3 1.9 %collective-permute-start.31 = (f32[32,1152]{1,0:T(8,128)S(1)}, f32[32,1152]{1,0:T(8,128)S(1)}, u32[]{:S(2)}, u32[]{:S(2)}) collective-permute-start(f32[32,1152]{1,0:T(8,128)S(1)} %get-tuple-element.391), channel_id=1, source_target_pairs={{0,2},{1,3},{2,0},{3,1},{4,6},{5,7},{6,4},{7,5},{8,10},{9,11},{10,... | collective-permute-start | bytes 442376 | tf_op jit(solution)/shard_map/ppermute | solution.py:713
  120.5 1.2 collective-permute-start.41
  122.4 1.7 collective-permute-start.38
  124.2 1.9 %collective-permute-start.37 = (f32[56,1152]{1,0:T(8,128)S(1)}, f32[56,1152]{1,0:T(8,128)S(1)}, u32[]{:S(2)}, u32[]{:S(2)}) collective-permute-start(f32[56,1152]{1,0:T(8,128)S(1)} %get-tuple-element.405.refs_0_), channel_id=1, source_target_pairs={{0,4},{1,5},{2,6},{3,7},{4,0},{5,1},{6,2},{7,3},{8,12},{9,13},{10,... | collective-permute-start | bytes 774152 | tf_op jit(solution)/shard_map/ppermute | solution.py:713
  126.1 1.9 %ffn_out_out.1 = (f32[1024,512]{1,0:T(8,128)}, f32[8,128]{1,0:T(8,128)S(1)}) custom-call(s32[5]{0:T(128)S(1)} %pad_add_fusion.refs_0_, f32[512,512]{1,0:T(8,128)S(1)} %get-tuple-element.407.refs_1_, f32[512,512]{1,0:T(8,128)S(1)} %collective-permute-done.39.refs_2_, f32[8,128]{1,0:T(8,128)S(1)} %get-tuple-element.408.refs_3_), custom_call_target="tpu_custom_call" | custom-call | flops 2000000000 | tf_op jit(solution)/shard_map/ffn_out_out/pallas_call | solution.py:81
  128.0 3.2 %collective-permute-done.38.refs_2_ = f32[32,1024]{1,0:T(8,128)S(1)} collective-permute-done((f32[32,1024]{1,0:T(8,128)S(1)}, f32[32,1024]{1,0:T(8,128)S(1)}, u32[]{:S(2)}, u32[]{:S(2)}) %collective-permute-start.38) | collective-permute-done | bytes 131104 | tf_op jit(solution)/shard_map/ppermute | solution.py:713
  132.3 8.0 %collective-permute-done.40.refs_2_ = f32[64,1024]{1,0:T(8,128)S(1)} collective-permute-done((f32[64,1024]{1,0:T(8,128)S(1)}, f32[64,1024]{1,0:T(8,128)S(1)}, u32[]{:S(2)}, u32[]{:S(2)}) %collective-permute-start.40) | collective-permute-done | bytes 262176 | tf_op jit(solution)/shard_map/ppermute | solution.py:713
  140.4 1.1 collective-permute-start.46
  142.7 15.7 %collective-permute-done.43.refs_2_ = f32[56,1152]{1,0:T(8,128)S(1)} collective-permute-done((f32[56,1152]{1,0:T(8,128)S(1)}, f32[56,1152]{1,0:T(8,128)S(1)}, u32[]{:S(2)}, u32[]{:S(2)}) %collective-permute-start.43) | collective-permute-done | bytes 258080 | tf_op jit(solution)/shard_map/ppermute | solution.py:713
  158.5 2.0 %collective-permute-start.44 = (f32[88,1152]{1,0:T(8,128)S(1)}, f32[88,1152]{1,0:T(8,128)S(1)}, u32[]{:S(2)}, u32[]{:S(2)}) collective-permute-start(f32[88,1152]{1,0:T(8,128)S(1)} %get-tuple-element.419.refs_1_), channel_id=1, source_target_pairs={{0,16},{1,9},{2,18},{3,11},{4,20},{5,13},{6,22},{7,15},{8,24},{9,1... | collective-permute-start | bytes 1216520 | tf_op jit(solution)/shard_map/ppermute | solution.py:713
  161.5 1.9 %collective-permute-done.47.refs_2_ = f32[256,1024]{1,0:T(8,128)S(1)} collective-permute-done((f32[256,1024]{1,0:T(8,128)S(1)}, f32[256,1024]{1,0:T(8,128)S(1)}, u32[]{:S(2)}, u32[]{:S(2)}) %collective-permute-start.47) | collective-permute-done | bytes 1048608 | tf_op jit(solution)/shard_map/ppermute | solution.py:685
  163.4 1.9 %reset_out.1 = (f32[512,2176]{1,0:T(8,128)}, f32[8,128]{1,0:T(8,128)S(1)}) custom-call(s32[5]{0:T(128)S(1)} %pad_add_fusion.refs_0_, f32[256,1024]{1,0:T(8,128)S(1)} %get-tuple-element.423.refs_1_, f32[256,1024]{1,0:T(8,128)S(1)} %collective-permute-done.47.refs_2_, f32[8,128]{1,0:T(8,128)S(1)} %get-tuple-element.426.refs_3_), custom_call_target="tpu_custom_call" | custom-call | flops 12000000000 | tf_op jit(solution)/shard_map/reset_out/pallas_call | solution.py:81
  166.6 1.3 collective-permute-start.49
  167.9 2.2 %ffn_in_out.1 = (f32[512,1024]{1,0:T(8,128)}, f32[512,2176]{1,0:T(8,128)}, f32[8,128]{1,0:T(8,128)S(1)}) custom-call(s32[5]{0:T(128)S(1)} %pad_add_fusion.refs_0_, f32[256,1536]{1,0:T(8,128)S(1)} %get-tuple-element.430.refs_1_, f32[256,1536]{1,0:T(8,128)S(1)} %collective-permute-done.50.refs_2_, ...), custom_call_target="tpu_custom_call", output_to_operand_aliasing={{1}: (3, {})} | custom-call | flops 12000000000 | tf_op jit(solution)/shard_map/ffn_in_out/pallas_call | solution.py:81
  170.1 7.6 %collective-permute-done.49.refs_2_ = f32[152,1152]{1,0:T(8,128)S(1)} collective-permute-done((f32[152,1152]{1,0:T(8,128)S(1)}, f32[152,1152]{1,0:T(8,128)S(1)}, u32[]{:S(2)}, u32[]{:S(2)}) %collective-permute-start.49) | collective-permute-done | bytes 700448 | tf_op jit(solution)/shard_map/ppermute | solution.py:713
  178.0 2.3 %out_out.1 = (f32[1024,512]{1,0:T(8,128)}, f32[512,2176]{1,0:T(8,128)}, f32[8,128]{1,0:T(8,128)S(1)}) custom-call(s32[5]{0:T(128)S(1)} %pad_add_fusion.refs_0_, f32[256,1536]{1,0:T(8,128)S(1)} %get-tuple-element.435.refs_1_, f32[256,1536]{1,0:T(8,128)S(1)} %collective-permute-done.52.refs_2_, ...), custom_call_target="tpu_custom_call", output_to_operand_aliasing={{1}: (3, {})} | custom-call | flops 6000000000 | tf_op jit(solution)/shard_map/out_out/pallas_call | solution.py:81
  181.0 2.7 %value_out.1 = (f32[512,1024]{1,0:T(8,128)}, f32[512,2176]{1,0:T(8,128)}, f32[16,512]{1,0:T(8,128)}, f32[16,512]{1,0:T(8,128)}, f32[16,512]{1,0:T(8,128)}, /*ind...) custom-call(s32[5]{0:T(128)S(1)} %pad_add_fusion.refs_0_, ...), custom_call_target="tpu_custom_call", output_to_operand_aliasing={{1}: (7, {})} | custom-call | flops 6000000000 | tf_op jit(solution)/shard_map/value_out/pallas_call | solution.py:81
  (168 shorter events, 29.3 us)
Async XLA Ops:
  3.2 3.3 %copy-start.12 = (s32[1,3]{1,0:T(1,128)S(1)}, s32[1,3]{1,0:T(1,128)}, u32[]{:S(2)}) copy-start(s32[1,3]{1,0:T(1,128)} %refs_0_.2) | copy-start | bytes 40
  6.0 1.4 collective-permute-start
  7.9 14.9 %collective-permute-start.3 = (f32[16,512]{1,0:T(8,128)S(1)}, f32[16,512]{1,0:T(8,128)S(1)}, u32[]{:S(2)}, u32[]{:S(2)}) collective-permute-start(f32[16,512]{1,0:T(8,128)S(1)} %get-tuple-element.238), channel_id=1, source_target_pairs={{0,6},{1,7},{8,14},{9,15},{16,22},{17,23},{24,30},{25,31}} | collective-permute-start | bytes 98312 | tf_op jit(solution)/shard_map/ppermute | solution.py:690
  14.8 8.0 %collective-permute-start.2 = (f32[16,512]{1,0:T(8,128)S(1)}, f32[16,512]{1,0:T(8,128)S(1)}, u32[]{:S(2)}, u32[]{:S(2)}) collective-permute-start(f32[16,512]{1,0:T(8,128)S(1)} %get-tuple-element.238), channel_id=1, source_target_pairs={{0,4},{1,5},{2,6},{3,7},{8,12},{9,13},{10,14},{11,15},{16,20},{17,... | collective-permute-start | bytes 98312 | tf_op jit(solution)/shard_map/ppermute | solution.py:690
  16.1 6.7 %collective-permute-start.1 = (f32[16,512]{1,0:T(8,128)S(1)}, f32[16,512]{1,0:T(8,128)S(1)}, u32[]{:S(2)}, u32[]{:S(2)}) collective-permute-start(f32[16,512]{1,0:T(8,128)S(1)} %get-tuple-element.238), channel_id=1, source_target_pairs={{0,2},{1,3},{2,4},{3,5},{4,6},{5,7},{8,10},{9,11},{10,12},{11,13},... | collective-permute-start | bytes 98312 | tf_op jit(solution)/shard_map/ppermute | solution.py:690
  18.6 3.1 %copy-start.1 = (bf16[512,1024]{1,0:T(8,128)(2,1)S(1)}, bf16[512,1024]{1,0:T(8,128)(2,1)}, u32[]{:S(2)}) copy-start(bf16[512,1024]{1,0:T(8,128)(2,1)} %refs_6_.1) | copy-start | bytes 3145732
  22.8 2.7 %copy-start = (bf16[512,2176]{1,0:T(8,128)(2,1)S(1)}, bf16[512,2176]{1,0:T(8,128)(2,1)}, u32[]{:S(2)}) copy-start(bf16[512,2176]{1,0:T(8,128)(2,1)} %refs_5_.3) | copy-start | bytes 6684676
  22.8 2.7 %copy-start.19 = (f32[2,128]{1,0:T(2,128)S(1)}, f32[2,128]{1,0:T(2,128)}, u32[]{:S(2)}) copy-start(f32[2,128]{1,0:T(2,128)} %refs_3_.1) | copy-start | bytes 3076
  22.8 2.7 %copy-start.20 = (f32[2,128]{1,0:T(2,128)S(1)}, f32[2,128]{1,0:T(2,128)}, u32[]{:S(2)}) copy-start(f32[2,128]{1,0:T(2,128)} %refs_8_.2) | copy-start | bytes 3076
  33.6 4.5 %collective-permute-start.4 = (f32[512,512]{1,0:T(8,128)S(1)}, f32[512,512]{1,0:T(8,128)S(1)}, u32[]{:S(2)}, u32[]{:S(2)}) collective-permute-start(f32[512,512]{1,0:T(8,128)S(1)} %get-tuple-element.275), channel_id=1, source_target_pairs={{0,1},{1,0},{2,3},{3,2},{4,5},{5,4},{6,7},{7,6},{8,9},{9,8},{10,11... | collective-permute-start | bytes 3145736 | tf_op jit(solution)/shard_map/ppermute | solution.py:685
  38.0 6.6 %collective-permute-start.5 = (f32[256,1536]{1,0:T(8,128)S(1)}, f32[256,1536]{1,0:T(8,128)S(1)}, u32[]{:S(2)}, u32[]{:S(2)}) collective-permute-start(f32[256,1536]{1,0:T(8,128)S(1)} %get-tuple-element.286), channel_id=1, source_target_pairs={{0,1},{1,0},{2,3},{3,2},{4,5},{5,4},{6,7},{7,6},{8,9},{9,8},{10,11... | collective-permute-start | bytes 4718600 | tf_op jit(solution)/shard_map/ppermute | solution.py:685
  38.3 11.1 %collective-permute-start.6 = (f32[256,512]{1,0:T(8,128)S(1)}, f32[256,512]{1,0:T(8,128)S(1)}, u32[]{:S(2)}, u32[]{:S(2)}) collective-permute-start(f32[256,512]{1,0:T(8,128)S(1)} %get-tuple-element.295), channel_id=1, source_target_pairs={{0,8},{1,17},{2,10},{3,19},{4,12},{5,21},{6,14},{7,23},{8,0},{9,25... | collective-permute-start | bytes 1572872 | tf_op jit(solution)/shard_map/ppermute | solution.py:713
  42.7 8.4 %collective-permute-start.8 = (f32[256,1536]{1,0:T(8,128)S(1)}, f32[256,1536]{1,0:T(8,128)S(1)}, u32[]{:S(2)}, u32[]{:S(2)}) collective-permute-start(f32[256,1536]{1,0:T(8,128)S(1)} %get-tuple-element.303), channel_id=1, source_target_pairs={{0,1},{1,0},{2,3},{3,2},{4,5},{5,4},{6,7},{7,6},{8,9},{9,8},{10,11... | collective-permute-start | bytes 4718600 | tf_op jit(solution)/shard_map/ppermute | solution.py:685
  44.4 19.8 %collective-permute-start.11 = (f32[256,1024]{1,0:T(8,128)S(1)}, f32[256,1024]{1,0:T(8,128)S(1)}, u32[]{:S(2)}, u32[]{:S(2)}) collective-permute-start(f32[256,1024]{1,0:T(8,128)S(1)} %get-tuple-element.312), channel_id=1, source_target_pairs={{0,1},{1,0},{2,3},{3,2},{4,5},{5,4},{6,7},{7,6},{8,9},{9,8},{10,11... | collective-permute-start | bytes 3145736 | tf_op jit(solution)/shard_map/ppermute | solution.py:685
  45.0 15.2 %collective-permute-start.13 = (f32[128,1536]{1,0:T(8,128)S(1)}, f32[128,1536]{1,0:T(8,128)S(1)}, u32[]{:S(2)}, u32[]{:S(2)}) collective-permute-start(f32[128,1536]{1,0:T(8,128)S(1)} %get-tuple-element.315), channel_id=1, source_target_pairs={{0,2},{1,17},{2,0},{3,19},{4,6},{5,21},{6,4},{7,23},{8,10},{9,25},... | collective-permute-start | bytes 2359304 | tf_op jit(solution)/shard_map/ppermute | solution.py:713
  49.5 9.3 %collective-permute-start.7 = (f32[128,512]{1,0:T(8,128)S(1)}, f32[128,512]{1,0:T(8,128)S(1)}, u32[]{:S(2)}, u32[]{:S(2)}) collective-permute-start(f32[128,512]{1,0:T(8,128)S(1)} %get-tuple-element.300), channel_id=1, source_target_pairs={{0,16},{1,9},{2,18},{3,11},{4,20},{5,13},{6,22},{7,15},{8,24},{9,1... | collective-permute-start | bytes 786440 | tf_op jit(solution)/shard_map/ppermute | solution.py:713
  54.0 1.5 collective-permute-start.9
  54.2 16.2 %collective-permute-start.17 = (f32[128,1536]{1,0:T(8,128)S(1)}, f32[128,1536]{1,0:T(8,128)S(1)}, u32[]{:S(2)}, u32[]{:S(2)}) collective-permute-start(f32[128,1536]{1,0:T(8,128)S(1)} %get-tuple-element.329), channel_id=1, source_target_pairs={{0,8},{1,3},{2,10},{3,1},{4,12},{5,7},{6,14},{7,5},{8,0},{9,11},{1... | collective-permute-start | bytes 2359304 | tf_op jit(solution)/shard_map/ppermute | solution.py:713
  56.1 6.2 %collective-permute-start.12 = (f32[16,512]{1,0:T(8,128)S(1)}, f32[16,512]{1,0:T(8,128)S(1)}, u32[]{:S(2)}, u32[]{:S(2)}) collective-permute-start(f32[16,512]{1,0:T(8,128)S(1)} %get-tuple-element.313.refs_1_), channel_id=1, source_target_pairs={{2,0},{3,1},{4,2},{5,3},{6,4},{7,5},{10,8},{11,9},{12,10},{13,11},... | collective-permute-start | bytes 98312 | tf_op jit(solution)/shard_map/ppermute | solution.py:695
  58.9 6.5 %collective-permute-start.10 = (f32[64,512]{1,0:T(8,128)S(1)}, f32[64,512]{1,0:T(8,128)S(1)}, u32[]{:S(2)}, u32[]{:S(2)}) collective-permute-start(f32[64,512]{1,0:T(8,128)S(1)} %get-tuple-element.310), channel_id=1, source_target_pairs={{0,2},{1,3},{2,0},{3,1},{4,6},{5,7},{6,4},{7,5},{8,10},{9,11},{10,... | collective-permute-start | bytes 393224 | tf_op jit(solution)/shard_map/ppermute | solution.py:713
  60.3 22.6 %collective-permute-start.21 = (f32[64,1536]{1,0:T(8,128)S(1)}, f32[64,1536]{1,0:T(8,128)S(1)}, u32[]{:S(2)}, u32[]{:S(2)}) collective-permute-start(f32[64,1536]{1,0:T(8,128)S(1)} %get-tuple-element.342), channel_id=1, source_target_pairs={{0,8},{1,9},{2,10},{3,11},{4,12},{5,13},{6,14},{7,15},{8,0},{9,1},... | collective-permute-start | bytes 1179656 | tf_op jit(solution)/shard_map/ppermute | solution.py:713
  62.9 13.0 %collective-permute-start.16 = (f32[16,512]{1,0:T(8,128)S(1)}, f32[16,512]{1,0:T(8,128)S(1)}, u32[]{:S(2)}, u32[]{:S(2)}) collective-permute-start(f32[16,512]{1,0:T(8,128)S(1)} %get-tuple-element.326), channel_id=1, source_target_pairs={{4,0},{5,1},{6,2},{7,3},{12,8},{13,9},{14,10},{15,11},{20,16},{21,... | collective-permute-start | bytes 98312 | tf_op jit(solution)/shard_map/ppermute | solution.py:695
  64.4 19.8 %collective-permute-start.20 = (f32[128,1024]{1,0:T(8,128)S(1)}, f32[128,1024]{1,0:T(8,128)S(1)}, u32[]{:S(2)}, u32[]{:S(2)}) collective-permute-start(f32[128,1024]{1,0:T(8,128)S(1)} %get-tuple-element.340), channel_id=1, source_target_pairs={{0,8},{1,17},{2,10},{3,19},{4,12},{5,21},{6,14},{7,23},{8,0},{9,25... | collective-permute-start | bytes 1572872 | tf_op jit(solution)/shard_map/ppermute | solution.py:713
  65.4 17.3 %collective-permute-start.15 = (f32[64,512]{1,0:T(8,128)S(1)}, f32[64,512]{1,0:T(8,128)S(1)}, u32[]{:S(2)}, u32[]{:S(2)}) collective-permute-start(f32[64,512]{1,0:T(8,128)S(1)} %get-tuple-element.323.refs_0_), channel_id=1, source_target_pairs={{0,4},{1,5},{2,6},{3,7},{4,0},{5,1},{6,2},{7,3},{8,12},{9,13},{10,... | collective-permute-start | bytes 393224 | tf_op jit(solution)/shard_map/ppermute | solution.py:713
  70.4 20.2 %collective-permute-start.14 = (f32[256,1152]{1,0:T(8,128)S(1)}, f32[256,1152]{1,0:T(8,128)S(1)}, u32[]{:S(2)}, u32[]{:S(2)}) collective-permute-start(f32[256,1152]{1,0:T(8,128)S(1)} %get-tuple-element.322), channel_id=1, source_target_pairs={{0,1},{1,0},{2,3},{3,2},{4,5},{5,4},{6,7},{7,6},{8,9},{9,8},{10,11... | collective-permute-start | bytes 3538952 | tf_op jit(solution)/shard_map/ppermute | solution.py:685
  75.9 11.1 %collective-permute-start.19 = (f32[64,1536]{1,0:T(8,128)S(1)}, f32[64,1536]{1,0:T(8,128)S(1)}, u32[]{:S(2)}, u32[]{:S(2)}) collective-permute-start(f32[64,1536]{1,0:T(8,128)S(1)} %get-tuple-element.338), channel_id=1, source_target_pairs={{0,16},{1,17},{2,18},{3,19},{4,20},{5,21},{6,22},{7,23},{8,24},{9,... | collective-permute-start | bytes 1179656 | tf_op jit(solution)/shard_map/ppermute | solution.py:713
  82.8 6.5 %collective-permute-start.18 = (f32[64,512]{1,0:T(8,128)S(1)}, f32[64,512]{1,0:T(8,128)S(1)}, u32[]{:S(2)}, u32[]{:S(2)}) collective-permute-start(f32[64,512]{1,0:T(8,128)S(1)} %get-tuple-element.336.refs_1_), channel_id=1, source_target_pairs={{0,2},{1,3},{2,0},{3,1},{4,6},{5,7},{6,4},{7,5},{8,10},{9,11},{10,... | collective-permute-start | bytes 393224 | tf_op jit(solution)/shard_map/ppermute | solution.py:713
  83.0 7.9 %collective-permute-start.24 = (f32[32,1536]{1,0:T(8,128)S(1)}, f32[32,1536]{1,0:T(8,128)S(1)}, u32[]{:S(2)}, u32[]{:S(2)}) collective-permute-start(f32[32,1536]{1,0:T(8,128)S(1)} %get-tuple-element.354), channel_id=1, source_target_pairs={{0,16},{1,3},{2,18},{3,1},{4,20},{5,7},{6,22},{7,5},{8,24},{9,11},... | collective-permute-start | bytes 589832 | tf_op jit(solution)/shard_map/ppermute | solution.py:713
  84.3 10.6 %collective-permute-start.26 = (f32[64,1024]{1,0:T(8,128)S(1)}, f32[64,1024]{1,0:T(8,128)S(1)}, u32[]{:S(2)}, u32[]{:S(2)}) collective-permute-start(f32[64,1024]{1,0:T(8,128)S(1)} %get-tuple-element.361), channel_id=1, source_target_pairs={{0,16},{1,9},{2,18},{3,11},{4,20},{5,13},{6,22},{7,15},{8,24},{9,1... | collective-permute-start | bytes 786440 | tf_op jit(solution)/shard_map/ppermute | solution.py:713
  87.1 9.0 %collective-permute-start.25 = (f32[32,1536]{1,0:T(8,128)S(1)}, f32[32,1536]{1,0:T(8,128)S(1)}, u32[]{:S(2)}, u32[]{:S(2)}) collective-permute-start(f32[32,1536]{1,0:T(8,128)S(1)} %get-tuple-element.359), channel_id=1, source_target_pairs={{0,2},{1,9},{2,0},{3,11},{4,6},{5,13},{6,4},{7,15},{8,10},{9,1},{1... | collective-permute-start | bytes 589832 | tf_op jit(solution)/shard_map/ppermute | solution.py:713
  89.3 12.7 %collective-permute-start.23 = (f32[128,512]{1,0:T(8,128)S(1)}, f32[128,512]{1,0:T(8,128)S(1)}, u32[]{:S(2)}, u32[]{:S(2)}) collective-permute-start(f32[128,512]{1,0:T(8,128)S(1)} %get-tuple-element.350.refs_1_), channel_id=1, source_target_pairs={{0,16},{1,9},{2,18},{3,11},{4,20},{5,13},{6,22},{7,15},{8,24},{9,1... | collective-permute-start | bytes 786440 | tf_op jit(solution)/shard_map/ppermute | solution.py:713
  90.9 17.4 %collective-permute-start.30 = (f32[32,1536]{1,0:T(8,128)S(1)}, f32[32,1536]{1,0:T(8,128)S(1)}, u32[]{:S(2)}, u32[]{:S(2)}) collective-permute-start(f32[32,1536]{1,0:T(8,128)S(1)} %get-tuple-element.385.refs_0_), channel_id=1, source_target_pairs={{0,4},{1,5},{2,6},{3,7},{4,0},{5,1},{6,2},{7,3},{8,12},{9,13},{10,... | collective-permute-start | bytes 589832 | tf_op jit(solution)/shard_map/ppermute | solution.py:713
  95.0 13.3 %collective-permute-start.29 = (f32[32,1024]{1,0:T(8,128)S(1)}, f32[32,1024]{1,0:T(8,128)S(1)}, u32[]{:S(2)}, u32[]{:S(2)}) collective-permute-start(f32[32,1024]{1,0:T(8,128)S(1)} %get-tuple-element.384), channel_id=1, source_target_pairs={{0,2},{1,3},{2,0},{3,1},{4,6},{5,7},{6,4},{7,5},{8,10},{9,11},{10,... | collective-permute-start | bytes 393224 | tf_op jit(solution)/shard_map/ppermute | solution.py:713
  95.1 9.9 %collective-permute-start.22 = (f32[128,1152]{1,0:T(8,128)S(1)}, f32[128,1152]{1,0:T(8,128)S(1)}, u32[]{:S(2)}, u32[]{:S(2)}) collective-permute-start(f32[128,1152]{1,0:T(8,128)S(1)} %get-tuple-element.349), channel_id=1, source_target_pairs={{0,8},{1,17},{2,10},{3,19},{4,12},{5,21},{6,14},{7,23},{8,0},{9,25... | collective-permute-start | bytes 1769480 | tf_op jit(solution)/shard_map/ppermute | solution.py:713
  96.1 4.1 %copy-start.4 = (bf16[512,512]{1,0:T(8,128)(2,1)S(1)}, bf16[512,512]{1,0:T(8,128)(2,1)}, u32[]{:S(2)}) copy-start(bf16[512,512]{1,0:T(8,128)(2,1)} %refs_8_.3) | copy-start | bytes 1572868
  96.1 4.1 %copy-start.9 = (f32[512]{0:T(512)S(1)}, f32[512]{0:T(512)}, u32[]{:S(2)}) copy-start(f32[512]{0:T(512)} %param.21) | copy-start | bytes 6148
  98.8 12.2 %collective-permute-start.28 = (f32[32,1536]{1,0:T(8,128)S(1)}, f32[32,1536]{1,0:T(8,128)S(1)}, u32[]{:S(2)}, u32[]{:S(2)}) collective-permute-start(f32[32,1536]{1,0:T(8,128)S(1)} %get-tuple-element.382.refs_0_), channel_id=1, source_target_pairs={{0,4},{1,5},{2,6},{3,7},{4,0},{5,1},{6,2},{7,3},{8,12},{9,13},{10,... | collective-permute-start | bytes 589832 | tf_op jit(solution)/shard_map/ppermute | solution.py:713
  102.1 18.1 %collective-permute-start.36 = (f32[256,512]{1,0:T(8,128)S(1)}, f32[256,512]{1,0:T(8,128)S(1)}, u32[]{:S(2)}, u32[]{:S(2)}) collective-permute-start(f32[256,512]{1,0:T(8,128)S(1)} %get-tuple-element.399.refs_1_), channel_id=1, source_target_pairs={{0,8},{1,17},{2,10},{3,19},{4,12},{5,21},{6,14},{7,23},{8,0},{9,25... | collective-permute-start | bytes 1572872 | tf_op jit(solution)/shard_map/ppermute | solution.py:713
  108.4 8.4 %collective-permute-start.32 = (f32[16,1024]{1,0:T(8,128)S(1)}, f32[16,1024]{1,0:T(8,128)S(1)}, u32[]{:S(2)}, u32[]{:S(2)}) collective-permute-start(f32[16,1024]{1,0:T(8,128)S(1)} %get-tuple-element.394), channel_id=1, source_target_pairs={{0,4},{1,5},{2,6},{3,7},{4,0},{5,1},{6,2},{7,3},{8,12},{9,13},{10,... | collective-permute-start | bytes 196616 | tf_op jit(solution)/shard_map/ppermute | solution.py:713
  110.0 6.7 %collective-permute-start.27 = (f32[64,1152]{1,0:T(8,128)S(1)}, f32[64,1152]{1,0:T(8,128)S(1)}, u32[]{:S(2)}, u32[]{:S(2)}) collective-permute-start(f32[64,1152]{1,0:T(8,128)S(1)} %get-tuple-element.381), channel_id=1, source_target_pairs={{0,16},{1,9},{2,18},{3,11},{4,20},{5,13},{6,22},{7,15},{8,24},{9,1... | collective-permute-start | bytes 884744 | tf_op jit(solution)/shard_map/ppermute | solution.py:713
  111.0 9.5 %collective-permute-start.34 = (f32[32,1536]{1,0:T(8,128)S(1)}, f32[32,1536]{1,0:T(8,128)S(1)}, u32[]{:S(2)}, u32[]{:S(2)}) collective-permute-start(f32[32,1536]{1,0:T(8,128)S(1)} %get-tuple-element.397.refs_1_), channel_id=1, source_target_pairs={{0,2},{1,9},{2,0},{3,11},{4,6},{5,13},{6,4},{7,15},{8,10},{9,1},{1... | collective-permute-start | bytes 589832 | tf_op jit(solution)/shard_map/ppermute | solution.py:713
  112.9 7.5 %collective-permute-start.35 = (f32[32,1536]{1,0:T(8,128)S(1)}, f32[32,1536]{1,0:T(8,128)S(1)}, u32[]{:S(2)}, u32[]{:S(2)}) collective-permute-start(f32[32,1536]{1,0:T(8,128)S(1)} %get-tuple-element.398.refs_1_), channel_id=1, source_target_pairs={{0,16},{1,3},{2,18},{3,1},{4,20},{5,7},{6,22},{7,5},{8,24},{9,11},... | collective-permute-start | bytes 589832 | tf_op jit(solution)/shard_map/ppermute | solution.py:713
  116.8 5.5 %collective-permute-start.33 = (f32[16,1024]{1,0:T(8,128)S(1)}, f32[16,1024]{1,0:T(8,128)S(1)}, u32[]{:S(2)}, u32[]{:S(2)}) collective-permute-start(f32[16,1024]{1,0:T(8,128)S(1)} %get-tuple-element.396.refs_1_), channel_id=1, source_target_pairs={{0,4},{1,5},{2,6},{3,7},{4,0},{5,1},{6,2},{7,3},{8,12},{9,13},{10,... | collective-permute-start | bytes 196616 | tf_op jit(solution)/shard_map/ppermute | solution.py:713
  118.3 5.9 %collective-permute-start.31 = (f32[32,1152]{1,0:T(8,128)S(1)}, f32[32,1152]{1,0:T(8,128)S(1)}, u32[]{:S(2)}, u32[]{:S(2)}) collective-permute-start(f32[32,1152]{1,0:T(8,128)S(1)} %get-tuple-element.391), channel_id=1, source_target_pairs={{0,2},{1,3},{2,0},{3,1},{4,6},{5,7},{6,4},{7,5},{8,10},{9,11},{10,... | collective-permute-start | bytes 442376 | tf_op jit(solution)/shard_map/ppermute | solution.py:713
  120.5 11.6 %collective-permute-start.41 = (f32[64,1536]{1,0:T(8,128)S(1)}, f32[64,1536]{1,0:T(8,128)S(1)}, u32[]{:S(2)}, u32[]{:S(2)}) collective-permute-start(f32[64,1536]{1,0:T(8,128)S(1)} %get-tuple-element.411.refs_1_), channel_id=1, source_target_pairs={{0,16},{1,17},{2,18},{3,19},{4,20},{5,21},{6,22},{7,23},{8,24},{9,... | collective-permute-start | bytes 1179656 | tf_op jit(solution)/shard_map/ppermute | solution.py:713
  121.7 9.9 %collective-permute-start.42 = (f32[64,1536]{1,0:T(8,128)S(1)}, f32[64,1536]{1,0:T(8,128)S(1)}, u32[]{:S(2)}, u32[]{:S(2)}) collective-permute-start(f32[64,1536]{1,0:T(8,128)S(1)} %get-tuple-element.412.refs_1_), channel_id=1, source_target_pairs={{0,8},{1,9},{2,10},{3,11},{4,12},{5,13},{6,14},{7,15},{8,0},{9,1},... | collective-permute-start | bytes 1179656 | tf_op jit(solution)/shard_map/ppermute | solution.py:713
  122.4 3.7 %collective-permute-start.39 = (f32[512,512]{1,0:T(8,128)S(1)}, f32[512,512]{1,0:T(8,128)S(1)}, u32[]{:S(2)}, u32[]{:S(2)}) collective-permute-start(f32[512,512]{1,0:T(8,128)S(1)} %get-tuple-element.407.refs_1_), channel_id=1, source_target_pairs={{0,1},{1,0},{2,3},{3,2},{4,5},{5,4},{6,7},{7,6},{8,9},{9,8},{10,11... | collective-permute-start | bytes 3145736 | tf_op jit(solution)/shard_map/ppermute | solution.py:685
  122.4 8.7 %collective-permute-start.38 = (f32[32,1024]{1,0:T(8,128)S(1)}, f32[32,1024]{1,0:T(8,128)S(1)}, u32[]{:S(2)}, u32[]{:S(2)}) collective-permute-start(f32[32,1024]{1,0:T(8,128)S(1)} %get-tuple-element.406.refs_1_), channel_id=1, source_target_pairs={{0,2},{1,3},{2,0},{3,1},{4,6},{5,7},{6,4},{7,5},{8,10},{9,11},{10,... | collective-permute-start | bytes 393224 | tf_op jit(solution)/shard_map/ppermute | solution.py:713
  124.2 17.4 %collective-permute-start.37 = (f32[56,1152]{1,0:T(8,128)S(1)}, f32[56,1152]{1,0:T(8,128)S(1)}, u32[]{:S(2)}, u32[]{:S(2)}) collective-permute-start(f32[56,1152]{1,0:T(8,128)S(1)} %get-tuple-element.405.refs_0_), channel_id=1, source_target_pairs={{0,4},{1,5},{2,6},{3,7},{4,0},{5,1},{6,2},{7,3},{8,12},{9,13},{10,... | collective-permute-start | bytes 774152 | tf_op jit(solution)/shard_map/ppermute | solution.py:713
  131.2 9.1 %collective-permute-start.40 = (f32[64,1024]{1,0:T(8,128)S(1)}, f32[64,1024]{1,0:T(8,128)S(1)}, u32[]{:S(2)}, u32[]{:S(2)}) collective-permute-start(f32[64,1024]{1,0:T(8,128)S(1)} %get-tuple-element.410.refs_1_), channel_id=1, source_target_pairs={{0,16},{1,9},{2,18},{3,11},{4,20},{5,13},{6,22},{7,15},{8,24},{9,1... | collective-permute-start | bytes 786440 | tf_op jit(solution)/shard_map/ppermute | solution.py:713
  131.7 29.0 %collective-permute-start.48 = (f32[128,1536]{1,0:T(8,128)S(1)}, f32[128,1536]{1,0:T(8,128)S(1)}, u32[]{:S(2)}, u32[]{:S(2)}) collective-permute-start(f32[128,1536]{1,0:T(8,128)S(1)} %get-tuple-element.424.refs_1_), channel_id=1, source_target_pairs={{0,2},{1,17},{2,0},{3,19},{4,6},{5,21},{6,4},{7,23},{8,10},{9,25},... | collective-permute-start | bytes 2359304 | tf_op jit(solution)/shard_map/ppermute | solution.py:713
  140.4 20.1 %collective-permute-start.46 = (f32[128,1024]{1,0:T(8,128)S(1)}, f32[128,1024]{1,0:T(8,128)S(1)}, u32[]{:S(2)}, u32[]{:S(2)}) collective-permute-start(f32[128,1024]{1,0:T(8,128)S(1)} %get-tuple-element.421.refs_1_), channel_id=1, source_target_pairs={{0,8},{1,17},{2,10},{3,19},{4,12},{5,21},{6,14},{7,23},{8,0},{9,25... | collective-permute-start | bytes 1572872 | tf_op jit(solution)/shard_map/ppermute | solution.py:713
  141.6 16.8 %collective-permute-start.43 = (f32[56,1152]{1,0:T(8,128)S(1)}, f32[56,1152]{1,0:T(8,128)S(1)}, u32[]{:S(2)}, u32[]{:S(2)}) collective-permute-start(f32[56,1152]{1,0:T(8,128)S(1)} %get-tuple-element.417.refs_1_), channel_id=1, source_target_pairs={{0,2},{1,3},{2,0},{3,1},{4,6},{5,7},{6,4},{7,5},{8,10},{9,11},{10,... | collective-permute-start | bytes 774152 | tf_op jit(solution)/shard_map/ppermute | solution.py:713
  141.7 23.6 %collective-permute-start.45 = (f32[128,1536]{1,0:T(8,128)S(1)}, f32[128,1536]{1,0:T(8,128)S(1)}, u32[]{:S(2)}, u32[]{:S(2)}) collective-permute-start(f32[128,1536]{1,0:T(8,128)S(1)} %get-tuple-element.420.refs_1_), channel_id=1, source_target_pairs={{0,8},{1,3},{2,10},{3,1},{4,12},{5,7},{6,14},{7,5},{8,0},{9,11},{1... | collective-permute-start | bytes 2359304 | tf_op jit(solution)/shard_map/ppermute | solution.py:713
  158.5 8.0 %collective-permute-start.44 = (f32[88,1152]{1,0:T(8,128)S(1)}, f32[88,1152]{1,0:T(8,128)S(1)}, u32[]{:S(2)}, u32[]{:S(2)}) collective-permute-start(f32[88,1152]{1,0:T(8,128)S(1)} %get-tuple-element.419.refs_1_), channel_id=1, source_target_pairs={{0,16},{1,9},{2,18},{3,11},{4,20},{5,13},{6,22},{7,15},{8,24},{9,1... | collective-permute-start | bytes 1216520 | tf_op jit(solution)/shard_map/ppermute | solution.py:713
  160.6 2.7 %collective-permute-start.47 = (f32[256,1024]{1,0:T(8,128)S(1)}, f32[256,1024]{1,0:T(8,128)S(1)}, u32[]{:S(2)}, u32[]{:S(2)}) collective-permute-start(f32[256,1024]{1,0:T(8,128)S(1)} %get-tuple-element.423.refs_1_), channel_id=1, source_target_pairs={{0,1},{1,0},{2,3},{3,2},{4,5},{5,4},{6,7},{7,6},{8,9},{9,8},{10,11... | collective-permute-start | bytes 3145736 | tf_op jit(solution)/shard_map/ppermute | solution.py:685
  161.0 6.9 %collective-permute-start.50 = (f32[256,1536]{1,0:T(8,128)S(1)}, f32[256,1536]{1,0:T(8,128)S(1)}, u32[]{:S(2)}, u32[]{:S(2)}) collective-permute-start(f32[256,1536]{1,0:T(8,128)S(1)} %get-tuple-element.430.refs_1_), channel_id=1, source_target_pairs={{0,1},{1,0},{2,3},{3,2},{4,5},{5,4},{6,7},{7,6},{8,9},{9,8},{10,11... | collective-permute-start | bytes 4718600 | tf_op jit(solution)/shard_map/ppermute | solution.py:685
  166.6 11.1 %collective-permute-start.49 = (f32[152,1152]{1,0:T(8,128)S(1)}, f32[152,1152]{1,0:T(8,128)S(1)}, u32[]{:S(2)}, u32[]{:S(2)}) collective-permute-start(f32[152,1152]{1,0:T(8,128)S(1)} %get-tuple-element.429.refs_1_), channel_id=1, source_target_pairs={{0,8},{1,17},{2,10},{3,19},{4,12},{5,21},{6,14},{7,23},{8,0},{9,25... | collective-permute-start | bytes 2101256 | tf_op jit(solution)/shard_map/ppermute | solution.py:713
  167.9 10.1 %collective-permute-start.52 = (f32[256,1536]{1,0:T(8,128)S(1)}, f32[256,1536]{1,0:T(8,128)S(1)}, u32[]{:S(2)}, u32[]{:S(2)}) collective-permute-start(f32[256,1536]{1,0:T(8,128)S(1)} %get-tuple-element.435.refs_1_), channel_id=1, source_target_pairs={{0,1},{1,0},{2,3},{3,2},{4,5},{5,4},{6,7},{7,6},{8,9},{9,8},{10,11... | collective-permute-start | bytes 4718600 | tf_op jit(solution)/shard_map/ppermute | solution.py:685
  177.9 3.1 %collective-permute-start.51 = (f32[280,1152]{1,0:T(8,128)S(1)}, f32[280,1152]{1,0:T(8,128)S(1)}, u32[]{:S(2)}, u32[]{:S(2)}) collective-permute-start(f32[280,1152]{1,0:T(8,128)S(1)} %get-tuple-element.434.refs_1_), channel_id=1, source_target_pairs={{0,1},{1,0},{2,3},{3,2},{4,5},{5,4},{6,7},{7,6},{8,9},{9,8},{10,11... | collective-permute-start | bytes 3870728 | tf_op jit(solution)/shard_map/ppermute | solution.py:685
  177.9 3.0 %copy-start.5 = (f32[512,16]{0,1:T(8,128)S(1)}, f32[512,16]{0,1:T(8,128)}, u32[]{:S(2)}) copy-start(f32[512,16]{0,1:T(8,128)} %param.24) | copy-start | bytes 98308
  178.0 3.0 %copy-start.6 = (f32[512,16]{0,1:T(8,128)S(1)}, f32[512,16]{0,1:T(8,128)}, u32[]{:S(2)}) copy-start(f32[512,16]{0,1:T(8,128)} %param.23) | copy-start | bytes 98308
  178.0 3.0 %copy-start.7 = (f32[512,16]{0,1:T(8,128)S(1)}, f32[512,16]{0,1:T(8,128)}, u32[]{:S(2)}) copy-start(f32[512,16]{0,1:T(8,128)} %param.26) | copy-start | bytes 98308
  178.0 3.0 %copy-start.8 = (f32[512,16]{0,1:T(8,128)S(1)}, f32[512,16]{0,1:T(8,128)}, u32[]{:S(2)}) copy-start(f32[512,16]{0,1:T(8,128)} %param.25) | copy-start | bytes 98308
  (13 other events, 18.5 us)

commit v4 on v3

--- a/solution.py
+++ b/solution.py
@@ -174,7 +174,7 @@
     return reach
 
 
-def start_body(lengths, tok, gain, logk, keep, normed, low, enter, end):
+def start_body(lengths, tok, gain, logk, keep, normed, low, enter, end, strips):
     meta = Place(lengths)
     tokens, width = tok.shape
     hidden = end.shape[0]
@@ -194,6 +194,7 @@
 
         def step(t, state):
             value = normed[tile, pl.ds(t, chunks, stride=CHUNK), :]
+            strips[tile, t] = value
             return tuple(k * u + value for k, u in zip(keeps, state))
 
         zero = jnp.zeros((chunks, 128), F32)
@@ -221,19 +222,17 @@
     return parts[0]
 
 
-def local_body(normed, enter, keep, mix, smooth):
-    chunks = enter.shape[1]
+def local_body(strips, enter, keep, mix, smooth):
     hidden = keep.shape[0]
-    for tile in range(normed.shape[0]):
+    for tile in range(strips.shape[0]):
         lanes = lanes_of(tile)
         keeps = [keep[h : h + 1, lanes] for h in range(hidden)]
         mixes = [mix[h : h + 1, lanes] for h in range(hidden)]
 
         def step(t, state):
-            place = (tile, pl.ds(t, chunks, stride=CHUNK), slice(None))
-            value = normed[place]
+            value = strips[tile, t]
             state = tuple(k * u + value for k, u in zip(keeps, state))
-            smooth[place] = add_up([c * u for c, u in zip(mixes, state)])
+            smooth[tile, t] = add_up([c * u for c, u in zip(mixes, state)])
             return state
 
         lax.fori_loop(0, CHUNK, step, tuple(enter[h, :, lanes] for h in range(hidden)), unroll=8)
@@ -297,10 +296,10 @@
 
 def carried_body(chips, meta, other, *rest):
     arrived = rest[:chips]
-    logk, keep, mix, omega, normed, smooth, enter, low, slope, states, carry, extra = rest[chips:]
-    tiles, tokens, _ = normed.shape
+    logk, keep, mix, omega, strips, smooth, enter, low, slope, states, carry, rows = rest[chips:]
+    tiles, _, chunks, _ = strips.shape
+    tokens = chunks * CHUNK
     hidden = keep.shape[0]
-    chunks = tokens // CHUNK
     carry[...] = carry_of(False, tokens, meta, other, list(enumerate(arrived)), logk)
     free = chunk_masks(meta, meta[0] * tokens, chunks)
     reach = prefix_mask(free, chunks, False)
@@ -314,15 +313,16 @@
             states[h, :, lanes] = enter[h, :, lanes] + first
             state.append(mix[h : h + 1, lanes] * first)
         keeps = [keep[h : h + 1, lanes] for h in range(hidden)]
+        skip = omega[:, lanes]
 
         def step(t, state):
-            place = pl.ds(t, chunks, stride=CHUNK)
             state = tuple(k * u for k, u in zip(keeps, state))
-            extra[place, :] = add_up(list(state))
+            pre = smooth[tile, t] + skip * strips[tile, t] + add_up(list(state))
+            rows[pl.ds(t, chunks, stride=CHUNK), :] = pre
             return state
 
         lax.fori_loop(0, CHUNK, step, tuple(state), unroll=8)
-        pre = smooth[tile] + extra[...] + omega[:, lanes] * normed[tile]
+        pre = rows[...]
         gate = sigmoid(pre)
         smoothed = pre * gate
         low[:, lanes] = smoothed.astype(BF16)
@@ -553,7 +553,7 @@
     omega_grad[...] = jnp.sum(grad * tiled(normed), axis=0, keepdims=True)
 
 
-def rise_body(meta, smooth_grad, logk, keep, enter, end):
+def rise_body(meta, smooth_grad, logk, keep, enter, end, strips):
     tiles, tokens, _ = smooth_grad.shape
     hidden = keep.shape[0]
     chunks = tokens // CHUNK
@@ -566,6 +566,7 @@
 
         def step(t, state):
             value = smooth_grad[tile, pl.ds(CHUNK - 1 - t, chunks, stride=CHUNK), :]
+            strips[tile, CHUNK - 1 - t] = value
             return tuple(k * u + value for k, u in zip(keeps, state))
 
         zero = jnp.zeros((chunks, 128), F32)
@@ -593,53 +594,55 @@
             later[h, :, lanes] = enter[h, :, lanes] + carry[h : h + 1, tile * 128 : (tile + 1) * 128] * entry
 
 
-def state_back_body(tile, normed, smooth_grad, norm_grad, states, later, keep, mix, total, sums, history):
+def state_back_body(tile, strips, grads, states, later, keep, mix, part, sums, history):
     hidden = keep.shape[0]
     chunks = states.shape[1]
     lanes = lanes_of(tile)
     heads = range(hidden)
     keeps = [keep[h : h + 1, lanes] for h in heads]
     mixes = [mix[h : h + 1, lanes] for h in heads]
-
-    def rise(t, state):
-        value = normed[tile, pl.ds(t, chunks, stride=CHUNK), :]
+    zeros = (jnp.zeros((chunks, 128), F32),) * hidden
+
+    def rise(t, held):
+        state, reads = held
+        value = strips[tile, t]
+        grad = grads[tile, t]
         state = tuple(k * u + value for k, u in zip(keeps, state))
+        reads = tuple(r + u * grad for r, u in zip(reads, state))
         for i in heads:
             history[t, i] = state[i]
-        return state
-
-    lax.fori_loop(0, CHUNK, rise, tuple(states[h, :, lanes] for h in heads), unroll=4)
-
-    def fall(i, held):
-        state, reads, marks = held
-        t = CHUNK - 1 - i
-        place = pl.ds(t, chunks, stride=CHUNK)
-        value = smooth_grad[tile, place, :]
-        row = normed[tile, place, :]
-        state = tuple(k * w + value for k, w in zip(keeps, state))
-        reads = tuple(r + w * row for r, w in zip(reads, state))
-        marks = tuple(m + w * history[t, j] for j, (m, w) in enumerate(zip(marks, state)))
-        total[place, :] = norm_grad[tile, place, :] + add_up([c * w for c, w in zip(mixes, state)])
-        return state, reads, marks
-
-    zeros = (jnp.zeros((chunks, 128), F32),) * hidden
-    first = tuple(later[h, :, lanes] for h in heads)
-    _, reads, marks = lax.fori_loop(0, CHUNK, fall, (first, zeros, zeros), unroll=4)
+        return state, reads
+
+    first = tuple(states[h, :, lanes] for h in heads)
+    _, reads = lax.fori_loop(0, CHUNK, rise, (first, zeros), unroll=4)
     for h in heads:
         sums[h : h + 1, :] = jnp.sum(reads[h], axis=0, keepdims=True)
+
+    def fall(i, held):
+        state, marks = held
+        t = CHUNK - 1 - i
+        grad = grads[tile, t]
+        state = tuple(k * w + grad for k, w in zip(keeps, state))
+        marks = tuple(m + w * history[t, j] for j, (m, w) in enumerate(zip(marks, state)))
+        part[pl.ds(t, chunks, stride=CHUNK), :] = add_up([c * w for c, w in zip(mixes, state)])
+        return state, marks
+
+    first = tuple(later[h, :, lanes] for h in heads)
+    _, marks = lax.fori_loop(0, CHUNK, fall, (first, zeros), unroll=4)
+    for h in heads:
         sums[hidden + h : hidden + h + 1, :] = jnp.sum(marks[h], axis=0, keepdims=True)
 
 
 def close_body(count, *refs):
     totals = refs[:count]
     sums = refs[count : 2 * count]
-    tok, gain, input_part, omega_grad, gain2_grad, small, input_grad, packed = refs[2 * count :]
+    tok, gain, norm_grad, input_part, omega_grad, gain2_grad, small, input_grad, packed = refs[2 * count :]
     x = tok[...].astype(F32)
     width = x.shape[1]
     centered = x - jnp.mean(x, axis=1, keepdims=True)
     inverse = lax.rsqrt(jnp.mean(centered * centered, axis=1, keepdims=True) + EPS)
     normal = centered * inverse
-    upstream = jnp.concatenate([t[...] for t in totals], axis=1)
+    upstream = tiled(norm_grad) + jnp.concatenate([t[...] for t in totals], axis=1)
     input_grad[...] = input_part[...] + layer_grad(upstream * gain[...], normal, inverse)
     at = sums[0].shape[0] // 2
     packed[...] = jnp.zeros_like(packed)
@@ -656,8 +659,7 @@
     delta_grad, alpha_grad, beta_grad, eta_grad, gain1_grad, gain2_grad, omega_grad, qk_gain_grad, qk_bias_grad, rel_grad = outs
     hidden, width = delta_grad.shape
     scale = 1.0 / math.sqrt(hidden)
-    low = own.shape[0] - SMALL_ROWS
-    packed = own[low:, :] + other[low:, :]
+    packed = own[...] + other[...]
     read = packed[0:hidden, :width]
     mark = packed[0:hidden, width : 2 * width]
     share = jax.nn.sigmoid(delta[...])
@@ -714,21 +716,22 @@
 
 
 ROUTES = (
+    (("xy", "yx"), "12"),
     (("xy1", "yx1"), "2"),
-    (("1xy", "yx1"), "2"),
-    (("xy1", "1yx"), "2"),
-    (("xy12", "yx12"), ""),
     (("xy1", "yx1"), "2"),
+    (("xy1", "yx1"), "2"),
+    (("1xy", "1yx"), "2"),
 )
 ORDER = (
-    "C0CC10C231KC02SK01K3042K",
-    "KK0132041K32KK04K1324301",
-    "2340312344313241424",
+    "CCKC1C410C40KK1K21042K13",
+    "K03K12041K321432K1K03402",
+    "143502435250S35425304235",
+    "3",
 )
 PACES = (
-    2, 2, 2, 2, 2, 2, 2, 2, 2, 8, 12, 12, 12, 12, 2, 12, 12, 12, 3, 12, 0, 2, 2, 2, 2, 2, 2, 2, 2,
-    2, 2, 2, 2, 2, 2, 12, 2, 2, 2, 2, 3, 0.5, 0.5, 12, 12, 12, 0, 12, 12, 12, 12, 2, 8, 8, 8, 8, 1,
-    6, 1, 12, 2, 2, 2, 2, 2, 2, 2, 2, 12, 12, 12, 12, 12, 6, 6, 6, 6, 6, 6, 6,
+    8, 8, 8, 8, 8, 8, 8, 8, 8, 8, 8, 8, 0, 0, 0, 0, 8, 8, 8, 8, 8, 8, 8, 12, 12, 12, 12, 8, 8, 8,
+    12, 4, 4, 10, 2, 2, 2, 2, 10, 10, 10, 8, 8, 8, 8, 8, 8, 8, 8, 8, 8, 8, 8, 8, 8, 8, 8, 8, 8, 8,
+    8, 8, 8, 8, 8, 8, 8, 8, 8, 8, 8, 8, 8, 12, 12, 12, 12, 8, 2, 0, 8, 8, 8, 12, 8, 0, 0, 0, 0, 8,
 )
 BITS = {"x": ("dp", 1), "y": ("dp", 2), "1": ("seq", 2), "2": ("seq", 4)}
 
@@ -765,25 +768,17 @@
     out[...] = kept[...] + arrived[...]
 
 
-def sum_more_body(kept, arrived, more, out):
-    rows = kept.shape[0]
-    out[:rows, :] = kept[...] + arrived[...]
-    out[rows:, :] = more[...]
-
-
-def join_body(index, extra, masks, own, other, out):
-    half = own.shape[0] - extra
+def join_body(index, masks, own, other, out):
+    half = own.shape[0]
     upper = masks[index, 0:1, 0:1] > 0.5
-    out[:half, :] = jnp.where(upper, other[:half, :], own[:half, :])
-    out[half : 2 * half, :] = jnp.where(upper, own[:half, :], other[:half, :])
-    if extra:
-        out[2 * half :, :] = own[half:, :] + other[half:, :]
+    out[:half, :] = jnp.where(upper, other[...], own[...])
+    out[half:, :] = jnp.where(upper, own[...], other[...])
 
 
 class Piece:
-    def __init__(self, line, made, steps, kept, sent, routes, outputs, name, more=None):
+    def __init__(self, line, made, steps, kept, sent, routes, outputs, name):
         self.line, self.made, self.steps, self.name = line, made, steps, name
-        self.outputs, self.more = outputs, more
+        self.outputs = outputs
         self.work = self.run(kept, sent, *routes)
         self.done = False
         self.advance()
@@ -807,19 +802,8 @@
             )
             arrived = [cross(send, step)]
             yield
-        extra = 0
         for step in list(wholes) + [None]:
-            rows, cols = kept.shape
-            if self.more is not None and not extra:
-                extra = SMALL_ROWS
-                kept = line(
-                    sum_more_body,
-                    (kept, arrived[0], self.more()),
-                    [((rows + extra, cols), F32)],
-                    name=self.name + "_sum",
-                )[0]
-            else:
-                kept = line(sum_body, (kept, arrived[0]), [(kept.shape, F32)], name=self.name + "_sum")[0]
+            kept = line(sum_body, (kept, arrived[0]), [(kept.shape, F32)], name=self.name + "_sum")[0]
             if step is not None:
                 arrived = [cross(kept, step)]
                 yield
@@ -829,17 +813,39 @@
             yield
             rows, cols = part.shape
             part = line(
-                lambda *refs, index=self.steps.index(step): join_body(index, extra, *refs),
+                lambda *refs, index=self.steps.index(step): join_body(index, *refs),
                 (masks, part, other),
-                [((2 * rows - extra, cols), F32)],
+                [((2 * rows, cols), F32)],
                 name=self.name + "_join",
             )[0]
         other = swap(part, "seq", 1)
         yield
-        self.outputs(part, other, part.shape[0] - extra)
-
-
-def place_body(plans, rows, extra, count, more, meta, own, other, *refs):
+        self.outputs(part, other, part.shape[0])
+
+
+class Small:
+    def __init__(self, line, part, last):
+        self.work = self.run(line, part, last)
+        self.done = False
+        self.advance()
+
+    def advance(self):
+        if not self.done:
+            self.done = next(self.work, "end") == "end"
+
+    def run(self, line, part, last):
+        flat = axis_bits("dp", 1)
+        steps = list(zip(flat, flat[::-1])) + [(bit, bit) for bit in axis_bits("seq", 2)]
+        other = swap(part, "seq", 1)
+        yield
+        for step in steps:
+            part = line(sum_body, (part, other), [(part.shape, F32)], name="small_sum")[0]
+            other = cross(part, step)
+            yield
+        last(part, other)
+
+
+def place_body(plans, rows, count, meta, own, other, *refs):
     outs = refs[count : count + len(plans)]
     sems = refs[-1]
     core = meta[0] % 2
@@ -856,8 +862,6 @@
                     )
                 )
                 copies[-1].start()
-    if more is not None:
-        more(own, other, *refs[:extra], *refs[count + len(plans) : -1])
     for copy in copies:
         copy.wait()
 
@@ -866,28 +870,21 @@
     def __init__(self, line, meta, shapes):
         self.line, self.meta, self.shapes, self.arrays = line, meta, shapes, {}
 
-    def placer(self, plans, name, more=None):
+    def placer(self, plans, name):
         def place(own, other, rows):
             names = list(plans)
             held = [n for n in names if n in self.arrays]
-            body, extra, shapes = (more[0], more[1], more[2]) if more else (None, (), [])
-            at = 3 + len(extra)
-            alias = {at + i: names.index(n) for i, n in enumerate(held)}
             results = self.line(
-                lambda *refs: place_body(
-                    list(plans.values()), rows, len(extra), len(extra) + len(held), body, *refs
-                ),
-                (self.meta, own, other, *extra, *[self.arrays[n] for n in held]),
-                [(self.shapes[n], F32) for n in names] + shapes,
+                lambda *refs: place_body(list(plans.values()), rows, len(held), *refs),
+                (self.meta, own, other, *[self.arrays[n] for n in held]),
+                [(self.shapes[n], F32) for n in names],
                 name=name + "_out",
-                held=own.size * 8 + 2**20 * len(shapes) // 8,
-                alias=alias,
+                held=own.size * 8,
+                alias={3 + i: names.index(n) for i, n in enumerate(held)},
                 out_left=len(names),
                 dma=2 * sum(len(p) for p in plans.values()),
             )
             self.arrays.update(zip(names, results))
-            if more:
-                more[3](results[len(names) :])
 
         return place
 
@@ -938,10 +935,11 @@
     keep = jnp.exp(logk)
     mix = share * ema_beta.T * (ema_eta.T * (1.0 / math.sqrt(hidden)))
     gain_rows = jnp.where(share > -1.0, gain1, 0.0)
-    normed, low_normed, enter, end = line(
+    strip = (width // 128, CHUNK, chunks, 128)
+    normed, low_normed, enter, end, strips = line(
         start_body,
         (seq_lengths, tokens, gain_rows, logk, keep),
-        [(tiles, F32), (full, BF16), (states, F32), (state, F32)],
+        [(tiles, F32), (full, BF16), (states, F32), (state, F32), (strip, F32)],
         name="norm_and_states",
     )
     other = swap(end, "seq", 1)
@@ -951,11 +949,11 @@
     arrived = [chip_before(chip_end, k) for k in range(1, lax.axis_size("seq") // 2)]
     routes = [route(halving, doubling) for halving, doubling in ROUTES]
     steps = sorted({step for halves, wholes in routes for step in halves})
-    smooth = line(local_body, (normed, enter, keep, mix), [(tiles, F32)], name="local_average")[0]
+    smooth = line(local_body, (strips, enter, keep, mix), [(strip, F32)], name="local_average")[0]
     values, values_slope = line(values_body, (low_normed, value_weight), [(wide, BF16), (wide, F32)], name="values")
     low_smoothed, slope_pre, entering = line(
         lambda *refs: carried_body(len(arrived), *refs),
-        (meta, other, *arrived, logk, keep, mix, omega, normed, smooth, enter),
+        (meta, other, *arrived, logk, keep, mix, omega, strips, smooth, enter),
         [(full, BF16), (full, F32), (states, F32)],
         scratch=[(state, F32), ((rows, 128), F32)],
         name="carried_average",
@@ -1001,15 +999,16 @@
             next(work)
         return results["packed"]
 
-    def take(values):
-        results["small"] = values
-
-    last = (
-        finish_body,
-        ema,
-        [(state, F32)] * 4 + [((1, width), F32)] * 3 + [((2, shared_width), F32)] * 2 + [((1, shared_width), F32)],
-        take,
-    )
+    def last(own, other):
+        results["small"] = line(
+            finish_body,
+            (own, other, *ema),
+            [(state, F32)] * 4 + [((1, width), F32)] * 3 + [((2, shared_width), F32)] * 2 + [((1, shared_width), F32)],
+            name="parameters",
+        )
+
+    def small_piece():
+        return Small(line, more(), last)
 
     def start_piece(number, parts, pairs, height, cols, plans, name):
         kept, *sent = line(
@@ -1018,9 +1017,8 @@
             [((height, cols), F32)] + [((height // SWAPS, cols), F32)] * SWAPS,
             name=name + "_grad",
         )
-        end = name == "value"
-        placer = outputs.placer(plans, name, last if end else None)
-        return Piece(line, made, steps, kept, sent, routes[number], placer, name, more if end else None)
+        placer = outputs.placer(plans, name)
+        return Piece(line, made, steps, kept, sent, routes[number], placer, name)
 
     def ffn_out_piece():
         return start_piece(
@@ -1075,7 +1073,7 @@
             "value",
         )
 
-    makers = (ffn_out_piece, ffn_in_piece, out_piece, reset_piece, value_piece)
+    makers = (ffn_out_piece, ffn_in_piece, out_piece, reset_piece, value_piece, small_piece)
     pieces = []
 
     def advance(i):
@@ -1123,8 +1121,11 @@
             name="smooth_back",
         )
         yield
-        later, begin = line(
-            rise_body, (meta, smooth_grad, logk, keep), [(states, F32), (state, F32)], name="states_back"
+        later, begin, grad_strips = line(
+            rise_body,
+            (meta, smooth_grad, logk, keep),
+            [(states, F32), (state, F32), (strip, F32)],
+            name="states_back",
         )
         other_begin = swap(begin, "seq", 1)
         yield
@@ -1159,7 +1160,7 @@
             backs.append(
                 line(
                     lambda *refs, tile=tile: state_back_body(tile, *refs),
-                    (normed, smooth_grad, norm_grad, entering, later, keep, mix),
+                    (strips, grad_strips, entering, later, keep, mix),
                     [((rows, 128), F32), ((2 * hidden, 128), F32)],
                     scratch=[((CHUNK, hidden, chunks, 128), F32)],
                     name="state_back",
@@ -1168,7 +1169,8 @@
             yield
         results["input_grad"], results["packed"] = line(
             lambda *refs: close_body(len(backs), *refs),
-            (*[b[0] for b in backs], *[b[1] for b in backs], tokens, gain1, input_part, omega_grad, gain2_grad, small),
+            (*[b[0] for b in backs], *[b[1] for b in backs], tokens, gain1, norm_grad, input_part)
+            + (omega_grad, gain2_grad, small),
             [(full, F32), ((SMALL_ROWS, value_width + shared_width), F32)],
             name="norm_back",
         )
@@ -1183,6 +1185,8 @@
             next(work, None)
     for _ in work:
         pass
+    for i in range(len(pieces), len(makers)):
+        advance(i)
     while not all(p.done for p in pieces):
         for i in range(len(pieces)):
             advance(i)

time: 184 us -> 176 us (0.957)
  waiting for transfers between devices: 49.4 us -> 44.9 us
  Pallas kernels: 65.2 us -> 61.1 us
    ppermute x36 -> x38, waiting for transfers between devices: 45 us -> 32 us  [cross(): return lax.ppermute(a, ('dp', 'seq'), moves)]
    ppermute x2, waiting for transfers between devices: 1.07 us -> 12.1 us  [chip_after(): lax.ppermute(state, 'seq', [(i, i - 2 * chips) for i in range(2 * chips,...]
    ppermute x36 -> x38, starting transfers between devices: 41.9 us -> 48.6 us  [cross(): return lax.ppermute(a, ('dp', 'seq'), moves)]
    ppermute x12 -> x13, starting transfers between devices: 7.52 us -> 2.23 us  [swap(): return lax.ppermute(a, axis, [(i, i ^ bit) for i in range(count)])]
    pallas_call x76 -> x79, Pallas kernels: 65.2 us -> 61.1 us  [__call__(): pl.pallas_call(run, in_specs=specs, out_specs=[pl.BlockSpec(memory_space=...]
    ppermute x12 -> x13, waiting for transfers between devices: 3.33 us -> 0.81 us  [swap(): return lax.ppermute(a, axis, [(i, i ^ bit) for i in range(count)])]
    unnamed x48 -> x44, local copies, waits for them, and re-layouts: 3.78 us -> 3.43 us
  transfers between devices with their start and end apart: 53 -> 56, of which waited for: 16 -> 20; matrix products, arithmetic and copies ran while one was open for 0% -> 0% of each run, Pallas kernels for 26% -> 24%
where the time goes in v4:
time: 176 us
  starting transfers between devices  64.1 us (36%)
  Pallas kernels  61.1 us (35%)
  waiting for transfers between devices  44.9 us (26%)
  local copies, waits for them, and re-layouts  3.43 us (2%)
    pallas_call x79, Pallas kernels, __call__(): pl.pallas_call(run, in_specs=specs, out_specs=[pl.BlockSpec(memory_space=...  61.1 us
    ppermute x38, starting transfers between devices, cross(): return lax.ppermute(a, ('dp', 'seq'), moves)  48.6 us
    ppermute x38, waiting for transfers between devices, cross(): return lax.ppermute(a, ('dp', 'seq'), moves)  32 us
    ppermute x2, waiting for transfers between devices, chip_after(): lax.ppermute(state, 'seq', [(i, i - 2 * chips) for i in range(2 * chips,...  12.1 us
    ppermute x3, starting transfers between devices, chip_before(): lax.ppermute(state, 'seq', [(i, i + 2 * chips) for i in range(count - 2 *...  10.6 us
  transfers between devices with their start and end apart: 56, of which 20 were waited for; matrix products, arithmetic and copies ran while one was open for 0% of the time, Pallas kernels for 24%

profile of v4, /device:TPU:0, one launch (start us, length us, event | category | flops | bytes accessed | tf_op | source)
XLA Modules:
  0.0 176.0 jit_solution(15092998282676916827)
XLA Ops:
  3.2 2.7 %norm_and_states.1 = (f32[4,512,128]{2,1,0:T(8,128)S(1)}, bf16[512,512]{1,0:T(8,128)(2,1)S(1)}, f32[16,8,512]{2,1,0:T(8,128)S(1)}, f32[16,512]{1,0:T(8,128)S(1)}...) custom-call(s32[1,3]{1,0:T(1,128)S(1)} %copy-done.7, bf16[512,512]{1,0:T(8,128)(2,1)S(1)} %copy-done.15, ...), custom_call_target="tpu_custom_call" | custom-call | flops 8000000000 | tf_op jit(solution)/shard_map/norm_and_states/pallas_call | solution.py:81
  7.9 4.8 %collective-permute-start.1 = (f32[16,512]{1,0:T(8,128)S(1)}, f32[16,512]{1,0:T(8,128)S(1)}, u32[]{:S(2)}, u32[]{:S(2)}) collective-permute-start(f32[16,512]{1,0:T(8,128)S(1)} %get-tuple-element.243), channel_id=1, source_target_pairs={{0,2},{1,3},{2,4},{3,5},{4,6},{5,7},{8,10},{9,11},{10,12},{11,13},... | collective-permute-start | bytes 98312 | tf_op jit(solution)/shard_map/ppermute | solution.py:692
  12.8 4.5 %collective-permute-start.2 = (f32[16,512]{1,0:T(8,128)S(1)}, f32[16,512]{1,0:T(8,128)S(1)}, u32[]{:S(2)}, u32[]{:S(2)}) collective-permute-start(f32[16,512]{1,0:T(8,128)S(1)} %get-tuple-element.243), channel_id=1, source_target_pairs={{0,4},{1,5},{2,6},{3,7},{8,12},{9,13},{10,14},{11,15},{16,20},{17,... | collective-permute-start | bytes 98312 | tf_op jit(solution)/shard_map/ppermute | solution.py:692
  17.3 1.3 collective-permute-start.3
  18.6 2.3 %local_average.1 = (f32[4,64,8,128]{3,2,1,0:T(8,128)S(1)}, f32[8,128]{1,0:T(8,128)S(1)}) custom-call(f32[4,64,8,128]{3,2,1,0:T(8,128)S(1)} %get-tuple-element.244.refs_0_.refs_9_, f32[16,8,512]{2,1,0:T(8,128)S(1)} %get-tuple-element.245.refs_1_.refs_11_, f32[16,512]{1,0:T(8,128)S(1)} %get-tuple-element.465.refs_4_.refs_2_.refs_6_.refs_3_, ...), custom_call_target="tpu_custom_call" | custom-call | flops 8000000000 | tf_op jit(solution)/shard_map/local_average/pallas_call | solution.py:81
  22.0 2.7 %carried_average.1 = (bf16[512,512]{1,0:T(8,128)(2,1)S(1)}, f32[512,512]{1,0:T(8,128)S(1)}, f32[16,8,512]{2,1,0:T(8,128)S(1)}, f32[8,128]{1,0:T(8,128)S(1)}) custom-call(s32[5]{0:T(128)S(1)} %pad_add_fusion.refs_0_, f32[16,512]{1,0:T(8,128)S(1)} %collective-permute-done.refs_2_.refs_1_, f32[16,512]{1,0:T(8,128)S(1)} %collective-permute-done.1.refs_2_, ...), custom_call_target="tpu_custom_call" | custom-call | flops 8000000000 | tf_op jit(solution)/shard_map/carried_average/pallas_call | solution.py:81
  24.8 1.4 mix.1
  26.3 2.1 %attention.1 = (f32[512,128]{1,0:T(8,128)S(1)}, f32[512,1024]{1,0:T(8,128)S(1)}, bf16[512,1024]{1,0:T(8,128)(2,1)S(1)}, f32[8,128]{1,0:T(8,128)S(1)}) custom-call(bf16[512,128]{1,0:T(8,128)(2,1)S(1)} %get-tuple-element.253.refs_0_.refs_2_, bf16[512,128]{1,0:T(8,128)(2,1)S(1)} %get-tuple-element.254.refs_1_.refs_3_, ...), custom_call_target="tpu_custom_call" | custom-call | flops 8000000000 | tf_op jit(solution)/shard_map/attention/pallas_call | solution.py:81
  28.5 1.4 hidden.1
  33.1 1.4 hidden_back.1
  34.5 1.3 reset_back.1
  35.8 1.6 ffn_in_grad.1
  37.4 2.1 %attention_back.1 = (bf16[512,1024]{1,0:T(8,128)(2,1)S(1)}, bf16[512,128]{1,0:T(8,128)(2,1)S(1)}, f32[8,128]{1,0:T(8,128)S(1)}, f32[8,128]{1,0:T(8,128)S(1)}) custom-call(bf16[512,1024]{1,0:T(8,128)(2,1)S(1)} %get-tuple-element.283.refs_0_, f32[512,128]{1,0:T(8,128)S(1)} %get-tuple-element.284.refs_1_, ...), custom_call_target="tpu_custom_call" | custom-call | tf_op jit(solution)/shard_map/attention_back/pallas_call | solution.py:81
  39.5 1.4 value_grad.1
  41.8 1.3 ffn_out_grad.1
  43.2 1.6 collective-permute-start.8
  44.7 2.2 %smooth_back.1 = (f32[4,512,128]{2,1,0:T(8,128)S(1)}, f32[4,512,128]{2,1,0:T(8,128)S(1)}, f32[1,512]{1,0:T(1,128)S(1)}, f32[8,128]{1,0:T(8,128)S(1)}) custom-call(bf16[512,512]{1,0:T(8,128)(2,1)S(1)} %get-tuple-element.276.refs_4_.refs_0_, bf16[512,128]{1,0:T(8,128)(2,1)S(1)} %get-tuple-element.290.refs_4_.refs_1_, ...), custom_call_target="tpu_custom_call" | custom-call | flops 8000000000 | tf_op jit(solution)/shard_map/smooth_back/pallas_call | solution.py:81
  47.5 2.5 %states_back.1 = (f32[16,8,512]{2,1,0:T(8,128)S(1)}, f32[16,512]{1,0:T(8,128)S(1)}, f32[4,64,8,128]{3,2,1,0:T(8,128)S(1)}, f32[8,128]{1,0:T(8,128)S(1)}) custom-call(s32[5]{0:T(128)S(1)} %pad_add_fusion.refs_0_, f32[4,512,128]{2,1,0:T(8,128)S(1)} %get-tuple-element.308.refs_1_, f32[16,512]{1,0:T(8,128)S(1)} %get-tuple-element.466.refs_3_.refs_5_.refs_2_.refs_4_, ...), custom_call_target="tpu_custom_call" | custom-call | flops 8000000000 | tf_op jit(solution)/shard_map/states_back/pallas_call | solution.py:81
  50.2 1.5 collective-permute-start.7
  52.3 1.3 collective-permute-start.11
  53.6 1.6 collective-permute-done.8.refs_2_
  55.4 1.6 collective-permute-start.10
  57.0 9.5 %collective-permute-done.11.refs_2_ = f32[16,512]{1,0:T(8,128)S(1)} collective-permute-done((f32[16,512]{1,0:T(8,128)S(1)}, f32[16,512]{1,0:T(8,128)S(1)}, u32[]{:S(2)}, u32[]{:S(2)}) %collective-permute-start.11) | collective-permute-done | bytes 32800 | tf_op jit(solution)/shard_map/ppermute | solution.py:697
  67.1 1.6 out_grad.1
  68.7 1.3 collective-permute-start.13
  70.3 1.6 collective-permute-start.12
  72.9 2.5 %collective-permute-done.13.refs_3_ = f32[16,512]{1,0:T(8,128)S(1)} collective-permute-done((f32[16,512]{1,0:T(8,128)S(1)}, f32[16,512]{1,0:T(8,128)S(1)}, u32[]{:S(2)}, u32[]{:S(2)}) %collective-permute-start.13) | collective-permute-done | bytes 32800 | tf_op jit(solution)/shard_map/ppermute | solution.py:697
  76.1 2.0 %collective-permute-done.16.refs_1_ = f32[32,1536]{1,0:T(8,128)S(1)} collective-permute-done((f32[32,1536]{1,0:T(8,128)S(1)}, f32[32,1536]{1,0:T(8,128)S(1)}, u32[]{:S(2)}, u32[]{:S(2)}) %collective-permute-start.16) | collective-permute-done | bytes 196640 | tf_op jit(solution)/shard_map/ppermute | solution.py:715
  78.2 1.3 reset_grad.1
  79.6 2.6 %collective-permute-start.19 = (f32[32,1536]{1,0:T(8,128)S(1)}, f32[32,1536]{1,0:T(8,128)S(1)}, u32[]{:S(2)}, u32[]{:S(2)}) collective-permute-start(f32[32,1536]{1,0:T(8,128)S(1)} %get-tuple-element.343.refs_0_), channel_id=1, source_target_pairs={{0,4},{1,5},{2,6},{3,7},{4,0},{5,1},{6,2},{7,3},{8,12},{9,13},{10,... | collective-permute-start | bytes 589832 | tf_op jit(solution)/shard_map/ppermute | solution.py:715
  83.4 1.8 %state_back.4 = (f32[512,128]{1,0:T(8,128)S(1)}, f32[32,128]{1,0:T(8,128)S(1)}, f32[8,128]{1,0:T(8,128)S(1)}) custom-call(f32[4,64,8,128]{3,2,1,0:T(8,128)S(1)} %get-tuple-element.244.refs_0_.refs_9_, f32[4,64,8,128]{3,2,1,0:T(8,128)S(1)} %get-tuple-element.322.refs_1_, f32[16,8,512]{2,1,0:T(8,128)S(1)} %get-tuple-element.323.refs_2_, ...), custom_call_target="tpu_custom_call" | custom-call | flops 10000000000 | tf_op jit(solution)/shard_map/state_back/pallas_call | solution.py:81
  85.9 1.8 %state_back.5 = (f32[512,128]{1,0:T(8,128)S(1)}, f32[32,128]{1,0:T(8,128)S(1)}, f32[8,128]{1,0:T(8,128)S(1)}) custom-call(f32[4,64,8,128]{3,2,1,0:T(8,128)S(1)} %get-tuple-element.244.refs_0_.refs_9_, f32[4,64,8,128]{3,2,1,0:T(8,128)S(1)} %get-tuple-element.322.refs_1_, f32[16,8,512]{2,1,0:T(8,128)S(1)} %get-tuple-element.323.refs_2_, ...), custom_call_target="tpu_custom_call" | custom-call | flops 2000000000 | tf_op jit(solution)/shard_map/state_back/pallas_call | solution.py:81
  87.8 4.0 %collective-permute-done.19.refs_1_ = f32[32,1536]{1,0:T(8,128)S(1)} collective-permute-done((f32[32,1536]{1,0:T(8,128)S(1)}, f32[32,1536]{1,0:T(8,128)S(1)}, u32[]{:S(2)}, u32[]{:S(2)}) %collective-permute-start.19) | collective-permute-done | bytes 196640 | tf_op jit(solution)/shard_map/ppermute | solution.py:715
  91.8 1.3 collective-permute-start.25
  94.4 1.6 collective-permute-start.24
  95.9 1.4 collective-permute-done.17.refs_1_
  97.4 1.6 collective-permute-start.28
  99.1 2.4 %collective-permute-done.22.refs_2_ = f32[32,1536]{1,0:T(8,128)S(1)} collective-permute-done((f32[32,1536]{1,0:T(8,128)S(1)}, f32[32,1536]{1,0:T(8,128)S(1)}, u32[]{:S(2)}, u32[]{:S(2)}) %collective-permute-start.22) | collective-permute-done | bytes 196640 | tf_op jit(solution)/shard_map/ppermute | solution.py:715
  102.8 1.8 %state_back.6 = (f32[512,128]{1,0:T(8,128)S(1)}, f32[32,128]{1,0:T(8,128)S(1)}, f32[8,128]{1,0:T(8,128)S(1)}) custom-call(f32[4,64,8,128]{3,2,1,0:T(8,128)S(1)} %get-tuple-element.244.refs_0_.refs_9_, f32[4,64,8,128]{3,2,1,0:T(8,128)S(1)} %get-tuple-element.322.refs_1_, f32[16,8,512]{2,1,0:T(8,128)S(1)} %get-tuple-element.323.refs_2_, ...), custom_call_target="tpu_custom_call" | custom-call | flops 8000000000 | tf_op jit(solution)/shard_map/state_back/pallas_call | solution.py:81
  106.0 1.6 collective-permute-start.27
  107.7 2.8 %collective-permute-start.26 = (f32[32,1536]{1,0:T(8,128)S(1)}, f32[32,1536]{1,0:T(8,128)S(1)}, u32[]{:S(2)}, u32[]{:S(2)}) collective-permute-start(f32[32,1536]{1,0:T(8,128)S(1)} %get-tuple-element.368), channel_id=1, source_target_pairs={{0,2},{1,3},{2,0},{3,1},{4,6},{5,7},{6,4},{7,5},{8,10},{9,11},{10,... | collective-permute-start | bytes 589832 | tf_op jit(solution)/shard_map/ppermute | solution.py:715
  111.6 2.5 %collective-permute-start.32 = (f32[32,1152]{1,0:T(8,128)S(1)}, f32[32,1152]{1,0:T(8,128)S(1)}, u32[]{:S(2)}, u32[]{:S(2)}) collective-permute-start(f32[32,1152]{1,0:T(8,128)S(1)} %get-tuple-element.394.refs_0_), channel_id=1, source_target_pairs={{0,4},{1,5},{2,6},{3,7},{4,0},{5,1},{6,2},{7,3},{8,12},{9,13},{10,... | collective-permute-start | bytes 442376 | tf_op jit(solution)/shard_map/ppermute | solution.py:715
  116.2 1.5 collective-permute-start.38
  117.7 1.8 %state_back.7 = (f32[512,128]{1,0:T(8,128)S(1)}, f32[32,128]{1,0:T(8,128)S(1)}, f32[8,128]{1,0:T(8,128)S(1)}) custom-call(f32[4,64,8,128]{3,2,1,0:T(8,128)S(1)} %get-tuple-element.244.refs_0_.refs_9_, f32[4,64,8,128]{3,2,1,0:T(8,128)S(1)} %get-tuple-element.322.refs_1_, f32[16,8,512]{2,1,0:T(8,128)S(1)} %get-tuple-element.323.refs_2_, ...), custom_call_target="tpu_custom_call" | custom-call | flops 8000000000 | tf_op jit(solution)/shard_map/state_back/pallas_call | solution.py:81
  119.6 3.1 %collective-permute-done.30.refs_2_ = f32[128,1536]{1,0:T(8,128)S(1)} collective-permute-done((f32[128,1536]{1,0:T(8,128)S(1)}, f32[128,1536]{1,0:T(8,128)S(1)}, u32[]{:S(2)}, u32[]{:S(2)}) %collective-permute-start.30) | collective-permute-done | bytes 786464 | tf_op jit(solution)/shard_map/ppermute | solution.py:715
  123.7 1.9 %norm_back.1 = (f32[512,512]{1,0:T(8,128)}, f32[24,1152]{1,0:T(8,128)S(1)}, f32[8,128]{1,0:T(8,128)S(1)}) custom-call(f32[512,128]{1,0:T(8,128)S(1)} %get-tuple-element.352.refs_0_, f32[512,128]{1,0:T(8,128)S(1)} %get-tuple-element.353.refs_1_, f32[512,128]{1,0:T(8,128)S(1)} %get-tuple-element.360.refs_2_, f32[512,128]{1,0:T(8,128)S(1)} %get-tuple-element.379.refs_3_, ...), custom_call_target="tpu_custom_call" | custom-call | flops 8000000000 | tf_op jit(solution)/shard_map/norm_back/pallas_call | solution.py:81
  127.8 2.6 %collective-permute-start.35 = (f32[32,1024]{1,0:T(8,128)S(1)}, f32[32,1024]{1,0:T(8,128)S(1)}, u32[]{:S(2)}, u32[]{:S(2)}) collective-permute-start(f32[32,1024]{1,0:T(8,128)S(1)} %get-tuple-element.401.refs_0_), channel_id=1, source_target_pairs={{0,4},{1,5},{2,6},{3,7},{4,0},{5,1},{6,2},{7,3},{8,12},{9,13},{10,... | collective-permute-start | bytes 393224 | tf_op jit(solution)/shard_map/ppermute | solution.py:715
  130.5 1.6 collective-permute-done.31.refs_2_
  133.2 1.7 collective-permute-start.43
  134.9 2.2 %ffn_in_out.1 = (f32[512,1024]{1,0:T(8,128)}, f32[512,2176]{1,0:T(8,128)}, f32[8,128]{1,0:T(8,128)S(1)}) custom-call(s32[5]{0:T(128)S(1)} %pad_add_fusion.refs_0_, f32[256,1536]{1,0:T(8,128)S(1)} %get-tuple-element.403.refs_1_, f32[256,1536]{1,0:T(8,128)S(1)} %collective-permute-done.37.refs_2_, f32[8,128]{1,0:T(8,128)S(1)} %get-tuple-element.406.refs_3_), custom_call_target="tpu_custom_call" | custom-call | flops 8000000000 | tf_op jit(solution)/shard_map/ffn_in_out/pallas_call | solution.py:81
  138.9 2.6 %collective-permute-done.34.refs_2_ = f32[256,512]{1,0:T(8,128)S(1)} collective-permute-done((f32[256,512]{1,0:T(8,128)S(1)}, f32[256,512]{1,0:T(8,128)S(1)}, u32[]{:S(2)}, u32[]{:S(2)}) %collective-permute-start.34) | collective-permute-done | bytes 524320 | tf_op jit(solution)/shard_map/ppermute | solution.py:715
  142.9 2.2 %collective-permute-done.42.refs_2_ = f32[64,1152]{1,0:T(8,128)S(1)} collective-permute-done((f32[64,1152]{1,0:T(8,128)S(1)}, f32[64,1152]{1,0:T(8,128)S(1)}, u32[]{:S(2)}, u32[]{:S(2)}) %collective-permute-start.42) | collective-permute-done | bytes 294944 | tf_op jit(solution)/shard_map/ppermute | solution.py:715
  146.7 2.3 %collective-permute-start.50 = (f32[128,1152]{1,0:T(8,128)S(1)}, f32[128,1152]{1,0:T(8,128)S(1)}, u32[]{:S(2)}, u32[]{:S(2)}) collective-permute-start(f32[128,1152]{1,0:T(8,128)S(1)} %get-tuple-element.433.refs_1_), channel_id=1, source_target_pairs={{0,2},{1,3},{2,0},{3,1},{4,6},{5,7},{6,4},{7,5},{8,10},{9,11},{10,... | collective-permute-start | bytes 1769480 | tf_op jit(solution)/shard_map/ppermute | solution.py:715
  149.0 1.7 collective-permute-done.45.refs_2_
  152.9 1.9 %ffn_out_out.1 = (f32[1024,512]{1,0:T(8,128)}, f32[8,128]{1,0:T(8,128)S(1)}) custom-call(s32[5]{0:T(128)S(1)} %pad_add_fusion.refs_0_, f32[512,512]{1,0:T(8,128)S(1)} %get-tuple-element.410.refs_1_, f32[512,512]{1,0:T(8,128)S(1)} %collective-permute-done.39.refs_2_, f32[8,128]{1,0:T(8,128)S(1)} %get-tuple-element.423.refs_3_), custom_call_target="tpu_custom_call" | custom-call | flops 8000000000 | tf_op jit(solution)/shard_map/ffn_out_out/pallas_call | solution.py:81
  154.8 1.7 block_out.1
  156.6 1.5 collective-permute-done.46.refs_1_
  158.1 1.5 collective-permute-start.48
  160.7 1.5 collective-permute-done.50.refs_2_
  163.5 2.7 %collective-permute-start.51 = (f32[24,1152]{1,0:T(8,128)S(1)}, f32[24,1152]{1,0:T(8,128)S(1)}, u32[]{:S(2)}, u32[]{:S(2)}) collective-permute-start(f32[24,1152]{1,0:T(8,128)S(1)} %get-tuple-element.437.refs_0_), channel_id=1, source_target_pairs={{0,4},{1,5},{2,6},{3,7},{4,0},{5,1},{6,2},{7,3},{8,12},{9,13},{10,... | collective-permute-start | bytes 331784 | tf_op jit(solution)/shard_map/ppermute | solution.py:715
  166.2 2.6 %collective-permute-done.52.refs_2_ = f32[128,1024]{1,0:T(8,128)S(1)} collective-permute-done((f32[128,1024]{1,0:T(8,128)S(1)}, f32[128,1024]{1,0:T(8,128)S(1)}, u32[]{:S(2)}, u32[]{:S(2)}) %collective-permute-start.52) | collective-permute-done | bytes 524320 | tf_op jit(solution)/shard_map/ppermute | solution.py:715
  169.0 2.0 %value_out.1 = (f32[512,1024]{1,0:T(8,128)}, f32[512,2176]{1,0:T(8,128)}, f32[8,128]{1,0:T(8,128)S(1)}) custom-call(s32[5]{0:T(128)S(1)} %pad_add_fusion.refs_0_, f32[256,1152]{1,0:T(8,128)S(1)} %get-tuple-element.442.refs_1_, f32[256,1152]{1,0:T(8,128)S(1)} %collective-permute-done.55.refs_2_, ...), custom_call_target="tpu_custom_call", output_to_operand_aliasing={{1}: (3, {})} | custom-call | flops 12000000000 | tf_op jit(solution)/shard_map/value_out/pallas_call | solution.py:81
  171.0 2.3 %out_out.1 = (f32[1024,512]{1,0:T(8,128)}, f32[512,2176]{1,0:T(8,128)}, f32[8,128]{1,0:T(8,128)S(1)}) custom-call(s32[5]{0:T(128)S(1)} %pad_add_fusion.refs_0_, f32[256,1536]{1,0:T(8,128)S(1)} %get-tuple-element.441.refs_1_, f32[256,1536]{1,0:T(8,128)S(1)} %collective-permute-done.54.refs_2_, ...), custom_call_target="tpu_custom_call", output_to_operand_aliasing={{1}: (3, {})} | custom-call | flops 12000000000 | tf_op jit(solution)/shard_map/out_out/pallas_call | solution.py:81
  173.4 1.9 %reset_out.1 = (f32[512,2176]{1,0:T(8,128)}, f32[8,128]{1,0:T(8,128)S(1)}) custom-call(s32[5]{0:T(128)S(1)} %pad_add_fusion.refs_0_, f32[256,1024]{1,0:T(8,128)S(1)} %get-tuple-element.440.refs_1_, f32[256,1024]{1,0:T(8,128)S(1)} %collective-permute-done.53.refs_2_, f32[512,2176]{1,0:T(8,128)} %get-tuple-element.447.refs_3_, ...), custom_call_target="tpu_custom_call", output_to_operand_aliasing={{0}: (3, {})} | custom-call | flops 8000000000 | tf_op jit(solution)/shard_map/reset_out/pallas_call | solution.py:81
  (173 shorter events, 37.8 us)
Async XLA Ops:
  3.2 3.3 %copy-start.8 = (s32[1,3]{1,0:T(1,128)S(1)}, s32[1,3]{1,0:T(1,128)}, u32[]{:S(2)}) copy-start(s32[1,3]{1,0:T(1,128)} %refs_0_.2) | copy-start | bytes 40
  6.0 1.4 collective-permute-start
  7.9 14.0 %collective-permute-start.1 = (f32[16,512]{1,0:T(8,128)S(1)}, f32[16,512]{1,0:T(8,128)S(1)}, u32[]{:S(2)}, u32[]{:S(2)}) collective-permute-start(f32[16,512]{1,0:T(8,128)S(1)} %get-tuple-element.243), channel_id=1, source_target_pairs={{0,2},{1,3},{2,4},{3,5},{4,6},{5,7},{8,10},{9,11},{10,12},{11,13},... | collective-permute-start | bytes 98312 | tf_op jit(solution)/shard_map/ppermute | solution.py:692
  12.8 9.2 %collective-permute-start.2 = (f32[16,512]{1,0:T(8,128)S(1)}, f32[16,512]{1,0:T(8,128)S(1)}, u32[]{:S(2)}, u32[]{:S(2)}) collective-permute-start(f32[16,512]{1,0:T(8,128)S(1)} %get-tuple-element.243), channel_id=1, source_target_pairs={{0,4},{1,5},{2,6},{3,7},{8,12},{9,13},{10,14},{11,15},{16,20},{17,... | collective-permute-start | bytes 98312 | tf_op jit(solution)/shard_map/ppermute | solution.py:692
  17.3 4.7 %collective-permute-start.3 = (f32[16,512]{1,0:T(8,128)S(1)}, f32[16,512]{1,0:T(8,128)S(1)}, u32[]{:S(2)}, u32[]{:S(2)}) collective-permute-start(f32[16,512]{1,0:T(8,128)S(1)} %get-tuple-element.243), channel_id=1, source_target_pairs={{0,6},{1,7},{8,14},{9,15},{16,22},{17,23},{24,30},{25,31}} | collective-permute-start | bytes 98312 | tf_op jit(solution)/shard_map/ppermute | solution.py:692
  18.6 2.3 %copy-start.11 = (bf16[512,1024]{1,0:T(8,128)(2,1)S(1)}, bf16[512,1024]{1,0:T(8,128)(2,1)}, u32[]{:S(2)}) copy-start(bf16[512,1024]{1,0:T(8,128)(2,1)} %refs_6_.1) | copy-start | bytes 3145732
  22.0 2.8 %copy-start.6 = (f32[2,128]{1,0:T(2,128)S(1)}, f32[2,128]{1,0:T(2,128)}, u32[]{:S(2)}) copy-start(f32[2,128]{1,0:T(2,128)} %refs_8_.2) | copy-start | bytes 3076
  22.0 2.8 %copy-start.9 = (bf16[512,2176]{1,0:T(8,128)(2,1)S(1)}, bf16[512,2176]{1,0:T(8,128)(2,1)}, u32[]{:S(2)}) copy-start(bf16[512,2176]{1,0:T(8,128)(2,1)} %refs_5_.3) | copy-start | bytes 6684676
  22.0 2.8 %copy-start.20 = (f32[2,128]{1,0:T(2,128)S(1)}, f32[2,128]{1,0:T(2,128)}, u32[]{:S(2)}) copy-start(f32[2,128]{1,0:T(2,128)} %refs_3_.1) | copy-start | bytes 3076
  26.3 2.2 %copy-start = (bf16[1024,512]{1,0:T(8,128)(2,1)S(1)}, bf16[1024,512]{1,0:T(8,128)(2,1)}, u32[]{:S(2)}) copy-start(bf16[1024,512]{1,0:T(8,128)(2,1)} %refs_1_.15) | copy-start | bytes 3145732
  26.3 2.2 %copy-start.16 = (bf16[512,512]{1,0:T(8,128)(2,1)S(1)}, bf16[512,512]{1,0:T(8,128)(2,1)}, u32[]{:S(2)}) copy-start(bf16[512,512]{1,0:T(8,128)(2,1)} %refs_8_.3) | copy-start | bytes 1572868
  26.3 2.2 %copy-start.18 = (f32[512]{0:T(512)S(1)}, f32[512]{0:T(512)}, u32[]{:S(2)}) copy-start(f32[512]{0:T(512)} %param.33) | copy-start | bytes 6148
  37.3 4.1 %collective-permute-start.4 = (f32[256,1536]{1,0:T(8,128)S(1)}, f32[256,1536]{1,0:T(8,128)S(1)}, u32[]{:S(2)}, u32[]{:S(2)}) collective-permute-start(f32[256,1536]{1,0:T(8,128)S(1)} %get-tuple-element.282), channel_id=1, source_target_pairs={{0,1},{1,0},{2,3},{3,2},{4,5},{5,4},{6,7},{7,6},{8,9},{9,8},{10,11... | collective-permute-start | bytes 4718600 | tf_op jit(solution)/shard_map/ppermute | solution.py:687
  40.9 6.1 %collective-permute-start.6 = (f32[256,1152]{1,0:T(8,128)S(1)}, f32[256,1152]{1,0:T(8,128)S(1)}, u32[]{:S(2)}, u32[]{:S(2)}) collective-permute-start(f32[256,1152]{1,0:T(8,128)S(1)} %get-tuple-element.297), channel_id=1, source_target_pairs={{0,1},{1,0},{2,3},{3,2},{4,5},{5,4},{6,7},{7,6},{8,9},{9,8},{10,11... | collective-permute-start | bytes 3538952 | tf_op jit(solution)/shard_map/ppermute | solution.py:687
  43.1 4.1 %collective-permute-start.5 = (f32[512,512]{1,0:T(8,128)S(1)}, f32[512,512]{1,0:T(8,128)S(1)}, u32[]{:S(2)}, u32[]{:S(2)}) collective-permute-start(f32[512,512]{1,0:T(8,128)S(1)} %get-tuple-element.295), channel_id=1, source_target_pairs={{0,1},{1,0},{2,3},{3,2},{4,5},{5,4},{6,7},{7,6},{8,9},{9,8},{10,11... | collective-permute-start | bytes 3145736 | tf_op jit(solution)/shard_map/ppermute | solution.py:687
  43.2 12.0 %collective-permute-start.8 = (f32[128,1536]{1,0:T(8,128)S(1)}, f32[128,1536]{1,0:T(8,128)S(1)}, u32[]{:S(2)}, u32[]{:S(2)}) collective-permute-start(f32[128,1536]{1,0:T(8,128)S(1)} %get-tuple-element.307), channel_id=1, source_target_pairs={{0,8},{1,17},{2,10},{3,19},{4,12},{5,21},{6,14},{7,23},{8,0},{9,25... | collective-permute-start | bytes 2359304 | tf_op jit(solution)/shard_map/ppermute | solution.py:715
  50.0 1.7 collective-permute-start.9
  50.2 21.7 %collective-permute-start.15 = (f32[128,1152]{1,0:T(8,128)S(1)}, f32[128,1152]{1,0:T(8,128)S(1)}, u32[]{:S(2)}, u32[]{:S(2)}) collective-permute-start(f32[128,1152]{1,0:T(8,128)S(1)} %get-tuple-element.329), channel_id=1, source_target_pairs={{0,2},{1,3},{2,0},{3,1},{4,6},{5,7},{6,4},{7,5},{8,10},{9,11},{10,... | collective-permute-start | bytes 1769480 | tf_op jit(solution)/shard_map/ppermute | solution.py:715
  50.2 20.0 %collective-permute-start.7 = (f32[256,512]{1,0:T(8,128)S(1)}, f32[256,512]{1,0:T(8,128)S(1)}, u32[]{:S(2)}, u32[]{:S(2)}) collective-permute-start(f32[256,512]{1,0:T(8,128)S(1)} %get-tuple-element.305), channel_id=1, source_target_pairs={{0,8},{1,17},{2,10},{3,19},{4,12},{5,21},{6,14},{7,23},{8,0},{9,25... | collective-permute-start | bytes 1572872 | tf_op jit(solution)/shard_map/ppermute | solution.py:715
  52.3 14.2 %collective-permute-start.11 = (f32[16,512]{1,0:T(8,128)S(1)}, f32[16,512]{1,0:T(8,128)S(1)}, u32[]{:S(2)}, u32[]{:S(2)}) collective-permute-start(f32[16,512]{1,0:T(8,128)S(1)} %get-tuple-element.315.refs_1_), channel_id=1, source_target_pairs={{2,0},{3,1},{4,2},{5,3},{6,4},{7,5},{10,8},{11,9},{12,10},{13,11},... | collective-permute-start | bytes 98312 | tf_op jit(solution)/shard_map/ppermute | solution.py:697
  55.4 14.6 %collective-permute-start.10 = (f32[64,1536]{1,0:T(8,128)S(1)}, f32[64,1536]{1,0:T(8,128)S(1)}, u32[]{:S(2)}, u32[]{:S(2)}) collective-permute-start(f32[64,1536]{1,0:T(8,128)S(1)} %get-tuple-element.314), channel_id=1, source_target_pairs={{0,16},{1,9},{2,18},{3,11},{4,20},{5,13},{6,22},{7,15},{8,24},{9,1... | collective-permute-start | bytes 1179656 | tf_op jit(solution)/shard_map/ppermute | solution.py:715
  68.7 4.0 %collective-permute-start.14 = (f32[256,1536]{1,0:T(8,128)S(1)}, f32[256,1536]{1,0:T(8,128)S(1)}, u32[]{:S(2)}, u32[]{:S(2)}) collective-permute-start(f32[256,1536]{1,0:T(8,128)S(1)} %get-tuple-element.327), channel_id=1, source_target_pairs={{0,1},{1,0},{2,3},{3,2},{4,5},{5,4},{6,7},{7,6},{8,9},{9,8},{10,11... | collective-permute-start | bytes 4718600 | tf_op jit(solution)/shard_map/ppermute | solution.py:687
  68.7 6.7 %collective-permute-start.13 = (f32[16,512]{1,0:T(8,128)S(1)}, f32[16,512]{1,0:T(8,128)S(1)}, u32[]{:S(2)}, u32[]{:S(2)}) collective-permute-start(f32[16,512]{1,0:T(8,128)S(1)} %get-tuple-element.324), channel_id=1, source_target_pairs={{4,0},{5,1},{6,2},{7,3},{12,8},{13,9},{14,10},{15,11},{20,16},{21,... | collective-permute-start | bytes 98312 | tf_op jit(solution)/shard_map/ppermute | solution.py:697
  70.1 8.1 %collective-permute-start.16 = (f32[32,1536]{1,0:T(8,128)S(1)}, f32[32,1536]{1,0:T(8,128)S(1)}, u32[]{:S(2)}, u32[]{:S(2)}) collective-permute-start(f32[32,1536]{1,0:T(8,128)S(1)} %get-tuple-element.335), channel_id=1, source_target_pairs={{0,2},{1,3},{2,0},{3,1},{4,6},{5,7},{6,4},{7,5},{8,10},{9,11},{10,... | collective-permute-start | bytes 589832 | tf_op jit(solution)/shard_map/ppermute | solution.py:715
  70.3 15.0 %collective-permute-start.12 = (f32[128,512]{1,0:T(8,128)S(1)}, f32[128,512]{1,0:T(8,128)S(1)}, u32[]{:S(2)}, u32[]{:S(2)}) collective-permute-start(f32[128,512]{1,0:T(8,128)S(1)} %get-tuple-element.321), channel_id=1, source_target_pairs={{0,16},{1,9},{2,18},{3,11},{4,20},{5,13},{6,22},{7,15},{8,24},{9,1... | collective-permute-start | bytes 786440 | tf_op jit(solution)/shard_map/ppermute | solution.py:715
  72.0 25.3 %collective-permute-start.23 = (f32[64,1152]{1,0:T(8,128)S(1)}, f32[64,1152]{1,0:T(8,128)S(1)}, u32[]{:S(2)}, u32[]{:S(2)}) collective-permute-start(f32[64,1152]{1,0:T(8,128)S(1)} %get-tuple-element.356), channel_id=1, source_target_pairs={{0,8},{1,17},{2,10},{3,19},{4,12},{5,21},{6,14},{7,23},{8,0},{9,25... | collective-permute-start | bytes 884744 | tf_op jit(solution)/shard_map/ppermute | solution.py:715
  79.5 6.2 %collective-permute-start.20 = (f32[256,1024]{1,0:T(8,128)S(1)}, f32[256,1024]{1,0:T(8,128)S(1)}, u32[]{:S(2)}, u32[]{:S(2)}) collective-permute-start(f32[256,1024]{1,0:T(8,128)S(1)} %get-tuple-element.345), channel_id=1, source_target_pairs={{0,1},{1,0},{2,3},{3,2},{4,5},{5,4},{6,7},{7,6},{8,9},{9,8},{10,11... | collective-permute-start | bytes 3145736 | tf_op jit(solution)/shard_map/ppermute | solution.py:687
  79.6 12.2 %collective-permute-start.19 = (f32[32,1536]{1,0:T(8,128)S(1)}, f32[32,1536]{1,0:T(8,128)S(1)}, u32[]{:S(2)}, u32[]{:S(2)}) collective-permute-start(f32[32,1536]{1,0:T(8,128)S(1)} %get-tuple-element.343.refs_0_), channel_id=1, source_target_pairs={{0,4},{1,5},{2,6},{3,7},{4,0},{5,1},{6,2},{7,3},{8,12},{9,13},{10,... | collective-permute-start | bytes 589832 | tf_op jit(solution)/shard_map/ppermute | solution.py:715
  82.2 12.0 %collective-permute-start.18 = (f32[128,1536]{1,0:T(8,128)S(1)}, f32[128,1536]{1,0:T(8,128)S(1)}, u32[]{:S(2)}, u32[]{:S(2)}) collective-permute-start(f32[128,1536]{1,0:T(8,128)S(1)} %get-tuple-element.342), channel_id=1, source_target_pairs={{0,8},{1,17},{2,10},{3,19},{4,12},{5,21},{6,14},{7,23},{8,0},{9,25... | collective-permute-start | bytes 2359304 | tf_op jit(solution)/shard_map/ppermute | solution.py:715
  85.3 12.0 %collective-permute-start.17 = (f32[128,512]{1,0:T(8,128)S(1)}, f32[128,512]{1,0:T(8,128)S(1)}, u32[]{:S(2)}, u32[]{:S(2)}) collective-permute-start(f32[128,512]{1,0:T(8,128)S(1)} %get-tuple-element.340.refs_0_), channel_id=1, source_target_pairs={{0,2},{1,3},{2,0},{3,1},{4,6},{5,7},{6,4},{7,5},{8,10},{9,11},{10,... | collective-permute-start | bytes 786440 | tf_op jit(solution)/shard_map/ppermute | solution.py:715
  91.8 9.7 %collective-permute-start.22 = (f32[32,1536]{1,0:T(8,128)S(1)}, f32[32,1536]{1,0:T(8,128)S(1)}, u32[]{:S(2)}, u32[]{:S(2)}) collective-permute-start(f32[32,1536]{1,0:T(8,128)S(1)} %get-tuple-element.354.refs_1_), channel_id=1, source_target_pairs={{0,2},{1,3},{2,0},{3,1},{4,6},{5,7},{6,4},{7,5},{8,10},{9,11},{10,... | collective-permute-start | bytes 589832 | tf_op jit(solution)/shard_map/ppermute | solution.py:715
  91.8 14.0 %collective-permute-start.25 = (f32[128,1024]{1,0:T(8,128)S(1)}, f32[128,1024]{1,0:T(8,128)S(1)}, u32[]{:S(2)}, u32[]{:S(2)}) collective-permute-start(f32[128,1024]{1,0:T(8,128)S(1)} %get-tuple-element.364), channel_id=1, source_target_pairs={{0,8},{1,17},{2,10},{3,19},{4,12},{5,21},{6,14},{7,23},{8,0},{9,25... | collective-permute-start | bytes 1572872 | tf_op jit(solution)/shard_map/ppermute | solution.py:715
  94.4 13.2 %collective-permute-start.24 = (f32[64,1536]{1,0:T(8,128)S(1)}, f32[64,1536]{1,0:T(8,128)S(1)}, u32[]{:S(2)}, u32[]{:S(2)}) collective-permute-start(f32[64,1536]{1,0:T(8,128)S(1)} %get-tuple-element.362), channel_id=1, source_target_pairs={{0,16},{1,9},{2,18},{3,11},{4,20},{5,13},{6,22},{7,15},{8,24},{9,1... | collective-permute-start | bytes 1179656 | tf_op jit(solution)/shard_map/ppermute | solution.py:715
  97.4 14.1 %collective-permute-start.28 = (f32[32,1152]{1,0:T(8,128)S(1)}, f32[32,1152]{1,0:T(8,128)S(1)}, u32[]{:S(2)}, u32[]{:S(2)}) collective-permute-start(f32[32,1152]{1,0:T(8,128)S(1)} %get-tuple-element.372), channel_id=1, source_target_pairs={{0,16},{1,9},{2,18},{3,11},{4,20},{5,13},{6,22},{7,15},{8,24},{9,1... | collective-permute-start | bytes 442376 | tf_op jit(solution)/shard_map/ppermute | solution.py:715
  99.1 26.5 %collective-permute-start.21 = (f32[128,512]{1,0:T(8,128)S(1)}, f32[128,512]{1,0:T(8,128)S(1)}, u32[]{:S(2)}, u32[]{:S(2)}) collective-permute-start(f32[128,512]{1,0:T(8,128)S(1)} %get-tuple-element.351.refs_0_), channel_id=1, source_target_pairs={{0,4},{1,5},{2,6},{3,7},{4,0},{5,1},{6,2},{7,3},{8,12},{9,13},{10,... | collective-permute-start | bytes 786440 | tf_op jit(solution)/shard_map/ppermute | solution.py:715
  101.5 8.9 %collective-permute-start.29 = (f32[64,1536]{1,0:T(8,128)S(1)}, f32[64,1536]{1,0:T(8,128)S(1)}, u32[]{:S(2)}, u32[]{:S(2)}) collective-permute-start(f32[64,1536]{1,0:T(8,128)S(1)} %get-tuple-element.373.refs_1_), channel_id=1, source_target_pairs={{0,16},{1,9},{2,18},{3,11},{4,20},{5,13},{6,22},{7,15},{8,24},{9,1... | collective-permute-start | bytes 1179656 | tf_op jit(solution)/shard_map/ppermute | solution.py:715
  106.0 8.2 %collective-permute-start.27 = (f32[64,1024]{1,0:T(8,128)S(1)}, f32[64,1024]{1,0:T(8,128)S(1)}, u32[]{:S(2)}, u32[]{:S(2)}) collective-permute-start(f32[64,1024]{1,0:T(8,128)S(1)} %get-tuple-element.370), channel_id=1, source_target_pairs={{0,16},{1,9},{2,18},{3,11},{4,20},{5,13},{6,22},{7,15},{8,24},{9,1... | collective-permute-start | bytes 786440 | tf_op jit(solution)/shard_map/ppermute | solution.py:715
  107.7 8.5 %collective-permute-start.26 = (f32[32,1536]{1,0:T(8,128)S(1)}, f32[32,1536]{1,0:T(8,128)S(1)}, u32[]{:S(2)}, u32[]{:S(2)}) collective-permute-start(f32[32,1536]{1,0:T(8,128)S(1)} %get-tuple-element.368), channel_id=1, source_target_pairs={{0,2},{1,3},{2,0},{3,1},{4,6},{5,7},{6,4},{7,5},{8,10},{9,11},{10,... | collective-permute-start | bytes 589832 | tf_op jit(solution)/shard_map/ppermute | solution.py:715
  110.6 12.1 %collective-permute-start.30 = (f32[128,1536]{1,0:T(8,128)S(1)}, f32[128,1536]{1,0:T(8,128)S(1)}, u32[]{:S(2)}, u32[]{:S(2)}) collective-permute-start(f32[128,1536]{1,0:T(8,128)S(1)} %get-tuple-element.389.refs_1_), channel_id=1, source_target_pairs={{0,8},{1,17},{2,10},{3,19},{4,12},{5,21},{6,14},{7,23},{8,0},{9,25... | collective-permute-start | bytes 2359304 | tf_op jit(solution)/shard_map/ppermute | solution.py:715
  111.6 15.3 %collective-permute-start.32 = (f32[32,1152]{1,0:T(8,128)S(1)}, f32[32,1152]{1,0:T(8,128)S(1)}, u32[]{:S(2)}, u32[]{:S(2)}) collective-permute-start(f32[32,1152]{1,0:T(8,128)S(1)} %get-tuple-element.394.refs_0_), channel_id=1, source_target_pairs={{0,4},{1,5},{2,6},{3,7},{4,0},{5,1},{6,2},{7,3},{8,12},{9,13},{10,... | collective-permute-start | bytes 442376 | tf_op jit(solution)/shard_map/ppermute | solution.py:715
  114.2 12.7 %collective-permute-start.33 = (f32[32,1024]{1,0:T(8,128)S(1)}, f32[32,1024]{1,0:T(8,128)S(1)}, u32[]{:S(2)}, u32[]{:S(2)}) collective-permute-start(f32[32,1024]{1,0:T(8,128)S(1)} %get-tuple-element.396), channel_id=1, source_target_pairs={{0,2},{1,3},{2,0},{3,1},{4,6},{5,7},{6,4},{7,5},{8,10},{9,11},{10,... | collective-permute-start | bytes 393224 | tf_op jit(solution)/shard_map/ppermute | solution.py:715
  116.2 15.9 %collective-permute-start.38 = (f32[32,1536]{1,0:T(8,128)S(1)}, f32[32,1536]{1,0:T(8,128)S(1)}, u32[]{:S(2)}, u32[]{:S(2)}) collective-permute-start(f32[32,1536]{1,0:T(8,128)S(1)} %get-tuple-element.404.refs_0_), channel_id=1, source_target_pairs={{0,4},{1,5},{2,6},{3,7},{4,0},{5,1},{6,2},{7,3},{8,12},{9,13},{10,... | collective-permute-start | bytes 589832 | tf_op jit(solution)/shard_map/ppermute | solution.py:715
  125.6 6.4 %collective-permute-start.31 = (f32[128,512]{1,0:T(8,128)S(1)}, f32[128,512]{1,0:T(8,128)S(1)}, u32[]{:S(2)}, u32[]{:S(2)}) collective-permute-start(f32[128,512]{1,0:T(8,128)S(1)} %get-tuple-element.393.refs_1_), channel_id=1, source_target_pairs={{0,16},{1,9},{2,18},{3,11},{4,20},{5,13},{6,22},{7,15},{8,24},{9,1... | collective-permute-start | bytes 786440 | tf_op jit(solution)/shard_map/ppermute | solution.py:715
  126.9 6.3 %collective-permute-start.37 = (f32[256,1536]{1,0:T(8,128)S(1)}, f32[256,1536]{1,0:T(8,128)S(1)}, u32[]{:S(2)}, u32[]{:S(2)}) collective-permute-start(f32[256,1536]{1,0:T(8,128)S(1)} %get-tuple-element.403.refs_1_), channel_id=1, source_target_pairs={{0,1},{1,0},{2,3},{3,2},{4,5},{5,4},{6,7},{7,6},{8,9},{9,8},{10,11... | collective-permute-start | bytes 4718600 | tf_op jit(solution)/shard_map/ppermute | solution.py:687
  127.0 10.2 %collective-permute-start.36 = (f32[32,1152]{1,0:T(8,128)S(1)}, f32[32,1152]{1,0:T(8,128)S(1)}, u32[]{:S(2)}, u32[]{:S(2)}) collective-permute-start(f32[32,1152]{1,0:T(8,128)S(1)} %get-tuple-element.402.refs_1_), channel_id=1, source_target_pairs={{0,16},{1,9},{2,18},{3,11},{4,20},{5,13},{6,22},{7,15},{8,24},{9,1... | collective-permute-start | bytes 442376 | tf_op jit(solution)/shard_map/ppermute | solution.py:715
  127.8 10.5 %collective-permute-start.35 = (f32[32,1024]{1,0:T(8,128)S(1)}, f32[32,1024]{1,0:T(8,128)S(1)}, u32[]{:S(2)}, u32[]{:S(2)}) collective-permute-start(f32[32,1024]{1,0:T(8,128)S(1)} %get-tuple-element.401.refs_0_), channel_id=1, source_target_pairs={{0,4},{1,5},{2,6},{3,7},{4,0},{5,1},{6,2},{7,3},{8,12},{9,13},{10,... | collective-permute-start | bytes 393224 | tf_op jit(solution)/shard_map/ppermute | solution.py:715
  132.1 13.2 %collective-permute-start.40 = (f32[24,1152]{1,0:T(8,128)S(1)}, f32[24,1152]{1,0:T(8,128)S(1)}, u32[]{:S(2)}, u32[]{:S(2)}) collective-permute-start(f32[24,1152]{1,0:T(8,128)S(1)} %get-tuple-element.411.refs_0_), channel_id=1, source_target_pairs={{0,1},{1,0},{2,3},{3,2},{4,5},{5,4},{6,7},{7,6},{8,9},{9,8},{10,11... | collective-permute-start | bytes 331784 | tf_op jit(solution)/shard_map/ppermute | solution.py:687
  132.2 9.2 %collective-permute-start.34 = (f32[256,512]{1,0:T(8,128)S(1)}, f32[256,512]{1,0:T(8,128)S(1)}, u32[]{:S(2)}, u32[]{:S(2)}) collective-permute-start(f32[256,512]{1,0:T(8,128)S(1)} %get-tuple-element.400.refs_1_), channel_id=1, source_target_pairs={{0,8},{1,17},{2,10},{3,19},{4,12},{5,21},{6,14},{7,23},{8,0},{9,25... | collective-permute-start | bytes 1572872 | tf_op jit(solution)/shard_map/ppermute | solution.py:715
  133.2 8.4 %collective-permute-start.43 = (f32[32,1536]{1,0:T(8,128)S(1)}, f32[32,1536]{1,0:T(8,128)S(1)}, u32[]{:S(2)}, u32[]{:S(2)}) collective-permute-start(f32[32,1536]{1,0:T(8,128)S(1)} %get-tuple-element.414.refs_1_), channel_id=1, source_target_pairs={{0,2},{1,3},{2,0},{3,1},{4,6},{5,7},{6,4},{7,5},{8,10},{9,11},{10,... | collective-permute-start | bytes 589832 | tf_op jit(solution)/shard_map/ppermute | solution.py:715
  137.2 7.9 %collective-permute-start.42 = (f32[64,1152]{1,0:T(8,128)S(1)}, f32[64,1152]{1,0:T(8,128)S(1)}, u32[]{:S(2)}, u32[]{:S(2)}) collective-permute-start(f32[64,1152]{1,0:T(8,128)S(1)} %get-tuple-element.413.refs_1_), channel_id=1, source_target_pairs={{0,8},{1,17},{2,10},{3,19},{4,12},{5,21},{6,14},{7,23},{8,0},{9,25... | collective-permute-start | bytes 884744 | tf_op jit(solution)/shard_map/ppermute | solution.py:715
  138.4 6.8 %collective-permute-start.41 = (f32[32,1024]{1,0:T(8,128)S(1)}, f32[32,1024]{1,0:T(8,128)S(1)}, u32[]{:S(2)}, u32[]{:S(2)}) collective-permute-start(f32[32,1024]{1,0:T(8,128)S(1)} %get-tuple-element.412.refs_1_), channel_id=1, source_target_pairs={{0,2},{1,3},{2,0},{3,1},{4,6},{5,7},{6,4},{7,5},{8,10},{9,11},{10,... | collective-permute-start | bytes 393224 | tf_op jit(solution)/shard_map/ppermute | solution.py:715
  141.6 9.0 %collective-permute-start.45 = (f32[64,1536]{1,0:T(8,128)S(1)}, f32[64,1536]{1,0:T(8,128)S(1)}, u32[]{:S(2)}, u32[]{:S(2)}) collective-permute-start(f32[64,1536]{1,0:T(8,128)S(1)} %get-tuple-element.420.refs_1_), channel_id=1, source_target_pairs={{0,16},{1,9},{2,18},{3,11},{4,20},{5,13},{6,22},{7,15},{8,24},{9,1... | collective-permute-start | bytes 1179656 | tf_op jit(solution)/shard_map/ppermute | solution.py:715
  142.9 10.0 %collective-permute-start.39 = (f32[512,512]{1,0:T(8,128)S(1)}, f32[512,512]{1,0:T(8,128)S(1)}, u32[]{:S(2)}, u32[]{:S(2)}) collective-permute-start(f32[512,512]{1,0:T(8,128)S(1)} %get-tuple-element.410.refs_1_), channel_id=1, source_target_pairs={{0,1},{1,0},{2,3},{3,2},{4,5},{5,4},{6,7},{7,6},{8,9},{9,8},{10,11... | collective-permute-start | bytes 3145736 | tf_op jit(solution)/shard_map/ppermute | solution.py:687
  145.3 6.6 %collective-permute-start.44 = (f32[24,1152]{1,0:T(8,128)S(1)}, f32[24,1152]{1,0:T(8,128)S(1)}, u32[]{:S(2)}, u32[]{:S(2)}) collective-permute-start(f32[24,1152]{1,0:T(8,128)S(1)} %get-tuple-element.419.refs_0_), channel_id=1, source_target_pairs={{0,8},{1,17},{2,10},{3,19},{4,12},{5,21},{6,14},{7,23},{8,0},{9,25... | collective-permute-start | bytes 331784 | tf_op jit(solution)/shard_map/ppermute | solution.py:715
  145.8 10.7 %collective-permute-start.47 = (f32[64,1024]{1,0:T(8,128)S(1)}, f32[64,1024]{1,0:T(8,128)S(1)}, u32[]{:S(2)}, u32[]{:S(2)}) collective-permute-start(f32[64,1024]{1,0:T(8,128)S(1)} %get-tuple-element.428.refs_1_), channel_id=1, source_target_pairs={{0,16},{1,9},{2,18},{3,11},{4,20},{5,13},{6,22},{7,15},{8,24},{9,1... | collective-permute-start | bytes 786440 | tf_op jit(solution)/shard_map/ppermute | solution.py:715
  146.7 15.5 %collective-permute-start.50 = (f32[128,1152]{1,0:T(8,128)S(1)}, f32[128,1152]{1,0:T(8,128)S(1)}, u32[]{:S(2)}, u32[]{:S(2)}) collective-permute-start(f32[128,1152]{1,0:T(8,128)S(1)} %get-tuple-element.433.refs_1_), channel_id=1, source_target_pairs={{0,2},{1,3},{2,0},{3,1},{4,6},{5,7},{6,4},{7,5},{8,10},{9,11},{10,... | collective-permute-start | bytes 1769480 | tf_op jit(solution)/shard_map/ppermute | solution.py:715
  150.8 12.1 %collective-permute-start.49 = (f32[128,1536]{1,0:T(8,128)S(1)}, f32[128,1536]{1,0:T(8,128)S(1)}, u32[]{:S(2)}, u32[]{:S(2)}) collective-permute-start(f32[128,1536]{1,0:T(8,128)S(1)} %get-tuple-element.432.refs_1_), channel_id=1, source_target_pairs={{0,8},{1,17},{2,10},{3,19},{4,12},{5,21},{6,14},{7,23},{8,0},{9,25... | collective-permute-start | bytes 2359304 | tf_op jit(solution)/shard_map/ppermute | solution.py:715
  152.0 6.1 %collective-permute-start.46 = (f32[24,1152]{1,0:T(8,128)S(1)}, f32[24,1152]{1,0:T(8,128)S(1)}, u32[]{:S(2)}, u32[]{:S(2)}) collective-permute-start(f32[24,1152]{1,0:T(8,128)S(1)} %get-tuple-element.427.refs_0_), channel_id=1, source_target_pairs={{0,16},{1,9},{2,18},{3,11},{4,20},{5,13},{6,22},{7,15},{8,24},{9,1... | collective-permute-start | bytes 331784 | tf_op jit(solution)/shard_map/ppermute | solution.py:715
  158.1 5.4 %collective-permute-start.48 = (f32[24,1152]{1,0:T(8,128)S(1)}, f32[24,1152]{1,0:T(8,128)S(1)}, u32[]{:S(2)}, u32[]{:S(2)}) collective-permute-start(f32[24,1152]{1,0:T(8,128)S(1)} %get-tuple-element.431.refs_0_), channel_id=1, source_target_pairs={{0,2},{1,3},{2,0},{3,1},{4,6},{5,7},{6,4},{7,5},{8,10},{9,11},{10,... | collective-permute-start | bytes 331784 | tf_op jit(solution)/shard_map/ppermute | solution.py:715
  159.6 9.2 %collective-permute-start.52 = (f32[128,1024]{1,0:T(8,128)S(1)}, f32[128,1024]{1,0:T(8,128)S(1)}, u32[]{:S(2)}, u32[]{:S(2)}) collective-permute-start(f32[128,1024]{1,0:T(8,128)S(1)} %get-tuple-element.438.refs_1_), channel_id=1, source_target_pairs={{0,8},{1,17},{2,10},{3,19},{4,12},{5,21},{6,14},{7,23},{8,0},{9,25... | collective-permute-start | bytes 1572872 | tf_op jit(solution)/shard_map/ppermute | solution.py:715
  162.4 6.7 %collective-permute-start.55 = (f32[256,1152]{1,0:T(8,128)S(1)}, f32[256,1152]{1,0:T(8,128)S(1)}, u32[]{:S(2)}, u32[]{:S(2)}) collective-permute-start(f32[256,1152]{1,0:T(8,128)S(1)} %get-tuple-element.442.refs_1_), channel_id=1, source_target_pairs={{0,1},{1,0},{2,3},{3,2},{4,5},{5,4},{6,7},{7,6},{8,9},{9,8},{10,11... | collective-permute-start | bytes 3538952 | tf_op jit(solution)/shard_map/ppermute | solution.py:687
  163.0 8.0 %collective-permute-start.54 = (f32[256,1536]{1,0:T(8,128)S(1)}, f32[256,1536]{1,0:T(8,128)S(1)}, u32[]{:S(2)}, u32[]{:S(2)}) collective-permute-start(f32[256,1536]{1,0:T(8,128)S(1)} %get-tuple-element.441.refs_1_), channel_id=1, source_target_pairs={{0,1},{1,0},{2,3},{3,2},{4,5},{5,4},{6,7},{7,6},{8,9},{9,8},{10,11... | collective-permute-start | bytes 4718600 | tf_op jit(solution)/shard_map/ppermute | solution.py:687
  163.5 11.8 %collective-permute-start.51 = (f32[24,1152]{1,0:T(8,128)S(1)}, f32[24,1152]{1,0:T(8,128)S(1)}, u32[]{:S(2)}, u32[]{:S(2)}) collective-permute-start(f32[24,1152]{1,0:T(8,128)S(1)} %get-tuple-element.437.refs_0_), channel_id=1, source_target_pairs={{0,4},{1,5},{2,6},{3,7},{4,0},{5,1},{6,2},{7,3},{8,12},{9,13},{10,... | collective-permute-start | bytes 331784 | tf_op jit(solution)/shard_map/ppermute | solution.py:715
  168.9 4.4 %collective-permute-start.53 = (f32[256,1024]{1,0:T(8,128)S(1)}, f32[256,1024]{1,0:T(8,128)S(1)}, u32[]{:S(2)}, u32[]{:S(2)}) collective-permute-start(f32[256,1024]{1,0:T(8,128)S(1)} %get-tuple-element.440.refs_1_), channel_id=1, source_target_pairs={{0,1},{1,0},{2,3},{3,2},{4,5},{5,4},{6,7},{7,6},{8,9},{9,8},{10,11... | collective-permute-start | bytes 3145736 | tf_op jit(solution)/shard_map/ppermute | solution.py:687
  (14 other events, 19.7 us)

commit v5 on v4

--- a/solution.py
+++ b/solution.py
@@ -723,15 +723,16 @@
     (("1xy", "1yx"), "2"),
 )
 ORDER = (
-    "CCKC1C410C40KK1K21042K13",
-    "K03K12041K321432K1K03402",
-    "143502435250S35425304235",
+    "CCKC1C410C40KK1K2104231K",
+    "KK0431201K32143K2K103405",
+    "214302435250S35425304235",
     "3",
 )
 PACES = (
-    8, 8, 8, 8, 8, 8, 8, 8, 8, 8, 8, 8, 0, 0, 0, 0, 8, 8, 8, 8, 8, 8, 8, 12, 12, 12, 12, 8, 8, 8,
-    12, 4, 4, 10, 2, 2, 2, 2, 10, 10, 10, 8, 8, 8, 8, 8, 8, 8, 8, 8, 8, 8, 8, 8, 8, 8, 8, 8, 8, 8,
-    8, 8, 8, 8, 8, 8, 8, 8, 8, 8, 8, 8, 8, 12, 12, 12, 12, 8, 2, 0, 8, 8, 8, 12, 8, 0, 0, 0, 0, 8,
+    8, 8, 8, 8, 8, 8, 8, 8, 8, 8, 8, 8, 0, 0, 0, 0, 8, 8, 12, 12, 12, 12, 8, 3, 12, 12, 12, 8, 12,
+    12, 10, 10, 10, 10, 2, 1, 1, 1, 1, 10, 10, 8, 8, 8, 8, 1.5, 0.6, 3, 8, 8, 8, 8, 8, 8, 12, 8, 4,
+    2, 8, 8, 8, 0.3, 0.3, 12, 12, 12, 8, 8, 0, 3, 8, 8, 8, 12, 12, 6, 10, 8, 12, 0, 8, 8, 8, 12, 8,
+    0, 0, 0, 0, 8,
 )
 BITS = {"x": ("dp", 1), "y": ("dp", 2), "1": ("seq", 2), "2": ("seq", 4)}
 

time: 176 us -> 175 us (level)
  starting transfers between devices: 64.1 us -> 56.6 us
  waiting for transfers between devices: 44.9 us -> 51.2 us
    ppermute x38, waiting for transfers between devices: 32 us -> 40.9 us  [cross(): return lax.ppermute(a, ('dp', 'seq'), moves)]
    ppermute x38, starting transfers between devices: 48.6 us -> 40 us  [cross(): return lax.ppermute(a, ('dp', 'seq'), moves)]
    ppermute x2, waiting for transfers between devices: 12.1 us -> 9.57 us  [chip_after(): lax.ppermute(state, 'seq', [(i, i - 2 * chips) for i in range(2 * chips,...]
  transfers between devices with their start and end apart: 56 -> 56, of which waited for: 20 -> 22; matrix products, arithmetic and copies ran while one was open for 0% -> 0% of each run, Pallas kernels for 24% -> 25%
where the time goes in v5:
time: 175 us
  Pallas kernels  61.1 us (35%)
  starting transfers between devices  56.6 us (32%)
  waiting for transfers between devices  51.2 us (29%)
  local copies, waits for them, and re-layouts  2.96 us (2%)
    pallas_call x79, Pallas kernels, __call__(): pl.pallas_call(run, in_specs=specs, out_specs=[pl.BlockSpec(memory_space=...  61.1 us
    ppermute x38, waiting for transfers between devices, cross(): return lax.ppermute(a, ('dp', 'seq'), moves)  40.9 us
    ppermute x38, starting transfers between devices, cross(): return lax.ppermute(a, ('dp', 'seq'), moves)  40 us
    ppermute x3, starting transfers between devices, chip_before(): lax.ppermute(state, 'seq', [(i, i + 2 * chips) for i in range(count - 2 *...  10.6 us
    ppermute x2, waiting for transfers between devices, chip_after(): lax.ppermute(state, 'seq', [(i, i - 2 * chips) for i in range(2 * chips,...  9.57 us
  transfers between devices with their start and end apart: 56, of which 22 were waited for; matrix products, arithmetic and copies ran while one was open for 0% of the time, Pallas kernels for 25%

profile of v5, /device:TPU:0, one launch (start us, length us, event | category | flops | bytes accessed | tf_op | source)
XLA Modules:
  0.0 174.6 jit_solution(9067760613639782713)
XLA Ops:
  3.2 2.7 %norm_and_states.1 = (f32[4,512,128]{2,1,0:T(8,128)S(1)}, bf16[512,512]{1,0:T(8,128)(2,1)S(1)}, f32[16,8,512]{2,1,0:T(8,128)S(1)}, f32[16,512]{1,0:T(8,128)S(1)}...) custom-call(s32[1,3]{1,0:T(1,128)S(1)} %copy-done.11, bf16[512,512]{1,0:T(8,128)(2,1)S(1)} %copy-done.17, ...), custom_call_target="tpu_custom_call" | custom-call | flops 8000000000 | tf_op jit(solution)/shard_map/norm_and_states/pallas_call | solution.py:81
  7.9 4.8 %collective-permute-start.1 = (f32[16,512]{1,0:T(8,128)S(1)}, f32[16,512]{1,0:T(8,128)S(1)}, u32[]{:S(2)}, u32[]{:S(2)}) collective-permute-start(f32[16,512]{1,0:T(8,128)S(1)} %get-tuple-element.243), channel_id=1, source_target_pairs={{0,2},{1,3},{2,4},{3,5},{4,6},{5,7},{8,10},{9,11},{10,12},{11,13},... | collective-permute-start | bytes 98312 | tf_op jit(solution)/shard_map/ppermute | solution.py:692
  12.8 4.5 %collective-permute-start.2 = (f32[16,512]{1,0:T(8,128)S(1)}, f32[16,512]{1,0:T(8,128)S(1)}, u32[]{:S(2)}, u32[]{:S(2)}) collective-permute-start(f32[16,512]{1,0:T(8,128)S(1)} %get-tuple-element.243), channel_id=1, source_target_pairs={{0,4},{1,5},{2,6},{3,7},{8,12},{9,13},{10,14},{11,15},{16,20},{17,... | collective-permute-start | bytes 98312 | tf_op jit(solution)/shard_map/ppermute | solution.py:692
  17.3 1.3 collective-permute-start.3
  18.6 2.3 %local_average.1 = (f32[4,64,8,128]{3,2,1,0:T(8,128)S(1)}, f32[8,128]{1,0:T(8,128)S(1)}) custom-call(f32[4,64,8,128]{3,2,1,0:T(8,128)S(1)} %get-tuple-element.244.refs_0_.refs_9_, f32[16,8,512]{2,1,0:T(8,128)S(1)} %get-tuple-element.245.refs_1_.refs_11_, f32[16,512]{1,0:T(8,128)S(1)} %get-tuple-element.465.refs_4_.refs_2_.refs_6_.refs_3_, ...), custom_call_target="tpu_custom_call" | custom-call | flops 8000000000 | tf_op jit(solution)/shard_map/local_average/pallas_call | solution.py:81
  22.0 2.7 %carried_average.1 = (bf16[512,512]{1,0:T(8,128)(2,1)S(1)}, f32[512,512]{1,0:T(8,128)S(1)}, f32[16,8,512]{2,1,0:T(8,128)S(1)}, f32[8,128]{1,0:T(8,128)S(1)}) custom-call(s32[5]{0:T(128)S(1)} %pad_add_fusion.refs_0_, f32[16,512]{1,0:T(8,128)S(1)} %collective-permute-done.refs_2_.refs_1_, f32[16,512]{1,0:T(8,128)S(1)} %collective-permute-done.1.refs_2_, ...), custom_call_target="tpu_custom_call" | custom-call | flops 8000000000 | tf_op jit(solution)/shard_map/carried_average/pallas_call | solution.py:81
  24.8 1.4 mix.1
  26.3 2.1 %attention.1 = (f32[512,128]{1,0:T(8,128)S(1)}, f32[512,1024]{1,0:T(8,128)S(1)}, bf16[512,1024]{1,0:T(8,128)(2,1)S(1)}, f32[8,128]{1,0:T(8,128)S(1)}) custom-call(bf16[512,128]{1,0:T(8,128)(2,1)S(1)} %get-tuple-element.253.refs_0_.refs_2_, bf16[512,128]{1,0:T(8,128)(2,1)S(1)} %get-tuple-element.254.refs_1_.refs_3_, ...), custom_call_target="tpu_custom_call" | custom-call | flops 8000000000 | tf_op jit(solution)/shard_map/attention/pallas_call | solution.py:81
  28.5 1.4 hidden.1
  33.4 1.4 hidden_back.1
  34.9 1.3 reset_back.1
  36.2 1.6 ffn_in_grad.1
  37.8 2.1 %attention_back.1 = (bf16[512,1024]{1,0:T(8,128)(2,1)S(1)}, bf16[512,128]{1,0:T(8,128)(2,1)S(1)}, f32[8,128]{1,0:T(8,128)S(1)}, f32[8,128]{1,0:T(8,128)S(1)}) custom-call(bf16[512,1024]{1,0:T(8,128)(2,1)S(1)} %get-tuple-element.283.refs_0_, f32[512,128]{1,0:T(8,128)S(1)} %get-tuple-element.284.refs_1_, ...), custom_call_target="tpu_custom_call" | custom-call | tf_op jit(solution)/shard_map/attention_back/pallas_call | solution.py:81
  39.9 1.4 value_grad.1
  42.2 1.3 ffn_out_grad.1
  43.6 1.5 collective-permute-start.8
  45.2 2.2 %smooth_back.1 = (f32[4,512,128]{2,1,0:T(8,128)S(1)}, f32[4,512,128]{2,1,0:T(8,128)S(1)}, f32[1,512]{1,0:T(1,128)S(1)}, f32[8,128]{1,0:T(8,128)S(1)}) custom-call(bf16[512,512]{1,0:T(8,128)(2,1)S(1)} %get-tuple-element.276.refs_4_.refs_0_, bf16[512,128]{1,0:T(8,128)(2,1)S(1)} %get-tuple-element.290.refs_4_.refs_1_, ...), custom_call_target="tpu_custom_call" | custom-call | flops 12000000000 | tf_op jit(solution)/shard_map/smooth_back/pallas_call | solution.py:81
  47.9 2.5 %states_back.1 = (f32[16,8,512]{2,1,0:T(8,128)S(1)}, f32[16,512]{1,0:T(8,128)S(1)}, f32[4,64,8,128]{3,2,1,0:T(8,128)S(1)}, f32[8,128]{1,0:T(8,128)S(1)}) custom-call(s32[5]{0:T(128)S(1)} %pad_add_fusion.refs_0_, f32[4,512,128]{2,1,0:T(8,128)S(1)} %get-tuple-element.308.refs_1_, f32[16,512]{1,0:T(8,128)S(1)} %get-tuple-element.466.refs_3_.refs_5_.refs_2_.refs_4_, ...), custom_call_target="tpu_custom_call" | custom-call | flops 12000000000 | tf_op jit(solution)/shard_map/states_back/pallas_call | solution.py:81
  50.7 1.5 collective-permute-start.7
  52.8 1.3 collective-permute-start.11
  54.1 1.6 collective-permute-done.8.refs_2_
  55.8 1.6 collective-permute-start.10
  57.4 9.6 %collective-permute-done.11.refs_2_ = f32[16,512]{1,0:T(8,128)S(1)} collective-permute-done((f32[16,512]{1,0:T(8,128)S(1)}, f32[16,512]{1,0:T(8,128)S(1)}, u32[]{:S(2)}, u32[]{:S(2)}) %collective-permute-start.11) | collective-permute-done | bytes 32800 | tf_op jit(solution)/shard_map/ppermute | solution.py:697
  67.5 1.6 out_grad.1
  69.2 1.3 collective-permute-start.13
  70.8 1.6 collective-permute-start.12
  73.4 1.3 reset_grad.1
  74.8 3.9 %collective-permute-done.14.refs_1_ = f32[32,1536]{1,0:T(8,128)S(1)} collective-permute-done((f32[32,1536]{1,0:T(8,128)S(1)}, f32[32,1536]{1,0:T(8,128)S(1)}, u32[]{:S(2)}, u32[]{:S(2)}) %collective-permute-start.14) | collective-permute-done | bytes 196640 | tf_op jit(solution)/shard_map/ppermute | solution.py:715
  78.7 2.6 %collective-permute-start.19 = (f32[32,1536]{1,0:T(8,128)S(1)}, f32[32,1536]{1,0:T(8,128)S(1)}, u32[]{:S(2)}, u32[]{:S(2)}) collective-permute-start(f32[32,1536]{1,0:T(8,128)S(1)} %get-tuple-element.344.refs_0_), channel_id=1, source_target_pairs={{0,4},{1,5},{2,6},{3,7},{4,0},{5,1},{6,2},{7,3},{8,12},{9,13},{10,... | collective-permute-start | bytes 589832 | tf_op jit(solution)/shard_map/ppermute | solution.py:715
  81.3 1.2 collective-permute-start.18
  83.2 1.9 %state_back.4 = (f32[512,128]{1,0:T(8,128)S(1)}, f32[32,128]{1,0:T(8,128)S(1)}, f32[8,128]{1,0:T(8,128)S(1)}) custom-call(f32[4,64,8,128]{3,2,1,0:T(8,128)S(1)} %get-tuple-element.244.refs_0_.refs_9_, f32[4,64,8,128]{3,2,1,0:T(8,128)S(1)} %get-tuple-element.322.refs_1_, f32[16,8,512]{2,1,0:T(8,128)S(1)} %get-tuple-element.323.refs_2_, ...), custom_call_target="tpu_custom_call" | custom-call | flops 10000000000 | tf_op jit(solution)/shard_map/state_back/pallas_call | solution.py:81
  85.1 1.9 %state_back.5 = (f32[512,128]{1,0:T(8,128)S(1)}, f32[32,128]{1,0:T(8,128)S(1)}, f32[8,128]{1,0:T(8,128)S(1)}) custom-call(f32[4,64,8,128]{3,2,1,0:T(8,128)S(1)} %get-tuple-element.244.refs_0_.refs_9_, f32[4,64,8,128]{3,2,1,0:T(8,128)S(1)} %get-tuple-element.322.refs_1_, f32[16,8,512]{2,1,0:T(8,128)S(1)} %get-tuple-element.323.refs_2_, ...), custom_call_target="tpu_custom_call" | custom-call | flops 2000000000 | tf_op jit(solution)/shard_map/state_back/pallas_call | solution.py:81
  88.5 1.6 collective-permute-done.19.refs_1_
  90.3 1.5 collective-permute-start.26
  91.8 3.2 %collective-permute-done.18.refs_2_ = f32[128,1536]{1,0:T(8,128)S(1)} collective-permute-done((f32[128,1536]{1,0:T(8,128)S(1)}, f32[128,1536]{1,0:T(8,128)S(1)}, u32[]{:S(2)}, u32[]{:S(2)}) %collective-permute-start.18) | collective-permute-done | bytes 786464 | tf_op jit(solution)/shard_map/ppermute | solution.py:715
  95.1 1.5 collective-permute-start.25
  97.1 2.9 %collective-permute-done.23.refs_2_ = f32[32,1536]{1,0:T(8,128)S(1)} collective-permute-done((f32[32,1536]{1,0:T(8,128)S(1)}, f32[32,1536]{1,0:T(8,128)S(1)}, u32[]{:S(2)}, u32[]{:S(2)}) %collective-permute-start.23) | collective-permute-done | bytes 196640 | tf_op jit(solution)/shard_map/ppermute | solution.py:715
  100.1 1.5 collective-permute-start.24
  101.6 1.8 %state_back.6 = (f32[512,128]{1,0:T(8,128)S(1)}, f32[32,128]{1,0:T(8,128)S(1)}, f32[8,128]{1,0:T(8,128)S(1)}) custom-call(f32[4,64,8,128]{3,2,1,0:T(8,128)S(1)} %get-tuple-element.244.refs_0_.refs_9_, f32[4,64,8,128]{3,2,1,0:T(8,128)S(1)} %get-tuple-element.322.refs_1_, f32[16,8,512]{2,1,0:T(8,128)S(1)} %get-tuple-element.323.refs_2_, ...), custom_call_target="tpu_custom_call" | custom-call | flops 8000000000 | tf_op jit(solution)/shard_map/state_back/pallas_call | solution.py:81
  103.4 2.8 %collective-permute-done.26.refs_2_ = f32[128,1024]{1,0:T(8,128)S(1)} collective-permute-done((f32[128,1024]{1,0:T(8,128)S(1)}, f32[128,1024]{1,0:T(8,128)S(1)}, u32[]{:S(2)}, u32[]{:S(2)}) %collective-permute-start.26) | collective-permute-done | bytes 524320 | tf_op jit(solution)/shard_map/ppermute | solution.py:715
  107.3 1.5 collective-permute-start.30
  110.8 2.8 %collective-permute-done.28.refs_2_ = f32[64,1024]{1,0:T(8,128)S(1)} collective-permute-done((f32[64,1024]{1,0:T(8,128)S(1)}, f32[64,1024]{1,0:T(8,128)S(1)}, u32[]{:S(2)}, u32[]{:S(2)}) %collective-permute-start.28) | collective-permute-done | bytes 262176 | tf_op jit(solution)/shard_map/ppermute | solution.py:715
  113.7 1.9 %state_back.7 = (f32[512,128]{1,0:T(8,128)S(1)}, f32[32,128]{1,0:T(8,128)S(1)}, f32[8,128]{1,0:T(8,128)S(1)}) custom-call(f32[4,64,8,128]{3,2,1,0:T(8,128)S(1)} %get-tuple-element.244.refs_0_.refs_9_, f32[4,64,8,128]{3,2,1,0:T(8,128)S(1)} %get-tuple-element.322.refs_1_, f32[16,8,512]{2,1,0:T(8,128)S(1)} %get-tuple-element.323.refs_2_, ...), custom_call_target="tpu_custom_call" | custom-call | flops 8000000000 | tf_op jit(solution)/shard_map/state_back/pallas_call | solution.py:81
  116.3 2.0 %collective-permute-start.38 = (f32[32,1536]{1,0:T(8,128)S(1)}, f32[32,1536]{1,0:T(8,128)S(1)}, u32[]{:S(2)}, u32[]{:S(2)}) collective-permute-start(f32[32,1536]{1,0:T(8,128)S(1)} %get-tuple-element.404.refs_0_), channel_id=1, source_target_pairs={{0,4},{1,5},{2,6},{3,7},{4,0},{5,1},{6,2},{7,3},{8,12},{9,13},{10,... | collective-permute-start | bytes 589832 | tf_op jit(solution)/shard_map/ppermute | solution.py:715
  118.4 1.8 %norm_back.1 = (f32[512,512]{1,0:T(8,128)}, f32[24,1152]{1,0:T(8,128)S(1)}, f32[8,128]{1,0:T(8,128)S(1)}) custom-call(f32[512,128]{1,0:T(8,128)S(1)} %get-tuple-element.367.refs_0_, f32[512,128]{1,0:T(8,128)S(1)} %get-tuple-element.368.refs_1_, f32[512,128]{1,0:T(8,128)S(1)} %get-tuple-element.369.refs_2_, f32[512,128]{1,0:T(8,128)S(1)} %get-tuple-element.377.refs_3_, ...), custom_call_target="tpu_custom_call" | custom-call | flops 8000000000 | tf_op jit(solution)/shard_map/norm_back/pallas_call | solution.py:81
  122.5 1.5 collective-permute-start.36
  124.0 4.0 %collective-permute-done.31.refs_2_ = f32[128,512]{1,0:T(8,128)S(1)} collective-permute-done((f32[128,512]{1,0:T(8,128)S(1)}, f32[128,512]{1,0:T(8,128)S(1)}, u32[]{:S(2)}, u32[]{:S(2)}) %collective-permute-start.31) | collective-permute-done | bytes 262176 | tf_op jit(solution)/shard_map/ppermute | solution.py:715
  128.0 1.9 %collective-permute-start.35 = (f32[32,1024]{1,0:T(8,128)S(1)}, f32[32,1024]{1,0:T(8,128)S(1)}, u32[]{:S(2)}, u32[]{:S(2)}) collective-permute-start(f32[32,1024]{1,0:T(8,128)S(1)} %get-tuple-element.401.refs_0_), channel_id=1, source_target_pairs={{0,4},{1,5},{2,6},{3,7},{4,0},{5,1},{6,2},{7,3},{8,12},{9,13},{10,... | collective-permute-start | bytes 393224 | tf_op jit(solution)/shard_map/ppermute | solution.py:715
  130.0 1.4 collective-permute-start.34
  131.7 2.2 %ffn_in_out.1 = (f32[512,1024]{1,0:T(8,128)}, f32[512,2176]{1,0:T(8,128)}, f32[8,128]{1,0:T(8,128)S(1)}) custom-call(s32[5]{0:T(128)S(1)} %pad_add_fusion.refs_0_, f32[256,1536]{1,0:T(8,128)S(1)} %get-tuple-element.403.refs_1_, f32[256,1536]{1,0:T(8,128)S(1)} %collective-permute-done.37.refs_2_, f32[8,128]{1,0:T(8,128)S(1)} %get-tuple-element.406.refs_3_), custom_call_target="tpu_custom_call" | custom-call | flops 2000000000 | tf_op jit(solution)/shard_map/ffn_in_out/pallas_call | solution.py:81
  134.0 1.5 collective-permute-start.42
  136.7 2.6 %collective-permute-done.34.refs_2_ = f32[256,512]{1,0:T(8,128)S(1)} collective-permute-done((f32[256,512]{1,0:T(8,128)S(1)}, f32[256,512]{1,0:T(8,128)S(1)}, u32[]{:S(2)}, u32[]{:S(2)}) %collective-permute-start.34) | collective-permute-done | bytes 524320 | tf_op jit(solution)/shard_map/ppermute | solution.py:715
  141.0 3.0 %collective-permute-done.42.refs_2_ = f32[64,1152]{1,0:T(8,128)S(1)} collective-permute-done((f32[64,1152]{1,0:T(8,128)S(1)}, f32[64,1152]{1,0:T(8,128)S(1)}, u32[]{:S(2)}, u32[]{:S(2)}) %collective-permute-start.42) | collective-permute-done | bytes 294944 | tf_op jit(solution)/shard_map/ppermute | solution.py:715
  144.2 2.0 %collective-permute-start.44 = (f32[24,1152]{1,0:T(8,128)S(1)}, f32[24,1152]{1,0:T(8,128)S(1)}, u32[]{:S(2)}, u32[]{:S(2)}) collective-permute-start(f32[24,1152]{1,0:T(8,128)S(1)} %get-tuple-element.419.refs_0_), channel_id=1, source_target_pairs={{0,8},{1,17},{2,10},{3,19},{4,12},{5,21},{6,14},{7,23},{8,0},{9,25... | collective-permute-start | bytes 331784 | tf_op jit(solution)/shard_map/ppermute | solution.py:715
  147.1 1.7 collective-permute-done.45.refs_2_
  150.3 2.2 %collective-permute-start.46 = (f32[24,1152]{1,0:T(8,128)S(1)}, f32[24,1152]{1,0:T(8,128)S(1)}, u32[]{:S(2)}, u32[]{:S(2)}) collective-permute-start(f32[24,1152]{1,0:T(8,128)S(1)} %get-tuple-element.427.refs_0_), channel_id=1, source_target_pairs={{0,16},{1,9},{2,18},{3,11},{4,20},{5,13},{6,22},{7,15},{8,24},{9,1... | collective-permute-start | bytes 331784 | tf_op jit(solution)/shard_map/ppermute | solution.py:715
  152.4 1.9 %ffn_out_out.1 = (f32[1024,512]{1,0:T(8,128)}, f32[8,128]{1,0:T(8,128)S(1)}) custom-call(s32[5]{0:T(128)S(1)} %pad_add_fusion.refs_0_, f32[512,512]{1,0:T(8,128)S(1)} %get-tuple-element.410.refs_1_, f32[512,512]{1,0:T(8,128)S(1)} %collective-permute-done.39.refs_2_, f32[8,128]{1,0:T(8,128)S(1)} %get-tuple-element.423.refs_3_), custom_call_target="tpu_custom_call" | custom-call | flops 8000000000 | tf_op jit(solution)/shard_map/ffn_out_out/pallas_call | solution.py:81
  154.4 1.7 block_out.1
  156.1 1.6 collective-permute-done.46.refs_1_
  159.7 1.3 collective-permute-done.49.refs_2_
  162.6 4.4 %collective-permute-done.52.refs_2_ = f32[128,1024]{1,0:T(8,128)S(1)} collective-permute-done((f32[128,1024]{1,0:T(8,128)S(1)}, f32[128,1024]{1,0:T(8,128)S(1)}, u32[]{:S(2)}, u32[]{:S(2)}) %collective-permute-start.52) | collective-permute-done | bytes 524320 | tf_op jit(solution)/shard_map/ppermute | solution.py:715
  167.6 2.0 %value_out.1 = (f32[512,1024]{1,0:T(8,128)}, f32[512,2176]{1,0:T(8,128)}, f32[8,128]{1,0:T(8,128)S(1)}) custom-call(s32[5]{0:T(128)S(1)} %pad_add_fusion.refs_0_, f32[256,1152]{1,0:T(8,128)S(1)} %get-tuple-element.442.refs_1_, f32[256,1152]{1,0:T(8,128)S(1)} %collective-permute-done.55.refs_2_, ...), custom_call_target="tpu_custom_call", output_to_operand_aliasing={{1}: (3, {})} | custom-call | flops 6000000000 | tf_op jit(solution)/shard_map/value_out/pallas_call | solution.py:81
  169.6 2.3 %out_out.1 = (f32[1024,512]{1,0:T(8,128)}, f32[512,2176]{1,0:T(8,128)}, f32[8,128]{1,0:T(8,128)S(1)}) custom-call(s32[5]{0:T(128)S(1)} %pad_add_fusion.refs_0_, f32[256,1536]{1,0:T(8,128)S(1)} %get-tuple-element.441.refs_1_, f32[256,1536]{1,0:T(8,128)S(1)} %collective-permute-done.54.refs_2_, ...), custom_call_target="tpu_custom_call", output_to_operand_aliasing={{1}: (3, {})} | custom-call | flops 10000000000 | tf_op jit(solution)/shard_map/out_out/pallas_call | solution.py:81
  171.9 1.9 %reset_out.1 = (f32[512,2176]{1,0:T(8,128)}, f32[8,128]{1,0:T(8,128)S(1)}) custom-call(s32[5]{0:T(128)S(1)} %pad_add_fusion.refs_0_, f32[256,1024]{1,0:T(8,128)S(1)} %get-tuple-element.440.refs_1_, f32[256,1024]{1,0:T(8,128)S(1)} %collective-permute-done.53.refs_2_, f32[512,2176]{1,0:T(8,128)} %get-tuple-element.447.refs_3_, ...), custom_call_target="tpu_custom_call", output_to_operand_aliasing={{0}: (3, {})} | custom-call | flops 8000000000 | tf_op jit(solution)/shard_map/reset_out/pallas_call | solution.py:81
  (177 shorter events, 33.9 us)
Async XLA Ops:
  3.2 3.3 %copy-start.12 = (s32[1,3]{1,0:T(1,128)S(1)}, s32[1,3]{1,0:T(1,128)}, u32[]{:S(2)}) copy-start(s32[1,3]{1,0:T(1,128)} %refs_0_.2) | copy-start | bytes 40
  6.0 1.4 collective-permute-start
  7.9 14.0 %collective-permute-start.1 = (f32[16,512]{1,0:T(8,128)S(1)}, f32[16,512]{1,0:T(8,128)S(1)}, u32[]{:S(2)}, u32[]{:S(2)}) collective-permute-start(f32[16,512]{1,0:T(8,128)S(1)} %get-tuple-element.243), channel_id=1, source_target_pairs={{0,2},{1,3},{2,4},{3,5},{4,6},{5,7},{8,10},{9,11},{10,12},{11,13},... | collective-permute-start | bytes 98312 | tf_op jit(solution)/shard_map/ppermute | solution.py:692
  12.8 9.2 %collective-permute-start.2 = (f32[16,512]{1,0:T(8,128)S(1)}, f32[16,512]{1,0:T(8,128)S(1)}, u32[]{:S(2)}, u32[]{:S(2)}) collective-permute-start(f32[16,512]{1,0:T(8,128)S(1)} %get-tuple-element.243), channel_id=1, source_target_pairs={{0,4},{1,5},{2,6},{3,7},{8,12},{9,13},{10,14},{11,15},{16,20},{17,... | collective-permute-start | bytes 98312 | tf_op jit(solution)/shard_map/ppermute | solution.py:692
  17.3 4.7 %collective-permute-start.3 = (f32[16,512]{1,0:T(8,128)S(1)}, f32[16,512]{1,0:T(8,128)S(1)}, u32[]{:S(2)}, u32[]{:S(2)}) collective-permute-start(f32[16,512]{1,0:T(8,128)S(1)} %get-tuple-element.243), channel_id=1, source_target_pairs={{0,6},{1,7},{8,14},{9,15},{16,22},{17,23},{24,30},{25,31}} | collective-permute-start | bytes 98312 | tf_op jit(solution)/shard_map/ppermute | solution.py:692
  18.6 2.3 %copy-start.15 = (bf16[512,1024]{1,0:T(8,128)(2,1)S(1)}, bf16[512,1024]{1,0:T(8,128)(2,1)}, u32[]{:S(2)}) copy-start(bf16[512,1024]{1,0:T(8,128)(2,1)} %refs_6_.1) | copy-start | bytes 3145732
  22.0 2.8 %copy-start.10 = (f32[2,128]{1,0:T(2,128)S(1)}, f32[2,128]{1,0:T(2,128)}, u32[]{:S(2)}) copy-start(f32[2,128]{1,0:T(2,128)} %refs_8_.2) | copy-start | bytes 3076
  22.0 2.8 %copy-start.13 = (bf16[512,2176]{1,0:T(8,128)(2,1)S(1)}, bf16[512,2176]{1,0:T(8,128)(2,1)}, u32[]{:S(2)}) copy-start(bf16[512,2176]{1,0:T(8,128)(2,1)} %refs_5_.3) | copy-start | bytes 6684676
  22.0 2.8 %copy-start.22 = (f32[2,128]{1,0:T(2,128)S(1)}, f32[2,128]{1,0:T(2,128)}, u32[]{:S(2)}) copy-start(f32[2,128]{1,0:T(2,128)} %refs_3_.1) | copy-start | bytes 3076
  26.3 2.2 %copy-start = (bf16[1024,512]{1,0:T(8,128)(2,1)S(1)}, bf16[1024,512]{1,0:T(8,128)(2,1)}, u32[]{:S(2)}) copy-start(bf16[1024,512]{1,0:T(8,128)(2,1)} %refs_1_.15) | copy-start | bytes 3145732
  26.3 2.2 %copy-start.18 = (bf16[512,512]{1,0:T(8,128)(2,1)S(1)}, bf16[512,512]{1,0:T(8,128)(2,1)}, u32[]{:S(2)}) copy-start(bf16[512,512]{1,0:T(8,128)(2,1)} %refs_8_.3) | copy-start | bytes 1572868
  30.9 11.3 %copy-start.3 = (bf16[512,1024]{1,0:T(8,128)(2,1)}, bf16[512,1024]{1,0:T(8,128)(2,1)S(1)}, u32[]{:S(2)}) copy-start(bf16[512,1024]{1,0:T(8,128)(2,1)S(1)} %get-tuple-element.265.refs_1_) | copy-start | bytes 3145732
  37.7 4.1 %collective-permute-start.4 = (f32[256,1536]{1,0:T(8,128)S(1)}, f32[256,1536]{1,0:T(8,128)S(1)}, u32[]{:S(2)}, u32[]{:S(2)}) collective-permute-start(f32[256,1536]{1,0:T(8,128)S(1)} %get-tuple-element.282), channel_id=1, source_target_pairs={{0,1},{1,0},{2,3},{3,2},{4,5},{5,4},{6,7},{7,6},{8,9},{9,8},{10,11... | collective-permute-start | bytes 4718600 | tf_op jit(solution)/shard_map/ppermute | solution.py:687
  41.3 6.1 %collective-permute-start.6 = (f32[256,1152]{1,0:T(8,128)S(1)}, f32[256,1152]{1,0:T(8,128)S(1)}, u32[]{:S(2)}, u32[]{:S(2)}) collective-permute-start(f32[256,1152]{1,0:T(8,128)S(1)} %get-tuple-element.297), channel_id=1, source_target_pairs={{0,1},{1,0},{2,3},{3,2},{4,5},{5,4},{6,7},{7,6},{8,9},{9,8},{10,11... | collective-permute-start | bytes 3538952 | tf_op jit(solution)/shard_map/ppermute | solution.py:687
  43.5 4.2 %collective-permute-start.5 = (f32[512,512]{1,0:T(8,128)S(1)}, f32[512,512]{1,0:T(8,128)S(1)}, u32[]{:S(2)}, u32[]{:S(2)}) collective-permute-start(f32[512,512]{1,0:T(8,128)S(1)} %get-tuple-element.295), channel_id=1, source_target_pairs={{0,1},{1,0},{2,3},{3,2},{4,5},{5,4},{6,7},{7,6},{8,9},{9,8},{10,11... | collective-permute-start | bytes 3145736 | tf_op jit(solution)/shard_map/ppermute | solution.py:687
  43.6 12.0 %collective-permute-start.8 = (f32[128,1536]{1,0:T(8,128)S(1)}, f32[128,1536]{1,0:T(8,128)S(1)}, u32[]{:S(2)}, u32[]{:S(2)}) collective-permute-start(f32[128,1536]{1,0:T(8,128)S(1)} %get-tuple-element.307), channel_id=1, source_target_pairs={{0,8},{1,17},{2,10},{3,19},{4,12},{5,21},{6,14},{7,23},{8,0},{9,25... | collective-permute-start | bytes 2359304 | tf_op jit(solution)/shard_map/ppermute | solution.py:715
  50.5 1.7 collective-permute-start.9
  50.7 21.7 %collective-permute-start.16 = (f32[128,1152]{1,0:T(8,128)S(1)}, f32[128,1152]{1,0:T(8,128)S(1)}, u32[]{:S(2)}, u32[]{:S(2)}) collective-permute-start(f32[128,1152]{1,0:T(8,128)S(1)} %get-tuple-element.331), channel_id=1, source_target_pairs={{0,2},{1,3},{2,0},{3,1},{4,6},{5,7},{6,4},{7,5},{8,10},{9,11},{10,... | collective-permute-start | bytes 1769480 | tf_op jit(solution)/shard_map/ppermute | solution.py:715
  50.7 20.0 %collective-permute-start.7 = (f32[256,512]{1,0:T(8,128)S(1)}, f32[256,512]{1,0:T(8,128)S(1)}, u32[]{:S(2)}, u32[]{:S(2)}) collective-permute-start(f32[256,512]{1,0:T(8,128)S(1)} %get-tuple-element.305), channel_id=1, source_target_pairs={{0,8},{1,17},{2,10},{3,19},{4,12},{5,21},{6,14},{7,23},{8,0},{9,25... | collective-permute-start | bytes 1572872 | tf_op jit(solution)/shard_map/ppermute | solution.py:715
  52.8 14.2 %collective-permute-start.11 = (f32[16,512]{1,0:T(8,128)S(1)}, f32[16,512]{1,0:T(8,128)S(1)}, u32[]{:S(2)}, u32[]{:S(2)}) collective-permute-start(f32[16,512]{1,0:T(8,128)S(1)} %get-tuple-element.315.refs_1_), channel_id=1, source_target_pairs={{2,0},{3,1},{4,2},{5,3},{6,4},{7,5},{10,8},{11,9},{12,10},{13,11},... | collective-permute-start | bytes 98312 | tf_op jit(solution)/shard_map/ppermute | solution.py:697
  55.8 14.7 %collective-permute-start.10 = (f32[64,1536]{1,0:T(8,128)S(1)}, f32[64,1536]{1,0:T(8,128)S(1)}, u32[]{:S(2)}, u32[]{:S(2)}) collective-permute-start(f32[64,1536]{1,0:T(8,128)S(1)} %get-tuple-element.314), channel_id=1, source_target_pairs={{0,16},{1,9},{2,18},{3,11},{4,20},{5,13},{6,22},{7,15},{8,24},{9,1... | collective-permute-start | bytes 1179656 | tf_op jit(solution)/shard_map/ppermute | solution.py:715
  69.1 4.0 %collective-permute-start.15 = (f32[256,1536]{1,0:T(8,128)S(1)}, f32[256,1536]{1,0:T(8,128)S(1)}, u32[]{:S(2)}, u32[]{:S(2)}) collective-permute-start(f32[256,1536]{1,0:T(8,128)S(1)} %get-tuple-element.329), channel_id=1, source_target_pairs={{0,1},{1,0},{2,3},{3,2},{4,5},{5,4},{6,7},{7,6},{8,9},{9,8},{10,11... | collective-permute-start | bytes 4718600 | tf_op jit(solution)/shard_map/ppermute | solution.py:687
  69.2 12.1 %collective-permute-start.13 = (f32[16,512]{1,0:T(8,128)S(1)}, f32[16,512]{1,0:T(8,128)S(1)}, u32[]{:S(2)}, u32[]{:S(2)}) collective-permute-start(f32[16,512]{1,0:T(8,128)S(1)} %get-tuple-element.324), channel_id=1, source_target_pairs={{4,0},{5,1},{6,2},{7,3},{12,8},{13,9},{14,10},{15,11},{20,16},{21,... | collective-permute-start | bytes 98312 | tf_op jit(solution)/shard_map/ppermute | solution.py:697
  70.6 8.1 %collective-permute-start.14 = (f32[32,1536]{1,0:T(8,128)S(1)}, f32[32,1536]{1,0:T(8,128)S(1)}, u32[]{:S(2)}, u32[]{:S(2)}) collective-permute-start(f32[32,1536]{1,0:T(8,128)S(1)} %get-tuple-element.327), channel_id=1, source_target_pairs={{0,2},{1,3},{2,0},{3,1},{4,6},{5,7},{6,4},{7,5},{8,10},{9,11},{10,... | collective-permute-start | bytes 589832 | tf_op jit(solution)/shard_map/ppermute | solution.py:715
  70.8 16.1 %collective-permute-start.12 = (f32[128,512]{1,0:T(8,128)S(1)}, f32[128,512]{1,0:T(8,128)S(1)}, u32[]{:S(2)}, u32[]{:S(2)}) collective-permute-start(f32[128,512]{1,0:T(8,128)S(1)} %get-tuple-element.321), channel_id=1, source_target_pairs={{0,16},{1,9},{2,18},{3,11},{4,20},{5,13},{6,22},{7,15},{8,24},{9,1... | collective-permute-start | bytes 786440 | tf_op jit(solution)/shard_map/ppermute | solution.py:715
  72.5 14.8 %collective-permute-start.21 = (f32[64,1152]{1,0:T(8,128)S(1)}, f32[64,1152]{1,0:T(8,128)S(1)}, u32[]{:S(2)}, u32[]{:S(2)}) collective-permute-start(f32[64,1152]{1,0:T(8,128)S(1)} %get-tuple-element.348), channel_id=1, source_target_pairs={{0,8},{1,17},{2,10},{3,19},{4,12},{5,21},{6,14},{7,23},{8,0},{9,25... | collective-permute-start | bytes 884744 | tf_op jit(solution)/shard_map/ppermute | solution.py:715
  74.7 13.6 %collective-permute-start.20 = (f32[256,1024]{1,0:T(8,128)S(1)}, f32[256,1024]{1,0:T(8,128)S(1)}, u32[]{:S(2)}, u32[]{:S(2)}) collective-permute-start(f32[256,1024]{1,0:T(8,128)S(1)} %get-tuple-element.346), channel_id=1, source_target_pairs={{0,1},{1,0},{2,3},{3,2},{4,5},{5,4},{6,7},{7,6},{8,9},{9,8},{10,11... | collective-permute-start | bytes 3145736 | tf_op jit(solution)/shard_map/ppermute | solution.py:687
  78.7 11.4 %collective-permute-start.19 = (f32[32,1536]{1,0:T(8,128)S(1)}, f32[32,1536]{1,0:T(8,128)S(1)}, u32[]{:S(2)}, u32[]{:S(2)}) collective-permute-start(f32[32,1536]{1,0:T(8,128)S(1)} %get-tuple-element.344.refs_0_), channel_id=1, source_target_pairs={{0,4},{1,5},{2,6},{3,7},{4,0},{5,1},{6,2},{7,3},{8,12},{9,13},{10,... | collective-permute-start | bytes 589832 | tf_op jit(solution)/shard_map/ppermute | solution.py:715
  81.3 13.7 %collective-permute-start.18 = (f32[128,1536]{1,0:T(8,128)S(1)}, f32[128,1536]{1,0:T(8,128)S(1)}, u32[]{:S(2)}, u32[]{:S(2)}) collective-permute-start(f32[128,1536]{1,0:T(8,128)S(1)} %get-tuple-element.343), channel_id=1, source_target_pairs={{0,8},{1,17},{2,10},{3,19},{4,12},{5,21},{6,14},{7,23},{8,0},{9,25... | collective-permute-start | bytes 2359304 | tf_op jit(solution)/shard_map/ppermute | solution.py:715
  87.0 9.7 %collective-permute-start.17 = (f32[128,512]{1,0:T(8,128)S(1)}, f32[128,512]{1,0:T(8,128)S(1)}, u32[]{:S(2)}, u32[]{:S(2)}) collective-permute-start(f32[128,512]{1,0:T(8,128)S(1)} %get-tuple-element.341.refs_0_), channel_id=1, source_target_pairs={{0,2},{1,3},{2,0},{3,1},{4,6},{5,7},{6,4},{7,5},{8,10},{9,11},{10,... | collective-permute-start | bytes 786440 | tf_op jit(solution)/shard_map/ppermute | solution.py:715
  87.4 22.2 %collective-permute-start.29 = (f32[32,1152]{1,0:T(8,128)S(1)}, f32[32,1152]{1,0:T(8,128)S(1)}, u32[]{:S(2)}, u32[]{:S(2)}) collective-permute-start(f32[32,1152]{1,0:T(8,128)S(1)} %get-tuple-element.373), channel_id=1, source_target_pairs={{0,16},{1,9},{2,18},{3,11},{4,20},{5,13},{6,22},{7,15},{8,24},{9,1... | collective-permute-start | bytes 442376 | tf_op jit(solution)/shard_map/ppermute | solution.py:715
  90.1 9.9 %collective-permute-start.23 = (f32[32,1536]{1,0:T(8,128)S(1)}, f32[32,1536]{1,0:T(8,128)S(1)}, u32[]{:S(2)}, u32[]{:S(2)}) collective-permute-start(f32[32,1536]{1,0:T(8,128)S(1)} %get-tuple-element.355.refs_1_), channel_id=1, source_target_pairs={{0,2},{1,3},{2,0},{3,1},{4,6},{5,7},{6,4},{7,5},{8,10},{9,11},{10,... | collective-permute-start | bytes 589832 | tf_op jit(solution)/shard_map/ppermute | solution.py:715
  90.3 15.9 %collective-permute-start.26 = (f32[128,1024]{1,0:T(8,128)S(1)}, f32[128,1024]{1,0:T(8,128)S(1)}, u32[]{:S(2)}, u32[]{:S(2)}) collective-permute-start(f32[128,1024]{1,0:T(8,128)S(1)} %get-tuple-element.361), channel_id=1, source_target_pairs={{0,8},{1,17},{2,10},{3,19},{4,12},{5,21},{6,14},{7,23},{8,0},{9,25... | collective-permute-start | bytes 1572872 | tf_op jit(solution)/shard_map/ppermute | solution.py:715
  95.1 12.1 %collective-permute-start.25 = (f32[64,1536]{1,0:T(8,128)S(1)}, f32[64,1536]{1,0:T(8,128)S(1)}, u32[]{:S(2)}, u32[]{:S(2)}) collective-permute-start(f32[64,1536]{1,0:T(8,128)S(1)} %get-tuple-element.359), channel_id=1, source_target_pairs={{0,16},{1,9},{2,18},{3,11},{4,20},{5,13},{6,22},{7,15},{8,24},{9,1... | collective-permute-start | bytes 1179656 | tf_op jit(solution)/shard_map/ppermute | solution.py:715
  96.7 24.8 %collective-permute-start.22 = (f32[128,512]{1,0:T(8,128)S(1)}, f32[128,512]{1,0:T(8,128)S(1)}, u32[]{:S(2)}, u32[]{:S(2)}) collective-permute-start(f32[128,512]{1,0:T(8,128)S(1)} %get-tuple-element.354.refs_0_), channel_id=1, source_target_pairs={{0,4},{1,5},{2,6},{3,7},{4,0},{5,1},{6,2},{7,3},{8,12},{9,13},{10,... | collective-permute-start | bytes 786440 | tf_op jit(solution)/shard_map/ppermute | solution.py:715
  100.1 8.8 %collective-permute-start.24 = (f32[64,1536]{1,0:T(8,128)S(1)}, f32[64,1536]{1,0:T(8,128)S(1)}, u32[]{:S(2)}, u32[]{:S(2)}) collective-permute-start(f32[64,1536]{1,0:T(8,128)S(1)} %get-tuple-element.357.refs_1_), channel_id=1, source_target_pairs={{0,16},{1,9},{2,18},{3,11},{4,20},{5,13},{6,22},{7,15},{8,24},{9,1... | collective-permute-start | bytes 1179656 | tf_op jit(solution)/shard_map/ppermute | solution.py:715
  106.3 7.3 %collective-permute-start.28 = (f32[64,1024]{1,0:T(8,128)S(1)}, f32[64,1024]{1,0:T(8,128)S(1)}, u32[]{:S(2)}, u32[]{:S(2)}) collective-permute-start(f32[64,1024]{1,0:T(8,128)S(1)} %get-tuple-element.371), channel_id=1, source_target_pairs={{0,16},{1,9},{2,18},{3,11},{4,20},{5,13},{6,22},{7,15},{8,24},{9,1... | collective-permute-start | bytes 786440 | tf_op jit(solution)/shard_map/ppermute | solution.py:715
  107.3 9.0 %collective-permute-start.30 = (f32[32,1536]{1,0:T(8,128)S(1)}, f32[32,1536]{1,0:T(8,128)S(1)}, u32[]{:S(2)}, u32[]{:S(2)}) collective-permute-start(f32[32,1536]{1,0:T(8,128)S(1)} %get-tuple-element.388), channel_id=1, source_target_pairs={{0,2},{1,3},{2,0},{3,1},{4,6},{5,7},{6,4},{7,5},{8,10},{9,11},{10,... | collective-permute-start | bytes 589832 | tf_op jit(solution)/shard_map/ppermute | solution.py:715
  109.0 12.1 %collective-permute-start.27 = (f32[128,1536]{1,0:T(8,128)S(1)}, f32[128,1536]{1,0:T(8,128)S(1)}, u32[]{:S(2)}, u32[]{:S(2)}) collective-permute-start(f32[128,1536]{1,0:T(8,128)S(1)} %get-tuple-element.366.refs_1_), channel_id=1, source_target_pairs={{0,8},{1,17},{2,10},{3,19},{4,12},{5,21},{6,14},{7,23},{8,0},{9,25... | collective-permute-start | bytes 2359304 | tf_op jit(solution)/shard_map/ppermute | solution.py:715
  109.6 12.8 %collective-permute-start.32 = (f32[32,1152]{1,0:T(8,128)S(1)}, f32[32,1152]{1,0:T(8,128)S(1)}, u32[]{:S(2)}, u32[]{:S(2)}) collective-permute-start(f32[32,1152]{1,0:T(8,128)S(1)} %get-tuple-element.394.refs_0_), channel_id=1, source_target_pairs={{0,4},{1,5},{2,6},{3,7},{4,0},{5,1},{6,2},{7,3},{8,12},{9,13},{10,... | collective-permute-start | bytes 442376 | tf_op jit(solution)/shard_map/ppermute | solution.py:715
  115.6 6.9 %collective-permute-start.33 = (f32[32,1024]{1,0:T(8,128)S(1)}, f32[32,1024]{1,0:T(8,128)S(1)}, u32[]{:S(2)}, u32[]{:S(2)}) collective-permute-start(f32[32,1024]{1,0:T(8,128)S(1)} %get-tuple-element.396), channel_id=1, source_target_pairs={{0,2},{1,3},{2,0},{3,1},{4,6},{5,7},{6,4},{7,5},{8,10},{9,11},{10,... | collective-permute-start | bytes 393224 | tf_op jit(solution)/shard_map/ppermute | solution.py:715
  116.3 13.7 %collective-permute-start.38 = (f32[32,1536]{1,0:T(8,128)S(1)}, f32[32,1536]{1,0:T(8,128)S(1)}, u32[]{:S(2)}, u32[]{:S(2)}) collective-permute-start(f32[32,1536]{1,0:T(8,128)S(1)} %get-tuple-element.404.refs_0_), channel_id=1, source_target_pairs={{0,4},{1,5},{2,6},{3,7},{4,0},{5,1},{6,2},{7,3},{8,12},{9,13},{10,... | collective-permute-start | bytes 589832 | tf_op jit(solution)/shard_map/ppermute | solution.py:715
  121.0 23.1 %collective-permute-start.40 = (f32[24,1152]{1,0:T(8,128)S(1)}, f32[24,1152]{1,0:T(8,128)S(1)}, u32[]{:S(2)}, u32[]{:S(2)}) collective-permute-start(f32[24,1152]{1,0:T(8,128)S(1)} %get-tuple-element.411.refs_0_), channel_id=1, source_target_pairs={{0,1},{1,0},{2,3},{3,2},{4,5},{5,4},{6,7},{7,6},{8,9},{9,8},{10,11... | collective-permute-start | bytes 331784 | tf_op jit(solution)/shard_map/ppermute | solution.py:687
  121.5 6.4 %collective-permute-start.31 = (f32[128,512]{1,0:T(8,128)S(1)}, f32[128,512]{1,0:T(8,128)S(1)}, u32[]{:S(2)}, u32[]{:S(2)}) collective-permute-start(f32[128,512]{1,0:T(8,128)S(1)} %get-tuple-element.393.refs_1_), channel_id=1, source_target_pairs={{0,16},{1,9},{2,18},{3,11},{4,20},{5,13},{6,22},{7,15},{8,24},{9,1... | collective-permute-start | bytes 786440 | tf_op jit(solution)/shard_map/ppermute | solution.py:715
  122.4 8.9 %collective-permute-start.37 = (f32[256,1536]{1,0:T(8,128)S(1)}, f32[256,1536]{1,0:T(8,128)S(1)}, u32[]{:S(2)}, u32[]{:S(2)}) collective-permute-start(f32[256,1536]{1,0:T(8,128)S(1)} %get-tuple-element.403.refs_1_), channel_id=1, source_target_pairs={{0,1},{1,0},{2,3},{3,2},{4,5},{5,4},{6,7},{7,6},{8,9},{9,8},{10,11... | collective-permute-start | bytes 4718600 | tf_op jit(solution)/shard_map/ppermute | solution.py:687
  122.5 11.4 %collective-permute-start.36 = (f32[32,1152]{1,0:T(8,128)S(1)}, f32[32,1152]{1,0:T(8,128)S(1)}, u32[]{:S(2)}, u32[]{:S(2)}) collective-permute-start(f32[32,1152]{1,0:T(8,128)S(1)} %get-tuple-element.402.refs_1_), channel_id=1, source_target_pairs={{0,16},{1,9},{2,18},{3,11},{4,20},{5,13},{6,22},{7,15},{8,24},{9,1... | collective-permute-start | bytes 442376 | tf_op jit(solution)/shard_map/ppermute | solution.py:715
  128.0 8.6 %collective-permute-start.35 = (f32[32,1024]{1,0:T(8,128)S(1)}, f32[32,1024]{1,0:T(8,128)S(1)}, u32[]{:S(2)}, u32[]{:S(2)}) collective-permute-start(f32[32,1024]{1,0:T(8,128)S(1)} %get-tuple-element.401.refs_0_), channel_id=1, source_target_pairs={{0,4},{1,5},{2,6},{3,7},{4,0},{5,1},{6,2},{7,3},{8,12},{9,13},{10,... | collective-permute-start | bytes 393224 | tf_op jit(solution)/shard_map/ppermute | solution.py:715
  130.0 9.2 %collective-permute-start.34 = (f32[256,512]{1,0:T(8,128)S(1)}, f32[256,512]{1,0:T(8,128)S(1)}, u32[]{:S(2)}, u32[]{:S(2)}) collective-permute-start(f32[256,512]{1,0:T(8,128)S(1)} %get-tuple-element.400.refs_1_), channel_id=1, source_target_pairs={{0,8},{1,17},{2,10},{3,19},{4,12},{5,21},{6,14},{7,23},{8,0},{9,25... | collective-permute-start | bytes 1572872 | tf_op jit(solution)/shard_map/ppermute | solution.py:715
  131.4 8.4 %collective-permute-start.43 = (f32[32,1536]{1,0:T(8,128)S(1)}, f32[32,1536]{1,0:T(8,128)S(1)}, u32[]{:S(2)}, u32[]{:S(2)}) collective-permute-start(f32[32,1536]{1,0:T(8,128)S(1)} %get-tuple-element.414.refs_1_), channel_id=1, source_target_pairs={{0,2},{1,3},{2,0},{3,1},{4,6},{5,7},{6,4},{7,5},{8,10},{9,11},{10,... | collective-permute-start | bytes 589832 | tf_op jit(solution)/shard_map/ppermute | solution.py:715
  134.0 10.0 %collective-permute-start.42 = (f32[64,1152]{1,0:T(8,128)S(1)}, f32[64,1152]{1,0:T(8,128)S(1)}, u32[]{:S(2)}, u32[]{:S(2)}) collective-permute-start(f32[64,1152]{1,0:T(8,128)S(1)} %get-tuple-element.413.refs_1_), channel_id=1, source_target_pairs={{0,8},{1,17},{2,10},{3,19},{4,12},{5,21},{6,14},{7,23},{8,0},{9,25... | collective-permute-start | bytes 884744 | tf_op jit(solution)/shard_map/ppermute | solution.py:715
  136.6 7.5 %collective-permute-start.41 = (f32[32,1024]{1,0:T(8,128)S(1)}, f32[32,1024]{1,0:T(8,128)S(1)}, u32[]{:S(2)}, u32[]{:S(2)}) collective-permute-start(f32[32,1024]{1,0:T(8,128)S(1)} %get-tuple-element.412.refs_1_), channel_id=1, source_target_pairs={{0,2},{1,3},{2,0},{3,1},{4,6},{5,7},{6,4},{7,5},{8,10},{9,11},{10,... | collective-permute-start | bytes 393224 | tf_op jit(solution)/shard_map/ppermute | solution.py:715
  139.9 9.0 %collective-permute-start.45 = (f32[64,1536]{1,0:T(8,128)S(1)}, f32[64,1536]{1,0:T(8,128)S(1)}, u32[]{:S(2)}, u32[]{:S(2)}) collective-permute-start(f32[64,1536]{1,0:T(8,128)S(1)} %get-tuple-element.420.refs_1_), channel_id=1, source_target_pairs={{0,16},{1,9},{2,18},{3,11},{4,20},{5,13},{6,22},{7,15},{8,24},{9,1... | collective-permute-start | bytes 1179656 | tf_op jit(solution)/shard_map/ppermute | solution.py:715
  141.0 11.4 %collective-permute-start.39 = (f32[512,512]{1,0:T(8,128)S(1)}, f32[512,512]{1,0:T(8,128)S(1)}, u32[]{:S(2)}, u32[]{:S(2)}) collective-permute-start(f32[512,512]{1,0:T(8,128)S(1)} %get-tuple-element.410.refs_1_), channel_id=1, source_target_pairs={{0,1},{1,0},{2,3},{3,2},{4,5},{5,4},{6,7},{7,6},{8,9},{9,8},{10,11... | collective-permute-start | bytes 3145736 | tf_op jit(solution)/shard_map/ppermute | solution.py:687
  144.2 6.1 %collective-permute-start.44 = (f32[24,1152]{1,0:T(8,128)S(1)}, f32[24,1152]{1,0:T(8,128)S(1)}, u32[]{:S(2)}, u32[]{:S(2)}) collective-permute-start(f32[24,1152]{1,0:T(8,128)S(1)} %get-tuple-element.419.refs_0_), channel_id=1, source_target_pairs={{0,8},{1,17},{2,10},{3,19},{4,12},{5,21},{6,14},{7,23},{8,0},{9,25... | collective-permute-start | bytes 331784 | tf_op jit(solution)/shard_map/ppermute | solution.py:715
  146.2 9.9 %collective-permute-start.47 = (f32[64,1024]{1,0:T(8,128)S(1)}, f32[64,1024]{1,0:T(8,128)S(1)}, u32[]{:S(2)}, u32[]{:S(2)}) collective-permute-start(f32[64,1024]{1,0:T(8,128)S(1)} %get-tuple-element.428.refs_1_), channel_id=1, source_target_pairs={{0,16},{1,9},{2,18},{3,11},{4,20},{5,13},{6,22},{7,15},{8,24},{9,1... | collective-permute-start | bytes 786440 | tf_op jit(solution)/shard_map/ppermute | solution.py:715
  146.9 12.6 %collective-permute-start.50 = (f32[128,1152]{1,0:T(8,128)S(1)}, f32[128,1152]{1,0:T(8,128)S(1)}, u32[]{:S(2)}, u32[]{:S(2)}) collective-permute-start(f32[128,1152]{1,0:T(8,128)S(1)} %get-tuple-element.433.refs_1_), channel_id=1, source_target_pairs={{0,2},{1,3},{2,0},{3,1},{4,6},{5,7},{6,4},{7,5},{8,10},{9,11},{10,... | collective-permute-start | bytes 1769480 | tf_op jit(solution)/shard_map/ppermute | solution.py:715
  149.0 12.1 %collective-permute-start.49 = (f32[128,1536]{1,0:T(8,128)S(1)}, f32[128,1536]{1,0:T(8,128)S(1)}, u32[]{:S(2)}, u32[]{:S(2)}) collective-permute-start(f32[128,1536]{1,0:T(8,128)S(1)} %get-tuple-element.432.refs_1_), channel_id=1, source_target_pairs={{0,8},{1,17},{2,10},{3,19},{4,12},{5,21},{6,14},{7,23},{8,0},{9,25... | collective-permute-start | bytes 2359304 | tf_op jit(solution)/shard_map/ppermute | solution.py:715
  150.3 7.4 %collective-permute-start.46 = (f32[24,1152]{1,0:T(8,128)S(1)}, f32[24,1152]{1,0:T(8,128)S(1)}, u32[]{:S(2)}, u32[]{:S(2)}) collective-permute-start(f32[24,1152]{1,0:T(8,128)S(1)} %get-tuple-element.427.refs_0_), channel_id=1, source_target_pairs={{0,16},{1,9},{2,18},{3,11},{4,20},{5,13},{6,22},{7,15},{8,24},{9,1... | collective-permute-start | bytes 331784 | tf_op jit(solution)/shard_map/ppermute | solution.py:715
  157.7 4.8 %collective-permute-start.48 = (f32[24,1152]{1,0:T(8,128)S(1)}, f32[24,1152]{1,0:T(8,128)S(1)}, u32[]{:S(2)}, u32[]{:S(2)}) collective-permute-start(f32[24,1152]{1,0:T(8,128)S(1)} %get-tuple-element.431.refs_0_), channel_id=1, source_target_pairs={{0,2},{1,3},{2,0},{3,1},{4,6},{5,7},{6,4},{7,5},{8,10},{9,11},{10,... | collective-permute-start | bytes 331784 | tf_op jit(solution)/shard_map/ppermute | solution.py:715
  157.8 9.2 %collective-permute-start.52 = (f32[128,1024]{1,0:T(8,128)S(1)}, f32[128,1024]{1,0:T(8,128)S(1)}, u32[]{:S(2)}, u32[]{:S(2)}) collective-permute-start(f32[128,1024]{1,0:T(8,128)S(1)} %get-tuple-element.438.refs_1_), channel_id=1, source_target_pairs={{0,8},{1,17},{2,10},{3,19},{4,12},{5,21},{6,14},{7,23},{8,0},{9,25... | collective-permute-start | bytes 1572872 | tf_op jit(solution)/shard_map/ppermute | solution.py:715
  159.7 7.9 %collective-permute-start.55 = (f32[256,1152]{1,0:T(8,128)S(1)}, f32[256,1152]{1,0:T(8,128)S(1)}, u32[]{:S(2)}, u32[]{:S(2)}) collective-permute-start(f32[256,1152]{1,0:T(8,128)S(1)} %get-tuple-element.442.refs_1_), channel_id=1, source_target_pairs={{0,1},{1,0},{2,3},{3,2},{4,5},{5,4},{6,7},{7,6},{8,9},{9,8},{10,11... | collective-permute-start | bytes 3538952 | tf_op jit(solution)/shard_map/ppermute | solution.py:687
  161.3 8.3 %collective-permute-start.54 = (f32[256,1536]{1,0:T(8,128)S(1)}, f32[256,1536]{1,0:T(8,128)S(1)}, u32[]{:S(2)}, u32[]{:S(2)}) collective-permute-start(f32[256,1536]{1,0:T(8,128)S(1)} %get-tuple-element.441.refs_1_), channel_id=1, source_target_pairs={{0,1},{1,0},{2,3},{3,2},{4,5},{5,4},{6,7},{7,6},{8,9},{9,8},{10,11... | collective-permute-start | bytes 4718600 | tf_op jit(solution)/shard_map/ppermute | solution.py:687
  162.6 11.2 %collective-permute-start.51 = (f32[24,1152]{1,0:T(8,128)S(1)}, f32[24,1152]{1,0:T(8,128)S(1)}, u32[]{:S(2)}, u32[]{:S(2)}) collective-permute-start(f32[24,1152]{1,0:T(8,128)S(1)} %get-tuple-element.437.refs_0_), channel_id=1, source_target_pairs={{0,4},{1,5},{2,6},{3,7},{4,0},{5,1},{6,2},{7,3},{8,12},{9,13},{10,... | collective-permute-start | bytes 331784 | tf_op jit(solution)/shard_map/ppermute | solution.py:715
  167.2 4.7 %collective-permute-start.53 = (f32[256,1024]{1,0:T(8,128)S(1)}, f32[256,1024]{1,0:T(8,128)S(1)}, u32[]{:S(2)}, u32[]{:S(2)}) collective-permute-start(f32[256,1024]{1,0:T(8,128)S(1)} %get-tuple-element.440.refs_1_), channel_id=1, source_target_pairs={{0,1},{1,0},{2,3},{3,2},{4,5},{5,4},{6,7},{7,6},{8,9},{9,8},{10,11... | collective-permute-start | bytes 3145736 | tf_op jit(solution)/shard_map/ppermute | solution.py:687
  (16 other events, 26.9 us)

commit v6 on v5

--- a/solution.py
+++ b/solution.py
@@ -198,7 +198,7 @@
             return tuple(k * u + value for k, u in zip(keeps, state))
 
         zero = jnp.zeros((chunks, 128), F32)
-        state = lax.fori_loop(0, CHUNK, step, (zero,) * hidden, unroll=8)
+        state = lax.fori_loop(0, CHUNK, step, (zero,) * hidden, unroll=16)
         for h in range(hidden):
             decay = jnp.exp(CHUNK * logk[h : h + 1, lanes])
             reached = scan_step(masks, state[h], decay, shifts, chunks)
@@ -235,7 +235,7 @@
             smooth[tile, t] = add_up([c * u for c, u in zip(mixes, state)])
             return state
 
-        lax.fori_loop(0, CHUNK, step, tuple(enter[h, :, lanes] for h in range(hidden)), unroll=8)
+        lax.fori_loop(0, CHUNK, step, tuple(enter[h, :, lanes] for h in range(hidden)), unroll=16)
 
 
 def pair_body(backward, tokens, meta, own, other, logk, out):
@@ -321,7 +321,7 @@
             rows[pl.ds(t, chunks, stride=CHUNK), :] = pre
             return state
 
-        lax.fori_loop(0, CHUNK, step, tuple(state), unroll=8)
+        lax.fori_loop(0, CHUNK, step, tuple(state), unroll=16)
         pre = rows[...]
         gate = sigmoid(pre)
         smoothed = pre * gate
@@ -570,7 +570,7 @@
             return tuple(k * u + value for k, u in zip(keeps, state))
 
         zero = jnp.zeros((chunks, 128), F32)
-        state = lax.fori_loop(0, CHUNK, step, (zero,) * hidden, unroll=8)
+        state = lax.fori_loop(0, CHUNK, step, (zero,) * hidden, unroll=16)
         for h in range(hidden):
             decay = jnp.exp(CHUNK * logk[h : h + 1, lanes])
             reached = scan_step(masks, state[h], decay, shifts, chunks)
@@ -614,7 +614,7 @@
         return state, reads
 
     first = tuple(states[h, :, lanes] for h in heads)
-    _, reads = lax.fori_loop(0, CHUNK, rise, (first, zeros), unroll=4)
+    _, reads = lax.fori_loop(0, CHUNK, rise, (first, zeros), unroll=8)
     for h in heads:
         sums[h : h + 1, :] = jnp.sum(reads[h], axis=0, keepdims=True)
 
@@ -628,7 +628,7 @@
         return state, marks
 
     first = tuple(later[h, :, lanes] for h in heads)
-    _, marks = lax.fori_loop(0, CHUNK, fall, (first, zeros), unroll=4)
+    _, marks = lax.fori_loop(0, CHUNK, fall, (first, zeros), unroll=8)
     for h in heads:
         sums[hidden + h : hidden + h + 1, :] = jnp.sum(marks[h], axis=0, keepdims=True)
 

time: 175 us -> 175 us (level)
  transfers between devices with their start and end apart: 56 -> 56, of which waited for: 22 -> 22; matrix products, arithmetic and copies ran while one was open for 0% -> 0% of each run, Pallas kernels for 25% -> 24%
where the time goes in v6:
time: 175 us; the launch traced here: 174 us
  Pallas kernels  59.9 us (34%)
  starting transfers between devices  57.2 us (33%)
  waiting for transfers between devices  51.4 us (29%)
  local copies, waits for them, and re-layouts  2.96 us (2%)
    pallas_call x79, Pallas kernels, __call__(): pl.pallas_call(run, in_specs=specs, out_specs=[pl.BlockSpec(memory_space=...  59.9 us
    ppermute x38, waiting for transfers between devices, cross(): return lax.ppermute(a, ('dp', 'seq'), moves)  41.2 us
    ppermute x38, starting transfers between devices, cross(): return lax.ppermute(a, ('dp', 'seq'), moves)  41 us
    ppermute x3, starting transfers between devices, chip_before(): lax.ppermute(state, 'seq', [(i, i + 2 * chips) for i in range(count - 2 *...  10.6 us
    ppermute x2, waiting for transfers between devices, chip_after(): lax.ppermute(state, 'seq', [(i, i - 2 * chips) for i in range(2 * chips,...  9.39 us
  transfers between devices with their start and end apart: 56, of which 22 were waited for; matrix products, arithmetic and copies ran while one was open for 0% of the time, Pallas kernels for 24%

profile of v6, /device:TPU:0, one launch (start us, length us, event | category | flops | bytes accessed | tf_op | source)
XLA Modules:
  0.0 174.2 jit_solution(13036727836111760483)
XLA Ops:
  3.2 2.6 %norm_and_states.1 = (f32[4,512,128]{2,1,0:T(8,128)S(1)}, bf16[512,512]{1,0:T(8,128)(2,1)S(1)}, f32[16,8,512]{2,1,0:T(8,128)S(1)}, f32[16,512]{1,0:T(8,128)S(1)}...) custom-call(s32[1,3]{1,0:T(1,128)S(1)} %copy-done.11, bf16[512,512]{1,0:T(8,128)(2,1)S(1)} %copy-done.17, ...), custom_call_target="tpu_custom_call" | custom-call | flops 8000000000 | tf_op jit(solution)/shard_map/norm_and_states/pallas_call | solution.py:81
  7.8 4.8 %collective-permute-start.1 = (f32[16,512]{1,0:T(8,128)S(1)}, f32[16,512]{1,0:T(8,128)S(1)}, u32[]{:S(2)}, u32[]{:S(2)}) collective-permute-start(f32[16,512]{1,0:T(8,128)S(1)} %get-tuple-element.243), channel_id=1, source_target_pairs={{0,2},{1,3},{2,4},{3,5},{4,6},{5,7},{8,10},{9,11},{10,12},{11,13},... | collective-permute-start | bytes 98312 | tf_op jit(solution)/shard_map/ppermute | solution.py:692
  12.6 4.5 %collective-permute-start.2 = (f32[16,512]{1,0:T(8,128)S(1)}, f32[16,512]{1,0:T(8,128)S(1)}, u32[]{:S(2)}, u32[]{:S(2)}) collective-permute-start(f32[16,512]{1,0:T(8,128)S(1)} %get-tuple-element.243), channel_id=1, source_target_pairs={{0,4},{1,5},{2,6},{3,7},{8,12},{9,13},{10,14},{11,15},{16,20},{17,... | collective-permute-start | bytes 98312 | tf_op jit(solution)/shard_map/ppermute | solution.py:692
  17.1 1.3 collective-permute-start.3
  18.4 2.2 %local_average.1 = (f32[4,64,8,128]{3,2,1,0:T(8,128)S(1)}, f32[8,128]{1,0:T(8,128)S(1)}) custom-call(f32[4,64,8,128]{3,2,1,0:T(8,128)S(1)} %get-tuple-element.244.refs_0_.refs_9_, f32[16,8,512]{2,1,0:T(8,128)S(1)} %get-tuple-element.245.refs_1_.refs_11_, f32[16,512]{1,0:T(8,128)S(1)} %get-tuple-element.465.refs_4_.refs_2_.refs_6_.refs_3_, ...), custom_call_target="tpu_custom_call" | custom-call | flops 8000000000 | tf_op jit(solution)/shard_map/local_average/pallas_call | solution.py:81
  21.8 2.7 %carried_average.1 = (bf16[512,512]{1,0:T(8,128)(2,1)S(1)}, f32[512,512]{1,0:T(8,128)S(1)}, f32[16,8,512]{2,1,0:T(8,128)S(1)}, f32[8,128]{1,0:T(8,128)S(1)}) custom-call(s32[5]{0:T(128)S(1)} %pad_add_fusion.refs_0_, f32[16,512]{1,0:T(8,128)S(1)} %collective-permute-done.refs_2_.refs_1_, f32[16,512]{1,0:T(8,128)S(1)} %collective-permute-done.1.refs_2_, ...), custom_call_target="tpu_custom_call" | custom-call | flops 8000000000 | tf_op jit(solution)/shard_map/carried_average/pallas_call | solution.py:81
  24.5 1.4 mix.1
  26.0 2.1 %attention.1 = (f32[512,128]{1,0:T(8,128)S(1)}, f32[512,1024]{1,0:T(8,128)S(1)}, bf16[512,1024]{1,0:T(8,128)(2,1)S(1)}, f32[8,128]{1,0:T(8,128)S(1)}) custom-call(bf16[512,128]{1,0:T(8,128)(2,1)S(1)} %get-tuple-element.253.refs_0_.refs_2_, bf16[512,128]{1,0:T(8,128)(2,1)S(1)} %get-tuple-element.254.refs_1_.refs_3_, ...), custom_call_target="tpu_custom_call" | custom-call | flops 8000000000 | tf_op jit(solution)/shard_map/attention/pallas_call | solution.py:81
  28.2 1.4 hidden.1
  33.1 1.4 hidden_back.1
  34.6 1.3 reset_back.1
  35.9 1.6 ffn_in_grad.1
  37.5 2.1 %attention_back.1 = (bf16[512,1024]{1,0:T(8,128)(2,1)S(1)}, bf16[512,128]{1,0:T(8,128)(2,1)S(1)}, f32[8,128]{1,0:T(8,128)S(1)}, f32[8,128]{1,0:T(8,128)S(1)}) custom-call(bf16[512,1024]{1,0:T(8,128)(2,1)S(1)} %get-tuple-element.283.refs_0_, f32[512,128]{1,0:T(8,128)S(1)} %get-tuple-element.284.refs_1_, ...), custom_call_target="tpu_custom_call" | custom-call | tf_op jit(solution)/shard_map/attention_back/pallas_call | solution.py:81
  39.6 1.4 value_grad.1
  41.9 1.3 ffn_out_grad.1
  43.3 1.5 collective-permute-start.8
  44.9 2.2 %smooth_back.1 = (f32[4,512,128]{2,1,0:T(8,128)S(1)}, f32[4,512,128]{2,1,0:T(8,128)S(1)}, f32[1,512]{1,0:T(1,128)S(1)}, f32[8,128]{1,0:T(8,128)S(1)}) custom-call(bf16[512,512]{1,0:T(8,128)(2,1)S(1)} %get-tuple-element.276.refs_4_.refs_0_, bf16[512,128]{1,0:T(8,128)(2,1)S(1)} %get-tuple-element.290.refs_4_.refs_1_, ...), custom_call_target="tpu_custom_call" | custom-call | flops 12000000000 | tf_op jit(solution)/shard_map/smooth_back/pallas_call | solution.py:81
  47.6 2.3 %states_back.1 = (f32[16,8,512]{2,1,0:T(8,128)S(1)}, f32[16,512]{1,0:T(8,128)S(1)}, f32[4,64,8,128]{3,2,1,0:T(8,128)S(1)}, f32[8,128]{1,0:T(8,128)S(1)}) custom-call(s32[5]{0:T(128)S(1)} %pad_add_fusion.refs_0_, f32[4,512,128]{2,1,0:T(8,128)S(1)} %get-tuple-element.308.refs_1_, f32[16,512]{1,0:T(8,128)S(1)} %get-tuple-element.466.refs_3_.refs_5_.refs_2_.refs_4_, ...), custom_call_target="tpu_custom_call" | custom-call | flops 12000000000 | tf_op jit(solution)/shard_map/states_back/pallas_call | solution.py:81
  50.2 1.5 collective-permute-start.7
  52.3 1.3 collective-permute-start.11
  53.6 1.8 %collective-permute-done.8.refs_2_ = f32[128,1536]{1,0:T(8,128)S(1)} collective-permute-done((f32[128,1536]{1,0:T(8,128)S(1)}, f32[128,1536]{1,0:T(8,128)S(1)}, u32[]{:S(2)}, u32[]{:S(2)}) %collective-permute-start.8) | collective-permute-done | bytes 786464 | tf_op jit(solution)/shard_map/ppermute | solution.py:715
  55.5 1.6 collective-permute-start.10
  57.1 9.4 %collective-permute-done.11.refs_2_ = f32[16,512]{1,0:T(8,128)S(1)} collective-permute-done((f32[16,512]{1,0:T(8,128)S(1)}, f32[16,512]{1,0:T(8,128)S(1)}, u32[]{:S(2)}, u32[]{:S(2)}) %collective-permute-start.11) | collective-permute-done | bytes 32800 | tf_op jit(solution)/shard_map/ppermute | solution.py:697
  67.1 1.6 out_grad.1
  68.7 1.3 collective-permute-start.13
  70.3 1.6 collective-permute-start.12
  72.9 1.3 reset_grad.1
  74.3 3.9 %collective-permute-done.14.refs_1_ = f32[32,1536]{1,0:T(8,128)S(1)} collective-permute-done((f32[32,1536]{1,0:T(8,128)S(1)}, f32[32,1536]{1,0:T(8,128)S(1)}, u32[]{:S(2)}, u32[]{:S(2)}) %collective-permute-start.14) | collective-permute-done | bytes 196640 | tf_op jit(solution)/shard_map/ppermute | solution.py:715
  78.2 2.6 %collective-permute-start.19 = (f32[32,1536]{1,0:T(8,128)S(1)}, f32[32,1536]{1,0:T(8,128)S(1)}, u32[]{:S(2)}, u32[]{:S(2)}) collective-permute-start(f32[32,1536]{1,0:T(8,128)S(1)} %get-tuple-element.344.refs_0_), channel_id=1, source_target_pairs={{0,4},{1,5},{2,6},{3,7},{4,0},{5,1},{6,2},{7,3},{8,12},{9,13},{10,... | collective-permute-start | bytes 589832 | tf_op jit(solution)/shard_map/ppermute | solution.py:715
  80.8 1.2 collective-permute-start.18
  82.7 1.7 state_back.4
  84.4 1.7 state_back.5
  87.7 2.0 %collective-permute-done.19.refs_1_ = f32[32,1536]{1,0:T(8,128)S(1)} collective-permute-done((f32[32,1536]{1,0:T(8,128)S(1)}, f32[32,1536]{1,0:T(8,128)S(1)}, u32[]{:S(2)}, u32[]{:S(2)}) %collective-permute-start.19) | collective-permute-done | bytes 196640 | tf_op jit(solution)/shard_map/ppermute | solution.py:715
  89.7 1.3 collective-permute-start.26
  91.0 3.4 %collective-permute-done.18.refs_2_ = f32[128,1536]{1,0:T(8,128)S(1)} collective-permute-done((f32[128,1536]{1,0:T(8,128)S(1)}, f32[128,1536]{1,0:T(8,128)S(1)}, u32[]{:S(2)}, u32[]{:S(2)}) %collective-permute-start.18) | collective-permute-done | bytes 786464 | tf_op jit(solution)/shard_map/ppermute | solution.py:715
  94.5 1.6 collective-permute-start.25
  96.6 2.8 %collective-permute-done.23.refs_2_ = f32[32,1536]{1,0:T(8,128)S(1)} collective-permute-done((f32[32,1536]{1,0:T(8,128)S(1)}, f32[32,1536]{1,0:T(8,128)S(1)}, u32[]{:S(2)}, u32[]{:S(2)}) %collective-permute-start.23) | collective-permute-done | bytes 196640 | tf_op jit(solution)/shard_map/ppermute | solution.py:715
  99.5 1.6 collective-permute-start.24
  101.1 1.7 state_back.6
  102.8 2.6 %collective-permute-done.26.refs_2_ = f32[128,1024]{1,0:T(8,128)S(1)} collective-permute-done((f32[128,1024]{1,0:T(8,128)S(1)}, f32[128,1024]{1,0:T(8,128)S(1)}, u32[]{:S(2)}, u32[]{:S(2)}) %collective-permute-start.26) | collective-permute-done | bytes 524320 | tf_op jit(solution)/shard_map/ppermute | solution.py:715
  106.5 1.9 %collective-permute-start.30 = (f32[32,1536]{1,0:T(8,128)S(1)}, f32[32,1536]{1,0:T(8,128)S(1)}, u32[]{:S(2)}, u32[]{:S(2)}) collective-permute-start(f32[32,1536]{1,0:T(8,128)S(1)} %get-tuple-element.388), channel_id=1, source_target_pairs={{0,2},{1,3},{2,0},{3,1},{4,6},{5,7},{6,4},{7,5},{8,10},{9,11},{10,... | collective-permute-start | bytes 589832 | tf_op jit(solution)/shard_map/ppermute | solution.py:715
  110.3 2.1 %collective-permute-done.28.refs_2_ = f32[64,1024]{1,0:T(8,128)S(1)} collective-permute-done((f32[64,1024]{1,0:T(8,128)S(1)}, f32[64,1024]{1,0:T(8,128)S(1)}, u32[]{:S(2)}, u32[]{:S(2)}) %collective-permute-start.28) | collective-permute-done | bytes 262176 | tf_op jit(solution)/shard_map/ppermute | solution.py:715
  112.5 1.7 state_back.7
  114.2 1.4 collective-permute-start.33
  115.6 1.8 %collective-permute-start.38 = (f32[32,1536]{1,0:T(8,128)S(1)}, f32[32,1536]{1,0:T(8,128)S(1)}, u32[]{:S(2)}, u32[]{:S(2)}) collective-permute-start(f32[32,1536]{1,0:T(8,128)S(1)} %get-tuple-element.404.refs_0_), channel_id=1, source_target_pairs={{0,4},{1,5},{2,6},{3,7},{4,0},{5,1},{6,2},{7,3},{8,12},{9,13},{10,... | collective-permute-start | bytes 589832 | tf_op jit(solution)/shard_map/ppermute | solution.py:715
  117.5 1.8 %norm_back.1 = (f32[512,512]{1,0:T(8,128)}, f32[24,1152]{1,0:T(8,128)S(1)}, f32[8,128]{1,0:T(8,128)S(1)}) custom-call(f32[512,128]{1,0:T(8,128)S(1)} %get-tuple-element.367.refs_0_, f32[512,128]{1,0:T(8,128)S(1)} %get-tuple-element.368.refs_1_, f32[512,128]{1,0:T(8,128)S(1)} %get-tuple-element.369.refs_2_, f32[512,128]{1,0:T(8,128)S(1)} %get-tuple-element.377.refs_3_, ...), custom_call_target="tpu_custom_call" | custom-call | flops 8000000000 | tf_op jit(solution)/shard_map/norm_back/pallas_call | solution.py:81
  123.0 4.2 %collective-permute-done.31.refs_2_ = f32[128,512]{1,0:T(8,128)S(1)} collective-permute-done((f32[128,512]{1,0:T(8,128)S(1)}, f32[128,512]{1,0:T(8,128)S(1)}, u32[]{:S(2)}, u32[]{:S(2)}) %collective-permute-start.31) | collective-permute-done | bytes 262176 | tf_op jit(solution)/shard_map/ppermute | solution.py:715
  127.2 2.3 %collective-permute-start.35 = (f32[32,1024]{1,0:T(8,128)S(1)}, f32[32,1024]{1,0:T(8,128)S(1)}, u32[]{:S(2)}, u32[]{:S(2)}) collective-permute-start(f32[32,1024]{1,0:T(8,128)S(1)} %get-tuple-element.401.refs_0_), channel_id=1, source_target_pairs={{0,4},{1,5},{2,6},{3,7},{4,0},{5,1},{6,2},{7,3},{8,12},{9,13},{10,... | collective-permute-start | bytes 393224 | tf_op jit(solution)/shard_map/ppermute | solution.py:715
  129.6 1.3 collective-permute-start.34
  131.2 2.2 %ffn_in_out.1 = (f32[512,1024]{1,0:T(8,128)}, f32[512,2176]{1,0:T(8,128)}, f32[8,128]{1,0:T(8,128)S(1)}) custom-call(s32[5]{0:T(128)S(1)} %pad_add_fusion.refs_0_, f32[256,1536]{1,0:T(8,128)S(1)} %get-tuple-element.403.refs_1_, f32[256,1536]{1,0:T(8,128)S(1)} %collective-permute-done.37.refs_2_, f32[8,128]{1,0:T(8,128)S(1)} %get-tuple-element.406.refs_3_), custom_call_target="tpu_custom_call" | custom-call | flops 2000000000 | tf_op jit(solution)/shard_map/ffn_in_out/pallas_call | solution.py:81
  133.5 1.5 collective-permute-start.42
  136.3 2.6 %collective-permute-done.34.refs_2_ = f32[256,512]{1,0:T(8,128)S(1)} collective-permute-done((f32[256,512]{1,0:T(8,128)S(1)}, f32[256,512]{1,0:T(8,128)S(1)}, u32[]{:S(2)}, u32[]{:S(2)}) %collective-permute-start.34) | collective-permute-done | bytes 524320 | tf_op jit(solution)/shard_map/ppermute | solution.py:715
  140.6 2.6 %collective-permute-done.42.refs_2_ = f32[64,1152]{1,0:T(8,128)S(1)} collective-permute-done((f32[64,1152]{1,0:T(8,128)S(1)}, f32[64,1152]{1,0:T(8,128)S(1)}, u32[]{:S(2)}, u32[]{:S(2)}) %collective-permute-start.42) | collective-permute-done | bytes 294944 | tf_op jit(solution)/shard_map/ppermute | solution.py:715
  143.4 2.3 %collective-permute-start.44 = (f32[24,1152]{1,0:T(8,128)S(1)}, f32[24,1152]{1,0:T(8,128)S(1)}, u32[]{:S(2)}, u32[]{:S(2)}) collective-permute-start(f32[24,1152]{1,0:T(8,128)S(1)} %get-tuple-element.419.refs_0_), channel_id=1, source_target_pairs={{0,8},{1,17},{2,10},{3,19},{4,12},{5,21},{6,14},{7,23},{8,0},{9,25... | collective-permute-start | bytes 331784 | tf_op jit(solution)/shard_map/ppermute | solution.py:715
  146.7 2.0 %collective-permute-done.45.refs_2_ = f32[64,1536]{1,0:T(8,128)S(1)} collective-permute-done((f32[64,1536]{1,0:T(8,128)S(1)}, f32[64,1536]{1,0:T(8,128)S(1)}, u32[]{:S(2)}, u32[]{:S(2)}) %collective-permute-start.45) | collective-permute-done | bytes 393248 | tf_op jit(solution)/shard_map/ppermute | solution.py:715
  149.7 2.3 %collective-permute-start.46 = (f32[24,1152]{1,0:T(8,128)S(1)}, f32[24,1152]{1,0:T(8,128)S(1)}, u32[]{:S(2)}, u32[]{:S(2)}) collective-permute-start(f32[24,1152]{1,0:T(8,128)S(1)} %get-tuple-element.427.refs_0_), channel_id=1, source_target_pairs={{0,16},{1,9},{2,18},{3,11},{4,20},{5,13},{6,22},{7,15},{8,24},{9,1... | collective-permute-start | bytes 331784 | tf_op jit(solution)/shard_map/ppermute | solution.py:715
  152.0 1.9 %ffn_out_out.1 = (f32[1024,512]{1,0:T(8,128)}, f32[8,128]{1,0:T(8,128)S(1)}) custom-call(s32[5]{0:T(128)S(1)} %pad_add_fusion.refs_0_, f32[512,512]{1,0:T(8,128)S(1)} %get-tuple-element.410.refs_1_, f32[512,512]{1,0:T(8,128)S(1)} %collective-permute-done.39.refs_2_, f32[8,128]{1,0:T(8,128)S(1)} %get-tuple-element.423.refs_3_), custom_call_target="tpu_custom_call" | custom-call | flops 8000000000 | tf_op jit(solution)/shard_map/ffn_out_out/pallas_call | solution.py:81
  153.9 1.7 block_out.1
  155.7 1.6 collective-permute-done.46.refs_1_
  159.3 1.5 collective-permute-done.49.refs_2_
  162.2 4.4 %collective-permute-done.52.refs_2_ = f32[128,1024]{1,0:T(8,128)S(1)} collective-permute-done((f32[128,1024]{1,0:T(8,128)S(1)}, f32[128,1024]{1,0:T(8,128)S(1)}, u32[]{:S(2)}, u32[]{:S(2)}) %collective-permute-start.52) | collective-permute-done | bytes 524320 | tf_op jit(solution)/shard_map/ppermute | solution.py:715
  167.2 2.0 %value_out.1 = (f32[512,1024]{1,0:T(8,128)}, f32[512,2176]{1,0:T(8,128)}, f32[8,128]{1,0:T(8,128)S(1)}) custom-call(s32[5]{0:T(128)S(1)} %pad_add_fusion.refs_0_, f32[256,1152]{1,0:T(8,128)S(1)} %get-tuple-element.442.refs_1_, f32[256,1152]{1,0:T(8,128)S(1)} %collective-permute-done.55.refs_2_, ...), custom_call_target="tpu_custom_call", output_to_operand_aliasing={{1}: (3, {})} | custom-call | flops 6000000000 | tf_op jit(solution)/shard_map/value_out/pallas_call | solution.py:81
  169.2 2.3 %out_out.1 = (f32[1024,512]{1,0:T(8,128)}, f32[512,2176]{1,0:T(8,128)}, f32[8,128]{1,0:T(8,128)S(1)}) custom-call(s32[5]{0:T(128)S(1)} %pad_add_fusion.refs_0_, f32[256,1536]{1,0:T(8,128)S(1)} %get-tuple-element.441.refs_1_, f32[256,1536]{1,0:T(8,128)S(1)} %collective-permute-done.54.refs_2_, ...), custom_call_target="tpu_custom_call", output_to_operand_aliasing={{1}: (3, {})} | custom-call | flops 10000000000 | tf_op jit(solution)/shard_map/out_out/pallas_call | solution.py:81
  171.5 1.9 %reset_out.1 = (f32[512,2176]{1,0:T(8,128)}, f32[8,128]{1,0:T(8,128)S(1)}) custom-call(s32[5]{0:T(128)S(1)} %pad_add_fusion.refs_0_, f32[256,1024]{1,0:T(8,128)S(1)} %get-tuple-element.440.refs_1_, f32[256,1024]{1,0:T(8,128)S(1)} %collective-permute-done.53.refs_2_, f32[512,2176]{1,0:T(8,128)} %get-tuple-element.447.refs_3_, ...), custom_call_target="tpu_custom_call", output_to_operand_aliasing={{0}: (3, {})} | custom-call | flops 8000000000 | tf_op jit(solution)/shard_map/reset_out/pallas_call | solution.py:81
  (177 shorter events, 33.8 us)
Async XLA Ops:
  3.2 3.1 %copy-start.12 = (s32[1,3]{1,0:T(1,128)S(1)}, s32[1,3]{1,0:T(1,128)}, u32[]{:S(2)}) copy-start(s32[1,3]{1,0:T(1,128)} %refs_0_.2) | copy-start | bytes 40
  5.8 1.4 collective-permute-start
  7.8 14.0 %collective-permute-start.1 = (f32[16,512]{1,0:T(8,128)S(1)}, f32[16,512]{1,0:T(8,128)S(1)}, u32[]{:S(2)}, u32[]{:S(2)}) collective-permute-start(f32[16,512]{1,0:T(8,128)S(1)} %get-tuple-element.243), channel_id=1, source_target_pairs={{0,2},{1,3},{2,4},{3,5},{4,6},{5,7},{8,10},{9,11},{10,12},{11,13},... | collective-permute-start | bytes 98312 | tf_op jit(solution)/shard_map/ppermute | solution.py:692
  12.6 9.1 %collective-permute-start.2 = (f32[16,512]{1,0:T(8,128)S(1)}, f32[16,512]{1,0:T(8,128)S(1)}, u32[]{:S(2)}, u32[]{:S(2)}) collective-permute-start(f32[16,512]{1,0:T(8,128)S(1)} %get-tuple-element.243), channel_id=1, source_target_pairs={{0,4},{1,5},{2,6},{3,7},{8,12},{9,13},{10,14},{11,15},{16,20},{17,... | collective-permute-start | bytes 98312 | tf_op jit(solution)/shard_map/ppermute | solution.py:692
  17.1 4.6 %collective-permute-start.3 = (f32[16,512]{1,0:T(8,128)S(1)}, f32[16,512]{1,0:T(8,128)S(1)}, u32[]{:S(2)}, u32[]{:S(2)}) collective-permute-start(f32[16,512]{1,0:T(8,128)S(1)} %get-tuple-element.243), channel_id=1, source_target_pairs={{0,6},{1,7},{8,14},{9,15},{16,22},{17,23},{24,30},{25,31}} | collective-permute-start | bytes 98312 | tf_op jit(solution)/shard_map/ppermute | solution.py:692
  18.4 2.2 %copy-start.15 = (bf16[512,1024]{1,0:T(8,128)(2,1)S(1)}, bf16[512,1024]{1,0:T(8,128)(2,1)}, u32[]{:S(2)}) copy-start(bf16[512,1024]{1,0:T(8,128)(2,1)} %refs_6_.1) | copy-start | bytes 3145732
  21.8 2.7 %copy-start.10 = (f32[2,128]{1,0:T(2,128)S(1)}, f32[2,128]{1,0:T(2,128)}, u32[]{:S(2)}) copy-start(f32[2,128]{1,0:T(2,128)} %refs_8_.2) | copy-start | bytes 3076
  21.8 2.7 %copy-start.13 = (bf16[512,2176]{1,0:T(8,128)(2,1)S(1)}, bf16[512,2176]{1,0:T(8,128)(2,1)}, u32[]{:S(2)}) copy-start(bf16[512,2176]{1,0:T(8,128)(2,1)} %refs_5_.3) | copy-start | bytes 6684676
  21.8 2.7 %copy-start.22 = (f32[2,128]{1,0:T(2,128)S(1)}, f32[2,128]{1,0:T(2,128)}, u32[]{:S(2)}) copy-start(f32[2,128]{1,0:T(2,128)} %refs_3_.1) | copy-start | bytes 3076
  26.0 2.2 %copy-start = (bf16[1024,512]{1,0:T(8,128)(2,1)S(1)}, bf16[1024,512]{1,0:T(8,128)(2,1)}, u32[]{:S(2)}) copy-start(bf16[1024,512]{1,0:T(8,128)(2,1)} %refs_1_.15) | copy-start | bytes 3145732
  26.0 2.2 %copy-start.18 = (bf16[512,512]{1,0:T(8,128)(2,1)S(1)}, bf16[512,512]{1,0:T(8,128)(2,1)}, u32[]{:S(2)}) copy-start(bf16[512,512]{1,0:T(8,128)(2,1)} %refs_8_.3) | copy-start | bytes 1572868
  30.6 11.3 %copy-start.3 = (bf16[512,1024]{1,0:T(8,128)(2,1)}, bf16[512,1024]{1,0:T(8,128)(2,1)S(1)}, u32[]{:S(2)}) copy-start(bf16[512,1024]{1,0:T(8,128)(2,1)S(1)} %get-tuple-element.265.refs_1_) | copy-start | bytes 3145732
  37.4 4.1 %collective-permute-start.4 = (f32[256,1536]{1,0:T(8,128)S(1)}, f32[256,1536]{1,0:T(8,128)S(1)}, u32[]{:S(2)}, u32[]{:S(2)}) collective-permute-start(f32[256,1536]{1,0:T(8,128)S(1)} %get-tuple-element.282), channel_id=1, source_target_pairs={{0,1},{1,0},{2,3},{3,2},{4,5},{5,4},{6,7},{7,6},{8,9},{9,8},{10,11... | collective-permute-start | bytes 4718600 | tf_op jit(solution)/shard_map/ppermute | solution.py:687
  41.0 6.1 %collective-permute-start.6 = (f32[256,1152]{1,0:T(8,128)S(1)}, f32[256,1152]{1,0:T(8,128)S(1)}, u32[]{:S(2)}, u32[]{:S(2)}) collective-permute-start(f32[256,1152]{1,0:T(8,128)S(1)} %get-tuple-element.297), channel_id=1, source_target_pairs={{0,1},{1,0},{2,3},{3,2},{4,5},{5,4},{6,7},{7,6},{8,9},{9,8},{10,11... | collective-permute-start | bytes 3538952 | tf_op jit(solution)/shard_map/ppermute | solution.py:687
  43.2 4.2 %collective-permute-start.5 = (f32[512,512]{1,0:T(8,128)S(1)}, f32[512,512]{1,0:T(8,128)S(1)}, u32[]{:S(2)}, u32[]{:S(2)}) collective-permute-start(f32[512,512]{1,0:T(8,128)S(1)} %get-tuple-element.295), channel_id=1, source_target_pairs={{0,1},{1,0},{2,3},{3,2},{4,5},{5,4},{6,7},{7,6},{8,9},{9,8},{10,11... | collective-permute-start | bytes 3145736 | tf_op jit(solution)/shard_map/ppermute | solution.py:687
  43.3 12.0 %collective-permute-start.8 = (f32[128,1536]{1,0:T(8,128)S(1)}, f32[128,1536]{1,0:T(8,128)S(1)}, u32[]{:S(2)}, u32[]{:S(2)}) collective-permute-start(f32[128,1536]{1,0:T(8,128)S(1)} %get-tuple-element.307), channel_id=1, source_target_pairs={{0,8},{1,17},{2,10},{3,19},{4,12},{5,21},{6,14},{7,23},{8,0},{9,25... | collective-permute-start | bytes 2359304 | tf_op jit(solution)/shard_map/ppermute | solution.py:715
  50.0 1.7 %collective-permute-start.9 = (f32[16,512]{1,0:T(8,128)S(1)}, f32[16,512]{1,0:T(8,128)S(1)}, u32[]{:S(2)}, u32[]{:S(2)}) collective-permute-start(f32[16,512]{1,0:T(8,128)S(1)} %get-tuple-element.310.refs_1_), channel_id=1, source_target_pairs={{0,1},{1,0},{2,3},{3,2},{4,5},{5,4},{6,7},{7,6},{8,9},{9,8},{10,11... | collective-permute-start | bytes 98312 | tf_op jit(solution)/shard_map/ppermute | solution.py:687
  50.2 21.7 %collective-permute-start.16 = (f32[128,1152]{1,0:T(8,128)S(1)}, f32[128,1152]{1,0:T(8,128)S(1)}, u32[]{:S(2)}, u32[]{:S(2)}) collective-permute-start(f32[128,1152]{1,0:T(8,128)S(1)} %get-tuple-element.331), channel_id=1, source_target_pairs={{0,2},{1,3},{2,0},{3,1},{4,6},{5,7},{6,4},{7,5},{8,10},{9,11},{10,... | collective-permute-start | bytes 1769480 | tf_op jit(solution)/shard_map/ppermute | solution.py:715
  50.2 20.0 %collective-permute-start.7 = (f32[256,512]{1,0:T(8,128)S(1)}, f32[256,512]{1,0:T(8,128)S(1)}, u32[]{:S(2)}, u32[]{:S(2)}) collective-permute-start(f32[256,512]{1,0:T(8,128)S(1)} %get-tuple-element.305), channel_id=1, source_target_pairs={{0,8},{1,17},{2,10},{3,19},{4,12},{5,21},{6,14},{7,23},{8,0},{9,25... | collective-permute-start | bytes 1572872 | tf_op jit(solution)/shard_map/ppermute | solution.py:715
  52.3 14.2 %collective-permute-start.11 = (f32[16,512]{1,0:T(8,128)S(1)}, f32[16,512]{1,0:T(8,128)S(1)}, u32[]{:S(2)}, u32[]{:S(2)}) collective-permute-start(f32[16,512]{1,0:T(8,128)S(1)} %get-tuple-element.315.refs_1_), channel_id=1, source_target_pairs={{2,0},{3,1},{4,2},{5,3},{6,4},{7,5},{10,8},{11,9},{12,10},{13,11},... | collective-permute-start | bytes 98312 | tf_op jit(solution)/shard_map/ppermute | solution.py:697
  55.5 14.5 %collective-permute-start.10 = (f32[64,1536]{1,0:T(8,128)S(1)}, f32[64,1536]{1,0:T(8,128)S(1)}, u32[]{:S(2)}, u32[]{:S(2)}) collective-permute-start(f32[64,1536]{1,0:T(8,128)S(1)} %get-tuple-element.314), channel_id=1, source_target_pairs={{0,16},{1,9},{2,18},{3,11},{4,20},{5,13},{6,22},{7,15},{8,24},{9,1... | collective-permute-start | bytes 1179656 | tf_op jit(solution)/shard_map/ppermute | solution.py:715
  68.6 4.0 %collective-permute-start.15 = (f32[256,1536]{1,0:T(8,128)S(1)}, f32[256,1536]{1,0:T(8,128)S(1)}, u32[]{:S(2)}, u32[]{:S(2)}) collective-permute-start(f32[256,1536]{1,0:T(8,128)S(1)} %get-tuple-element.329), channel_id=1, source_target_pairs={{0,1},{1,0},{2,3},{3,2},{4,5},{5,4},{6,7},{7,6},{8,9},{9,8},{10,11... | collective-permute-start | bytes 4718600 | tf_op jit(solution)/shard_map/ppermute | solution.py:687
  68.7 12.1 %collective-permute-start.13 = (f32[16,512]{1,0:T(8,128)S(1)}, f32[16,512]{1,0:T(8,128)S(1)}, u32[]{:S(2)}, u32[]{:S(2)}) collective-permute-start(f32[16,512]{1,0:T(8,128)S(1)} %get-tuple-element.324), channel_id=1, source_target_pairs={{4,0},{5,1},{6,2},{7,3},{12,8},{13,9},{14,10},{15,11},{20,16},{21,... | collective-permute-start | bytes 98312 | tf_op jit(solution)/shard_map/ppermute | solution.py:697
  70.1 8.1 %collective-permute-start.14 = (f32[32,1536]{1,0:T(8,128)S(1)}, f32[32,1536]{1,0:T(8,128)S(1)}, u32[]{:S(2)}, u32[]{:S(2)}) collective-permute-start(f32[32,1536]{1,0:T(8,128)S(1)} %get-tuple-element.327), channel_id=1, source_target_pairs={{0,2},{1,3},{2,0},{3,1},{4,6},{5,7},{6,4},{7,5},{8,10},{9,11},{10,... | collective-permute-start | bytes 589832 | tf_op jit(solution)/shard_map/ppermute | solution.py:715
  70.3 15.8 %collective-permute-start.12 = (f32[128,512]{1,0:T(8,128)S(1)}, f32[128,512]{1,0:T(8,128)S(1)}, u32[]{:S(2)}, u32[]{:S(2)}) collective-permute-start(f32[128,512]{1,0:T(8,128)S(1)} %get-tuple-element.321), channel_id=1, source_target_pairs={{0,16},{1,9},{2,18},{3,11},{4,20},{5,13},{6,22},{7,15},{8,24},{9,1... | collective-permute-start | bytes 786440 | tf_op jit(solution)/shard_map/ppermute | solution.py:715
  72.0 14.5 %collective-permute-start.21 = (f32[64,1152]{1,0:T(8,128)S(1)}, f32[64,1152]{1,0:T(8,128)S(1)}, u32[]{:S(2)}, u32[]{:S(2)}) collective-permute-start(f32[64,1152]{1,0:T(8,128)S(1)} %get-tuple-element.348), channel_id=1, source_target_pairs={{0,8},{1,17},{2,10},{3,19},{4,12},{5,21},{6,14},{7,23},{8,0},{9,25... | collective-permute-start | bytes 884744 | tf_op jit(solution)/shard_map/ppermute | solution.py:715
  74.2 13.2 %collective-permute-start.20 = (f32[256,1024]{1,0:T(8,128)S(1)}, f32[256,1024]{1,0:T(8,128)S(1)}, u32[]{:S(2)}, u32[]{:S(2)}) collective-permute-start(f32[256,1024]{1,0:T(8,128)S(1)} %get-tuple-element.346), channel_id=1, source_target_pairs={{0,1},{1,0},{2,3},{3,2},{4,5},{5,4},{6,7},{7,6},{8,9},{9,8},{10,11... | collective-permute-start | bytes 3145736 | tf_op jit(solution)/shard_map/ppermute | solution.py:687
  78.2 11.4 %collective-permute-start.19 = (f32[32,1536]{1,0:T(8,128)S(1)}, f32[32,1536]{1,0:T(8,128)S(1)}, u32[]{:S(2)}, u32[]{:S(2)}) collective-permute-start(f32[32,1536]{1,0:T(8,128)S(1)} %get-tuple-element.344.refs_0_), channel_id=1, source_target_pairs={{0,4},{1,5},{2,6},{3,7},{4,0},{5,1},{6,2},{7,3},{8,12},{9,13},{10,... | collective-permute-start | bytes 589832 | tf_op jit(solution)/shard_map/ppermute | solution.py:715
  80.8 13.6 %collective-permute-start.18 = (f32[128,1536]{1,0:T(8,128)S(1)}, f32[128,1536]{1,0:T(8,128)S(1)}, u32[]{:S(2)}, u32[]{:S(2)}) collective-permute-start(f32[128,1536]{1,0:T(8,128)S(1)} %get-tuple-element.343), channel_id=1, source_target_pairs={{0,8},{1,17},{2,10},{3,19},{4,12},{5,21},{6,14},{7,23},{8,0},{9,25... | collective-permute-start | bytes 2359304 | tf_op jit(solution)/shard_map/ppermute | solution.py:715
  86.1 10.0 %collective-permute-start.17 = (f32[128,512]{1,0:T(8,128)S(1)}, f32[128,512]{1,0:T(8,128)S(1)}, u32[]{:S(2)}, u32[]{:S(2)}) collective-permute-start(f32[128,512]{1,0:T(8,128)S(1)} %get-tuple-element.341.refs_0_), channel_id=1, source_target_pairs={{0,2},{1,3},{2,0},{3,1},{4,6},{5,7},{6,4},{7,5},{8,10},{9,11},{10,... | collective-permute-start | bytes 786440 | tf_op jit(solution)/shard_map/ppermute | solution.py:715
  86.6 22.6 %collective-permute-start.29 = (f32[32,1152]{1,0:T(8,128)S(1)}, f32[32,1152]{1,0:T(8,128)S(1)}, u32[]{:S(2)}, u32[]{:S(2)}) collective-permute-start(f32[32,1152]{1,0:T(8,128)S(1)} %get-tuple-element.373), channel_id=1, source_target_pairs={{0,16},{1,9},{2,18},{3,11},{4,20},{5,13},{6,22},{7,15},{8,24},{9,1... | collective-permute-start | bytes 442376 | tf_op jit(solution)/shard_map/ppermute | solution.py:715
  89.7 9.8 %collective-permute-start.23 = (f32[32,1536]{1,0:T(8,128)S(1)}, f32[32,1536]{1,0:T(8,128)S(1)}, u32[]{:S(2)}, u32[]{:S(2)}) collective-permute-start(f32[32,1536]{1,0:T(8,128)S(1)} %get-tuple-element.355.refs_1_), channel_id=1, source_target_pairs={{0,2},{1,3},{2,0},{3,1},{4,6},{5,7},{6,4},{7,5},{8,10},{9,11},{10,... | collective-permute-start | bytes 589832 | tf_op jit(solution)/shard_map/ppermute | solution.py:715
  89.7 15.7 %collective-permute-start.26 = (f32[128,1024]{1,0:T(8,128)S(1)}, f32[128,1024]{1,0:T(8,128)S(1)}, u32[]{:S(2)}, u32[]{:S(2)}) collective-permute-start(f32[128,1024]{1,0:T(8,128)S(1)} %get-tuple-element.361), channel_id=1, source_target_pairs={{0,8},{1,17},{2,10},{3,19},{4,12},{5,21},{6,14},{7,23},{8,0},{9,25... | collective-permute-start | bytes 1572872 | tf_op jit(solution)/shard_map/ppermute | solution.py:715
  94.5 11.8 %collective-permute-start.25 = (f32[64,1536]{1,0:T(8,128)S(1)}, f32[64,1536]{1,0:T(8,128)S(1)}, u32[]{:S(2)}, u32[]{:S(2)}) collective-permute-start(f32[64,1536]{1,0:T(8,128)S(1)} %get-tuple-element.359), channel_id=1, source_target_pairs={{0,16},{1,9},{2,18},{3,11},{4,20},{5,13},{6,22},{7,15},{8,24},{9,1... | collective-permute-start | bytes 1179656 | tf_op jit(solution)/shard_map/ppermute | solution.py:715
  96.2 24.5 %collective-permute-start.22 = (f32[128,512]{1,0:T(8,128)S(1)}, f32[128,512]{1,0:T(8,128)S(1)}, u32[]{:S(2)}, u32[]{:S(2)}) collective-permute-start(f32[128,512]{1,0:T(8,128)S(1)} %get-tuple-element.354.refs_0_), channel_id=1, source_target_pairs={{0,4},{1,5},{2,6},{3,7},{4,0},{5,1},{6,2},{7,3},{8,12},{9,13},{10,... | collective-permute-start | bytes 786440 | tf_op jit(solution)/shard_map/ppermute | solution.py:715
  99.5 8.8 %collective-permute-start.24 = (f32[64,1536]{1,0:T(8,128)S(1)}, f32[64,1536]{1,0:T(8,128)S(1)}, u32[]{:S(2)}, u32[]{:S(2)}) collective-permute-start(f32[64,1536]{1,0:T(8,128)S(1)} %get-tuple-element.357.refs_1_), channel_id=1, source_target_pairs={{0,16},{1,9},{2,18},{3,11},{4,20},{5,13},{6,22},{7,15},{8,24},{9,1... | collective-permute-start | bytes 1179656 | tf_op jit(solution)/shard_map/ppermute | solution.py:715
  105.5 7.0 %collective-permute-start.28 = (f32[64,1024]{1,0:T(8,128)S(1)}, f32[64,1024]{1,0:T(8,128)S(1)}, u32[]{:S(2)}, u32[]{:S(2)}) collective-permute-start(f32[64,1024]{1,0:T(8,128)S(1)} %get-tuple-element.371), channel_id=1, source_target_pairs={{0,16},{1,9},{2,18},{3,11},{4,20},{5,13},{6,22},{7,15},{8,24},{9,1... | collective-permute-start | bytes 786440 | tf_op jit(solution)/shard_map/ppermute | solution.py:715
  106.5 9.1 %collective-permute-start.30 = (f32[32,1536]{1,0:T(8,128)S(1)}, f32[32,1536]{1,0:T(8,128)S(1)}, u32[]{:S(2)}, u32[]{:S(2)}) collective-permute-start(f32[32,1536]{1,0:T(8,128)S(1)} %get-tuple-element.388), channel_id=1, source_target_pairs={{0,2},{1,3},{2,0},{3,1},{4,6},{5,7},{6,4},{7,5},{8,10},{9,11},{10,... | collective-permute-start | bytes 589832 | tf_op jit(solution)/shard_map/ppermute | solution.py:715
  108.5 12.1 %collective-permute-start.27 = (f32[128,1536]{1,0:T(8,128)S(1)}, f32[128,1536]{1,0:T(8,128)S(1)}, u32[]{:S(2)}, u32[]{:S(2)}) collective-permute-start(f32[128,1536]{1,0:T(8,128)S(1)} %get-tuple-element.366.refs_1_), channel_id=1, source_target_pairs={{0,8},{1,17},{2,10},{3,19},{4,12},{5,21},{6,14},{7,23},{8,0},{9,25... | collective-permute-start | bytes 2359304 | tf_op jit(solution)/shard_map/ppermute | solution.py:715
  109.1 12.6 %collective-permute-start.32 = (f32[32,1152]{1,0:T(8,128)S(1)}, f32[32,1152]{1,0:T(8,128)S(1)}, u32[]{:S(2)}, u32[]{:S(2)}) collective-permute-start(f32[32,1152]{1,0:T(8,128)S(1)} %get-tuple-element.394.refs_0_), channel_id=1, source_target_pairs={{0,4},{1,5},{2,6},{3,7},{4,0},{5,1},{6,2},{7,3},{8,12},{9,13},{10,... | collective-permute-start | bytes 442376 | tf_op jit(solution)/shard_map/ppermute | solution.py:715
  114.2 7.5 %collective-permute-start.33 = (f32[32,1024]{1,0:T(8,128)S(1)}, f32[32,1024]{1,0:T(8,128)S(1)}, u32[]{:S(2)}, u32[]{:S(2)}) collective-permute-start(f32[32,1024]{1,0:T(8,128)S(1)} %get-tuple-element.396), channel_id=1, source_target_pairs={{0,2},{1,3},{2,0},{3,1},{4,6},{5,7},{6,4},{7,5},{8,10},{9,11},{10,... | collective-permute-start | bytes 393224 | tf_op jit(solution)/shard_map/ppermute | solution.py:715
  115.6 13.9 %collective-permute-start.38 = (f32[32,1536]{1,0:T(8,128)S(1)}, f32[32,1536]{1,0:T(8,128)S(1)}, u32[]{:S(2)}, u32[]{:S(2)}) collective-permute-start(f32[32,1536]{1,0:T(8,128)S(1)} %get-tuple-element.404.refs_0_), channel_id=1, source_target_pairs={{0,4},{1,5},{2,6},{3,7},{4,0},{5,1},{6,2},{7,3},{8,12},{9,13},{10,... | collective-permute-start | bytes 589832 | tf_op jit(solution)/shard_map/ppermute | solution.py:715
  120.5 22.9 %collective-permute-start.40 = (f32[24,1152]{1,0:T(8,128)S(1)}, f32[24,1152]{1,0:T(8,128)S(1)}, u32[]{:S(2)}, u32[]{:S(2)}) collective-permute-start(f32[24,1152]{1,0:T(8,128)S(1)} %get-tuple-element.411.refs_0_), channel_id=1, source_target_pairs={{0,1},{1,0},{2,3},{3,2},{4,5},{5,4},{6,7},{7,6},{8,9},{9,8},{10,11... | collective-permute-start | bytes 331784 | tf_op jit(solution)/shard_map/ppermute | solution.py:687
  120.8 6.4 %collective-permute-start.31 = (f32[128,512]{1,0:T(8,128)S(1)}, f32[128,512]{1,0:T(8,128)S(1)}, u32[]{:S(2)}, u32[]{:S(2)}) collective-permute-start(f32[128,512]{1,0:T(8,128)S(1)} %get-tuple-element.393.refs_1_), channel_id=1, source_target_pairs={{0,16},{1,9},{2,18},{3,11},{4,20},{5,13},{6,22},{7,15},{8,24},{9,1... | collective-permute-start | bytes 786440 | tf_op jit(solution)/shard_map/ppermute | solution.py:715
  121.7 9.2 %collective-permute-start.37 = (f32[256,1536]{1,0:T(8,128)S(1)}, f32[256,1536]{1,0:T(8,128)S(1)}, u32[]{:S(2)}, u32[]{:S(2)}) collective-permute-start(f32[256,1536]{1,0:T(8,128)S(1)} %get-tuple-element.403.refs_1_), channel_id=1, source_target_pairs={{0,1},{1,0},{2,3},{3,2},{4,5},{5,4},{6,7},{7,6},{8,9},{9,8},{10,11... | collective-permute-start | bytes 4718600 | tf_op jit(solution)/shard_map/ppermute | solution.py:687
  121.8 11.7 %collective-permute-start.36 = (f32[32,1152]{1,0:T(8,128)S(1)}, f32[32,1152]{1,0:T(8,128)S(1)}, u32[]{:S(2)}, u32[]{:S(2)}) collective-permute-start(f32[32,1152]{1,0:T(8,128)S(1)} %get-tuple-element.402.refs_1_), channel_id=1, source_target_pairs={{0,16},{1,9},{2,18},{3,11},{4,20},{5,13},{6,22},{7,15},{8,24},{9,1... | collective-permute-start | bytes 442376 | tf_op jit(solution)/shard_map/ppermute | solution.py:715
  127.2 8.9 %collective-permute-start.35 = (f32[32,1024]{1,0:T(8,128)S(1)}, f32[32,1024]{1,0:T(8,128)S(1)}, u32[]{:S(2)}, u32[]{:S(2)}) collective-permute-start(f32[32,1024]{1,0:T(8,128)S(1)} %get-tuple-element.401.refs_0_), channel_id=1, source_target_pairs={{0,4},{1,5},{2,6},{3,7},{4,0},{5,1},{6,2},{7,3},{8,12},{9,13},{10,... | collective-permute-start | bytes 393224 | tf_op jit(solution)/shard_map/ppermute | solution.py:715
  129.6 9.2 %collective-permute-start.34 = (f32[256,512]{1,0:T(8,128)S(1)}, f32[256,512]{1,0:T(8,128)S(1)}, u32[]{:S(2)}, u32[]{:S(2)}) collective-permute-start(f32[256,512]{1,0:T(8,128)S(1)} %get-tuple-element.400.refs_1_), channel_id=1, source_target_pairs={{0,8},{1,17},{2,10},{3,19},{4,12},{5,21},{6,14},{7,23},{8,0},{9,25... | collective-permute-start | bytes 1572872 | tf_op jit(solution)/shard_map/ppermute | solution.py:715
  130.9 8.6 %collective-permute-start.43 = (f32[32,1536]{1,0:T(8,128)S(1)}, f32[32,1536]{1,0:T(8,128)S(1)}, u32[]{:S(2)}, u32[]{:S(2)}) collective-permute-start(f32[32,1536]{1,0:T(8,128)S(1)} %get-tuple-element.414.refs_1_), channel_id=1, source_target_pairs={{0,2},{1,3},{2,0},{3,1},{4,6},{5,7},{6,4},{7,5},{8,10},{9,11},{10,... | collective-permute-start | bytes 589832 | tf_op jit(solution)/shard_map/ppermute | solution.py:715
  133.5 9.7 %collective-permute-start.42 = (f32[64,1152]{1,0:T(8,128)S(1)}, f32[64,1152]{1,0:T(8,128)S(1)}, u32[]{:S(2)}, u32[]{:S(2)}) collective-permute-start(f32[64,1152]{1,0:T(8,128)S(1)} %get-tuple-element.413.refs_1_), channel_id=1, source_target_pairs={{0,8},{1,17},{2,10},{3,19},{4,12},{5,21},{6,14},{7,23},{8,0},{9,25... | collective-permute-start | bytes 884744 | tf_op jit(solution)/shard_map/ppermute | solution.py:715
  136.1 7.2 %collective-permute-start.41 = (f32[32,1024]{1,0:T(8,128)S(1)}, f32[32,1024]{1,0:T(8,128)S(1)}, u32[]{:S(2)}, u32[]{:S(2)}) collective-permute-start(f32[32,1024]{1,0:T(8,128)S(1)} %get-tuple-element.412.refs_1_), channel_id=1, source_target_pairs={{0,2},{1,3},{2,0},{3,1},{4,6},{5,7},{6,4},{7,5},{8,10},{9,11},{10,... | collective-permute-start | bytes 393224 | tf_op jit(solution)/shard_map/ppermute | solution.py:715
  139.6 9.0 %collective-permute-start.45 = (f32[64,1536]{1,0:T(8,128)S(1)}, f32[64,1536]{1,0:T(8,128)S(1)}, u32[]{:S(2)}, u32[]{:S(2)}) collective-permute-start(f32[64,1536]{1,0:T(8,128)S(1)} %get-tuple-element.420.refs_1_), channel_id=1, source_target_pairs={{0,16},{1,9},{2,18},{3,11},{4,20},{5,13},{6,22},{7,15},{8,24},{9,1... | collective-permute-start | bytes 1179656 | tf_op jit(solution)/shard_map/ppermute | solution.py:715
  140.6 11.4 %collective-permute-start.39 = (f32[512,512]{1,0:T(8,128)S(1)}, f32[512,512]{1,0:T(8,128)S(1)}, u32[]{:S(2)}, u32[]{:S(2)}) collective-permute-start(f32[512,512]{1,0:T(8,128)S(1)} %get-tuple-element.410.refs_1_), channel_id=1, source_target_pairs={{0,1},{1,0},{2,3},{3,2},{4,5},{5,4},{6,7},{7,6},{8,9},{9,8},{10,11... | collective-permute-start | bytes 3145736 | tf_op jit(solution)/shard_map/ppermute | solution.py:687
  143.4 6.2 %collective-permute-start.44 = (f32[24,1152]{1,0:T(8,128)S(1)}, f32[24,1152]{1,0:T(8,128)S(1)}, u32[]{:S(2)}, u32[]{:S(2)}) collective-permute-start(f32[24,1152]{1,0:T(8,128)S(1)} %get-tuple-element.419.refs_0_), channel_id=1, source_target_pairs={{0,8},{1,17},{2,10},{3,19},{4,12},{5,21},{6,14},{7,23},{8,0},{9,25... | collective-permute-start | bytes 331784 | tf_op jit(solution)/shard_map/ppermute | solution.py:715
  145.7 9.9 %collective-permute-start.47 = (f32[64,1024]{1,0:T(8,128)S(1)}, f32[64,1024]{1,0:T(8,128)S(1)}, u32[]{:S(2)}, u32[]{:S(2)}) collective-permute-start(f32[64,1024]{1,0:T(8,128)S(1)} %get-tuple-element.428.refs_1_), channel_id=1, source_target_pairs={{0,16},{1,9},{2,18},{3,11},{4,20},{5,13},{6,22},{7,15},{8,24},{9,1... | collective-permute-start | bytes 786440 | tf_op jit(solution)/shard_map/ppermute | solution.py:715
  146.2 12.9 %collective-permute-start.50 = (f32[128,1152]{1,0:T(8,128)S(1)}, f32[128,1152]{1,0:T(8,128)S(1)}, u32[]{:S(2)}, u32[]{:S(2)}) collective-permute-start(f32[128,1152]{1,0:T(8,128)S(1)} %get-tuple-element.433.refs_1_), channel_id=1, source_target_pairs={{0,2},{1,3},{2,0},{3,1},{4,6},{5,7},{6,4},{7,5},{8,10},{9,11},{10,... | collective-permute-start | bytes 1769480 | tf_op jit(solution)/shard_map/ppermute | solution.py:715
  148.8 12.1 %collective-permute-start.49 = (f32[128,1536]{1,0:T(8,128)S(1)}, f32[128,1536]{1,0:T(8,128)S(1)}, u32[]{:S(2)}, u32[]{:S(2)}) collective-permute-start(f32[128,1536]{1,0:T(8,128)S(1)} %get-tuple-element.432.refs_1_), channel_id=1, source_target_pairs={{0,8},{1,17},{2,10},{3,19},{4,12},{5,21},{6,14},{7,23},{8,0},{9,25... | collective-permute-start | bytes 2359304 | tf_op jit(solution)/shard_map/ppermute | solution.py:715
  149.7 7.6 %collective-permute-start.46 = (f32[24,1152]{1,0:T(8,128)S(1)}, f32[24,1152]{1,0:T(8,128)S(1)}, u32[]{:S(2)}, u32[]{:S(2)}) collective-permute-start(f32[24,1152]{1,0:T(8,128)S(1)} %get-tuple-element.427.refs_0_), channel_id=1, source_target_pairs={{0,16},{1,9},{2,18},{3,11},{4,20},{5,13},{6,22},{7,15},{8,24},{9,1... | collective-permute-start | bytes 331784 | tf_op jit(solution)/shard_map/ppermute | solution.py:715
  157.3 4.8 %collective-permute-start.48 = (f32[24,1152]{1,0:T(8,128)S(1)}, f32[24,1152]{1,0:T(8,128)S(1)}, u32[]{:S(2)}, u32[]{:S(2)}) collective-permute-start(f32[24,1152]{1,0:T(8,128)S(1)} %get-tuple-element.431.refs_0_), channel_id=1, source_target_pairs={{0,2},{1,3},{2,0},{3,1},{4,6},{5,7},{6,4},{7,5},{8,10},{9,11},{10,... | collective-permute-start | bytes 331784 | tf_op jit(solution)/shard_map/ppermute | solution.py:715
  157.3 9.2 %collective-permute-start.52 = (f32[128,1024]{1,0:T(8,128)S(1)}, f32[128,1024]{1,0:T(8,128)S(1)}, u32[]{:S(2)}, u32[]{:S(2)}) collective-permute-start(f32[128,1024]{1,0:T(8,128)S(1)} %get-tuple-element.438.refs_1_), channel_id=1, source_target_pairs={{0,8},{1,17},{2,10},{3,19},{4,12},{5,21},{6,14},{7,23},{8,0},{9,25... | collective-permute-start | bytes 1572872 | tf_op jit(solution)/shard_map/ppermute | solution.py:715
  159.2 8.0 %collective-permute-start.55 = (f32[256,1152]{1,0:T(8,128)S(1)}, f32[256,1152]{1,0:T(8,128)S(1)}, u32[]{:S(2)}, u32[]{:S(2)}) collective-permute-start(f32[256,1152]{1,0:T(8,128)S(1)} %get-tuple-element.442.refs_1_), channel_id=1, source_target_pairs={{0,1},{1,0},{2,3},{3,2},{4,5},{5,4},{6,7},{7,6},{8,9},{9,8},{10,11... | collective-permute-start | bytes 3538952 | tf_op jit(solution)/shard_map/ppermute | solution.py:687
  161.0 8.2 %collective-permute-start.54 = (f32[256,1536]{1,0:T(8,128)S(1)}, f32[256,1536]{1,0:T(8,128)S(1)}, u32[]{:S(2)}, u32[]{:S(2)}) collective-permute-start(f32[256,1536]{1,0:T(8,128)S(1)} %get-tuple-element.441.refs_1_), channel_id=1, source_target_pairs={{0,1},{1,0},{2,3},{3,2},{4,5},{5,4},{6,7},{7,6},{8,9},{9,8},{10,11... | collective-permute-start | bytes 4718600 | tf_op jit(solution)/shard_map/ppermute | solution.py:687
  162.1 11.3 %collective-permute-start.51 = (f32[24,1152]{1,0:T(8,128)S(1)}, f32[24,1152]{1,0:T(8,128)S(1)}, u32[]{:S(2)}, u32[]{:S(2)}) collective-permute-start(f32[24,1152]{1,0:T(8,128)S(1)} %get-tuple-element.437.refs_0_), channel_id=1, source_target_pairs={{0,4},{1,5},{2,6},{3,7},{4,0},{5,1},{6,2},{7,3},{8,12},{9,13},{10,... | collective-permute-start | bytes 331784 | tf_op jit(solution)/shard_map/ppermute | solution.py:715
  166.7 4.7 %collective-permute-start.53 = (f32[256,1024]{1,0:T(8,128)S(1)}, f32[256,1024]{1,0:T(8,128)S(1)}, u32[]{:S(2)}, u32[]{:S(2)}) collective-permute-start(f32[256,1024]{1,0:T(8,128)S(1)} %get-tuple-element.440.refs_1_), channel_id=1, source_target_pairs={{0,1},{1,0},{2,3},{3,2},{4,5},{5,4},{6,7},{7,6},{8,9},{9,8},{10,11... | collective-permute-start | bytes 3145736 | tf_op jit(solution)/shard_map/ppermute | solution.py:687
  (16 other events, 26.5 us)
